TPU v7x, 512 devices: a whole 4x4x16 slice. The times are simulated.
512 devices in a mesh: dp: 8 (over z_hi, x), grid: 64 (over z_lo, y, core).
Axes of the slice: x: 4, y: 4, z: 16 (z_hi: 2, z_lo: 8; z = z_hi * 8 + z_lo), core: 2. Of those that a mesh axis runs over, the one named last changes fastest.
Arguments:
- tokens: bfloat16 [8, 128, 64, 512], P('dp', 'grid'), may hold values from -16 to 16
- grad_out: bfloat16 [8, 128, 64, 512], P('dp', 'grid'), may hold values from -6 to 6
- gain: float32 [512], replicated, may hold values from 0.1 to 1.9
- w_qkv: bfloat16 [512, 1536], P('grid'), as said below
- w_out: bfloat16 [512, 512], P('grid'), may hold values from -0.25 to 0.25
Outputs:
- grad_tokens: bfloat16 [8, 128, 64, 512], P('dp', 'grid')
- grad_qkv: float32 [512, 1536], P('grid')
- grad_wout: float32 [512, 512], P('grid')
- grad_gain: float32 [512], replicated
Inputs may be any that keep to these rules, and one draw needn't show every extreme that they name: `w_qkv`: query, key and value projection columns in that order.
All inputs are finite; a program needn't handle non-finite values.
Results may differ from a plain program's by a relative error of at most 0.015.
Values may be sent and summed in bfloat16 or wider, within the bound.
No kernel may reach another device: no remote copies, remote signals or barrier semaphores. Data moves between devices by JAX's collectives and lax.ppermute only.
A program may use at most 64 MiB of HBM per device.

v0:
```python
import jax
import jax.numpy as jnp
from jax import lax
from jax.sharding import PartitionSpec as P

HEADS = 8


EPS = 1e-06


def normalize(block_in, gain):
    values = block_in.astype(jnp.float32)
    inverse = lax.rsqrt(jnp.mean(values * values, axis=-1, keepdims=True) + EPS)
    scaled = values * inverse
    normed = (scaled * gain).astype(jnp.bfloat16)
    return (scaled, inverse, normed)


def attend_backward(queries, keys, values, upstream, heads):
    freq, frames, width = queries.shape
    size = width // heads
    scale = size ** (-0.5)

    def split(arr):
        return arr.reshape(freq, frames, heads, size)

    qry, kys, vls, ups = (split(queries), split(keys), split(values), split(upstream))
    scores = jnp.einsum("fnhd,gnhd->nhfg", qry, kys, preferred_element_type=jnp.float32) * scale
    top = jnp.max(scores, axis=-1, keepdims=True)
    expo = jnp.exp(scores - top)
    probs = expo / jnp.sum(expo, axis=-1, keepdims=True)
    weights = probs.astype(jnp.bfloat16)
    attended = jnp.einsum("nhfg,gnhd->fnhd", weights, vls, preferred_element_type=jnp.float32)
    dprob = jnp.einsum("fnhd,gnhd->nhfg", ups, vls, preferred_element_type=jnp.float32)
    dvals = jnp.einsum("nhfg,fnhd->gnhd", weights, ups, preferred_element_type=jnp.float32)
    dscore = (probs * (dprob - jnp.sum(probs * dprob, axis=-1, keepdims=True)) * scale).astype(
        jnp.bfloat16
    )
    dquery = jnp.einsum("nhfg,gnhd->fnhd", dscore, kys, preferred_element_type=jnp.float32)
    dkey = jnp.einsum("nhfg,fnhd->gnhd", dscore, qry, preferred_element_type=jnp.float32)

    def join(arr):
        return arr.reshape(freq, frames, width).astype(jnp.bfloat16)

    return (join(attended), join(dquery), join(dkey), join(dvals))


def project_in(block_in, block_grad, gain, w_qkv, w_out):
    freq, frames, width = block_in.shape
    scaled, inverse, normed = normalize(block_in, gain)
    flat = normed.reshape(-1, width)
    qkv = jnp.dot(flat, w_qkv, preferred_element_type=jnp.float32).astype(jnp.bfloat16)
    grad_rows = block_grad.reshape(-1, width)
    upstream = lax.dot_general(
        grad_rows, w_out, (((1,), (1,)), ((), ())), preferred_element_type=jnp.float32
    )
    upstream = upstream.astype(jnp.bfloat16)
    return (
        scaled,
        inverse,
        flat,
        grad_rows,
        qkv.reshape(freq, frames, 3 * width),
        upstream.reshape(freq, frames, width),
    )


def attend_all(qkv, upstream):
    width = upstream.shape[-1]
    attended, dquery, dkey, dvals = attend_backward(
        qkv[..., :width], qkv[..., width : 2 * width], qkv[..., 2 * width :], upstream, HEADS
    )
    return (attended, jnp.concatenate([dquery, dkey, dvals], axis=-1))


def finish(scaled, inverse, flat, grad_rows, attended, dqkv, gain, w_qkv):
    width = flat.shape[-1]
    attended_rows = attended.reshape(-1, width)
    dqkv_rows = dqkv.reshape(-1, 3 * width)
    grad_wout = lax.dot_general(
        attended_rows, grad_rows, (((0,), (0,)), ((), ())), preferred_element_type=jnp.float32
    )
    grad_qkv = lax.dot_general(
        flat, dqkv_rows, (((0,), (0,)), ((), ())), preferred_element_type=jnp.float32
    )
    dnormed = lax.dot_general(
        dqkv_rows, w_qkv, (((1,), (1,)), ((), ())), preferred_element_type=jnp.float32
    )
    scaled_rows = scaled.reshape(-1, width)
    inverse_rows = inverse.reshape(-1, 1)
    grad_gain = jnp.sum(dnormed * scaled_rows, axis=0)
    dscaled = dnormed * gain
    result = grad_rows.astype(jnp.float32) + inverse_rows * (
        dscaled - scaled_rows * jnp.mean(dscaled * scaled_rows, axis=-1, keepdims=True)
    )
    return (result.astype(jnp.bfloat16), grad_qkv, grad_wout, grad_gain)


def on_device(tokens, grad_out, gain, w_qkv, w_out):
    full_qkv, full_out = (
        lax.all_gather(w_qkv, "grid", axis=0, tiled=True),
        lax.all_gather(w_out, "grid", axis=0, tiled=True),
    )
    width = tokens.shape[3]
    moved_in, moved_grad = (
        lax.all_to_all(tokens, "grid", split_axis=2, concat_axis=1, tiled=True),
        lax.all_to_all(grad_out, "grid", split_axis=2, concat_axis=1, tiled=True),
    )
    block_in, block_grad = (moved_in[0], moved_grad[0])
    freq, frames = (block_in.shape[0], block_in.shape[1])
    scaled, inverse, flat, grad_rows, qkv, upstream = project_in(
        block_in, block_grad, gain, full_qkv, full_out
    )
    attended, dqkv = attend_all(qkv, upstream)
    result, grad_qkv, grad_wout, grad_gain = finish(
        scaled, inverse, flat, grad_rows, attended, dqkv, gain, full_qkv
    )
    grad_tokens = lax.all_to_all(
        result.reshape(1, freq, frames, width), "grid", split_axis=1, concat_axis=2, tiled=True
    )
    shard_qkv, shard_wout = (
        lax.psum_scatter(grad_qkv, "grid", scatter_dimension=0, tiled=True),
        lax.psum_scatter(grad_wout, "grid", scatter_dimension=0, tiled=True),
    )
    shard_qkv, shard_wout = (
        lax.psum(shard_qkv.astype(jnp.bfloat16), "dp").astype(jnp.float32),
        lax.psum(shard_wout.astype(jnp.bfloat16), "dp").astype(jnp.float32),
    )
    total_gain = lax.psum(grad_gain, ("dp", "grid"))
    return (grad_tokens, shard_qkv, shard_wout, total_gain)


def solution(mesh):
    placed = (
        P("dp", "grid", None, None),
        P("dp", "grid", None, None),
        P(),
        P("grid", None),
        P("grid", None),
    )
    return jax.shard_map(
        on_device,
        mesh=mesh,
        in_specs=placed,
        out_specs=(P("dp", "grid", None, None), P("grid", None), P("grid", None), P()),
        check_vma=False,
    )
```

profile of v0, /device:TPU:0, one launch (start us, length us, event | category | flops | bytes accessed | tf_op | source)
XLA Modules:
  0.0 1083.3 jit_solution(16730877820972936392)
XLA Ops:
  7.2 0.7 all-gather.2.cloned.1.call-update
  7.9 1.7 copy.51
  9.6 10.8 all-to-all-start.1
  20.4 1.7 copy.50
  22.1 12.9 %all-to-all-done.1 = bf16[1,2,64,512]{3,1,0,2:T(2,128)(2,1)S(1)} async-done(((bf16[1,2,64,512]{3,1,0,2:T(2,128)(2,1)}), bf16[1,2,64,512]{3,1,0,2:T(2,128)(2,1)S(1)}, u32[]{:S(2)}, u32[]{:S(2)}) %all-to-all-start.1) | async-done | bytes 131104 | tf_op jit(solution)/shard_map/all_to_all | solution.py:107
  35.0 5.8 all-to-all-start
  41.4 14.6 %all-to-all-done = bf16[1,2,64,512]{3,1,0,2:T(2,128)(2,1)S(1)} async-done(((bf16[1,2,64,512]{3,1,0,2:T(2,128)(2,1)}), bf16[1,2,64,512]{3,1,0,2:T(2,128)(2,1)S(1)}, u32[]{:S(2)}, u32[]{:S(2)}) %all-to-all-start) | async-done | bytes 131104 | tf_op jit(solution)/shard_map/all_to_all | solution.py:108
  56.3 74.3 %all-gather.2.cloned.1.call-done = bf16[512,1536]{1,0:T(8,128)(2,1)} async-done(((bf16[8,1536]{1,0:T(8,128)(2,1)}), bf16[512,1536]{1,0:T(8,128)(2,1)}) %all-gather.2.cloned.1.call-update) | async-done | bytes 1572880 | tf_op jit(solution)/shard_map/all_gather | solution.py:102
  130.7 1.8 fusion.2
  132.9 0.4 fusion.34
  133.3 0.5 convolution_convert_fusion.1
  133.8 1.3 fusion.36
  135.2 118.2 %all_gather.7 = bf16[512,512]{1,0:T(8,128)(2,1)S(1)} all-gather(bf16[8,512]{1,0:T(8,128)(2,1)S(1)} %copy-done.2), channel_id=1, replica_groups=mesh['dp'=8,'grid'=64] {'grid'}, dimensions={0}, use_global_device_ids=true | all-gather | bytes 532480 | tf_op jit(solution)/shard_map/all_gather | solution.py:103
  253.4 0.4 reshape.278
  255.5 0.5 convolution_convert_fusion.2
  256.1 2.3 fusion.16
  258.4 1.4 copy-done
  259.7 0.7 multiply_reduce_fusion.1
  260.8 0.5 broadcast.114
  261.4 1.4 reduce.12
  262.8 0.7 reshape.282
  263.5 4.6 all-to-all-start.2
  268.1 108.0 %psum.23 = f32[512]{0:T(512)} all-reduce(f32[512]{0:T(512)S(1)} %get-tuple-element.8), channel_id=1, replica_groups=mesh['dp'=8,'grid'=64] {'dp','grid'}, use_global_device_ids=true, to_apply=%region_10.0 | all-reduce | flops 512 | bytes 4096 | tf_op jit(solution)/shard_map/psum | solution.py:130
  376.2 0.7 bitcast_reduce_fusion
  377.0 0.7 copy.63
  377.7 190.6 %reduce-scatter.5.cloned.1.call-done = f32[8,512]{1,0:T(8,128)} async-done(((f32[512,512]{1,0:T(8,128)}), f32[8,512]{1,0:T(8,128)}) %reduce-scatter.5.cloned.1.call-update) | async-done | bytes 16400 | tf_op jit(solution)/shard_map/reduce_scatter | solution.py:124
  568.3 0.7 convert_element_type.207
  569.0 434.0 %reduce-scatter.3.cloned.1.call-done = f32[8,1536]{1,0:T(8,128)} async-done(((f32[512,1536]{1,0:T(8,128)}), f32[8,1536]{1,0:T(8,128)}) %reduce-scatter.3.cloned.1.call-update) | async-done | bytes 49168 | tf_op jit(solution)/shard_map/reduce_scatter | solution.py:123
  1003.0 0.8 convert_element_type.201
  1003.8 71.7 %all-reduce = (bf16[8,1536]{1,0:T(8,128)(2,1)S(1)}, bf16[8,512]{1,0:T(8,128)(2,1)S(1)}) all-reduce(bf16[8,1536]{1,0:T(8,128)(2,1)S(1)} %convert_element_type.201, bf16[8,512]{1,0:T(8,128)(2,1)S(1)} %convert_element_type.207), channel_id=1, replica_groups=mesh['dp'=8,'grid'=64] {'dp'}, use_global_device_ids=true, to_apply=%region_6.0 | all-reduce | flops 16384 | bytes 65536 | tf_op jit(solution)/shard_map/psum | solution.py:127
  1075.5 0.6 convert_element_type.208
  1076.1 0.6 convert_element_type.202
  (34 shorter events, 3.6 us)
Async XLA Ops:
  7.2 123.5 %copy-start.1 = (f32[512]{0:T(512)S(1)}, f32[512]{0:T(512)}, u32[]{:S(2)}) copy-start(f32[512]{0:T(512)} %param.7) | copy-start | bytes 6148
  7.2 123.5 %all-gather.2.cloned.1.call-start = ((), (), s32[]{:S(2)}) async-start(), calls=%async_computation.5 | async-start | bytes 1597440 | tf_op jit(solution)/shard_map/all_gather | solution.py:102
  9.6 25.4 %all-to-all-start.1 = ((bf16[1,2,64,512]{3,1,0,2:T(2,128)(2,1)}), bf16[1,2,64,512]{3,1,0,2:T(2,128)(2,1)S(1)}, u32[]{:S(2)}, u32[]{:S(2)}) async-start(bf16[1,2,64,512]{3,1,0,2:T(2,128)(2,1)} %copy.51), calls=%async_computation.1 | async-start | bytes 262144 | tf_op jit(solution)/shard_map/all_to_all | solution.py:107
  35.0 21.0 %all-to-all-start = ((bf16[1,2,64,512]{3,1,0,2:T(2,128)(2,1)}), bf16[1,2,64,512]{3,1,0,2:T(2,128)(2,1)S(1)}, u32[]{:S(2)}, u32[]{:S(2)}) async-start(bf16[1,2,64,512]{3,1,0,2:T(2,128)(2,1)} %copy.50), calls=%async_computation | async-start | bytes 262144 | tf_op jit(solution)/shard_map/all_to_all | solution.py:108
  40.8 527.5 %reduce-scatter.5.cloned.1.call-start = ((), (), s32[]{:S(2)}) async-start(), calls=%async_computation.7 | async-start | bytes 1064960 | tf_op jit(solution)/shard_map/reduce_scatter | solution.py:124
  133.8 1.4 copy-start.2
  135.2 867.8 %reduce-scatter.3.cloned.1.call-start = ((), (), s32[]{:S(2)}) async-start(), calls=%async_computation.6 | async-start | bytes 3194880 | tf_op jit(solution)/shard_map/reduce_scatter | solution.py:123
  258.3 1.4 copy-start
  263.5 112.6 %all-to-all-start.2 = ((bf16[64,2,512]{2,1,0:T(2,128)(2,1)}), bf16[64,2,512]{2,1,0:T(2,128)(2,1)S(1)}, u32[]{:S(2)}, u32[]{:S(2)}) async-start(bf16[64,2,512]{2,1,0:T(2,128)(2,1)} %reshape.282), calls=%async_computation.2 | async-start | bytes 262144 | tf_op jit(solution)/shard_map/all_to_all | solution.py:119
Sparse Core Ops, SparseCore 0:
  10.2 120.4 all-gather.1
  135.3 432.9 reduce-scatter.4
  571.3 431.6 reduce-scatter.2
where the time goes:
time: 1080 us
  waiting for transfers between devices  727 us (67%)
  blocking collectives  298 us (28%)
  starting transfers between devices  21.3 us (2%)
  between operations  14 us (1%)
    reduce_scatter x1, waiting for transfers between devices, on_device(): lax.psum_scatter(grad_qkv, 'grid', scatter_dimension=0, tiled=True)  434 us
    reduce_scatter x1, waiting for transfers between devices, on_device(): lax.psum_scatter(grad_wout, 'grid', scatter_dimension=0, tiled=True)  191 us
    all_gather x1, blocking collectives, on_device(): lax.all_gather(w_out, 'grid', axis=0, tiled=True)  118 us
    psum x1, blocking collectives, on_device(): total_gain = lax.psum(grad_gain, ('dp', 'grid'))  108 us
    all_gather x1, waiting for transfers between devices, on_device(): lax.all_gather(w_qkv, 'grid', axis=0, tiled=True)  74.3 us
    psum x1, blocking collectives, on_device(): lax.psum(shard_qkv.astype(jnp.bfloat16), 'dp').astype(jnp.float32)  71.7 us
  transfers between devices with their start and end apart: 6, of which 5 were waited for; matrix products, arithmetic and copies ran while one was open for 1% of the time, Pallas kernels for 0%

commit v1 on v0

v1 whole, which is shorter than its diff:
```python
import jax
import jax.numpy as jnp
from jax import lax
from jax.sharding import Mesh
from jax.sharding import PartitionSpec as P

HEADS = 8
EPS = 1e-06
BF = jnp.bfloat16
F32 = jnp.float32

ZH, X, ZL, Y, C = 2, 4, 8, 4, 2
ND = ZL * Y
SWAP = [(0, 1), (1, 0)]


def share(block, axes, count):
    wide = jnp.broadcast_to(block[None], (count,) + block.shape)
    return lax.all_to_all(wide, axes, split_axis=0, concat_axis=0, tiled=True)


def gather_weights(w_qkv, w_out, core):
    halves = w_qkv.reshape(8, 3, 2, 256)
    mine = lax.dynamic_index_in_dim(halves, core, 2, keepdims=False).reshape(8, 768)
    other = lax.dynamic_index_in_dim(halves, 1 - core, 2, keepdims=False).reshape(8, 768)
    sent = jnp.concatenate([other, w_out], axis=1)
    got = lax.ppermute(sent, "c", SWAP)
    kept = jnp.concatenate([mine, w_out], axis=1)
    first = jnp.where(core == 0, kept, got)
    second = jnp.where(core == 0, got, kept)
    rows = jnp.concatenate([first, second], axis=0)
    plane = share(rows, "zl", ZL)
    out_part = lax.dynamic_slice_in_dim(plane[:, :, 768:], core * 4, 4, 0)
    out_part = out_part.reshape(4, 16, 2, 256).transpose(2, 0, 1, 3).reshape(8, 16, 256)
    block = jnp.concatenate([plane[:, :, :768], out_part], axis=2)
    full = share(block, "y", Y)
    wh = full[..., :768].transpose(1, 0, 2, 3).reshape(512, 768)
    wo = full[..., 768:].reshape(Y, 2, 4, 16, 256).transpose(2, 0, 3, 1, 4).reshape(256, 512)
    return wh, wo


def normalize(tokens, gain):
    values = tokens.astype(F32)
    inverse = lax.rsqrt(jnp.mean(values * values, axis=-1, keepdims=True) + EPS)
    scaled = values * inverse
    return scaled, inverse, (scaled * gain).astype(BF)


def attend(qkv, ups):
    q, k, v = (qkv[..., i * 256 : (i + 1) * 256].reshape(2, 128, 4, 64) for i in range(3))
    u = ups.reshape(2, 128, 4, 64)
    scale = 64 ** (-0.5)
    scores = jnp.einsum("nfhd,nghd->nhfg", q, k, preferred_element_type=F32) * scale
    top = jnp.max(scores, axis=-1, keepdims=True)
    expo = jnp.exp(scores - top)
    probs = expo / jnp.sum(expo, axis=-1, keepdims=True)
    weights = probs.astype(BF)
    att = jnp.einsum("nhfg,nghd->nfhd", weights, v, preferred_element_type=F32)
    dprob = jnp.einsum("nfhd,nghd->nhfg", u, v, preferred_element_type=F32)
    dv = jnp.einsum("nhfg,nfhd->nghd", weights, u, preferred_element_type=F32)
    ds = (probs * (dprob - jnp.sum(probs * dprob, axis=-1, keepdims=True)) * scale).astype(BF)
    dq = jnp.einsum("nhfg,nghd->nfhd", ds, k, preferred_element_type=F32)
    dk = jnp.einsum("nhfg,nfhd->nghd", ds, q, preferred_element_type=F32)

    def join(arr):
        return arr.reshape(2, 128, 256).astype(BF)

    return join(att), jnp.concatenate([join(dq), join(dk), join(dv)], axis=-1)


def on_device(tokens, grad_out, gain, w_qkv, w_out):
    core = lax.axis_index("c")
    third = lax.axis_index("x") == 3

    both = jnp.stack([tokens[0], grad_out[0]])
    both = both.reshape(2, 2, 2, ND, 512).transpose(3, 0, 2, 1, 4)
    moved = lax.all_to_all(
        both.reshape(ND, 8, 512), ("zl", "y"), split_axis=0, concat_axis=0, tiled=True
    )
    far = lax.ppermute(moved, "c", SWAP)

    def rows_of(arr):
        return arr.reshape(ND, 2, 2, 2, 512).transpose(1, 2, 0, 3, 4).reshape(2, 2, 64, 512)

    pair = jnp.concatenate([rows_of(moved), rows_of(far)], axis=2)
    x_in, g_in = pair[0], pair[1]

    wh, wo = gather_weights(w_qkv, w_out, core)

    scaled, inverse, normed = normalize(x_in, gain)
    flat = normed.reshape(256, 512)
    grows = g_in.reshape(256, 512)
    qkv = jnp.dot(flat, wh, preferred_element_type=F32).astype(BF)
    ups = lax.dot_general(grows, wo, (((1,), (1,)), ((), ())), preferred_element_type=F32)
    ups = ups.astype(BF)
    att, dqkv = attend(qkv.reshape(2, 128, 768), ups.reshape(2, 128, 256))
    att, dqkv = att.reshape(256, 256), dqkv.reshape(256, 768)

    over = (((0,), (0,)), ((), ()))
    g_wout = lax.dot_general(att, grows, over, preferred_element_type=F32).astype(BF)
    g_qkv = lax.dot_general(flat, dqkv, over, preferred_element_type=F32).astype(BF)
    dn = lax.dot_general(dqkv, wh, (((1,), (1,)), ((), ())), preferred_element_type=F32)
    dn = dn.reshape(2, 128, 512)

    q_part = g_qkv.reshape(ND, 2, 8, 3, 256).transpose(3, 1, 0, 2, 4).reshape(3, 2, 256, 256)
    o_part = g_wout.reshape(16, 2, 8, 2, 256).transpose(1, 3, 0, 2, 4).reshape(1, 2, 256, 256)
    parts = jnp.concatenate([q_part, o_part], axis=0).reshape(8, 256, 256)
    got = lax.all_to_all(parts, ("x", "c"), split_axis=0, concat_axis=0, tiled=True)
    part = jnp.sum(got.reshape(X, C, 256, 256).astype(F32), axis=0).astype(BF)
    as_cols = jnp.concatenate([part[0], part[1]], axis=1)
    as_rows = part.reshape(2, 2, 128, 256).transpose(0, 2, 1, 3).reshape(256, 512)
    part = jnp.where(third, as_rows, as_cols)

    dn_far = lax.ppermute(dn[:, 64:].astype(BF), "c", SWAP)
    dn_own = dn[:, :64] + dn_far.astype(F32)
    s_own, i_own, g_own = scaled[:, :64], inverse[:, :64], g_in[:, :64].astype(F32)
    gg = jnp.sum(dn_own * s_own, axis=(0, 1))
    dscaled = dn_own * gain
    result = g_own + i_own * (
        dscaled - s_own * jnp.mean(dscaled * s_own, axis=-1, keepdims=True)
    )
    result = result.astype(BF)
    gg = gg + lax.ppermute(gg, "c", SWAP)

    def split(vec):
        high = vec.astype(BF)
        low = (vec - high.astype(F32)).astype(BF)
        return jnp.concatenate([high, low])

    out_rows = result.reshape(2, ND, 2, 512).transpose(1, 0, 2, 3).reshape(ND, 2048)
    gain_rows = jnp.broadcast_to(split(gg)[None], (ND, 1024))
    sent = jnp.concatenate([part.reshape(ND, 4096), out_rows, gain_rows], axis=1)
    back = lax.all_to_all(
        sent.reshape(ND, 7, 1024), ("zl", "y"), split_axis=0, concat_axis=0, tiled=True
    ).reshape(ND, 7168)
    grads = jnp.sum(back[:, :4096].astype(F32), axis=0).astype(BF)
    gg = jnp.sum(back[:, 6144:].reshape(ND, 2, 512).astype(F32), axis=(0, 1))
    grad_tokens = (
        back[:, 4096:6144].reshape(ND, 2, 2, 512).transpose(2, 1, 0, 3).reshape(1, 2, 64, 512)
    )

    last = jnp.concatenate([grads, split(gg)])
    all_dp = share(last.reshape(10, 512), ("zh", "x"), ZH * X).astype(F32)
    sums = jnp.sum(all_dp[:, :8].reshape(ZH, X, 8, 512), axis=0)
    shard_qkv = jnp.concatenate([sums[0], sums[1], sums[2]], axis=1)
    shard_wout = sums[3]
    total_gain = jnp.sum(all_dp[:, 8:], axis=(0, 1))
    return grad_tokens, shard_qkv, shard_wout, total_gain


def solution(mesh):
    inner = Mesh(mesh.devices.reshape(ZH, X, ZL, Y, C), ("zh", "x", "zl", "y", "c"))
    grid = ("zl", "y", "c")
    tok = P(("zh", "x"), grid, None, None)
    return jax.shard_map(
        on_device,
        mesh=inner,
        in_specs=(tok, tok, P(), P(grid, None), P(grid, None)),
        out_specs=(tok, P(grid, None), P(grid, None), P()),
        check_vma=False,
    )
```

time: 1080 us -> 181 us (0.17)
  the two profiles are of different devices: /device:TPU:0 before, /device:TPU:32 now
where the time goes in v1:
time: 181 us; the launch traced here: 180 us
  waiting for transfers between devices  74.2 us (41%)
  starting transfers between devices  45.6 us (25%)
  blocking collectives  35.7 us (20%)
  local copies, waits for them, and re-layouts  11.5 us (6%)
  matrix products  7.27 us (4%)
  other arithmetic  4.56 us (3%)
    all_to_all x3, waiting for transfers between devices, share(): return lax.all_to_all(wide, axes, split_axis=0, concat_axis=0, tiled=True)  45.2 us
    all_to_all x1, blocking collectives, on_device(): lax.all_to_all(sent.reshape(ND, 7, 1024), ('zl', 'y'), split_axis=0, conc...  35.7 us
    all_to_all x3, starting transfers between devices, share(): return lax.all_to_all(wide, axes, split_axis=0, concat_axis=0, tiled=True)  17.5 us
    all_to_all x1, starting transfers between devices, on_device(): lax.all_to_all(both.reshape(ND, 8, 512), ('zl', 'y'), split_axis=0, conca...  15.4 us
    all_to_all x1, waiting for transfers between devices, on_device(): lax.all_to_all(both.reshape(ND, 8, 512), ('zl', 'y'), split_axis=0, conca...  14.8 us
    all_to_all x1, waiting for transfers between devices, on_device(): lax.all_to_all(parts, ('x', 'c'), split_axis=0, concat_axis=0, tiled=True)  12.6 us
    all_to_all x1, starting transfers between devices, on_device(): lax.all_to_all(parts, ('x', 'c'), split_axis=0, concat_axis=0, tiled=True)  4.52 us
  transfers between devices with their start and end apart: 9, of which 7 were waited for; matrix products, arithmetic and copies ran while one was open for 3% of the time, Pallas kernels for 0%

profile of v1, /device:TPU:32, one launch (start us, length us, event | category | flops | bytes accessed | tf_op | source)
XLA Modules:
  0.0 180.1 jit_solution(15198303001961853239)
XLA Ops:
  0.7 1.0 pad_maximum_fusion.2
  1.7 0.8 copy.130
  2.5 15.4 %all-to-all-start = ((bf16[32,8,512]{2,1,0:T(8,128)(2,1)}), bf16[32,8,512]{2,1,0:T(8,128)(2,1)S(1)}, u32[]{:S(2)}, u32[]{:S(2)}) async-start(bf16[32,8,512]{2,1,0:T(8,128)(2,1)} %copy.130), calls=%async_computation | async-start | bytes 524288 | tf_op jit(solution)/shard_map/all_to_all | solution.py:77
  18.0 1.9 %collective-permute-start.1 = (bf16[8,1280]{1,0:T(8,128)(2,1)S(1)}, bf16[8,1280]{1,0:T(8,128)(2,1)S(1)}, u32[]{:S(2)}, u32[]{:S(2)}) collective-permute-start(bf16[8,1280]{1,0:T(8,128)(2,1)S(1)} %pad_maximum_fusion.9), channel_id=1, source_target_pairs={{0,1},{1,0},{2,3},{3,2},{4,5},{5,4},{6,7},{7,6},{8,9},{9,8},{10,11... | collective-permute-start | bytes 61448 | tf_op jit(solution)/shard_map/ppermute | solution.py:27
  19.9 1.2 collective-permute-done.1
  21.1 14.8 %all-to-all-done = bf16[32,8,512]{2,1,0:T(8,128)(2,1)S(1)} async-done(((bf16[32,8,512]{2,1,0:T(8,128)(2,1)}), bf16[32,8,512]{2,1,0:T(8,128)(2,1)S(1)}, u32[]{:S(2)}, u32[]{:S(2)}) %all-to-all-start) | async-done | bytes 262176 | tf_op jit(solution)/shard_map/all_to_all | solution.py:77
  36.0 0.7 broadcast_in_dim.10
  36.7 5.8 %all-to-all-start.1 = ((bf16[8,16,1280]{2,1,0:T(8,128)(2,1)}), bf16[8,16,1280]{2,1,0:T(8,128)(2,1)S(1)}, u32[]{:S(2)}, u32[]{:S(2)}) async-start(bf16[8,16,1280]{2,1,0:T(8,128)(2,1)} %broadcast_in_dim.10), calls=%async_computation.1 | async-start | bytes 655360 | tf_op jit(solution)/shard_map/all_to_all | solution.py:19
  42.5 1.9 %collective-permute-start = (bf16[32,8,512]{2,0,1:T(8,128)(2,1)S(1)}, bf16[32,8,512]{2,0,1:T(8,128)(2,1)S(1)}, u32[]{:S(2)}, u32[]{:S(2)}) collective-permute-start(bf16[32,8,512]{2,0,1:T(8,128)(2,1)S(1)} %copy.131), channel_id=1, source_target_pairs={{0,1},{1,0},{2,3},{3,2},{4,5},{5,4},{6,7},{7,6},{8,9},{9,8},{10,11... | collective-permute-start | bytes 786440 | tf_op jit(solution)/shard_map/ppermute | solution.py:80
  44.9 15.8 %all-to-all-done.1 = bf16[8,16,1280]{2,1,0:T(8,128)(2,1)S(1)} async-done(((bf16[8,16,1280]{2,1,0:T(8,128)(2,1)}), bf16[8,16,1280]{2,1,0:T(8,128)(2,1)S(1)}, u32[]{:S(2)}, u32[]{:S(2)}) %all-to-all-start.1) | async-done | bytes 327712 | tf_op jit(solution)/shard_map/all_to_all | solution.py:19
  60.8 1.1 broadcast_in_dim.11
  62.0 3.5 %all-to-all-start.2 = ((bf16[4,8,16,1024]{3,2,1,0:T(8,128)(2,1)}), bf16[4,8,16,1024]{3,2,1,0:T(8,128)(2,1)S(1)}, u32[]{:S(2)}, u32[]{:S(2)}) async-start(bf16[4,8,16,1024]{3,2,1,0:T(8,128)(2,1)} %broadcast_in_dim.11), calls=%async_computation.2 | async-start | bytes 2097152 | tf_op jit(solution)/shard_map/all_to_all | solution.py:19
  66.1 0.8 fusion.36
  67.1 12.2 %all-to-all-done.2 = bf16[4,8,16,1024]{3,2,1,0:T(8,128)(2,1)S(1)} async-done(((bf16[4,8,16,1024]{3,2,1,0:T(8,128)(2,1)}), bf16[4,8,16,1024]{3,2,1,0:T(8,128)(2,1)S(1)}, u32[]{:S(2)}, u32[]{:S(2)}) %all-to-all-start.2) | async-done | bytes 1048608 | tf_op jit(solution)/shard_map/all_to_all | solution.py:19
  79.8 0.7 fusion.37
  80.5 1.0 copy.141
  83.0 1.2 fusion.38
  84.2 1.5 convolution_convert_fusion.5
  85.7 1.5 convolution_convert_fusion.4
  89.6 1.9 %collective-permute-start.2 = (bf16[2,64,512]{2,1,0:T(8,128)(2,1)S(1)}, bf16[2,64,512]{2,1,0:T(8,128)(2,1)S(1)}, u32[]{:S(2)}, u32[]{:S(2)}) collective-permute-start(bf16[2,64,512]{2,1,0:T(8,128)(2,1)S(1)} %slice.155), channel_id=1, source_target_pairs={{0,1},{1,0},{2,3},{3,2},{4,5},{5,4},{6,7},{7,6},{8,9},{9,8},{10,11... | collective-permute-start | bytes 393224 | tf_op jit(solution)/shard_map/ppermute | solution.py:114
  92.0 1.1 pad_maximum_fusion
  93.1 4.5 %all-to-all-start.3 = ((bf16[8,256,256]{2,1,0:T(8,128)(2,1)}), bf16[8,256,256]{2,1,0:T(8,128)(2,1)S(1)}, u32[]{:S(2)}, u32[]{:S(2)}) async-start(bf16[8,256,256]{2,1,0:T(8,128)(2,1)} %bitcast.37), calls=%async_computation.3 | async-start | bytes 2097152 | tf_op jit(solution)/shard_map/all_to_all | solution.py:108
  97.8 2.4 %collective-permute-start.3 = (f32[512]{0:T(512)S(1)}, f32[512]{0:T(512)S(1)}, u32[]{:S(2)}, u32[]{:S(2)}) collective-permute-start(f32[512]{0:T(512)S(1)} %get-tuple-element.4), channel_id=1, source_target_pairs={{0,1},{1,0},{2,3},{3,2},{4,5},{5,4},{6,7},{7,6},{8,9},{9,8},{10,11... | collective-permute-start | bytes 6152 | tf_op jit(solution)/shard_map/ppermute | solution.py:123
  101.0 12.6 %all-to-all-done.3 = bf16[8,256,256]{2,1,0:T(8,128)(2,1)S(1)} async-done(((bf16[8,256,256]{2,1,0:T(8,128)(2,1)}), bf16[8,256,256]{2,1,0:T(8,128)(2,1)S(1)}, u32[]{:S(2)}, u32[]{:S(2)}) %all-to-all-start.3) | async-done | bytes 1048608 | tf_op jit(solution)/shard_map/all_to_all | solution.py:108
  115.2 35.7 %all_to_all.30 = bf16[32,7,1024]{2,1,0:T(8,128)(2,1)S(1)} all-to-all(bf16[32,7,1024]{2,1,0:T(8,128)(2,1)S(1)} %reshape.218), channel_id=1, replica_groups=mesh['zh'=2,'x'=4,'zl'=8,'y'=4,'c'=2] {'zl','y'}, dimensions={0} | all-to-all | bytes 917504 | tf_op jit(solution)/shard_map/all_to_all | solution.py:133
  151.4 0.6 broadcast_in_dim.14
  152.1 8.2 %all-to-all-start.5 = ((bf16[8,10,512]{2,1,0:T(8,128)(2,1)}), bf16[8,10,512]{2,1,0:T(8,128)(2,1)S(1)}, u32[]{:S(2)}, u32[]{:S(2)}) async-start(bf16[8,10,512]{2,1,0:T(8,128)(2,1)} %broadcast_in_dim.14), calls=%async_computation.5 | async-start | bytes 262144 | tf_op jit(solution)/shard_map/all_to_all | solution.py:19
  160.4 0.7 copy.157
  161.0 17.2 %all-to-all-done.5 = bf16[8,10,512]{2,1,0:T(8,128)(2,1)S(1)} async-done(((bf16[8,10,512]{2,1,0:T(8,128)(2,1)}), bf16[8,10,512]{2,1,0:T(8,128)(2,1)S(1)}, u32[]{:S(2)}, u32[]{:S(2)}) %all-to-all-start.5) | async-done | bytes 81952 | tf_op jit(solution)/shard_map/all_to_all | solution.py:19
  178.2 0.6 slice_bitcast_fusion.3
  178.9 0.6 slice_reduce_fusion.1
  179.5 0.6 pad_maximum_fusion.7
  (88 shorter events, 9.2 us)
Async XLA Ops:
  0.6 17.3 %copy-start.2 = (bf16[8,1536]{1,0:T(8,128)(2,1)S(1)}, bf16[8,1536]{1,0:T(8,128)(2,1)}, u32[]{:S(2)}) copy-start(bf16[8,1536]{1,0:T(8,128)(2,1)} %param.8) | copy-start | bytes 73732
  0.6 17.3 %copy-start.1 = (bf16[8,512]{1,0:T(8,128)(2,1)S(1)}, bf16[8,512]{1,0:T(8,128)(2,1)}, u32[]{:S(2)}) copy-start(bf16[8,512]{1,0:T(8,128)(2,1)} %param.9) | copy-start | bytes 24580
  2.5 33.4 %all-to-all-start = ((bf16[32,8,512]{2,1,0:T(8,128)(2,1)}), bf16[32,8,512]{2,1,0:T(8,128)(2,1)S(1)}, u32[]{:S(2)}, u32[]{:S(2)}) async-start(bf16[32,8,512]{2,1,0:T(8,128)(2,1)} %copy.130), calls=%async_computation | async-start | bytes 524288 | tf_op jit(solution)/shard_map/all_to_all | solution.py:77
  18.0 3.1 %collective-permute-start.1 = (bf16[8,1280]{1,0:T(8,128)(2,1)S(1)}, bf16[8,1280]{1,0:T(8,128)(2,1)S(1)}, u32[]{:S(2)}, u32[]{:S(2)}) collective-permute-start(bf16[8,1280]{1,0:T(8,128)(2,1)S(1)} %pad_maximum_fusion.9), channel_id=1, source_target_pairs={{0,1},{1,0},{2,3},{3,2},{4,5},{5,4},{6,7},{7,6},{8,9},{9,8},{10,11... | collective-permute-start | bytes 61448 | tf_op jit(solution)/shard_map/ppermute | solution.py:27
  36.7 24.0 %all-to-all-start.1 = ((bf16[8,16,1280]{2,1,0:T(8,128)(2,1)}), bf16[8,16,1280]{2,1,0:T(8,128)(2,1)S(1)}, u32[]{:S(2)}, u32[]{:S(2)}) async-start(bf16[8,16,1280]{2,1,0:T(8,128)(2,1)} %broadcast_in_dim.10), calls=%async_computation.1 | async-start | bytes 655360 | tf_op jit(solution)/shard_map/all_to_all | solution.py:19
  42.5 22.9 %collective-permute-start = (bf16[32,8,512]{2,0,1:T(8,128)(2,1)S(1)}, bf16[32,8,512]{2,0,1:T(8,128)(2,1)S(1)}, u32[]{:S(2)}, u32[]{:S(2)}) collective-permute-start(bf16[32,8,512]{2,0,1:T(8,128)(2,1)S(1)} %copy.131), channel_id=1, source_target_pairs={{0,1},{1,0},{2,3},{3,2},{4,5},{5,4},{6,7},{7,6},{8,9},{9,8},{10,11... | collective-permute-start | bytes 786440 | tf_op jit(solution)/shard_map/ppermute | solution.py:80
  62.0 17.3 %all-to-all-start.2 = ((bf16[4,8,16,1024]{3,2,1,0:T(8,128)(2,1)}), bf16[4,8,16,1024]{3,2,1,0:T(8,128)(2,1)S(1)}, u32[]{:S(2)}, u32[]{:S(2)}) async-start(bf16[4,8,16,1024]{3,2,1,0:T(8,128)(2,1)} %broadcast_in_dim.11), calls=%async_computation.2 | async-start | bytes 2097152 | tf_op jit(solution)/shard_map/all_to_all | solution.py:19
  65.8 1.1 copy-start.3
  89.6 8.0 %collective-permute-start.2 = (bf16[2,64,512]{2,1,0:T(8,128)(2,1)S(1)}, bf16[2,64,512]{2,1,0:T(8,128)(2,1)S(1)}, u32[]{:S(2)}, u32[]{:S(2)}) collective-permute-start(bf16[2,64,512]{2,1,0:T(8,128)(2,1)S(1)} %slice.155), channel_id=1, source_target_pairs={{0,1},{1,0},{2,3},{3,2},{4,5},{5,4},{6,7},{7,6},{8,9},{9,8},{10,11... | collective-permute-start | bytes 393224 | tf_op jit(solution)/shard_map/ppermute | solution.py:114
  93.1 7.1 %copy-start = (bf16[2,128,512]{2,1,0:T(8,128)(2,1)S(1)}, bf16[2,128,512]{2,1,0:T(8,128)(2,1)}, u32[]{:S(2)}) copy-start(bf16[2,128,512]{2,1,0:T(8,128)(2,1)} %get-tuple-element.9) | copy-start | bytes 786436
  93.1 20.5 %all-to-all-start.3 = ((bf16[8,256,256]{2,1,0:T(8,128)(2,1)}), bf16[8,256,256]{2,1,0:T(8,128)(2,1)S(1)}, u32[]{:S(2)}, u32[]{:S(2)}) async-start(bf16[8,256,256]{2,1,0:T(8,128)(2,1)} %bitcast.37), calls=%async_computation.3 | async-start | bytes 2097152 | tf_op jit(solution)/shard_map/all_to_all | solution.py:108
  97.8 3.2 %collective-permute-start.3 = (f32[512]{0:T(512)S(1)}, f32[512]{0:T(512)S(1)}, u32[]{:S(2)}, u32[]{:S(2)}) collective-permute-start(f32[512]{0:T(512)S(1)} %get-tuple-element.4), channel_id=1, source_target_pairs={{0,1},{1,0},{2,3},{3,2},{4,5},{5,4},{6,7},{7,6},{8,9},{9,8},{10,11... | collective-permute-start | bytes 6152 | tf_op jit(solution)/shard_map/ppermute | solution.py:123
  152.1 26.1 %all-to-all-start.5 = ((bf16[8,10,512]{2,1,0:T(8,128)(2,1)}), bf16[8,10,512]{2,1,0:T(8,128)(2,1)S(1)}, u32[]{:S(2)}, u32[]{:S(2)}) async-start(bf16[8,10,512]{2,1,0:T(8,128)(2,1)} %broadcast_in_dim.14), calls=%async_computation.5 | async-start | bytes 262144 | tf_op jit(solution)/shard_map/all_to_all | solution.py:19

commit v2 on v1

v2 whole, which is shorter than its diff:
```python
import jax
import jax.numpy as jnp
from jax import lax
from jax.experimental import pallas as pl
from jax.experimental.pallas import tpu as pltpu
from jax.sharding import Mesh
from jax.sharding import PartitionSpec as P

EPS = 1e-06
BF = jnp.bfloat16
F32 = jnp.float32

ZH, X, ZL, Y, C = 2, 4, 8, 4, 2
ND = ZL * Y
SWAP = [(0, 1), (1, 0)]
PLANE = ("zl", "y")


def flip(arr, axis, count, bits):
    return lax.ppermute(arr, axis, [(i, i ^ bits) for i in range(count)])


def share(block, axes, count):
    wide = jnp.broadcast_to(block[None], (count,) + block.shape)
    return lax.all_to_all(wide, axes, split_axis=0, concat_axis=0, tiled=True)


def call(body, outs, *args, scratch=(), smem=0):
    specs = [pl.BlockSpec(memory_space=pltpu.SMEM)] * smem
    specs += [pl.BlockSpec(memory_space=pltpu.VMEM)] * (len(args) - smem)
    return pl.pallas_call(
        body,
        out_shape=[jax.ShapeDtypeStruct(shape, kind) for shape, kind in outs],
        in_specs=specs,
        out_specs=[pl.BlockSpec(memory_space=pltpu.VMEM)] * len(outs),
        scratch_shapes=list(scratch),
        compiler_params=pltpu.CompilerParams(vmem_limit_bytes=40 * 2**20),
    )(*args)


def dot(a, b, ca=1, cb=0):
    return lax.dot_general(a, b, (((ca,), (cb,)), ((), ())), preferred_element_type=F32)


def chooser(rows, cols, source_of):
    row = lax.broadcasted_iota(jnp.int32, (rows, cols), 0)
    col = lax.broadcasted_iota(jnp.int32, (rows, cols), 1)
    return (col == source_of(row)).astype(F32).astype(BF)


def mover(rows, cols, target_of):
    return chooser(rows, cols, target_of)


def pack_body(tok_ref, grad_ref, out_ref):
    both = jnp.concatenate([tok_ref[...], grad_ref[...]], axis=0)
    pick = chooser(
        256, 256, lambda i: (i >> 2 & 1) * 128 + (i & 1) * 64 + (i >> 1 & 1) * 32 + (i >> 3)
    )
    out_ref[...] = dot(pick, both).astype(BF)


def main_body(
    where_ref, own_ref, far_ref, blk_ref, pa_ref, pb_ref, pc_ref, pd_ref, gain_ref,
    parts_ref, send_ref, keep_ref, mine_ref, wh_ref, wo_ref,
):
    zl, y = where_ref[0], where_ref[1]

    def place(ref, jy, jz, at):
        row = pl.multiple_of(((zl ^ jz) * Y + (y ^ jy)) * 16, 16)
        wh_ref[pl.ds(row, 16), :] = ref[at : at + 16, :768]
        low = pl.multiple_of((((zl & 3) ^ (jz & 3)) * Y + (y ^ jy)) * 16, 16)
        half = (jz >> 2) * 256
        wo_ref[pl.ds(low, 16), half : half + 256] = ref[at : at + 16, 768:]

    for jz in range(8):
        place(blk_ref, 0, jz, jz * 16)
        place(pa_ref, 1, jz, jz * 16)
        place(pb_ref, 3, jz, jz * 16)
        if jz < 4:
            place(pc_ref, 2, jz, jz * 16)
        else:
            place(pd_ref, 2, jz, jz * 16 - 64)

    pick = chooser(
        256, 256, lambda i: (i >> 1 & 31) * 8 + (i >> 7) * 4 + (i >> 6 & 1) * 2 + (i & 1)
    )
    own = dot(pick, own_ref[...]).astype(BF)
    far = dot(pick, far_ref[...]).astype(BF)
    mine_ref[...] = own
    x_in = jnp.concatenate([own[0:64], far[0:64], own[64:128], far[64:128]], axis=0)
    g_in = jnp.concatenate([own[128:192], far[128:192], own[192:], far[192:]], axis=0)

    values = x_in.astype(F32)
    inverse = lax.rsqrt(jnp.mean(values * values, axis=-1, keepdims=True) + EPS)
    normed = (values * inverse * gain_ref[...]).astype(BF)
    wh = wh_ref[...]
    qkv = dot(normed, wh).astype(BF)
    ups = dot(g_in, wo_ref[...], 1, 1).astype(BF)

    lane = lax.broadcasted_iota(jnp.int32, (128, 128), 1)
    first = lane < 64
    zero = jnp.zeros((128, 128), BF)

    def stack(arr):
        return jnp.concatenate([jnp.where(first, arr, zero), jnp.where(first, zero, arr)], axis=0)

    def pile(arr):
        return jnp.concatenate([arr[:, :128], arr[:, 128:]], axis=0)

    atts, dqs, dks, dvs = [], [], [], []
    for f in range(2):
        rows = slice(f * 128, (f + 1) * 128)
        for pair in range(2):
            at = pair * 128
            q = qkv[rows, at : at + 128]
            k2 = stack(qkv[rows, 256 + at : 256 + at + 128])
            v2 = stack(qkv[rows, 512 + at : 512 + at + 128])
            u = ups[rows, at : at + 128]
            scores = dot(q, k2, 1, 1) * 0.125
            dprob = dot(u, v2, 1, 1)
            weights, dscores = [], []
            for head in range(2):
                cols = slice(head * 128, (head + 1) * 128)
                s = scores[:, cols]
                expo = jnp.exp(s - jnp.max(s, axis=-1, keepdims=True))
                probs = expo * (1.0 / jnp.sum(expo, axis=-1, keepdims=True))
                dp = dprob[:, cols]
                weights.append(probs.astype(BF))
                inner = jnp.sum(probs * dp, axis=-1, keepdims=True)
                dscores.append((probs * (dp - inner) * 0.125).astype(BF))
            weight = jnp.concatenate(weights, axis=1)
            dscore = jnp.concatenate(dscores, axis=1)
            atts.append(dot(weight, v2).astype(BF))
            dqs.append(dot(dscore, k2).astype(BF))
            dks.append(dot(pile(dscore), stack(q), 0, 0).astype(BF))
            dvs.append(dot(pile(weight), stack(u), 0, 0).astype(BF))

    def frames(items):
        return [
            jnp.concatenate([items[0], items[2]], axis=0),
            jnp.concatenate([items[1], items[3]], axis=0),
        ]

    att = jnp.concatenate(frames(atts), axis=1)
    dqkv = jnp.concatenate(frames(dqs) + frames(dks) + frames(dvs), axis=1)

    dn = dot(dqkv, wh, 1, 1)
    keep_ref[...] = jnp.concatenate([dn[0:64], dn[128:192]], axis=0)
    send_ref[...] = jnp.concatenate([dn[64:128], dn[192:]], axis=0).astype(BF)

    shuffle = mover(
        512, 512, lambda i: (i >> 1 & 3) * 128 + (i >> 3 & 1) * 64 + (i >> 4) * 2 + (i & 1)
    )
    flat = dot(normed, shuffle).astype(BF)
    g_qkv = dot(flat, dqkv, 0, 0).astype(BF)
    shuffle = mover(
        256, 256, lambda i: (i >> 1 & 3) * 64 + (i >> 3 & 1) * 32 + (i >> 4) * 2 + (i & 1)
    )
    att = dot(att, shuffle).astype(BF)
    g_out = dot(att, g_in, 0, 0).astype(BF)
    for yc in range(8):
        for part in range(3):
            parts_ref[part * 8 + yc] = g_qkv[yc * 64 : yc * 64 + 64, part * 256 : part * 256 + 256]
        block = g_out[yc * 32 : yc * 32 + 32]
        parts_ref[24 + yc] = jnp.concatenate([block[:, :256], block[:, 256:]], axis=0)


def finish_body(mine_ref, keep_ref, far_ref, gain_ref, out_ref, gg_ref):
    gain = gain_ref[...]
    values = mine_ref[0:128, :].astype(F32)
    inverse = lax.rsqrt(jnp.mean(values * values, axis=-1, keepdims=True) + EPS)
    scaled = values * inverse
    dn = keep_ref[...] + far_ref[...].astype(F32)
    gg_ref[...] = jnp.sum(dn * scaled, axis=0, keepdims=True)
    ds = dn * gain
    inner = jnp.mean(ds * scaled, axis=-1, keepdims=True)
    out_ref[...] = (mine_ref[128:256, :].astype(F32) + inverse * (ds - scaled * inner)).astype(BF)


def two_rows(vec):
    high = vec.astype(BF).astype(F32)
    return jnp.concatenate([high, vec - high, jnp.zeros((6, vec.shape[1]), F32)], axis=0)


def merge_body(where_ref, got_ref, rows_ref, gg_ref, far_ref, out_ref):
    total = got_ref[0:2].astype(F32)
    for i in range(1, 16):
        total = total + got_ref[2 * i : 2 * i + 2].astype(F32)
    low, high = total[0], total[1]
    cols = jnp.concatenate([low, high], axis=1)
    rows = jnp.concatenate(
        [
            jnp.concatenate([low[:32], low[32:]], axis=1),
            jnp.concatenate([high[:32], high[32:]], axis=1),
        ],
        axis=0,
    )
    grads = jnp.where(where_ref[2] == 3, rows, cols).astype(BF)
    gains = two_rows(gg_ref[...] + far_ref[...])
    gains = jnp.concatenate([gains, jnp.zeros((56, 512), F32)], axis=0).astype(BF)
    every = jnp.concatenate([grads, gains, rows_ref[...]], axis=0)

    def source(i):
        d, k = i >> 3, i & 7
        token = 128 + (k >> 1 & 1) * 64 + d * 2 + (k & 1)
        return jnp.where(k < 4, token, jnp.where(k < 6, d * 2 + (k & 1), 64 + (k & 1)))

    out_ref[...] = dot(chooser(256, 256, source), every).astype(BF)


def split_body(back_ref, tokens_ref, last_ref):
    back = back_ref[...]
    pick = chooser(
        128, 256, lambda i: (i & 31) * 8 + (i >> 5 & 1) * 2 + (i >> 6)
    )
    tokens_ref[...] = dot(pick, back).astype(BF)
    row = lax.broadcasted_iota(jnp.int32, (16, 256), 0)
    col = lax.broadcasted_iota(jnp.int32, (16, 256), 1)
    kind = col & 7
    grads = (row < 8) & (kind == 4 + (row & 1)) & ((col >> 3 & 3) == row >> 1)
    gains = (row == 8) & (kind >= 6)
    sums = dot((grads | gains).astype(F32).astype(BF), back)
    last_ref[...] = jnp.concatenate([sums[0:8], two_rows(sums[8:9])], axis=0).astype(BF)


def end_body(got_ref, qkv_ref, out_ref, gain_ref):
    for x in range(X):
        pair = got_ref[x].astype(F32) + got_ref[X + x].astype(F32)
        if x < 3:
            qkv_ref[:, x * 512 : x * 512 + 512] = pair[0:8]
        else:
            out_ref[...] = pair[0:8]
        gain = jnp.sum(pair[8:16], axis=0, keepdims=True)
        total = gain if x == 0 else total + gain
    gain_ref[...] = total


def gather_weights(w_qkv, w_out, core, zl):
    halves = w_qkv.reshape(8, 3, 2, 256)
    mine = lax.dynamic_index_in_dim(halves, core, 2, keepdims=False).reshape(8, 768)
    other = lax.dynamic_index_in_dim(halves, 1 - core, 2, keepdims=False).reshape(8, 768)
    got = lax.ppermute(jnp.concatenate([other, w_out], axis=1), "c", SWAP)
    kept = jnp.concatenate([mine, w_out], axis=1)
    first = jnp.where(core == 0, kept, got)
    second = jnp.where(core == 0, got, kept)
    cur = jnp.concatenate([first, second], axis=0)
    for bits in (1, 2, 4):
        cur = jnp.concatenate([cur, flip(cur, "zl", ZL, bits)], axis=0)
    side = (core ^ (zl >> 2)) * 64
    outs = lax.dynamic_slice_in_dim(cur[:, 768:], side, 64, 0)
    outs = jnp.concatenate([outs[:, :256], outs[:, 256:]], axis=0)
    block = jnp.concatenate([cur[:, :768], outs], axis=1)
    pa = flip(block, "y", Y, 1)
    pb = flip(block, "y", Y, 3)
    pc = flip(pb[:64], "y", Y, 1)
    pd = flip(pa[64:], "y", Y, 3)
    return block, pa, pb, pc, pd


def on_device(tokens, grad_out, gain, w_qkv, w_out):
    core, zl, y, x = (lax.axis_index(a) for a in ("c", "zl", "y", "x"))
    where = jnp.stack([zl, y, x, core]).astype(jnp.int32)
    row = gain.reshape(1, 512)

    [packed] = call(
        pack_body, [((256, 512), BF)], tokens.reshape(128, 512), grad_out.reshape(128, 512)
    )
    moved = lax.all_to_all(
        packed.reshape(ND, 8, 512), PLANE, split_axis=0, concat_axis=0, tiled=True
    )
    pieces = gather_weights(w_qkv, w_out, core, zl)
    moved = moved.reshape(256, 512)
    far = lax.ppermute(moved, "c", SWAP)
    parts, send, keep, mine = call(
        main_body,
        [((32, 64, 256), BF), ((128, 512), BF), ((128, 512), F32), ((256, 512), BF)],
        where, moved, far, *pieces, row,
        scratch=[pltpu.VMEM((512, 768), BF), pltpu.VMEM((256, 512), BF)],
        smem=1,
    )
    got = lax.all_to_all(parts, ("x", "y", "c"), split_axis=0, concat_axis=0, tiled=True)
    dn_far = lax.ppermute(send, "c", SWAP)
    rows, gg = call(
        finish_body, [((128, 512), BF), ((1, 512), F32)], mine, keep, dn_far, row
    )
    gg_far = lax.ppermute(gg, "c", SWAP)
    [sent] = call(merge_body, [((256, 512), BF)], where, got, rows, gg, gg_far, smem=1)
    back = lax.all_to_all(
        sent.reshape(ND, 8, 512), PLANE, split_axis=0, concat_axis=0, tiled=True
    )
    grad_tokens, last = call(
        split_body, [((128, 512), BF), ((16, 512), BF)], back.reshape(256, 512)
    )
    ends = share(last, ("zh", "x"), ZH * X)
    shard_qkv, shard_out, total = call(
        end_body, [((8, 1536), F32), ((8, 512), F32), ((1, 512), F32)], ends
    )
    return grad_tokens.reshape(1, 2, 64, 512), shard_qkv, shard_out, total.reshape(512)


def solution(mesh):
    inner = Mesh(mesh.devices.reshape(ZH, X, ZL, Y, C), ("zh", "x", "zl", "y", "c"))
    grid = ("zl", "y", "c")
    tok = P(("zh", "x"), grid, None, None)
    return jax.shard_map(
        on_device,
        mesh=inner,
        in_specs=(tok, tok, P(), P(grid, None), P(grid, None)),
        out_specs=(tok, P(grid, None), P(grid, None), P()),
        check_vma=False,
    )
```

time: 181 us -> 163 us (0.901)
  waiting for transfers between devices: 74.2 us -> 42.2 us
  blocking collectives: 35.7 us -> 56 us
  local copies, waits for them, and re-layouts: 11.5 us -> 0.85 us
  Pallas kernels: 0 us -> 8.95 us
  starting transfers between devices: 45.6 us -> 53.3 us
  matrix products: 7.27 us -> 0 us
  other arithmetic: 4.56 us -> 0.15 us
    all_to_all x5 -> x2, waiting for transfers between devices: 72.6 us -> 10.3 us  [the longest x1 10.3 us: on_device(): lax.all_to_all(parts, ('x', 'y', 'c'), split_axis=0, concat_axis=0, tiled...]
    ppermute x3 -> x10, waiting for transfers between devices: 1.55 us -> 31.9 us  [the longest x7 28.8 us: flip(): return lax.ppermute(arr, axis, [(i, i ^ bits) for i in range(count)])]
    ppermute x3 -> x10, starting transfers between devices: 6.25 us -> 35 us  [the longest x7 28.6 us: flip(): return lax.ppermute(arr, axis, [(i, i ^ bits) for i in range(count)])]
    all_to_all x5 -> x2, starting transfers between devices: 37.4 us -> 16.4 us  [the longest x1 10.5 us: on_device(): lax.all_to_all(packed.reshape(ND, 8, 512), PLANE, split_axis=0, concat_ax...]
    all_to_all x1 -> x2, blocking collectives: 35.7 us -> 56 us  [the longest x1 29.7 us: on_device(): lax.all_to_all(sent.reshape(ND, 8, 512), PLANE, split_axis=0, concat_axis...]
    pallas_call x0 -> x6, Pallas kernels: none -> 8.95 us  [call(): pl.pallas_call(body, out_shape=[jax.ShapeDtypeStruct(shape, kind) for sha...]
    dot_general x10 -> x0, matrix products: 6.12 us -> none  [the longest x1 1.53 us: attend(): dk = jnp.einsum('nhfg,nfhd->nghd', ds, q, preferred_element_type=F32)]
    slice x11 -> x5, local copies, waits for them, and re-layouts: 2.8 us -> 0.06 us  [the longest x1 0.01 us: gather_weights(): block = jnp.concatenate([cur[:, :768], outs], axis=1)]
  transfers between devices with their start and end apart: 9 -> 13, of which waited for: 7 -> 9; matrix products, arithmetic and copies ran while one was open for 3% -> 0% of each run, Pallas kernels for 0% -> 1%
where the time goes in v2:
time: 163 us; the launch traced here: 162 us
  blocking collectives  56 us (34%)
  starting transfers between devices  53.3 us (33%)
  waiting for transfers between devices  42.2 us (26%)
  Pallas kernels  8.95 us (5%)
    all_to_all x1, blocking collectives, on_device(): lax.all_to_all(sent.reshape(ND, 8, 512), PLANE, split_axis=0, concat_axis...  29.7 us
    ppermute x7, waiting for transfers between devices, flip(): return lax.ppermute(arr, axis, [(i, i ^ bits) for i in range(count)])  28.8 us
    ppermute x7, starting transfers between devices, flip(): return lax.ppermute(arr, axis, [(i, i ^ bits) for i in range(count)])  28.6 us
    all_to_all x1, blocking collectives, share(): return lax.all_to_all(wide, axes, split_axis=0, concat_axis=0, tiled=True)  26.4 us
    all_to_all x1, starting transfers between devices, on_device(): lax.all_to_all(packed.reshape(ND, 8, 512), PLANE, split_axis=0, concat_ax...  10.5 us
    all_to_all x1, waiting for transfers between devices, on_device(): lax.all_to_all(parts, ('x', 'y', 'c'), split_axis=0, concat_axis=0, tiled...  10.3 us
    pallas_call x6, Pallas kernels, call(): pl.pallas_call(body, out_shape=[jax.ShapeDtypeStruct(shape, kind) for sha...  8.95 us
    all_to_all x1, starting transfers between devices, on_device(): lax.all_to_all(parts, ('x', 'y', 'c'), split_axis=0, concat_axis=0, tiled...  5.87 us
  transfers between devices with their start and end apart: 13, of which 9 were waited for; matrix products, arithmetic and copies ran while one was open for 0% of the time, Pallas kernels for 1%

profile of v2, /device:TPU:32, one launch (start us, length us, event | category | flops | bytes accessed | tf_op | source)
XLA Modules:
  0.0 162.4 jit_solution(13038007120576078169)
XLA Ops:
  0.6 0.7 constant_dynamic-slice_fusion.2
  1.4 2.1 %collective-permute-start.1 = (bf16[8,1280]{1,0:T(8,128)(2,1)S(1)}, bf16[8,1280]{1,0:T(8,128)(2,1)S(1)}, u32[]{:S(2)}, u32[]{:S(2)}) collective-permute-start(bf16[8,1280]{1,0:T(8,128)(2,1)S(1)} %pad_maximum_fusion.3), channel_id=1, source_target_pairs={{0,1},{1,0},{2,3},{3,2},{4,5},{5,4},{6,7},{7,6},{8,9},{9,8},{10,11... | collective-permute-start | bytes 61448 | tf_op jit(solution)/shard_map/ppermute | solution.py:243
  3.5 1.1 collective-permute-done.1
  4.7 7.4 %collective-permute-start.2 = (bf16[16,1280]{1,0:T(8,128)(2,1)S(1)}, bf16[16,1280]{1,0:T(8,128)(2,1)S(1)}, u32[]{:S(2)}, u32[]{:S(2)}) collective-permute-start(bf16[16,1280]{1,0:T(8,128)(2,1)S(1)} %pad_maximum_fusion.2), channel_id=1, source_target_pairs={{0,8},{8,0},{16,24},{24,16},{32,40},{40,32},{48,56},{56,48},{1,9},... | collective-permute-start | bytes 122888 | tf_op jit(solution)/shard_map/ppermute | solution.py:20
  12.1 0.9 shard_map.84
  13.0 10.5 %all-to-all-start = ((bf16[32,8,512]{2,1,0:T(8,128)(2,1)}), bf16[32,8,512]{2,1,0:T(8,128)(2,1)S(1)}, u32[]{:S(2)}, u32[]{:S(2)}) async-start(bf16[32,8,512]{2,1,0:T(8,128)(2,1)} %bitcast.6), calls=%async_computation | async-start | bytes 524288 | tf_op jit(solution)/shard_map/all_to_all | solution.py:269
  23.6 4.3 %collective-permute-start.3 = (bf16[32,1280]{1,0:T(8,128)(2,1)S(1)}, bf16[32,1280]{1,0:T(8,128)(2,1)S(1)}, u32[]{:S(2)}, u32[]{:S(2)}) collective-permute-start(bf16[32,1280]{1,0:T(8,128)(2,1)S(1)} %pad_maximum_fusion.1), channel_id=1, source_target_pairs={{0,16},{8,24},{16,0},{24,8},{32,48},{40,56},{48,32},{56,40},{1,17}... | collective-permute-start | bytes 245768 | tf_op jit(solution)/shard_map/ppermute | solution.py:20
  27.9 8.9 %collective-permute-done.3 = bf16[32,1280]{1,0:T(8,128)(2,1)S(1)} collective-permute-done((bf16[32,1280]{1,0:T(8,128)(2,1)S(1)}, bf16[32,1280]{1,0:T(8,128)(2,1)S(1)}, u32[]{:S(2)}, u32[]{:S(2)}) %collective-permute-start.3) | collective-permute-done | bytes 81952 | tf_op jit(solution)/shard_map/ppermute | solution.py:20
  36.8 3.5 %collective-permute-start.4 = (bf16[64,1280]{1,0:T(8,128)(2,1)S(1)}, bf16[64,1280]{1,0:T(8,128)(2,1)S(1)}, u32[]{:S(2)}, u32[]{:S(2)}) collective-permute-start(bf16[64,1280]{1,0:T(8,128)(2,1)S(1)} %pad_maximum_fusion), channel_id=1, source_target_pairs={{0,32},{8,40},{16,48},{24,56},{32,0},{40,8},{48,16},{56,24},{1,33}... | collective-permute-start | bytes 491528 | tf_op jit(solution)/shard_map/ppermute | solution.py:20
  40.2 13.7 %collective-permute-done.4 = bf16[64,1280]{1,0:T(8,128)(2,1)S(1)} collective-permute-done((bf16[64,1280]{1,0:T(8,128)(2,1)S(1)}, bf16[64,1280]{1,0:T(8,128)(2,1)S(1)}, u32[]{:S(2)}, u32[]{:S(2)}) %collective-permute-start.4) | collective-permute-done | bytes 163872 | tf_op jit(solution)/shard_map/ppermute | solution.py:20
  54.1 5.2 %collective-permute-start.6 = (bf16[128,1024]{1,0:T(8,128)(2,1)S(1)}, bf16[128,1024]{1,0:T(8,128)(2,1)S(1)}, u32[]{:S(2)}, u32[]{:S(2)}) collective-permute-start(bf16[128,1024]{1,0:T(8,128)(2,1)S(1)} %maximum_maximum_fusion.blk_ref), channel_id=1, source_target_pairs={{0,6},{2,4},{4,2},{6,0},{1,7},{3,5},{5,3},{7,1},{8,14},{10,12},{12... | collective-permute-start | bytes 786440 | tf_op jit(solution)/shard_map/ppermute | solution.py:20
  59.3 2.1 %collective-permute-start.5 = (bf16[128,1024]{1,0:T(8,128)(2,1)S(1)}, bf16[128,1024]{1,0:T(8,128)(2,1)S(1)}, u32[]{:S(2)}, u32[]{:S(2)}) collective-permute-start(bf16[128,1024]{1,0:T(8,128)(2,1)S(1)} %maximum_maximum_fusion.blk_ref), channel_id=1, source_target_pairs={{0,2},{2,0},{4,6},{6,4},{1,3},{3,1},{5,7},{7,5},{8,10},{10,8},{12,... | collective-permute-start | bytes 786440 | tf_op jit(solution)/shard_map/ppermute | solution.py:20
  61.4 1.9 %collective-permute-start = (bf16[256,512]{1,0:T(8,128)(2,1)S(1)}, bf16[256,512]{1,0:T(8,128)(2,1)S(1)}, u32[]{:S(2)}, u32[]{:S(2)}) collective-permute-start(bf16[256,512]{1,0:T(8,128)(2,1)S(1)} %bitcast.21), channel_id=1, source_target_pairs={{0,1},{1,0},{2,3},{3,2},{4,5},{5,4},{6,7},{7,6},{8,9},{9,8},{10,11... | collective-permute-start | bytes 786440 | tf_op jit(solution)/shard_map/ppermute | solution.py:274
  63.3 1.0 collective-permute-done.6.pb_ref
  64.4 2.7 %collective-permute-start.7 = (bf16[64,1024]{1,0:T(8,128)(2,1)S(1)}, bf16[64,1024]{1,0:T(8,128)(2,1)S(1)}, u32[]{:S(2)}, u32[]{:S(2)}) collective-permute-start(bf16[64,1024]{1,0:T(8,128)(2,1)S(1)} %slice.26), channel_id=1, source_target_pairs={{0,2},{2,0},{4,6},{6,4},{1,3},{3,1},{5,7},{7,5},{8,10},{10,8},{12,... | collective-permute-start | bytes 393224 | tf_op jit(solution)/shard_map/ppermute | solution.py:20
  67.1 0.6 collective-permute-done.5.pa_ref
  67.8 3.4 %collective-permute-start.8 = (bf16[64,1024]{1,0:T(8,128)(2,1)S(1)}, bf16[64,1024]{1,0:T(8,128)(2,1)S(1)}, u32[]{:S(2)}, u32[]{:S(2)}) collective-permute-start(bf16[64,1024]{1,0:T(8,128)(2,1)S(1)} %slice.27), channel_id=1, source_target_pairs={{0,6},{2,4},{4,2},{6,0},{1,7},{3,5},{5,3},{7,1},{8,14},{10,12},{12... | collective-permute-start | bytes 393224 | tf_op jit(solution)/shard_map/ppermute | solution.py:20
  71.2 0.1 pad_add_fusion.where_ref
  71.3 4.6 %collective-permute-done.8.pd_ref = bf16[64,1024]{1,0:T(8,128)(2,1)S(1)} collective-permute-done((bf16[64,1024]{1,0:T(8,128)(2,1)S(1)}, bf16[64,1024]{1,0:T(8,128)(2,1)S(1)}, u32[]{:S(2)}, u32[]{:S(2)}) %collective-permute-start.8) | collective-permute-done | bytes 131104 | tf_op jit(solution)/shard_map/ppermute | solution.py:20
  75.9 5.4 %shard_map.85 = (bf16[32,64,256]{2,1,0:T(8,128)(2,1)}, bf16[128,512]{1,0:T(8,128)(2,1)S(1)}, f32[128,512]{1,0:T(8,128)S(1)}, bf16[256,512]{1,0:T(8,128)(2,1)S(1)}) custom-call(s32[4]{0:T(128)S(1)} %pad_add_fusion.where_ref, bf16[256,512]{1,0:T(8,128)(2,1)S(1)} %bitcast.22, bf16[256,512]{1,0:T(8,128)(2,1)S(1)} %collective-permute-done.far_ref, ...), custom_call_target="tpu_custom_call" | custom-call | tf_op jit(solution)/shard_map/pallas_call | solution.py:31
  81.3 5.9 %all-to-all-start.1 = ((bf16[32,64,256]{2,1,0:T(8,128)(2,1)}), bf16[32,64,256]{2,1,0:T(8,128)(2,1)S(1)}, u32[]{:S(2)}, u32[]{:S(2)}) async-start(bf16[32,64,256]{2,1,0:T(8,128)(2,1)} %get-tuple-element.15), calls=%async_computation.1 | async-start | bytes 2097152 | tf_op jit(solution)/shard_map/all_to_all | solution.py:282
  87.1 2.2 %collective-permute-start.9 = (bf16[128,512]{1,0:T(8,128)(2,1)S(1)}, bf16[128,512]{1,0:T(8,128)(2,1)S(1)}, u32[]{:S(2)}, u32[]{:S(2)}) collective-permute-start(bf16[128,512]{1,0:T(8,128)(2,1)S(1)} %get-tuple-element.18), channel_id=1, source_target_pairs={{0,1},{1,0},{2,3},{3,2},{4,5},{5,4},{6,7},{7,6},{8,9},{9,8},{10,11... | collective-permute-start | bytes 393224 | tf_op jit(solution)/shard_map/ppermute | solution.py:283
  89.3 1.1 collective-permute-done.9.far_ref
  90.4 0.2 shard_map.86
  90.6 2.2 %collective-permute-start.10 = (f32[1,512]{1,0:T(1,128)S(1)}, f32[1,512]{1,0:T(1,128)S(1)}, u32[]{:S(2)}, u32[]{:S(2)}) collective-permute-start(f32[1,512]{1,0:T(1,128)S(1)} %get-tuple-element.20.gg_ref), channel_id=1, source_target_pairs={{0,1},{1,0},{2,3},{3,2},{4,5},{5,4},{6,7},{7,6},{8,9},{9,8},{10,11... | collective-permute-start | bytes 6152 | tf_op jit(solution)/shard_map/ppermute | solution.py:287
  92.8 0.9 collective-permute-done.10.far_ref
  93.7 10.3 %all-to-all-done.1.got_ref = bf16[32,64,256]{2,1,0:T(8,128)(2,1)S(1)} async-done(((bf16[32,64,256]{2,1,0:T(8,128)(2,1)}), bf16[32,64,256]{2,1,0:T(8,128)(2,1)S(1)}, u32[]{:S(2)}, u32[]{:S(2)}) %all-to-all-start.1) | async-done | bytes 1048608 | tf_op jit(solution)/shard_map/all_to_all | solution.py:282
  104.0 0.9 shard_map.87
  104.9 29.7 %all_to_all.20 = bf16[32,8,512]{2,1,0:T(8,128)(2,1)S(1)} all-to-all(bf16[32,8,512]{2,1,0:T(8,128)(2,1)S(1)} %bitcast.23), channel_id=1, replica_groups=mesh['zh'=2,'x'=4,'zl'=8,'y'=4,'c'=2] {'zl','y'}, dimensions={0} | all-to-all | bytes 524288 | tf_op jit(solution)/shard_map/all_to_all | solution.py:289
  134.6 0.8 shard_map.88
  135.4 26.4 %all_to_all.21.got_ref = bf16[8,16,512]{2,1,0:T(8,128)(2,1)S(1)} all-to-all(bf16[8,16,512]{2,1,0:T(8,128)(2,1)S(1)} %broadcast_in_dim.2), channel_id=1, replica_groups=mesh['zh'=2,'x'=4,'zl'=8,'y'=4,'c'=2] {'zh','x'}, dimensions={0} | all-to-all | bytes 262144 | tf_op jit(solution)/shard_map/all_to_all | solution.py:25
  161.8 0.6 shard_map.89
  (28 shorter events, 0.2 us)
Async XLA Ops:
  0.6 0.7 copy-start.3
  1.4 10.7 %copy-start = (bf16[1,2,64,512]{3,2,1,0:T(8,128)(2,1)S(1)}, bf16[1,2,64,512]{3,2,1,0:T(8,128)(2,1)}, u32[]{:S(2)}) copy-start(bf16[1,2,64,512]{3,2,1,0:T(8,128)(2,1)} %param.5) | copy-start | bytes 393220
  1.4 10.7 %copy-start.1 = (bf16[1,2,64,512]{3,2,1,0:T(8,128)(2,1)S(1)}, bf16[1,2,64,512]{3,2,1,0:T(8,128)(2,1)}, u32[]{:S(2)}) copy-start(bf16[1,2,64,512]{3,2,1,0:T(8,128)(2,1)} %param.6) | copy-start | bytes 393220
  1.4 3.2 %collective-permute-start.1 = (bf16[8,1280]{1,0:T(8,128)(2,1)S(1)}, bf16[8,1280]{1,0:T(8,128)(2,1)S(1)}, u32[]{:S(2)}, u32[]{:S(2)}) collective-permute-start(bf16[8,1280]{1,0:T(8,128)(2,1)S(1)} %pad_maximum_fusion.3), channel_id=1, source_target_pairs={{0,1},{1,0},{2,3},{3,2},{4,5},{5,4},{6,7},{7,6},{8,9},{9,8},{10,11... | collective-permute-start | bytes 61448 | tf_op jit(solution)/shard_map/ppermute | solution.py:243
  4.7 18.9 %collective-permute-start.2 = (bf16[16,1280]{1,0:T(8,128)(2,1)S(1)}, bf16[16,1280]{1,0:T(8,128)(2,1)S(1)}, u32[]{:S(2)}, u32[]{:S(2)}) collective-permute-start(bf16[16,1280]{1,0:T(8,128)(2,1)S(1)} %pad_maximum_fusion.2), channel_id=1, source_target_pairs={{0,8},{8,0},{16,24},{24,16},{32,40},{40,32},{48,56},{56,48},{1,9},... | collective-permute-start | bytes 122888 | tf_op jit(solution)/shard_map/ppermute | solution.py:20
  13.0 48.4 %all-to-all-start = ((bf16[32,8,512]{2,1,0:T(8,128)(2,1)}), bf16[32,8,512]{2,1,0:T(8,128)(2,1)S(1)}, u32[]{:S(2)}, u32[]{:S(2)}) async-start(bf16[32,8,512]{2,1,0:T(8,128)(2,1)} %bitcast.6), calls=%async_computation | async-start | bytes 524288 | tf_op jit(solution)/shard_map/all_to_all | solution.py:269
  23.6 13.2 %collective-permute-start.3 = (bf16[32,1280]{1,0:T(8,128)(2,1)S(1)}, bf16[32,1280]{1,0:T(8,128)(2,1)S(1)}, u32[]{:S(2)}, u32[]{:S(2)}) collective-permute-start(bf16[32,1280]{1,0:T(8,128)(2,1)S(1)} %pad_maximum_fusion.1), channel_id=1, source_target_pairs={{0,16},{8,24},{16,0},{24,8},{32,48},{40,56},{48,32},{56,40},{1,17}... | collective-permute-start | bytes 245768 | tf_op jit(solution)/shard_map/ppermute | solution.py:20
  36.8 17.2 %collective-permute-start.4 = (bf16[64,1280]{1,0:T(8,128)(2,1)S(1)}, bf16[64,1280]{1,0:T(8,128)(2,1)S(1)}, u32[]{:S(2)}, u32[]{:S(2)}) collective-permute-start(bf16[64,1280]{1,0:T(8,128)(2,1)S(1)} %pad_maximum_fusion), channel_id=1, source_target_pairs={{0,32},{8,40},{16,48},{24,56},{32,0},{40,8},{48,16},{56,24},{1,33}... | collective-permute-start | bytes 491528 | tf_op jit(solution)/shard_map/ppermute | solution.py:20
  54.1 10.3 %collective-permute-start.6 = (bf16[128,1024]{1,0:T(8,128)(2,1)S(1)}, bf16[128,1024]{1,0:T(8,128)(2,1)S(1)}, u32[]{:S(2)}, u32[]{:S(2)}) collective-permute-start(bf16[128,1024]{1,0:T(8,128)(2,1)S(1)} %maximum_maximum_fusion.blk_ref), channel_id=1, source_target_pairs={{0,6},{2,4},{4,2},{6,0},{1,7},{3,5},{5,3},{7,1},{8,14},{10,12},{12... | collective-permute-start | bytes 786440 | tf_op jit(solution)/shard_map/ppermute | solution.py:20
  59.3 8.5 %collective-permute-start.5 = (bf16[128,1024]{1,0:T(8,128)(2,1)S(1)}, bf16[128,1024]{1,0:T(8,128)(2,1)S(1)}, u32[]{:S(2)}, u32[]{:S(2)}) collective-permute-start(bf16[128,1024]{1,0:T(8,128)(2,1)S(1)} %maximum_maximum_fusion.blk_ref), channel_id=1, source_target_pairs={{0,2},{2,0},{4,6},{6,4},{1,3},{3,1},{5,7},{7,5},{8,10},{10,8},{12,... | collective-permute-start | bytes 786440 | tf_op jit(solution)/shard_map/ppermute | solution.py:20
  61.4 14.5 %collective-permute-start = (bf16[256,512]{1,0:T(8,128)(2,1)S(1)}, bf16[256,512]{1,0:T(8,128)(2,1)S(1)}, u32[]{:S(2)}, u32[]{:S(2)}) collective-permute-start(bf16[256,512]{1,0:T(8,128)(2,1)S(1)} %bitcast.21), channel_id=1, source_target_pairs={{0,1},{1,0},{2,3},{3,2},{4,5},{5,4},{6,7},{7,6},{8,9},{9,8},{10,11... | collective-permute-start | bytes 786440 | tf_op jit(solution)/shard_map/ppermute | solution.py:274
  64.4 6.9 %collective-permute-start.7 = (bf16[64,1024]{1,0:T(8,128)(2,1)S(1)}, bf16[64,1024]{1,0:T(8,128)(2,1)S(1)}, u32[]{:S(2)}, u32[]{:S(2)}) collective-permute-start(bf16[64,1024]{1,0:T(8,128)(2,1)S(1)} %slice.26), channel_id=1, source_target_pairs={{0,2},{2,0},{4,6},{6,4},{1,3},{3,1},{5,7},{7,5},{8,10},{10,8},{12,... | collective-permute-start | bytes 393224 | tf_op jit(solution)/shard_map/ppermute | solution.py:20
  67.8 8.1 %collective-permute-start.8 = (bf16[64,1024]{1,0:T(8,128)(2,1)S(1)}, bf16[64,1024]{1,0:T(8,128)(2,1)S(1)}, u32[]{:S(2)}, u32[]{:S(2)}) collective-permute-start(bf16[64,1024]{1,0:T(8,128)(2,1)S(1)} %slice.27), channel_id=1, source_target_pairs={{0,6},{2,4},{4,2},{6,0},{1,7},{3,5},{5,3},{7,1},{8,14},{10,12},{12... | collective-permute-start | bytes 393224 | tf_op jit(solution)/shard_map/ppermute | solution.py:20
  71.2 4.7 %copy-start.2 = (f32[512]{0:T(512)S(1)}, f32[512]{0:T(512)}, u32[]{:S(2)}) copy-start(f32[512]{0:T(512)} %param.7) | copy-start | bytes 6148
  81.3 22.7 %all-to-all-start.1 = ((bf16[32,64,256]{2,1,0:T(8,128)(2,1)}), bf16[32,64,256]{2,1,0:T(8,128)(2,1)S(1)}, u32[]{:S(2)}, u32[]{:S(2)}) async-start(bf16[32,64,256]{2,1,0:T(8,128)(2,1)} %get-tuple-element.15), calls=%async_computation.1 | async-start | bytes 2097152 | tf_op jit(solution)/shard_map/all_to_all | solution.py:282
  87.1 3.2 %collective-permute-start.9 = (bf16[128,512]{1,0:T(8,128)(2,1)S(1)}, bf16[128,512]{1,0:T(8,128)(2,1)S(1)}, u32[]{:S(2)}, u32[]{:S(2)}) collective-permute-start(bf16[128,512]{1,0:T(8,128)(2,1)S(1)} %get-tuple-element.18), channel_id=1, source_target_pairs={{0,1},{1,0},{2,3},{3,2},{4,5},{5,4},{6,7},{7,6},{8,9},{9,8},{10,11... | collective-permute-start | bytes 393224 | tf_op jit(solution)/shard_map/ppermute | solution.py:283
  90.6 3.1 %collective-permute-start.10 = (f32[1,512]{1,0:T(1,128)S(1)}, f32[1,512]{1,0:T(1,128)S(1)}, u32[]{:S(2)}, u32[]{:S(2)}) collective-permute-start(f32[1,512]{1,0:T(1,128)S(1)} %get-tuple-element.20.gg_ref), channel_id=1, source_target_pairs={{0,1},{1,0},{2,3},{3,2},{4,5},{5,4},{6,7},{7,6},{8,9},{9,8},{10,11... | collective-permute-start | bytes 6152 | tf_op jit(solution)/shard_map/ppermute | solution.py:287

commit v3 on v2

--- a/solution.py
+++ b/solution.py
@@ -16,13 +16,8 @@
 PLANE = ("zl", "y")
 
 
-def flip(arr, axis, count, bits):
-    return lax.ppermute(arr, axis, [(i, i ^ bits) for i in range(count)])
-
-
-def share(block, axes, count):
-    wide = jnp.broadcast_to(block[None], (count,) + block.shape)
-    return lax.all_to_all(wide, axes, split_axis=0, concat_axis=0, tiled=True)
+def exchange(arr, axes):
+    return lax.all_to_all(arr, axes, split_axis=0, concat_axis=0, tiled=True)
 
 
 def call(body, outs, *args, scratch=(), smem=0):
@@ -52,40 +47,75 @@
     return chooser(rows, cols, target_of)
 
 
-def pack_body(tok_ref, grad_ref, out_ref):
+def pack_body(where_ref, tok_ref, grad_ref, wq_ref, wo_ref, out_ref):
     both = jnp.concatenate([tok_ref[...], grad_ref[...]], axis=0)
     pick = chooser(
         256, 256, lambda i: (i >> 2 & 1) * 128 + (i & 1) * 64 + (i >> 1 & 1) * 32 + (i >> 3)
     )
-    out_ref[...] = dot(pick, both).astype(BF)
+    out_ref[:, :512] = dot(pick, both).astype(BF)
+    x = where_ref[0]
+    part = wo_ref[...].astype(F32)
+    for i in range(3):
+        part = jnp.where(x == i, wq_ref[:, i * 512 : i * 512 + 512].astype(F32), part)
+    blocks = jnp.concatenate([part[:, y * 128 : y * 128 + 128] for y in range(Y)], axis=0)
+    out_ref[:, 512:] = jnp.concatenate([blocks] * ZL, axis=0).astype(BF)
+
+
+def halves(arr):
+    return arr[:, :64], arr[:, 64:]
+
+
+def weights_body(where_ref, moved_ref, sent_ref, tok_ref):
+    tok_ref[...] = moved_ref[:, :512]
+    block = moved_ref[:, 512:].astype(F32)
+    (low0, low1), (high0, high1) = halves(block[:128]), halves(block[128:])
+    planes = block.reshape(4, 2, 32, 128)
+    outs = x_is_last(where_ref)
+    for core, cols in ((0, (low0, high0)), (1, (low1, high1))):
+        mine = jnp.where(
+            outs, planes[:, core].reshape(128, 128), jnp.concatenate(cols, axis=1)
+        ).astype(BF)
+        for xy in range(X * Y):
+            sent_ref[2 * xy + core] = mine
+
+
+def x_is_last(where_ref):
+    return where_ref[0] == 3
+
+
+def weave(first, second):
+    rows, cols = first.shape
+    blocks = [arr.reshape(rows // 8, 1, 8, cols) for arr in (first, second)]
+    return jnp.concatenate(blocks, axis=1).reshape(2 * rows, cols)
 
 
 def main_body(
-    where_ref, own_ref, far_ref, blk_ref, pa_ref, pb_ref, pc_ref, pd_ref, gain_ref,
-    parts_ref, send_ref, keep_ref, mine_ref, wh_ref, wo_ref,
+    tok_ref, far_ref, w_ref, gain_ref, parts_ref, send_ref, keep_ref, mine_ref
 ):
-    zl, y = where_ref[0], where_ref[1]
-
-    def place(ref, jy, jz, at):
-        row = pl.multiple_of(((zl ^ jz) * Y + (y ^ jy)) * 16, 16)
-        wh_ref[pl.ds(row, 16), :] = ref[at : at + 16, :768]
-        low = pl.multiple_of((((zl & 3) ^ (jz & 3)) * Y + (y ^ jy)) * 16, 16)
-        half = (jz >> 2) * 256
-        wo_ref[pl.ds(low, 16), half : half + 256] = ref[at : at + 16, 768:]
-
-    for jz in range(8):
-        place(blk_ref, 0, jz, jz * 16)
-        place(pa_ref, 1, jz, jz * 16)
-        place(pb_ref, 3, jz, jz * 16)
-        if jz < 4:
-            place(pc_ref, 2, jz, jz * 16)
-        else:
-            place(pd_ref, 2, jz, jz * 16 - 64)
+    lanes = []
+    for x in range(3):
+        for pair in range(2):
+            tops, bots = [], []
+            for core in range(2):
+                at = x * 8 + pair * 4 + core
+                (a0, a1), (b0, b1) = (
+                    halves(w_ref[at].astype(F32)),
+                    halves(w_ref[at + 2].astype(F32)),
+                )
+                tops.append(jnp.concatenate([a0, b0], axis=1))
+                bots.append(jnp.concatenate([a1, b1], axis=1))
+            lanes.append(jnp.concatenate([weave(*tops), weave(*bots)], axis=0).astype(BF))
+    wh = jnp.concatenate(lanes, axis=1)
+    lanes = [
+        weave(w_ref[24 + 2 * y].astype(F32), w_ref[25 + 2 * y].astype(F32)).astype(BF)
+        for y in range(Y)
+    ]
+    wo = jnp.concatenate(lanes, axis=1)
 
     pick = chooser(
         256, 256, lambda i: (i >> 1 & 31) * 8 + (i >> 7) * 4 + (i >> 6 & 1) * 2 + (i & 1)
     )
-    own = dot(pick, own_ref[...]).astype(BF)
+    own = dot(pick, tok_ref[...]).astype(BF)
     far = dot(pick, far_ref[...]).astype(BF)
     mine_ref[...] = own
     x_in = jnp.concatenate([own[0:64], far[0:64], own[64:128], far[64:128]], axis=0)
@@ -94,9 +124,8 @@
     values = x_in.astype(F32)
     inverse = lax.rsqrt(jnp.mean(values * values, axis=-1, keepdims=True) + EPS)
     normed = (values * inverse * gain_ref[...]).astype(BF)
-    wh = wh_ref[...]
     qkv = dot(normed, wh).astype(BF)
-    ups = dot(g_in, wo_ref[...], 1, 1).astype(BF)
+    ups = dot(g_in, wo, 1, 1).astype(BF)
 
     lane = lax.broadcasted_iota(jnp.int32, (128, 128), 1)
     first = lane < 64
@@ -188,15 +217,14 @@
     for i in range(1, 16):
         total = total + got_ref[2 * i : 2 * i + 2].astype(F32)
     low, high = total[0], total[1]
-    cols = jnp.concatenate([low, high], axis=1)
-    rows = jnp.concatenate(
-        [
-            jnp.concatenate([low[:32], low[32:]], axis=1),
-            jnp.concatenate([high[:32], high[32:]], axis=1),
-        ],
-        axis=0,
-    )
-    grads = jnp.where(where_ref[2] == 3, rows, cols).astype(BF)
+    cols = jnp.concatenate(
+        [piece[:, j * 64 : j * 64 + 64] for j in range(4) for piece in (low, high)], axis=1
+    )
+    rows = weave(
+        jnp.concatenate([low[:32], low[32:]], axis=1),
+        jnp.concatenate([high[:32], high[32:]], axis=1),
+    )
+    grads = jnp.where(x_is_last(where_ref), rows, cols).astype(BF)
     gains = two_rows(gg_ref[...] + far_ref[...])
     gains = jnp.concatenate([gains, jnp.zeros((56, 512), F32)], axis=0).astype(BF)
     every = jnp.concatenate([grads, gains, rows_ref[...]], axis=0)
@@ -221,80 +249,57 @@
     grads = (row < 8) & (kind == 4 + (row & 1)) & ((col >> 3 & 3) == row >> 1)
     gains = (row == 8) & (kind >= 6)
     sums = dot((grads | gains).astype(F32).astype(BF), back)
-    last_ref[...] = jnp.concatenate([sums[0:8], two_rows(sums[8:9])], axis=0).astype(BF)
+    last_ref[:, :512] = sums[0:8].astype(BF)
+    gain = jnp.concatenate([sums[8:9, i * 128 : i * 128 + 128] for i in range(4)], axis=0)
+    high = gain.astype(BF).astype(F32)
+    last_ref[:, 512:] = jnp.concatenate([high, gain - high], axis=0).astype(BF)
 
 
 def end_body(got_ref, qkv_ref, out_ref, gain_ref):
     for x in range(X):
         pair = got_ref[x].astype(F32) + got_ref[X + x].astype(F32)
         if x < 3:
-            qkv_ref[:, x * 512 : x * 512 + 512] = pair[0:8]
+            qkv_ref[:, x * 512 : x * 512 + 512] = pair[:, :512]
         else:
-            out_ref[...] = pair[0:8]
-        gain = jnp.sum(pair[8:16], axis=0, keepdims=True)
+            out_ref[...] = pair[:, :512]
+        gain = pair[0:4, 512:] + pair[4:8, 512:]
         total = gain if x == 0 else total + gain
     gain_ref[...] = total
 
 
-def gather_weights(w_qkv, w_out, core, zl):
-    halves = w_qkv.reshape(8, 3, 2, 256)
-    mine = lax.dynamic_index_in_dim(halves, core, 2, keepdims=False).reshape(8, 768)
-    other = lax.dynamic_index_in_dim(halves, 1 - core, 2, keepdims=False).reshape(8, 768)
-    got = lax.ppermute(jnp.concatenate([other, w_out], axis=1), "c", SWAP)
-    kept = jnp.concatenate([mine, w_out], axis=1)
-    first = jnp.where(core == 0, kept, got)
-    second = jnp.where(core == 0, got, kept)
-    cur = jnp.concatenate([first, second], axis=0)
-    for bits in (1, 2, 4):
-        cur = jnp.concatenate([cur, flip(cur, "zl", ZL, bits)], axis=0)
-    side = (core ^ (zl >> 2)) * 64
-    outs = lax.dynamic_slice_in_dim(cur[:, 768:], side, 64, 0)
-    outs = jnp.concatenate([outs[:, :256], outs[:, 256:]], axis=0)
-    block = jnp.concatenate([cur[:, :768], outs], axis=1)
-    pa = flip(block, "y", Y, 1)
-    pb = flip(block, "y", Y, 3)
-    pc = flip(pb[:64], "y", Y, 1)
-    pd = flip(pa[64:], "y", Y, 3)
-    return block, pa, pb, pc, pd
-
-
 def on_device(tokens, grad_out, gain, w_qkv, w_out):
-    core, zl, y, x = (lax.axis_index(a) for a in ("c", "zl", "y", "x"))
-    where = jnp.stack([zl, y, x, core]).astype(jnp.int32)
+    where = lax.axis_index("x").astype(jnp.int32).reshape(1)
     row = gain.reshape(1, 512)
 
     [packed] = call(
-        pack_body, [((256, 512), BF)], tokens.reshape(128, 512), grad_out.reshape(128, 512)
-    )
-    moved = lax.all_to_all(
-        packed.reshape(ND, 8, 512), PLANE, split_axis=0, concat_axis=0, tiled=True
-    )
-    pieces = gather_weights(w_qkv, w_out, core, zl)
-    moved = moved.reshape(256, 512)
-    far = lax.ppermute(moved, "c", SWAP)
+        pack_body,
+        [((256, 640), BF)],
+        where, tokens.reshape(128, 512), grad_out.reshape(128, 512), w_qkv, w_out,
+        smem=1,
+    )
+    moved = exchange(packed.reshape(ND, 8, 640), PLANE).reshape(256, 640)
+    sent, tok = call(
+        weights_body, [((32, 128, 128), BF), ((256, 512), BF)], where, moved, smem=1
+    )
+    weights = exchange(sent, ("x", "y", "c"))
+    far = lax.ppermute(tok, "c", SWAP)
     parts, send, keep, mine = call(
         main_body,
         [((32, 64, 256), BF), ((128, 512), BF), ((128, 512), F32), ((256, 512), BF)],
-        where, moved, far, *pieces, row,
-        scratch=[pltpu.VMEM((512, 768), BF), pltpu.VMEM((256, 512), BF)],
-        smem=1,
-    )
-    got = lax.all_to_all(parts, ("x", "y", "c"), split_axis=0, concat_axis=0, tiled=True)
+        tok, far, weights, row,
+    )
+    got = exchange(parts, ("x", "y", "c"))
     dn_far = lax.ppermute(send, "c", SWAP)
     rows, gg = call(
         finish_body, [((128, 512), BF), ((1, 512), F32)], mine, keep, dn_far, row
     )
     gg_far = lax.ppermute(gg, "c", SWAP)
     [sent] = call(merge_body, [((256, 512), BF)], where, got, rows, gg, gg_far, smem=1)
-    back = lax.all_to_all(
-        sent.reshape(ND, 8, 512), PLANE, split_axis=0, concat_axis=0, tiled=True
-    )
-    grad_tokens, last = call(
-        split_body, [((128, 512), BF), ((16, 512), BF)], back.reshape(256, 512)
-    )
-    ends = share(last, ("zh", "x"), ZH * X)
+    back = exchange(sent.reshape(ND, 8, 512), PLANE).reshape(256, 512)
+    grad_tokens, last = call(split_body, [((128, 512), BF), ((8, 640), BF)], back)
+    ends = exchange(jnp.broadcast_to(last[None], (ZH * X, 8, 640)), ("zh", "x"))
     shard_qkv, shard_out, total = call(
-        end_body, [((8, 1536), F32), ((8, 512), F32), ((1, 512), F32)], ends
+        end_body, [((8, 1536), F32), ((8, 512), F32), ((4, 128), F32)], ends
     )
     return grad_tokens.reshape(1, 2, 64, 512), shard_qkv, shard_out, total.reshape(512)
 

time: 163 us -> 141 us (0.87)
  starting transfers between devices: 53.3 us -> 16.1 us
  blocking collectives: 56 us -> 85.3 us
  waiting for transfers between devices: 42.2 us -> 26.8 us
  local copies, waits for them, and re-layouts: 0.85 us -> 3.24 us
    ppermute x9 -> x1, starting transfers between devices: 32.6 us -> 2.18 us  [on_device(): far = lax.ppermute(tok, 'c', SWAP)]
    all_to_all x2 -> x3, blocking collectives: 56 us -> 85.3 us  [exchange(): return lax.all_to_all(arr, axes, split_axis=0, concat_axis=0, tiled=True)]
    ppermute x9 -> x1, waiting for transfers between devices: 30 us -> 1.24 us  [on_device(): far = lax.ppermute(tok, 'c', SWAP)]
    all_to_all x2, waiting for transfers between devices: 10.3 us -> 23.7 us  [exchange(): return lax.all_to_all(arr, axes, split_axis=0, concat_axis=0, tiled=True)]
    all_to_all x2, starting transfers between devices: 16.4 us -> 9.51 us  [exchange(): return lax.all_to_all(arr, axes, split_axis=0, concat_axis=0, tiled=True)]
    unnamed x10, local copies, waits for them, and re-layouts: 0.03 us -> 3.24 us
    pallas_call x6 -> x7, Pallas kernels: 8.95 us -> 8.43 us  [call(): pl.pallas_call(body, out_shape=[jax.ShapeDtypeStruct(shape, kind) for sha...]
  transfers between devices with their start and end apart: 13 -> 5, of which waited for: 9 -> 5; matrix products, arithmetic and copies ran while one was open for 0% -> 0% of each run, Pallas kernels for 1% -> 0%
where the time goes in v3:
time: 141 us
  blocking collectives  85.3 us (60%)
  waiting for transfers between devices  26.8 us (19%)
  starting transfers between devices  16.1 us (11%)
  Pallas kernels  8.43 us (6%)
  local copies, waits for them, and re-layouts  3.24 us (2%)
    all_to_all x3, blocking collectives, exchange(): return lax.all_to_all(arr, axes, split_axis=0, concat_axis=0, tiled=True)  85.3 us
    all_to_all x2, waiting for transfers between devices, exchange(): return lax.all_to_all(arr, axes, split_axis=0, concat_axis=0, tiled=True)  23.7 us
    all_to_all x2, starting transfers between devices, exchange(): return lax.all_to_all(arr, axes, split_axis=0, concat_axis=0, tiled=True)  9.51 us
    pallas_call x7, Pallas kernels, call(): pl.pallas_call(body, out_shape=[jax.ShapeDtypeStruct(shape, kind) for sha...  8.43 us
    unnamed x10, local copies, waits for them, and re-layouts  3.24 us
  transfers between devices with their start and end apart: 5, of which 5 were waited for; matrix products, arithmetic and copies ran while one was open for 0% of the time, Pallas kernels for 0%

profile of v3, /device:TPU:32, one launch (start us, length us, event | category | flops | bytes accessed | tf_op | source)
XLA Modules:
  0.0 140.5 jit_solution(14088046725622006975)
XLA Ops:
  0.6 0.0 copy-start.3
  0.6 0.7 copy-done.3
  1.3 0.0 copy-start
  1.3 0.9 copy-done
  2.2 0.0 copy-start.1
  2.2 0.9 copy-done.1
  3.1 0.0 copy-start.2
  3.1 0.7 copy-done.2
  3.9 0.2 shard_map.84
  4.1 35.8 %all_to_all.25 = bf16[32,8,640]{2,1,0:T(8,128)(2,1)S(1)} all-to-all(bf16[32,8,640]{2,1,0:T(8,128)(2,1)S(1)} %bitcast.11), channel_id=1, replica_groups=mesh['zh'=2,'x'=4,'zl'=8,'y'=4,'c'=2] {'zl','y'}, dimensions={0} | all-to-all | bytes 655360 | tf_op jit(solution)/shard_map/all_to_all | solution.py:20
  39.9 1.2 shard_map.85
  41.1 5.5 %all-to-all-start.1 = ((bf16[32,128,128]{2,1,0:T(8,128)(2,1)}), bf16[32,128,128]{2,1,0:T(8,128)(2,1)S(1)}, u32[]{:S(2)}, u32[]{:S(2)}) async-start(bf16[32,128,128]{2,1,0:T(8,128)(2,1)} %get-tuple-element.18), calls=%async_computation.1 | async-start | bytes 2097152 | tf_op jit(solution)/shard_map/all_to_all | solution.py:20
  46.5 0.0 copy-start.4
  46.5 2.2 %collective-permute-start = (bf16[256,512]{1,0:T(8,128)(2,1)S(1)}, bf16[256,512]{1,0:T(8,128)(2,1)S(1)}, u32[]{:S(2)}, u32[]{:S(2)}) collective-permute-start(bf16[256,512]{1,0:T(8,128)(2,1)S(1)} %get-tuple-element.17.tok_ref), channel_id=1, source_target_pairs={{0,1},{1,0},{2,3},{3,2},{4,5},{5,4},{6,7},{7,6},{8,9},{9,8},{10,11... | collective-permute-start | bytes 786440 | tf_op jit(solution)/shard_map/ppermute | solution.py:285
  48.7 1.2 collective-permute-done.far_ref
  50.0 13.4 %all-to-all-done.1.w_ref = bf16[32,128,128]{2,1,0:T(8,128)(2,1)S(1)} async-done(((bf16[32,128,128]{2,1,0:T(8,128)(2,1)}), bf16[32,128,128]{2,1,0:T(8,128)(2,1)S(1)}, u32[]{:S(2)}, u32[]{:S(2)}) %all-to-all-start.1) | async-done | bytes 1048608 | tf_op jit(solution)/shard_map/all_to_all | solution.py:20
  63.3 0.0 copy-done.4
  63.3 4.9 %shard_map.86 = (bf16[32,64,256]{2,1,0:T(8,128)(2,1)}, bf16[128,512]{1,0:T(8,128)(2,1)S(1)}, f32[128,512]{1,0:T(8,128)S(1)}, bf16[256,512]{1,0:T(8,128)(2,1)S(1)}) custom-call(bf16[256,512]{1,0:T(8,128)(2,1)S(1)} %get-tuple-element.17.tok_ref, bf16[256,512]{1,0:T(8,128)(2,1)S(1)} %collective-permute-done.far_ref, ...), custom_call_target="tpu_custom_call" | custom-call | tf_op jit(solution)/shard_map/pallas_call | solution.py:26
  68.2 4.0 %all-to-all-start.2 = ((bf16[32,64,256]{2,1,0:T(8,128)(2,1)}), bf16[32,64,256]{2,1,0:T(8,128)(2,1)S(1)}, u32[]{:S(2)}, u32[]{:S(2)}) async-start(bf16[32,64,256]{2,1,0:T(8,128)(2,1)} %get-tuple-element.19), calls=%async_computation.2 | async-start | bytes 2097152 | tf_op jit(solution)/shard_map/all_to_all | solution.py:20
  72.3 2.2 %collective-permute-start.1 = (bf16[128,512]{1,0:T(8,128)(2,1)S(1)}, bf16[128,512]{1,0:T(8,128)(2,1)S(1)}, u32[]{:S(2)}, u32[]{:S(2)}) collective-permute-start(bf16[128,512]{1,0:T(8,128)(2,1)S(1)} %get-tuple-element.22), channel_id=1, source_target_pairs={{0,1},{1,0},{2,3},{3,2},{4,5},{5,4},{6,7},{7,6},{8,9},{9,8},{10,11... | collective-permute-start | bytes 393224 | tf_op jit(solution)/shard_map/ppermute | solution.py:292
  74.5 1.1 collective-permute-done.1.far_ref
  75.5 0.2 shard_map.87
  75.8 2.2 %collective-permute-start.2 = (f32[1,512]{1,0:T(1,128)S(1)}, f32[1,512]{1,0:T(1,128)S(1)}, u32[]{:S(2)}, u32[]{:S(2)}) collective-permute-start(f32[1,512]{1,0:T(1,128)S(1)} %get-tuple-element.24.gg_ref), channel_id=1, source_target_pairs={{0,1},{1,0},{2,3},{3,2},{4,5},{5,4},{6,7},{7,6},{8,9},{9,8},{10,11... | collective-permute-start | bytes 6152 | tf_op jit(solution)/shard_map/ppermute | solution.py:296
  78.0 0.9 collective-permute-done.2.far_ref
  78.8 10.3 %all-to-all-done.2.got_ref = bf16[32,64,256]{2,1,0:T(8,128)(2,1)S(1)} async-done(((bf16[32,64,256]{2,1,0:T(8,128)(2,1)}), bf16[32,64,256]{2,1,0:T(8,128)(2,1)S(1)}, u32[]{:S(2)}, u32[]{:S(2)}) %all-to-all-start.2) | async-done | bytes 1048608 | tf_op jit(solution)/shard_map/all_to_all | solution.py:20
  89.1 0.4 shard_map.88
  89.6 25.3 %all_to_all.26 = bf16[32,8,512]{2,1,0:T(8,128)(2,1)S(1)} all-to-all(bf16[32,8,512]{2,1,0:T(8,128)(2,1)S(1)} %bitcast.13), channel_id=1, replica_groups=mesh['zh'=2,'x'=4,'zl'=8,'y'=4,'c'=2] {'zl','y'}, dimensions={0} | all-to-all | bytes 524288 | tf_op jit(solution)/shard_map/all_to_all | solution.py:20
  114.8 0.8 shard_map.89
  115.7 24.2 %all_to_all.27.got_ref = bf16[8,8,640]{2,1,0:T(8,128)(2,1)S(1)} all-to-all(bf16[8,8,640]{2,1,0:T(8,128)(2,1)S(1)} %broadcast_in_dim.2), channel_id=1, replica_groups=mesh['zh'=2,'x'=4,'zl'=8,'y'=4,'c'=2] {'zh','x'}, dimensions={0} | all-to-all | bytes 163840 | tf_op jit(solution)/shard_map/all_to_all | solution.py:20
  139.9 0.6 shard_map.90
  (1 shorter events, 0.0 us)
Async XLA Ops:
  0.6 0.7 copy-start.3
  1.3 0.9 copy-start
  2.2 0.9 copy-start.1
  3.1 0.7 copy-start.2
  41.1 22.3 %all-to-all-start.1 = ((bf16[32,128,128]{2,1,0:T(8,128)(2,1)}), bf16[32,128,128]{2,1,0:T(8,128)(2,1)S(1)}, u32[]{:S(2)}, u32[]{:S(2)}) async-start(bf16[32,128,128]{2,1,0:T(8,128)(2,1)} %get-tuple-element.18), calls=%async_computation.1 | async-start | bytes 2097152 | tf_op jit(solution)/shard_map/all_to_all | solution.py:20
  46.5 16.8 %copy-start.4 = (f32[512]{0:T(512)S(1)}, f32[512]{0:T(512)}, u32[]{:S(2)}) copy-start(f32[512]{0:T(512)} %param.7) | copy-start | bytes 6148
  46.5 3.4 %collective-permute-start = (bf16[256,512]{1,0:T(8,128)(2,1)S(1)}, bf16[256,512]{1,0:T(8,128)(2,1)S(1)}, u32[]{:S(2)}, u32[]{:S(2)}) collective-permute-start(bf16[256,512]{1,0:T(8,128)(2,1)S(1)} %get-tuple-element.17.tok_ref), channel_id=1, source_target_pairs={{0,1},{1,0},{2,3},{3,2},{4,5},{5,4},{6,7},{7,6},{8,9},{9,8},{10,11... | collective-permute-start | bytes 786440 | tf_op jit(solution)/shard_map/ppermute | solution.py:285
  68.2 20.9 %all-to-all-start.2 = ((bf16[32,64,256]{2,1,0:T(8,128)(2,1)}), bf16[32,64,256]{2,1,0:T(8,128)(2,1)S(1)}, u32[]{:S(2)}, u32[]{:S(2)}) async-start(bf16[32,64,256]{2,1,0:T(8,128)(2,1)} %get-tuple-element.19), calls=%async_computation.2 | async-start | bytes 2097152 | tf_op jit(solution)/shard_map/all_to_all | solution.py:20
  72.3 3.2 %collective-permute-start.1 = (bf16[128,512]{1,0:T(8,128)(2,1)S(1)}, bf16[128,512]{1,0:T(8,128)(2,1)S(1)}, u32[]{:S(2)}, u32[]{:S(2)}) collective-permute-start(bf16[128,512]{1,0:T(8,128)(2,1)S(1)} %get-tuple-element.22), channel_id=1, source_target_pairs={{0,1},{1,0},{2,3},{3,2},{4,5},{5,4},{6,7},{7,6},{8,9},{9,8},{10,11... | collective-permute-start | bytes 393224 | tf_op jit(solution)/shard_map/ppermute | solution.py:292
  75.8 3.1 %collective-permute-start.2 = (f32[1,512]{1,0:T(1,128)S(1)}, f32[1,512]{1,0:T(1,128)S(1)}, u32[]{:S(2)}, u32[]{:S(2)}) collective-permute-start(f32[1,512]{1,0:T(1,128)S(1)} %get-tuple-element.24.gg_ref), channel_id=1, source_target_pairs={{0,1},{1,0},{2,3},{3,2},{4,5},{5,4},{6,7},{7,6},{8,9},{9,8},{10,11... | collective-permute-start | bytes 6152 | tf_op jit(solution)/shard_map/ppermute | solution.py:296

commit v4 on v3

v4 whole, which is shorter than its diff:
```python
import jax
import jax.numpy as jnp
from jax import lax
from jax.experimental import pallas as pl
from jax.experimental.pallas import tpu as pltpu
from jax.sharding import Mesh
from jax.sharding import PartitionSpec as P

EPS = 1e-06
BF = jnp.bfloat16
F32 = jnp.float32

ZH, X, ZL, Y, C = 2, 4, 8, 4, 2
SWAP = [(0, 1), (1, 0)]


def exchange(arr, axes):
    return lax.all_to_all(arr, axes, split_axis=0, concat_axis=0, tiled=True)


def over_y(blocks):
    moved = [lax.ppermute(blocks[k], "y", [(i, i ^ k) for i in range(Y)]) for k in range(1, Y)]
    return [blocks[0]] + moved


def call(body, outs, *args, scratch=(), smem=0):
    specs = [pl.BlockSpec(memory_space=pltpu.SMEM)] * smem
    specs += [pl.BlockSpec(memory_space=pltpu.VMEM)] * (len(args) - smem)
    return pl.pallas_call(
        body,
        out_shape=[jax.ShapeDtypeStruct(shape, kind) for shape, kind in outs],
        in_specs=specs,
        out_specs=[pl.BlockSpec(memory_space=pltpu.VMEM)] * len(outs),
        scratch_shapes=list(scratch),
        compiler_params=pltpu.CompilerParams(vmem_limit_bytes=40 * 2**20),
    )(*args)


def dot(a, b, ca=1, cb=0):
    return lax.dot_general(a, b, (((ca,), (cb,)), ((), ())), preferred_element_type=F32)


def chooser(rows, cols, source_of):
    row = lax.broadcasted_iota(jnp.int32, (rows, cols), 0)
    col = lax.broadcasted_iota(jnp.int32, (rows, cols), 1)
    return (col == source_of(row)).astype(F32).astype(BF)


def pack_body(where_ref, tok_ref, grad_ref, wq_ref, wo_ref, out_ref):
    both = jnp.concatenate([tok_ref[...], grad_ref[...]], axis=0)
    pick = chooser(
        256, 256, lambda i: (i >> 2 & 1) * 128 + (i & 1) * 64 + (i >> 1 & 1) * 32 + (i >> 3)
    )
    out_ref[:, :512] = dot(pick, both).astype(BF)
    x = where_ref[0]
    part = wo_ref[...].astype(F32)
    for i in range(3):
        part = jnp.where(x == i, wq_ref[:, i * 512 : i * 512 + 512].astype(F32), part)
    blocks = jnp.concatenate([part[:, y * 128 : y * 128 + 128] for y in range(Y)], axis=0)
    out_ref[:, 512:] = jnp.concatenate([blocks] * ZL, axis=0).astype(BF)


def weights_body(where_ref, moved_ref, sent_ref, hop_ref):
    y = where_ref[1]
    pick = chooser(
        256,
        256,
        lambda i: (i >> 1 & 7) * 32 + ((i >> 6) ^ y) * 8 + (i >> 4 & 3) * 2 + (i & 1),
    )
    tokens = dot(pick, moved_ref[:, :512]).astype(BF)
    for k in range(Y):
        hop_ref[k] = tokens[k * 64 : k * 64 + 64]
    block = moved_ref[:, 512:].astype(F32).reshape(ZL, 4, 8, 128)
    cols = [block[:, lb].reshape(64, 128) for lb in range(4)]
    full = jnp.concatenate(cols, axis=1)
    planes = full.reshape(4, 2, 8, 512)
    outs = x_is_last(where_ref)
    for core in range(2):
        own = planes[:, core].reshape(32, 512)
        own = jnp.concatenate([own[:, :256], own[:, 256:]], axis=0)
        heads = jnp.concatenate([col[:, core * 64 : core * 64 + 64] for col in cols], axis=1)
        mine = jnp.where(outs, own, heads).astype(BF)
        for xy in range(X * Y):
            sent_ref[2 * xy + core] = mine


def gather_body(b0_ref, b1_ref, b2_ref, b3_ref, out_ref):
    for tf in range(4):
        for k, ref in enumerate((b0_ref, b1_ref, b2_ref, b3_ref)):
            out_ref[tf * 64 + k * 16 : tf * 64 + k * 16 + 16] = ref[tf * 16 : tf * 16 + 16]


def x_is_last(where_ref):
    return where_ref[0] == 3


def weave(first, second):
    rows, cols = first.shape
    blocks = [arr.reshape(rows // 8, 1, 8, cols) for arr in (first, second)]
    return jnp.concatenate(blocks, axis=1).reshape(2 * rows, cols)


def main_body(
    own_ref, far_ref, w_ref, gain_ref, parts_ref, send_ref, keep_ref
):
    def gathered(part, count, width, piece):
        blocks = [piece(w_ref[part * 8 + yc].astype(F32)) for yc in range(8)]
        blocks = [block.reshape(count, 1, 8, width) for block in blocks]
        return jnp.concatenate(blocks, axis=1).reshape(count * 64, width).astype(BF)

    wh = jnp.concatenate([gathered(x, 8, 256, lambda arr: arr) for x in range(3)], axis=1)
    wo = gathered(3, 4, 512, lambda arr: jnp.concatenate([arr[:32], arr[32:]], axis=1))

    own, far = own_ref[...], far_ref[...]
    x_in = jnp.concatenate([own[0:64], far[0:64], own[64:128], far[64:128]], axis=0)
    g_in = jnp.concatenate([own[128:192], far[128:192], own[192:], far[192:]], axis=0)

    values = x_in.astype(F32)
    inverse = lax.rsqrt(jnp.mean(values * values, axis=-1, keepdims=True) + EPS)
    scaled = values * inverse
    normed = (scaled * gain_ref[...]).astype(BF)
    qkv = dot(normed, wh).astype(BF)
    ups = dot(g_in, wo, 1, 1).astype(BF)

    lane = lax.broadcasted_iota(jnp.int32, (128, 128), 1)
    first = lane < 64
    zero = jnp.zeros((128, 128), BF)

    def stack(arr):
        return jnp.concatenate([jnp.where(first, arr, zero), jnp.where(first, zero, arr)], axis=0)

    def pile(arr):
        return jnp.concatenate([arr[:, :128], arr[:, 128:]], axis=0)

    atts, dqs, dks, dvs = [], [], [], []
    for f in range(2):
        rows = slice(f * 128, (f + 1) * 128)
        for pair in range(2):
            at = pair * 128
            q = qkv[rows, at : at + 128]
            k2 = stack(qkv[rows, 256 + at : 256 + at + 128])
            v2 = stack(qkv[rows, 512 + at : 512 + at + 128])
            u = ups[rows, at : at + 128]
            scores = dot(q, k2, 1, 1) * 0.125
            dprob = dot(u, v2, 1, 1)
            weights, dscores = [], []
            for head in range(2):
                cols = slice(head * 128, (head + 1) * 128)
                s = scores[:, cols]
                expo = jnp.exp(s - jnp.max(s, axis=-1, keepdims=True))
                probs = expo * (1.0 / jnp.sum(expo, axis=-1, keepdims=True))
                dp = dprob[:, cols]
                weights.append(probs.astype(BF))
                inner = jnp.sum(probs * dp, axis=-1, keepdims=True)
                dscores.append((probs * (dp - inner) * 0.125).astype(BF))
            weight = jnp.concatenate(weights, axis=1)
            dscore = jnp.concatenate(dscores, axis=1)
            atts.append(dot(weight, v2).astype(BF))
            dqs.append(dot(dscore, k2).astype(BF))
            dks.append(dot(pile(dscore), stack(q), 0, 0).astype(BF))
            dvs.append(dot(pile(weight), stack(u), 0, 0).astype(BF))

    def frames(items):
        return [
            jnp.concatenate([items[0], items[2]], axis=0),
            jnp.concatenate([items[1], items[3]], axis=0),
        ]

    att = jnp.concatenate(frames(atts), axis=1)
    dqkv = jnp.concatenate(frames(dqs) + frames(dks) + frames(dvs), axis=1)

    dn = dot(dqkv, wh, 1, 1)
    keep_ref[...] = jnp.concatenate([dn[0:64], dn[128:192]], axis=0)
    send_ref[...] = jnp.concatenate([dn[64:128], dn[192:]], axis=0).astype(BF)

    gg = two_rows(jnp.sum(dn * scaled, axis=0, keepdims=True))
    gg = jnp.concatenate([gg[0:2, i * 128 : i * 128 + 128] for i in range(4)], axis=0)

    g_qkv = dot(normed, dqkv, 0, 0).reshape(ZL, Y, 2, 8, 768)
    g_out = dot(att, g_in, 0, 0).reshape(4, Y, 2, 8, 512)
    for yc in range(8):
        block = g_qkv[:, yc // 2, yc % 2].reshape(64, 768)
        for part in range(3):
            at = part * 256
            pieces = [block[:, at : at + 128], block[:, at + 128 : at + 256], gg]
            parts_ref[part * 8 + yc] = jnp.concatenate(pieces, axis=0).astype(BF)
        block = g_out[:, yc // 2, yc % 2].reshape(32, 512)
        pieces = [block[:, i * 128 : i * 128 + 128] for i in range(4)] + [gg]
        parts_ref[24 + yc] = jnp.concatenate(pieces, axis=0).astype(BF)


def finish_body(own_ref, keep_ref, far_ref, gain_ref, out_ref):
    gain = gain_ref[...]
    values = own_ref[0:128, :].astype(F32)
    inverse = lax.rsqrt(jnp.mean(values * values, axis=-1, keepdims=True) + EPS)
    scaled = values * inverse
    ds = (keep_ref[...] + far_ref[...].astype(F32)) * gain
    inner = jnp.mean(ds * scaled, axis=-1, keepdims=True)
    result = (own_ref[128:256, :].astype(F32) + inverse * (ds - scaled * inner)).astype(BF)
    for k in range(Y):
        out_ref[k] = jnp.concatenate(
            [result[k * 16 : k * 16 + 16], result[64 + k * 16 : 64 + k * 16 + 16]], axis=0
        )


def two_rows(vec):
    high = vec.astype(BF).astype(F32)
    return jnp.concatenate([high, vec - high, jnp.zeros((6, vec.shape[1]), F32)], axis=0)


def two_blocks(rows):
    high = rows.astype(BF).astype(F32)
    return jnp.concatenate([high, rows - high], axis=0)


def merge_body(where_ref, got_ref, b0_ref, b1_ref, b2_ref, b3_ref, out_ref):
    total = got_ref[0:2].astype(F32)
    for i in range(1, 16):
        total = total + got_ref[2 * i : 2 * i + 2].astype(F32)
    low, high = total[0, :128], total[1, :128]
    wide_low = jnp.concatenate([low[:64], low[64:]], axis=1)
    wide_high = jnp.concatenate([high[:64], high[64:]], axis=1)
    cols = jnp.concatenate(
        [piece[:, j * 64 : j * 64 + 64] for j in range(4) for piece in (wide_low, wide_high)],
        axis=1,
    )
    rows = weave(
        jnp.concatenate([low[i * 32 : i * 32 + 32] for i in range(4)], axis=1),
        jnp.concatenate([high[i * 32 : i * 32 + 32] for i in range(4)], axis=1),
    )
    out_ref[:, :512] = jnp.where(x_is_last(where_ref), rows, cols).astype(BF)
    pick = chooser(64, 64, lambda i: (i >> 1 & 3) * 16 + (i >> 3) * 2 + (i & 1))
    for f in range(2):
        blocks = [ref[f * 16 : f * 16 + 16] for ref in (b0_ref, b1_ref, b2_ref, b3_ref)]
        rows = dot(pick, jnp.concatenate(blocks, axis=0)).astype(BF)
        out_ref[:, 512 + f * 512 : 1024 + f * 512] = rows
    gains = total[0, 128:] + total[1, 128:]
    gains = two_blocks(unpair(gains))
    out_ref[:, 1536:] = jnp.concatenate([gains] * ZL, axis=0).astype(BF)


def unpair(rows):
    return jnp.concatenate(
        [rows[2 * i : 2 * i + 1] + rows[2 * i + 1 : 2 * i + 2] for i in range(4)], axis=0
    )


def split_body(where_ref, back_ref, tokens_ref, last_ref):
    y = where_ref[1]
    pick = chooser(64, 64, lambda i: (i >> 2 & 7) * 8 + ((i & 3) ^ y) * 2 + (i >> 5))
    for f in range(2):
        rows = dot(pick, back_ref[:, 512 + f * 512 : 1024 + f * 512]).astype(BF)
        for b in range(2):
            tokens_ref[b * 64 + f * 32 : b * 64 + f * 32 + 32] = rows[b * 32 : b * 32 + 32]
    sums = jnp.sum(back_ref[:, :512].astype(F32).reshape(ZL, 8, 512), axis=0)
    last_ref[:, :512] = sums.astype(BF)
    gains = jnp.sum(back_ref[:, 1536:].astype(F32).reshape(ZL, 8, 128), axis=0)
    last_ref[:, 512:] = two_blocks(gains[0:4] + gains[4:8]).astype(BF)


def end_body(got_ref, qkv_ref, out_ref, gain_ref):
    for x in range(X):
        pair = got_ref[x].astype(F32) + got_ref[X + x].astype(F32)
        if x < 3:
            qkv_ref[:, x * 512 : x * 512 + 512] = pair[:, :512]
        else:
            out_ref[...] = pair[:, :512]
        if x == 0:
            gain_ref[...] = pair[0:4, 512:] + pair[4:8, 512:]


def on_device(tokens, grad_out, gain, w_qkv, w_out):
    where = jnp.stack([lax.axis_index("x"), lax.axis_index("y")]).astype(jnp.int32)
    row = gain.reshape(1, 512)
    plane = ("x", "y", "c")

    [packed] = call(
        pack_body,
        [((256, 640), BF)],
        where, tokens.reshape(128, 512), grad_out.reshape(128, 512), w_qkv, w_out,
        smem=1,
    )
    moved = exchange(packed.reshape(ZL, 32, 640), "zl").reshape(256, 640)
    sent, hop = call(
        weights_body, [((32, 64, 256), BF), ((Y, 64, 512), BF)], where, moved, smem=1
    )
    weights = exchange(sent, plane)
    [own] = call(gather_body, [((256, 512), BF)], *over_y(hop))
    far = lax.ppermute(own, "c", SWAP)
    parts, send, keep = call(
        main_body,
        [((32, 136, 128), BF), ((128, 512), BF), ((128, 512), F32)],
        own, far, weights, row,
    )
    got = exchange(parts, plane)
    dn_far = lax.ppermute(send, "c", SWAP)
    [result] = call(finish_body, [((Y, 32, 512), BF)], own, keep, dn_far, row)
    [sent] = call(merge_body, [((64, 1664), BF)], where, got, *over_y(result), smem=1)
    back = exchange(sent.reshape(ZL, 8, 1664), "zl").reshape(64, 1664)
    grad_tokens, last = call(
        split_body, [((128, 512), BF), ((8, 640), BF)], where, back, smem=1
    )
    ends = exchange(jnp.broadcast_to(last[None], (ZH * X, 8, 640)), ("zh", "x"))
    shard_qkv, shard_out, total = call(
        end_body, [((8, 1536), F32), ((8, 512), F32), ((4, 128), F32)], ends
    )
    return grad_tokens.reshape(1, 2, 64, 512), shard_qkv, shard_out, total.reshape(512)


def solution(mesh):
    inner = Mesh(mesh.devices.reshape(ZH, X, ZL, Y, C), ("zh", "x", "zl", "y", "c"))
    grid = ("zl", "y", "c")
    tok = P(("zh", "x"), grid, None, None)
    return jax.shard_map(
        on_device,
        mesh=inner,
        in_specs=(tok, tok, P(), P(grid, None), P(grid, None)),
        out_specs=(tok, P(grid, None), P(grid, None), P()),
        check_vma=False,
    )
```

time: 141 us -> 142 us (level)
  starting transfers between devices: 16.1 us -> 36.7 us
  waiting for transfers between devices: 26.8 us -> 16 us
  blocking collectives: 85.3 us -> 74.9 us
    all_to_all x2, waiting for transfers between devices: 23.7 us -> 0.01 us  [exchange(): return lax.all_to_all(arr, axes, split_axis=0, concat_axis=0, tiled=True)]
    ppermute x2 -> x7, starting transfers between devices: 4.36 us -> 21.6 us  [the longest x6 19.6 us: over_y(): lax.ppermute(blocks[k], 'y', [(i, i ^ k) for i in range(Y)])]
    ppermute x2 -> x7, waiting for transfers between devices: 2.1 us -> 15 us  [the longest x6 13.5 us: over_y(): lax.ppermute(blocks[k], 'y', [(i, i ^ k) for i in range(Y)])]
    all_to_all x3, blocking collectives: 85.3 us -> 74.9 us  [exchange(): return lax.all_to_all(arr, axes, split_axis=0, concat_axis=0, tiled=True)]
    all_to_all x2, starting transfers between devices: 9.51 us -> 13 us  [exchange(): return lax.all_to_all(arr, axes, split_axis=0, concat_axis=0, tiled=True)]
    pallas_call x7 -> x8, Pallas kernels: 8.43 us -> 9.64 us  [call(): pl.pallas_call(body, out_shape=[jax.ShapeDtypeStruct(shape, kind) for sha...]
  transfers between devices with their start and end apart: 5 -> 10, of which waited for: 5 -> 4; matrix products, arithmetic and copies ran while one was open for 0% -> 0% of each run, Pallas kernels for 0% -> 0%
where the time goes in v4:
time: 142 us; the launch traced here: 141 us
  blocking collectives  74.9 us (53%)
  starting transfers between devices  36.7 us (26%)
  waiting for transfers between devices  16 us (11%)
  Pallas kernels  9.64 us (7%)
  local copies, waits for them, and re-layouts  3.28 us (2%)
    all_to_all x3, blocking collectives, exchange(): return lax.all_to_all(arr, axes, split_axis=0, concat_axis=0, tiled=True)  74.9 us
    ppermute x6, starting transfers between devices, over_y(): lax.ppermute(blocks[k], 'y', [(i, i ^ k) for i in range(Y)])  19.6 us
    ppermute x6, waiting for transfers between devices, over_y(): lax.ppermute(blocks[k], 'y', [(i, i ^ k) for i in range(Y)])  13.5 us
    all_to_all x2, starting transfers between devices, exchange(): return lax.all_to_all(arr, axes, split_axis=0, concat_axis=0, tiled=True)  13 us
    pallas_call x8, Pallas kernels, call(): pl.pallas_call(body, out_shape=[jax.ShapeDtypeStruct(shape, kind) for sha...  9.64 us
    unnamed x10, local copies, waits for them, and re-layouts  3.24 us
  transfers between devices with their start and end apart: 10, of which 4 were waited for; matrix products, arithmetic and copies ran while one was open for 0% of the time, Pallas kernels for 0%

profile of v4, /device:TPU:32, one launch (start us, length us, event | category | flops | bytes accessed | tf_op | source)
XLA Modules:
  0.0 141.4 jit_solution(17357524460132919468)
XLA Ops:
  0.6 0.1 pad_add_fusion.where_ref
  0.7 0.9 copy-done
  1.6 0.9 copy-done.1
  2.5 0.7 copy-done.2
  3.3 0.7 copy-done.3
  4.0 0.8 shard_map.84
  4.7 31.3 %all_to_all.25 = bf16[8,32,640]{2,1,0:T(8,128)(2,1)S(1)} all-to-all(bf16[8,32,640]{2,1,0:T(8,128)(2,1)S(1)} %bitcast.28), channel_id=1, replica_groups=mesh['zh'=2,'x'=4,'zl'=8,'y'=4,'c'=2] {'zl'}, dimensions={0} | all-to-all | bytes 655360 | tf_op jit(solution)/shard_map/all_to_all | solution.py:18
  36.1 1.8 %shard_map.85 = (bf16[32,64,256]{2,1,0:T(8,128)(2,1)}, bf16[4,64,512]{2,1,0:T(8,128)(2,1)S(1)}) custom-call(s32[2]{0:T(128)S(1)} %pad_add_fusion.where_ref, bf16[256,640]{1,0:T(8,128)(2,1)S(1)} %bitcast.27), custom_call_target="tpu_custom_call" | custom-call | tf_op jit(solution)/shard_map/pallas_call | solution.py:29
  37.9 7.4 %all-to-all-start.1 = ((bf16[32,64,256]{2,1,0:T(8,128)(2,1)}), bf16[32,64,256]{2,1,0:T(8,128)(2,1)S(1)}, u32[]{:S(2)}, u32[]{:S(2)}) async-start(bf16[32,64,256]{2,1,0:T(8,128)(2,1)} %get-tuple-element.15), calls=%async_computation.1 | async-start | bytes 2097152 | tf_op jit(solution)/shard_map/all_to_all | solution.py:18
  45.4 4.9 %collective-permute-start.2 = (bf16[64,512]{1,0:T(8,128)(2,1)S(1)}, bf16[64,512]{1,0:T(8,128)(2,1)S(1)}, u32[]{:S(2)}, u32[]{:S(2)}) collective-permute-start(bf16[64,512]{1,0:T(8,128)(2,1)S(1)} %get-tuple-element.24), channel_id=1, source_target_pairs={{0,6},{2,4},{4,2},{6,0},{1,7},{3,5},{5,3},{7,1},{8,14},{10,12},{12... | collective-permute-start | bytes 196616 | tf_op jit(solution)/shard_map/ppermute | solution.py:22
  50.3 2.8 %collective-permute-start.1 = (bf16[64,512]{1,0:T(8,128)(2,1)S(1)}, bf16[64,512]{1,0:T(8,128)(2,1)S(1)}, u32[]{:S(2)}, u32[]{:S(2)}) collective-permute-start(bf16[64,512]{1,0:T(8,128)(2,1)S(1)} %get-tuple-element.25), channel_id=1, source_target_pairs={{0,4},{2,6},{4,0},{6,2},{1,5},{3,7},{5,1},{7,3},{8,12},{10,14},{12... | collective-permute-start | bytes 196616 | tf_op jit(solution)/shard_map/ppermute | solution.py:22
  53.0 2.1 %collective-permute-start = (bf16[64,512]{1,0:T(8,128)(2,1)S(1)}, bf16[64,512]{1,0:T(8,128)(2,1)S(1)}, u32[]{:S(2)}, u32[]{:S(2)}) collective-permute-start(bf16[64,512]{1,0:T(8,128)(2,1)S(1)} %get-tuple-element.26), channel_id=1, source_target_pairs={{0,2},{2,0},{4,6},{6,4},{1,3},{3,1},{5,7},{7,5},{8,10},{10,8},{12,... | collective-permute-start | bytes 196616 | tf_op jit(solution)/shard_map/ppermute | solution.py:22
  55.2 8.3 %collective-permute-done.2.b3_ref = bf16[64,512]{1,0:T(8,128)(2,1)S(1)} collective-permute-done((bf16[64,512]{1,0:T(8,128)(2,1)S(1)}, bf16[64,512]{1,0:T(8,128)(2,1)S(1)}, u32[]{:S(2)}, u32[]{:S(2)}) %collective-permute-start.2) | collective-permute-done | bytes 65568 | tf_op jit(solution)/shard_map/ppermute | solution.py:22
  63.5 0.0 collective-permute-done.b1_ref
  63.5 1.9 %collective-permute-start.3 = (bf16[256,512]{1,0:T(8,128)(2,1)S(1)}, bf16[256,512]{1,0:T(8,128)(2,1)S(1)}, u32[]{:S(2)}, u32[]{:S(2)}) collective-permute-start(bf16[256,512]{1,0:T(8,128)(2,1)S(1)} %shard_map.86.own_ref), channel_id=1, source_target_pairs={{0,1},{1,0},{2,3},{3,2},{4,5},{5,4},{6,7},{7,6},{8,9},{9,8},{10,11... | collective-permute-start | bytes 786440 | tf_op jit(solution)/shard_map/ppermute | solution.py:289
  65.4 1.5 %collective-permute-done.3.far_ref = bf16[256,512]{1,0:T(8,128)(2,1)S(1)} collective-permute-done((bf16[256,512]{1,0:T(8,128)(2,1)S(1)}, bf16[256,512]{1,0:T(8,128)(2,1)S(1)}, u32[]{:S(2)}, u32[]{:S(2)}) %collective-permute-start.3) | collective-permute-done | bytes 262176 | tf_op jit(solution)/shard_map/ppermute | solution.py:289
  66.9 4.0 %shard_map.87 = (bf16[32,136,128]{2,1,0:T(8,128)(2,1)}, bf16[128,512]{1,0:T(8,128)(2,1)S(1)}, f32[128,512]{1,0:T(8,128)S(1)}) custom-call(bf16[256,512]{1,0:T(8,128)(2,1)S(1)} %shard_map.86.own_ref, bf16[256,512]{1,0:T(8,128)(2,1)S(1)} %collective-permute-done.3.far_ref, bf16[32,64,256]{2,1,0:T(8,128)(2,1)S(1)} %all-to-all-done.1.w_ref, f32[1,512]{1,0:T(1,128)S(1)} %bitcast.33), custom_call_target="tpu_custom_call" | custom-call | tf_op jit(solution)/shard_map/pallas_call | solution.py:29
  71.0 5.5 %all-to-all-start.2 = ((bf16[32,136,128]{2,1,0:T(8,128)(2,1)}), bf16[32,136,128]{2,1,0:T(8,128)(2,1)S(1)}, u32[]{:S(2)}, u32[]{:S(2)}) async-start(bf16[32,136,128]{2,1,0:T(8,128)(2,1)} %get-tuple-element.16), calls=%async_computation.2 | async-start | bytes 2228224 | tf_op jit(solution)/shard_map/all_to_all | solution.py:18
  76.5 2.2 %collective-permute-start.4 = (bf16[128,512]{1,0:T(8,128)(2,1)S(1)}, bf16[128,512]{1,0:T(8,128)(2,1)S(1)}, u32[]{:S(2)}, u32[]{:S(2)}) collective-permute-start(bf16[128,512]{1,0:T(8,128)(2,1)S(1)} %get-tuple-element.18), channel_id=1, source_target_pairs={{0,1},{1,0},{2,3},{3,2},{4,5},{5,4},{6,7},{7,6},{8,9},{9,8},{10,11... | collective-permute-start | bytes 393224 | tf_op jit(solution)/shard_map/ppermute | solution.py:296
  78.7 1.1 collective-permute-done.4.far_ref
  79.7 0.2 shard_map.88
  80.0 4.9 %collective-permute-start.7 = (bf16[32,512]{1,0:T(8,128)(2,1)S(1)}, bf16[32,512]{1,0:T(8,128)(2,1)S(1)}, u32[]{:S(2)}, u32[]{:S(2)}) collective-permute-start(bf16[32,512]{1,0:T(8,128)(2,1)S(1)} %get-tuple-element.28), channel_id=1, source_target_pairs={{0,6},{2,4},{4,2},{6,0},{1,7},{3,5},{5,3},{7,1},{8,14},{10,12},{12... | collective-permute-start | bytes 98312 | tf_op jit(solution)/shard_map/ppermute | solution.py:22
  84.9 2.8 %collective-permute-start.6 = (bf16[32,512]{1,0:T(8,128)(2,1)S(1)}, bf16[32,512]{1,0:T(8,128)(2,1)S(1)}, u32[]{:S(2)}, u32[]{:S(2)}) collective-permute-start(bf16[32,512]{1,0:T(8,128)(2,1)S(1)} %get-tuple-element.29), channel_id=1, source_target_pairs={{0,4},{2,6},{4,0},{6,2},{1,5},{3,7},{5,1},{7,3},{8,12},{10,14},{12... | collective-permute-start | bytes 98312 | tf_op jit(solution)/shard_map/ppermute | solution.py:22
  87.7 2.1 %collective-permute-start.5 = (bf16[32,512]{1,0:T(8,128)(2,1)S(1)}, bf16[32,512]{1,0:T(8,128)(2,1)S(1)}, u32[]{:S(2)}, u32[]{:S(2)}) collective-permute-start(bf16[32,512]{1,0:T(8,128)(2,1)S(1)} %get-tuple-element.30), channel_id=1, source_target_pairs={{0,2},{2,0},{4,6},{6,4},{1,3},{3,1},{5,7},{7,5},{8,10},{10,8},{12,... | collective-permute-start | bytes 98312 | tf_op jit(solution)/shard_map/ppermute | solution.py:22
  89.8 0.0 collective-permute-done.7.b3_ref
  89.8 5.2 %collective-permute-done.6.b2_ref = bf16[32,512]{1,0:T(8,128)(2,1)S(1)} collective-permute-done((bf16[32,512]{1,0:T(8,128)(2,1)S(1)}, bf16[32,512]{1,0:T(8,128)(2,1)S(1)}, u32[]{:S(2)}, u32[]{:S(2)}) %collective-permute-start.6) | collective-permute-done | bytes 32800 | tf_op jit(solution)/shard_map/ppermute | solution.py:22
  95.0 0.0 all-to-all-done.2.got_ref
  95.0 0.8 shard_map.89
  95.8 19.4 %all_to_all.26 = bf16[8,8,1664]{2,1,0:T(8,128)(2,1)S(1)} all-to-all(bf16[8,8,1664]{2,1,0:T(8,128)(2,1)S(1)} %bitcast.29), channel_id=1, replica_groups=mesh['zh'=2,'x'=4,'zl'=8,'y'=4,'c'=2] {'zl'}, dimensions={0} | all-to-all | bytes 425984 | tf_op jit(solution)/shard_map/all_to_all | solution.py:18
  115.3 1.4 shard_map.90
  116.6 24.2 %all_to_all.27.got_ref = bf16[8,8,640]{2,1,0:T(8,128)(2,1)S(1)} all-to-all(bf16[8,8,640]{2,1,0:T(8,128)(2,1)S(1)} %broadcast_in_dim.2), channel_id=1, replica_groups=mesh['zh'=2,'x'=4,'zl'=8,'y'=4,'c'=2] {'zh','x'}, dimensions={0} | all-to-all | bytes 163840 | tf_op jit(solution)/shard_map/all_to_all | solution.py:18
  140.8 0.6 shard_map.91
  (13 shorter events, 0.1 us)
Async XLA Ops:
  0.7 0.9 copy-start
  1.6 0.9 copy-start.1
  2.5 0.7 copy-start.2
  3.3 0.7 copy-start.3
  37.9 29.1 %copy-start.4 = (f32[512]{0:T(512)S(1)}, f32[512]{0:T(512)}, u32[]{:S(2)}) copy-start(f32[512]{0:T(512)} %param.7) | copy-start | bytes 6148
  37.9 29.1 %all-to-all-start.1 = ((bf16[32,64,256]{2,1,0:T(8,128)(2,1)}), bf16[32,64,256]{2,1,0:T(8,128)(2,1)S(1)}, u32[]{:S(2)}, u32[]{:S(2)}) async-start(bf16[32,64,256]{2,1,0:T(8,128)(2,1)} %get-tuple-element.15), calls=%async_computation.1 | async-start | bytes 2097152 | tf_op jit(solution)/shard_map/all_to_all | solution.py:18
  45.4 18.1 %collective-permute-start.2 = (bf16[64,512]{1,0:T(8,128)(2,1)S(1)}, bf16[64,512]{1,0:T(8,128)(2,1)S(1)}, u32[]{:S(2)}, u32[]{:S(2)}) collective-permute-start(bf16[64,512]{1,0:T(8,128)(2,1)S(1)} %get-tuple-element.24), channel_id=1, source_target_pairs={{0,6},{2,4},{4,2},{6,0},{1,7},{3,5},{5,3},{7,1},{8,14},{10,12},{12... | collective-permute-start | bytes 196616 | tf_op jit(solution)/shard_map/ppermute | solution.py:22
  50.3 13.2 %collective-permute-start.1 = (bf16[64,512]{1,0:T(8,128)(2,1)S(1)}, bf16[64,512]{1,0:T(8,128)(2,1)S(1)}, u32[]{:S(2)}, u32[]{:S(2)}) collective-permute-start(bf16[64,512]{1,0:T(8,128)(2,1)S(1)} %get-tuple-element.25), channel_id=1, source_target_pairs={{0,4},{2,6},{4,0},{6,2},{1,5},{3,7},{5,1},{7,3},{8,12},{10,14},{12... | collective-permute-start | bytes 196616 | tf_op jit(solution)/shard_map/ppermute | solution.py:22
  53.0 10.4 %collective-permute-start = (bf16[64,512]{1,0:T(8,128)(2,1)S(1)}, bf16[64,512]{1,0:T(8,128)(2,1)S(1)}, u32[]{:S(2)}, u32[]{:S(2)}) collective-permute-start(bf16[64,512]{1,0:T(8,128)(2,1)S(1)} %get-tuple-element.26), channel_id=1, source_target_pairs={{0,2},{2,0},{4,6},{6,4},{1,3},{3,1},{5,7},{7,5},{8,10},{10,8},{12,... | collective-permute-start | bytes 196616 | tf_op jit(solution)/shard_map/ppermute | solution.py:22
  63.5 3.4 %collective-permute-start.3 = (bf16[256,512]{1,0:T(8,128)(2,1)S(1)}, bf16[256,512]{1,0:T(8,128)(2,1)S(1)}, u32[]{:S(2)}, u32[]{:S(2)}) collective-permute-start(bf16[256,512]{1,0:T(8,128)(2,1)S(1)} %shard_map.86.own_ref), channel_id=1, source_target_pairs={{0,1},{1,0},{2,3},{3,2},{4,5},{5,4},{6,7},{7,6},{8,9},{9,8},{10,11... | collective-permute-start | bytes 786440 | tf_op jit(solution)/shard_map/ppermute | solution.py:289
  71.0 24.1 %all-to-all-start.2 = ((bf16[32,136,128]{2,1,0:T(8,128)(2,1)}), bf16[32,136,128]{2,1,0:T(8,128)(2,1)S(1)}, u32[]{:S(2)}, u32[]{:S(2)}) async-start(bf16[32,136,128]{2,1,0:T(8,128)(2,1)} %get-tuple-element.16), calls=%async_computation.2 | async-start | bytes 2228224 | tf_op jit(solution)/shard_map/all_to_all | solution.py:18
  76.5 3.2 %collective-permute-start.4 = (bf16[128,512]{1,0:T(8,128)(2,1)S(1)}, bf16[128,512]{1,0:T(8,128)(2,1)S(1)}, u32[]{:S(2)}, u32[]{:S(2)}) collective-permute-start(bf16[128,512]{1,0:T(8,128)(2,1)S(1)} %get-tuple-element.18), channel_id=1, source_target_pairs={{0,1},{1,0},{2,3},{3,2},{4,5},{5,4},{6,7},{7,6},{8,9},{9,8},{10,11... | collective-permute-start | bytes 393224 | tf_op jit(solution)/shard_map/ppermute | solution.py:296
  80.0 9.8 %collective-permute-start.7 = (bf16[32,512]{1,0:T(8,128)(2,1)S(1)}, bf16[32,512]{1,0:T(8,128)(2,1)S(1)}, u32[]{:S(2)}, u32[]{:S(2)}) collective-permute-start(bf16[32,512]{1,0:T(8,128)(2,1)S(1)} %get-tuple-element.28), channel_id=1, source_target_pairs={{0,6},{2,4},{4,2},{6,0},{1,7},{3,5},{5,3},{7,1},{8,14},{10,12},{12... | collective-permute-start | bytes 98312 | tf_op jit(solution)/shard_map/ppermute | solution.py:22
  84.9 10.1 %collective-permute-start.6 = (bf16[32,512]{1,0:T(8,128)(2,1)S(1)}, bf16[32,512]{1,0:T(8,128)(2,1)S(1)}, u32[]{:S(2)}, u32[]{:S(2)}) collective-permute-start(bf16[32,512]{1,0:T(8,128)(2,1)S(1)} %get-tuple-element.29), channel_id=1, source_target_pairs={{0,4},{2,6},{4,0},{6,2},{1,5},{3,7},{5,1},{7,3},{8,12},{10,14},{12... | collective-permute-start | bytes 98312 | tf_op jit(solution)/shard_map/ppermute | solution.py:22
  87.7 7.4 %collective-permute-start.5 = (bf16[32,512]{1,0:T(8,128)(2,1)S(1)}, bf16[32,512]{1,0:T(8,128)(2,1)S(1)}, u32[]{:S(2)}, u32[]{:S(2)}) collective-permute-start(bf16[32,512]{1,0:T(8,128)(2,1)S(1)} %get-tuple-element.30), channel_id=1, source_target_pairs={{0,2},{2,0},{4,6},{6,4},{1,3},{3,1},{5,7},{7,5},{8,10},{10,8},{12,... | collective-permute-start | bytes 98312 | tf_op jit(solution)/shard_map/ppermute | solution.py:22

commit v5 on v4

--- a/solution.py
+++ b/solution.py
@@ -46,48 +46,55 @@
     return (col == source_of(row)).astype(F32).astype(BF)
 
 
-def pack_body(where_ref, tok_ref, grad_ref, wq_ref, wo_ref, out_ref):
-    both = jnp.concatenate([tok_ref[...], grad_ref[...]], axis=0)
+def pack_body(
+    where_ref, tok_ref, grad_ref, wq_ref, wo_ref, out_ref, both_vm, wq_vm, wo_vm, sems
+):
+    copies = [
+        pltpu.make_async_copy(src, dst, sems.at[i])
+        for i, (src, dst) in enumerate(
+            [
+                (tok_ref, both_vm.at[0:128]),
+                (grad_ref, both_vm.at[128:256]),
+                (wq_ref, wq_vm),
+                (wo_ref, wo_vm),
+            ]
+        )
+    ]
+    for copy in copies:
+        copy.start()
     pick = chooser(
         256, 256, lambda i: (i >> 2 & 1) * 128 + (i & 1) * 64 + (i >> 1 & 1) * 32 + (i >> 3)
     )
-    out_ref[:, :512] = dot(pick, both).astype(BF)
+    for copy in copies:
+        copy.wait()
+    out_ref[:, :512] = dot(pick, both_vm[...]).astype(BF)
     x = where_ref[0]
-    part = wo_ref[...].astype(F32)
+    part = wo_vm[...].astype(F32)
     for i in range(3):
-        part = jnp.where(x == i, wq_ref[:, i * 512 : i * 512 + 512].astype(F32), part)
+        part = jnp.where(x == i, wq_vm[:, i * 512 : i * 512 + 512].astype(F32), part)
     blocks = jnp.concatenate([part[:, y * 128 : y * 128 + 128] for y in range(Y)], axis=0)
     out_ref[:, 512:] = jnp.concatenate([blocks] * ZL, axis=0).astype(BF)
 
 
-def weights_body(where_ref, moved_ref, sent_ref, hop_ref):
-    y = where_ref[1]
+def halves(arr):
+    return arr[:, :64], arr[:, 64:]
+
+
+def weights_body(where_ref, moved_ref, sent_ref, own_ref):
     pick = chooser(
-        256,
-        256,
-        lambda i: (i >> 1 & 7) * 32 + ((i >> 6) ^ y) * 8 + (i >> 4 & 3) * 2 + (i & 1),
-    )
-    tokens = dot(pick, moved_ref[:, :512]).astype(BF)
-    for k in range(Y):
-        hop_ref[k] = tokens[k * 64 : k * 64 + 64]
-    block = moved_ref[:, 512:].astype(F32).reshape(ZL, 4, 8, 128)
-    cols = [block[:, lb].reshape(64, 128) for lb in range(4)]
-    full = jnp.concatenate(cols, axis=1)
-    planes = full.reshape(4, 2, 8, 512)
+        256, 256, lambda i: (i >> 1 & 31) * 8 + (i >> 7) * 4 + (i >> 6 & 1) * 2 + (i & 1)
+    )
+    own_ref[...] = dot(pick, moved_ref[:, :512]).astype(BF)
+    block = moved_ref[:, 512:].astype(F32)
+    (low0, low1), (high0, high1) = halves(block[:128]), halves(block[128:])
+    planes = block.reshape(4, 2, 32, 128)
     outs = x_is_last(where_ref)
-    for core in range(2):
-        own = planes[:, core].reshape(32, 512)
-        own = jnp.concatenate([own[:, :256], own[:, 256:]], axis=0)
-        heads = jnp.concatenate([col[:, core * 64 : core * 64 + 64] for col in cols], axis=1)
-        mine = jnp.where(outs, own, heads).astype(BF)
+    for core, cols in ((0, (low0, high0)), (1, (low1, high1))):
+        mine = jnp.where(
+            outs, planes[:, core].reshape(128, 128), jnp.concatenate(cols, axis=1)
+        ).astype(BF)
         for xy in range(X * Y):
             sent_ref[2 * xy + core] = mine
-
-
-def gather_body(b0_ref, b1_ref, b2_ref, b3_ref, out_ref):
-    for tf in range(4):
-        for k, ref in enumerate((b0_ref, b1_ref, b2_ref, b3_ref)):
-            out_ref[tf * 64 + k * 16 : tf * 64 + k * 16 + 16] = ref[tf * 16 : tf * 16 + 16]
 
 
 def x_is_last(where_ref):
@@ -103,13 +110,25 @@
 def main_body(
     own_ref, far_ref, w_ref, gain_ref, parts_ref, send_ref, keep_ref
 ):
-    def gathered(part, count, width, piece):
-        blocks = [piece(w_ref[part * 8 + yc].astype(F32)) for yc in range(8)]
-        blocks = [block.reshape(count, 1, 8, width) for block in blocks]
-        return jnp.concatenate(blocks, axis=1).reshape(count * 64, width).astype(BF)
-
-    wh = jnp.concatenate([gathered(x, 8, 256, lambda arr: arr) for x in range(3)], axis=1)
-    wo = gathered(3, 4, 512, lambda arr: jnp.concatenate([arr[:32], arr[32:]], axis=1))
+    lanes = []
+    for x in range(3):
+        for pair in range(2):
+            tops, bots = [], []
+            for core in range(2):
+                at = x * 8 + pair * 4 + core
+                (a0, a1), (b0, b1) = (
+                    halves(w_ref[at].astype(F32)),
+                    halves(w_ref[at + 2].astype(F32)),
+                )
+                tops.append(jnp.concatenate([a0, b0], axis=1))
+                bots.append(jnp.concatenate([a1, b1], axis=1))
+            lanes.append(jnp.concatenate([weave(*tops), weave(*bots)], axis=0).astype(BF))
+    wh = jnp.concatenate(lanes, axis=1)
+    lanes = [
+        weave(w_ref[24 + 2 * y].astype(F32), w_ref[25 + 2 * y].astype(F32)).astype(BF)
+        for y in range(Y)
+    ]
+    wo = jnp.concatenate(lanes, axis=1)
 
     own, far = own_ref[...], far_ref[...]
     x_in = jnp.concatenate([own[0:64], far[0:64], own[64:128], far[64:128]], axis=0)
@@ -196,11 +215,7 @@
     scaled = values * inverse
     ds = (keep_ref[...] + far_ref[...].astype(F32)) * gain
     inner = jnp.mean(ds * scaled, axis=-1, keepdims=True)
-    result = (own_ref[128:256, :].astype(F32) + inverse * (ds - scaled * inner)).astype(BF)
-    for k in range(Y):
-        out_ref[k] = jnp.concatenate(
-            [result[k * 16 : k * 16 + 16], result[64 + k * 16 : 64 + k * 16 + 16]], axis=0
-        )
+    out_ref[...] = (own_ref[128:256, :].astype(F32) + inverse * (ds - scaled * inner)).astype(BF)
 
 
 def two_rows(vec):
@@ -213,7 +228,7 @@
     return jnp.concatenate([high, rows - high], axis=0)
 
 
-def merge_body(where_ref, got_ref, b0_ref, b1_ref, b2_ref, b3_ref, out_ref):
+def merge_body(where_ref, got_ref, rows_ref, out_ref):
     total = got_ref[0:2].astype(F32)
     for i in range(1, 16):
         total = total + got_ref[2 * i : 2 * i + 2].astype(F32)
@@ -229,11 +244,8 @@
         jnp.concatenate([high[i * 32 : i * 32 + 32] for i in range(4)], axis=1),
     )
     out_ref[:, :512] = jnp.where(x_is_last(where_ref), rows, cols).astype(BF)
-    pick = chooser(64, 64, lambda i: (i >> 1 & 3) * 16 + (i >> 3) * 2 + (i & 1))
     for f in range(2):
-        blocks = [ref[f * 16 : f * 16 + 16] for ref in (b0_ref, b1_ref, b2_ref, b3_ref)]
-        rows = dot(pick, jnp.concatenate(blocks, axis=0)).astype(BF)
-        out_ref[:, 512 + f * 512 : 1024 + f * 512] = rows
+        out_ref[:, 512 + f * 512 : 1024 + f * 512] = rows_ref[f * 64 : f * 64 + 64]
     gains = total[0, 128:] + total[1, 128:]
     gains = two_blocks(unpair(gains))
     out_ref[:, 1536:] = jnp.concatenate([gains] * ZL, axis=0).astype(BF)
@@ -245,17 +257,27 @@
     )
 
 
-def split_body(where_ref, back_ref, tokens_ref, last_ref):
+def split_body(where_ref, back_ref, hop_ref, last_ref):
     y = where_ref[1]
-    pick = chooser(64, 64, lambda i: (i >> 2 & 7) * 8 + ((i & 3) ^ y) * 2 + (i >> 5))
+    pick = chooser(64, 64, lambda i: (i >> 1 & 7) * 8 + ((i >> 4) ^ y) * 2 + (i & 1))
     for f in range(2):
         rows = dot(pick, back_ref[:, 512 + f * 512 : 1024 + f * 512]).astype(BF)
-        for b in range(2):
-            tokens_ref[b * 64 + f * 32 : b * 64 + f * 32 + 32] = rows[b * 32 : b * 32 + 32]
+        for k in range(Y):
+            hop_ref[k, f * 16 : f * 16 + 16] = rows[k * 16 : k * 16 + 16]
     sums = jnp.sum(back_ref[:, :512].astype(F32).reshape(ZL, 8, 512), axis=0)
     last_ref[:, :512] = sums.astype(BF)
     gains = jnp.sum(back_ref[:, 1536:].astype(F32).reshape(ZL, 8, 128), axis=0)
     last_ref[:, 512:] = two_blocks(gains[0:4] + gains[4:8]).astype(BF)
+
+
+def tokens_body(where_ref, b0_ref, b1_ref, b2_ref, b3_ref, out_ref):
+    y = where_ref[1]
+    blocks = jnp.concatenate([ref[...] for ref in (b0_ref, b1_ref, b2_ref, b3_ref)], axis=0)
+
+    def source(i):
+        return ((i & 3) ^ y) * 32 + (i >> 5 & 1) * 16 + (i >> 2 & 7) * 2 + (i >> 6)
+
+    out_ref[...] = dot(chooser(128, 128, source), blocks).astype(BF)
 
 
 def end_body(got_ref, qkv_ref, out_ref, gain_ref):
@@ -274,18 +296,25 @@
     row = gain.reshape(1, 512)
     plane = ("x", "y", "c")
 
-    [packed] = call(
+    hbm = pl.BlockSpec(memory_space=pl.ANY)
+    packed = pl.pallas_call(
         pack_body,
-        [((256, 640), BF)],
-        where, tokens.reshape(128, 512), grad_out.reshape(128, 512), w_qkv, w_out,
-        smem=1,
-    )
-    moved = exchange(packed.reshape(ZL, 32, 640), "zl").reshape(256, 640)
-    sent, hop = call(
-        weights_body, [((32, 64, 256), BF), ((Y, 64, 512), BF)], where, moved, smem=1
+        out_shape=jax.ShapeDtypeStruct((256, 640), BF),
+        in_specs=[pl.BlockSpec(memory_space=pltpu.SMEM)] + [hbm] * 4,
+        out_specs=pl.BlockSpec(memory_space=pltpu.VMEM),
+        scratch_shapes=[
+            pltpu.VMEM((256, 512), BF),
+            pltpu.VMEM((8, 1536), BF),
+            pltpu.VMEM((8, 512), BF),
+            pltpu.SemaphoreType.DMA((4,)),
+        ],
+        compiler_params=pltpu.CompilerParams(vmem_limit_bytes=60 * 2**20),
+    )(where, tokens.reshape(128, 512), grad_out.reshape(128, 512), w_qkv, w_out)
+    moved = exchange(packed.reshape(ZL * Y, 8, 640), ("zl", "y")).reshape(256, 640)
+    sent, own = call(
+        weights_body, [((32, 128, 128), BF), ((256, 512), BF)], where, moved, smem=1
     )
     weights = exchange(sent, plane)
-    [own] = call(gather_body, [((256, 512), BF)], *over_y(hop))
     far = lax.ppermute(own, "c", SWAP)
     parts, send, keep = call(
         main_body,
@@ -294,13 +323,14 @@
     )
     got = exchange(parts, plane)
     dn_far = lax.ppermute(send, "c", SWAP)
-    [result] = call(finish_body, [((Y, 32, 512), BF)], own, keep, dn_far, row)
-    [sent] = call(merge_body, [((64, 1664), BF)], where, got, *over_y(result), smem=1)
+    [result] = call(finish_body, [((128, 512), BF)], own, keep, dn_far, row)
+    [sent] = call(merge_body, [((64, 1664), BF)], where, got, result, smem=1)
     back = exchange(sent.reshape(ZL, 8, 1664), "zl").reshape(64, 1664)
-    grad_tokens, last = call(
-        split_body, [((128, 512), BF), ((8, 640), BF)], where, back, smem=1
+    hop, last = call(
+        split_body, [((Y, 32, 512), BF), ((8, 640), BF)], where, back, smem=1
     )
     ends = exchange(jnp.broadcast_to(last[None], (ZH * X, 8, 640)), ("zh", "x"))
+    [grad_tokens] = call(tokens_body, [((128, 512), BF)], where, *over_y(hop), smem=1)
     shard_qkv, shard_out, total = call(
         end_body, [((8, 1536), F32), ((8, 512), F32), ((4, 128), F32)], ends
     )

time: 142 us -> 138 us (0.972)
  blocking collectives: 74.9 us -> 56.4 us
  waiting for transfers between devices: 16 us -> 33.7 us
  starting transfers between devices: 36.7 us -> 32.4 us
  Pallas kernels: 9.64 us -> 12.6 us
  local copies, waits for them, and re-layouts: 3.28 us -> 0.66 us
    all_to_all x2 -> x3, waiting for transfers between devices: 0.01 us -> 28.9 us  [exchange(): return lax.all_to_all(arr, axes, split_axis=0, concat_axis=0, tiled=True)]
    all_to_all x3 -> x2, blocking collectives: 74.9 us -> 56.4 us  [exchange(): return lax.all_to_all(arr, axes, split_axis=0, concat_axis=0, tiled=True)]
    ppermute x6 -> x3, waiting for transfers between devices: 13.5 us -> 2.43 us  [over_y(): lax.ppermute(blocks[k], 'y', [(i, i ^ k) for i in range(Y)])]
    ppermute x6 -> x3, starting transfers between devices: 19.6 us -> 9.82 us  [over_y(): lax.ppermute(blocks[k], 'y', [(i, i ^ k) for i in range(Y)])]
    all_to_all x2 -> x3, starting transfers between devices: 13 us -> 18.2 us  [exchange(): return lax.all_to_all(arr, axes, split_axis=0, concat_axis=0, tiled=True)]
    unnamed x10 -> x4, local copies, waits for them, and re-layouts: 3.24 us -> 0.01 us
    pallas_call x0 -> x1, Pallas kernels: none -> 2.75 us  [on_device(): pl.pallas_call(pack_body, out_shape=jax.ShapeDtypeStruct((256, 640), BF),...]
    pallas_call x8 -> x7, Pallas kernels: 9.64 us -> 9.87 us  [call(): pl.pallas_call(body, out_shape=[jax.ShapeDtypeStruct(shape, kind) for sha...]
  transfers between devices with their start and end apart: 10 -> 8, of which waited for: 4 -> 7; matrix products, arithmetic and copies ran while one was open for 0% -> 0% of each run, Pallas kernels for 0% -> 1%
where the time goes in v5:
time: 138 us; the launch traced here: 137 us
  blocking collectives  56.4 us (41%)
  waiting for transfers between devices  33.7 us (24%)
  starting transfers between devices  32.4 us (23%)
  Pallas kernels  12.6 us (9%)
    all_to_all x2, blocking collectives, exchange(): return lax.all_to_all(arr, axes, split_axis=0, concat_axis=0, tiled=True)  56.4 us
    all_to_all x3, waiting for transfers between devices, exchange(): return lax.all_to_all(arr, axes, split_axis=0, concat_axis=0, tiled=True)  28.9 us
    all_to_all x3, starting transfers between devices, exchange(): return lax.all_to_all(arr, axes, split_axis=0, concat_axis=0, tiled=True)  18.2 us
    pallas_call x7, Pallas kernels, call(): pl.pallas_call(body, out_shape=[jax.ShapeDtypeStruct(shape, kind) for sha...  9.87 us
    ppermute x3, starting transfers between devices, over_y(): lax.ppermute(blocks[k], 'y', [(i, i ^ k) for i in range(Y)])  9.82 us
  transfers between devices with their start and end apart: 8, of which 7 were waited for; matrix products, arithmetic and copies ran while one was open for 0% of the time, Pallas kernels for 1%

profile of v5, /device:TPU:32, one launch (start us, length us, event | category | flops | bytes accessed | tf_op | source)
XLA Modules:
  0.0 137.0 jit_solution(16162431986377862453)
XLA Ops:
  0.6 0.6 pad_add_fusion.where_ref
  1.2 0.0 copy-start
  1.2 2.7 %shard_map.84 = bf16[256,640]{1,0:T(8,128)(2,1)} custom-call(s32[2]{0:T(128)} %pad_add_fusion.where_ref, bf16[128,512]{1,0:T(8,128)(2,1)} %bitcast.26, bf16[128,512]{1,0:T(8,128)(2,1)} %bitcast.27, bf16[8,1536]{1,0:T(8,128)(2,1)} %wq_ref.1, bf16[8,512]{1,0:T(8,128)(2,1)} %wo_ref.1), custom_call_target="tpu_custom_call" | custom-call | tf_op jit(solution)/shard_map/pallas_call | solution.py:300
  4.0 36.0 %all_to_all.25 = bf16[32,8,640]{2,1,0:T(8,128)(2,1)S(1)} all-to-all(bf16[32,8,640]{2,1,0:T(8,128)(2,1)} %bitcast.24), channel_id=1, replica_groups=mesh['zh'=2,'x'=4,'zl'=8,'y'=4,'c'=2] {'zl','y'}, dimensions={0} | all-to-all | bytes 655360 | tf_op jit(solution)/shard_map/all_to_all | solution.py:18
  40.0 0.0 copy-done
  40.0 1.8 %shard_map.85 = (bf16[32,128,128]{2,1,0:T(8,128)(2,1)}, bf16[256,512]{1,0:T(8,128)(2,1)S(1)}) custom-call(s32[2]{0:T(128)S(1)} %copy-done, bf16[256,640]{1,0:T(8,128)(2,1)S(1)} %bitcast.19), custom_call_target="tpu_custom_call" | custom-call | tf_op jit(solution)/shard_map/pallas_call | solution.py:29
  41.8 0.0 copy-start.1
  41.8 5.6 %all-to-all-start.1 = ((bf16[32,128,128]{2,1,0:T(8,128)(2,1)}), bf16[32,128,128]{2,1,0:T(8,128)(2,1)S(1)}, u32[]{:S(2)}, u32[]{:S(2)}) async-start(bf16[32,128,128]{2,1,0:T(8,128)(2,1)} %get-tuple-element.15), calls=%async_computation.1 | async-start | bytes 2097152 | tf_op jit(solution)/shard_map/all_to_all | solution.py:18
  47.4 2.2 %collective-permute-start = (bf16[256,512]{1,0:T(8,128)(2,1)S(1)}, bf16[256,512]{1,0:T(8,128)(2,1)S(1)}, u32[]{:S(2)}, u32[]{:S(2)}) collective-permute-start(bf16[256,512]{1,0:T(8,128)(2,1)S(1)} %get-tuple-element.14.own_ref), channel_id=1, source_target_pairs={{0,1},{1,0},{2,3},{3,2},{4,5},{5,4},{6,7},{7,6},{8,9},{9,8},{10,11... | collective-permute-start | bytes 786440 | tf_op jit(solution)/shard_map/ppermute | solution.py:318
  49.6 1.2 collective-permute-done.far_ref
  50.8 13.4 %all-to-all-done.1.w_ref = bf16[32,128,128]{2,1,0:T(8,128)(2,1)S(1)} async-done(((bf16[32,128,128]{2,1,0:T(8,128)(2,1)}), bf16[32,128,128]{2,1,0:T(8,128)(2,1)S(1)}, u32[]{:S(2)}, u32[]{:S(2)}) %all-to-all-start.1) | async-done | bytes 1048608 | tf_op jit(solution)/shard_map/all_to_all | solution.py:18
  64.2 0.0 copy-done.1
  64.2 4.4 %shard_map.86 = (bf16[32,136,128]{2,1,0:T(8,128)(2,1)}, bf16[128,512]{1,0:T(8,128)(2,1)S(1)}, f32[128,512]{1,0:T(8,128)S(1)}) custom-call(bf16[256,512]{1,0:T(8,128)(2,1)S(1)} %get-tuple-element.14.own_ref, bf16[256,512]{1,0:T(8,128)(2,1)S(1)} %collective-permute-done.far_ref, bf16[32,128,128]{2,1,0:T(8,128)(2,1)S(1)} %all-to-all-done.1.w_ref, ...), custom_call_target="tpu_custom_call" | custom-call | tf_op jit(solution)/shard_map/pallas_call | solution.py:29
  68.6 4.1 %all-to-all-start.2 = ((bf16[32,136,128]{2,1,0:T(8,128)(2,1)}), bf16[32,136,128]{2,1,0:T(8,128)(2,1)S(1)}, u32[]{:S(2)}, u32[]{:S(2)}) async-start(bf16[32,136,128]{2,1,0:T(8,128)(2,1)} %get-tuple-element.16), calls=%async_computation.2 | async-start | bytes 2228224 | tf_op jit(solution)/shard_map/all_to_all | solution.py:18
  72.6 2.2 %collective-permute-start.1 = (bf16[128,512]{1,0:T(8,128)(2,1)S(1)}, bf16[128,512]{1,0:T(8,128)(2,1)S(1)}, u32[]{:S(2)}, u32[]{:S(2)}) collective-permute-start(bf16[128,512]{1,0:T(8,128)(2,1)S(1)} %get-tuple-element.18), channel_id=1, source_target_pairs={{0,1},{1,0},{2,3},{3,2},{4,5},{5,4},{6,7},{7,6},{8,9},{9,8},{10,11... | collective-permute-start | bytes 393224 | tf_op jit(solution)/shard_map/ppermute | solution.py:325
  74.8 1.1 collective-permute-done.1.far_ref
  75.9 0.2 shard_map.87.rows_ref
  76.1 14.1 %all-to-all-done.2.got_ref = bf16[32,136,128]{2,1,0:T(8,128)(2,1)S(1)} async-done(((bf16[32,136,128]{2,1,0:T(8,128)(2,1)}), bf16[32,136,128]{2,1,0:T(8,128)(2,1)S(1)}, u32[]{:S(2)}, u32[]{:S(2)}) %all-to-all-start.2) | async-done | bytes 1114144 | tf_op jit(solution)/shard_map/all_to_all | solution.py:18
  90.2 0.8 shard_map.88
  91.0 20.4 %all_to_all.26 = bf16[8,8,1664]{2,1,0:T(8,128)(2,1)S(1)} all-to-all(bf16[8,8,1664]{2,1,0:T(8,128)(2,1)S(1)} %bitcast.21), channel_id=1, replica_groups=mesh['zh'=2,'x'=4,'zl'=8,'y'=4,'c'=2] {'zl'}, dimensions={0} | all-to-all | bytes 425984 | tf_op jit(solution)/shard_map/all_to_all | solution.py:18
  111.4 0.7 shard_map.89
  112.1 0.6 broadcast_in_dim.2
  112.7 8.5 %all-to-all-start.4 = ((bf16[8,8,640]{2,1,0:T(8,128)(2,1)}), bf16[8,8,640]{2,1,0:T(8,128)(2,1)S(1)}, u32[]{:S(2)}, u32[]{:S(2)}) async-start(bf16[8,8,640]{2,1,0:T(8,128)(2,1)} %broadcast_in_dim.2), calls=%async_computation.4 | async-start | bytes 163840 | tf_op jit(solution)/shard_map/all_to_all | solution.py:18
  121.3 3.0 %collective-permute-start.4 = (bf16[32,512]{1,0:T(8,128)(2,1)S(1)}, bf16[32,512]{1,0:T(8,128)(2,1)S(1)}, u32[]{:S(2)}, u32[]{:S(2)}) collective-permute-start(bf16[32,512]{1,0:T(8,128)(2,1)S(1)} %get-tuple-element.24), channel_id=1, source_target_pairs={{0,6},{2,4},{4,2},{6,0},{1,7},{3,5},{5,3},{7,1},{8,14},{10,12},{12... | collective-permute-start | bytes 98312 | tf_op jit(solution)/shard_map/ppermute | solution.py:22
  124.3 3.5 %collective-permute-start.3 = (bf16[32,512]{1,0:T(8,128)(2,1)S(1)}, bf16[32,512]{1,0:T(8,128)(2,1)S(1)}, u32[]{:S(2)}, u32[]{:S(2)}) collective-permute-start(bf16[32,512]{1,0:T(8,128)(2,1)S(1)} %get-tuple-element.25), channel_id=1, source_target_pairs={{0,4},{2,6},{4,0},{6,2},{1,5},{3,7},{5,1},{7,3},{8,12},{10,14},{12... | collective-permute-start | bytes 98312 | tf_op jit(solution)/shard_map/ppermute | solution.py:22
  127.7 3.4 %collective-permute-start.2 = (bf16[32,512]{1,0:T(8,128)(2,1)S(1)}, bf16[32,512]{1,0:T(8,128)(2,1)S(1)}, u32[]{:S(2)}, u32[]{:S(2)}) collective-permute-start(bf16[32,512]{1,0:T(8,128)(2,1)S(1)} %get-tuple-element.26), channel_id=1, source_target_pairs={{0,2},{2,0},{4,6},{6,4},{1,3},{3,1},{5,7},{7,5},{8,10},{10,8},{12,... | collective-permute-start | bytes 98312 | tf_op jit(solution)/shard_map/ppermute | solution.py:22
  131.1 0.0 collective-permute-done.4.b3_ref
  131.1 0.7 collective-permute-done.3.b2_ref
  131.8 1.7 %collective-permute-done.2.b1_ref = bf16[32,512]{1,0:T(8,128)(2,1)S(1)} collective-permute-done((bf16[32,512]{1,0:T(8,128)(2,1)S(1)}, bf16[32,512]{1,0:T(8,128)(2,1)S(1)}, u32[]{:S(2)}, u32[]{:S(2)}) %collective-permute-start.2) | collective-permute-done | bytes 32800 | tf_op jit(solution)/shard_map/ppermute | solution.py:22
  133.5 1.4 %shard_map.90 = bf16[128,512]{1,0:T(8,128)(2,1)} custom-call(s32[2]{0:T(128)S(1)} %copy-done, bf16[32,512]{1,0:T(8,128)(2,1)S(1)} %get-tuple-element.27.b0_ref, bf16[32,512]{1,0:T(8,128)(2,1)S(1)} %collective-permute-done.2.b1_ref, bf16[32,512]{1,0:T(8,128)(2,1)S(1)} %collective-permute-done.3.b2_ref, bf16[32,512]{1,0:T(8,128)(2,1)S(1)} %collective-permute-done.4.b3_ref), custom_call_target="tpu_custom_call" | custom-call | tf_op jit(solution)/shard_map/pallas_call | solution.py:29
  134.9 1.4 %all-to-all-done.4.got_ref = bf16[8,8,640]{2,1,0:T(8,128)(2,1)S(1)} async-done(((bf16[8,8,640]{2,1,0:T(8,128)(2,1)}), bf16[8,8,640]{2,1,0:T(8,128)(2,1)S(1)}, u32[]{:S(2)}, u32[]{:S(2)}) %all-to-all-start.4) | async-done | bytes 81952 | tf_op jit(solution)/shard_map/all_to_all | solution.py:18
  136.4 0.6 shard_map.91
  (1 shorter events, 0.0 us)
Async XLA Ops:
  1.2 38.8 %copy-start = (s32[2]{0:T(128)S(1)}, s32[2]{0:T(128)}, u32[]{:S(2)}) copy-start(s32[2]{0:T(128)} %pad_add_fusion.where_ref) | copy-start | bytes 28
  41.8 22.4 %copy-start.1 = (f32[512]{0:T(512)S(1)}, f32[512]{0:T(512)}, u32[]{:S(2)}) copy-start(f32[512]{0:T(512)} %param.7) | copy-start | bytes 6148
  41.8 22.4 %all-to-all-start.1 = ((bf16[32,128,128]{2,1,0:T(8,128)(2,1)}), bf16[32,128,128]{2,1,0:T(8,128)(2,1)S(1)}, u32[]{:S(2)}, u32[]{:S(2)}) async-start(bf16[32,128,128]{2,1,0:T(8,128)(2,1)} %get-tuple-element.15), calls=%async_computation.1 | async-start | bytes 2097152 | tf_op jit(solution)/shard_map/all_to_all | solution.py:18
  47.4 3.4 %collective-permute-start = (bf16[256,512]{1,0:T(8,128)(2,1)S(1)}, bf16[256,512]{1,0:T(8,128)(2,1)S(1)}, u32[]{:S(2)}, u32[]{:S(2)}) collective-permute-start(bf16[256,512]{1,0:T(8,128)(2,1)S(1)} %get-tuple-element.14.own_ref), channel_id=1, source_target_pairs={{0,1},{1,0},{2,3},{3,2},{4,5},{5,4},{6,7},{7,6},{8,9},{9,8},{10,11... | collective-permute-start | bytes 786440 | tf_op jit(solution)/shard_map/ppermute | solution.py:318
  68.6 21.6 %all-to-all-start.2 = ((bf16[32,136,128]{2,1,0:T(8,128)(2,1)}), bf16[32,136,128]{2,1,0:T(8,128)(2,1)S(1)}, u32[]{:S(2)}, u32[]{:S(2)}) async-start(bf16[32,136,128]{2,1,0:T(8,128)(2,1)} %get-tuple-element.16), calls=%async_computation.2 | async-start | bytes 2228224 | tf_op jit(solution)/shard_map/all_to_all | solution.py:18
  72.6 3.2 %collective-permute-start.1 = (bf16[128,512]{1,0:T(8,128)(2,1)S(1)}, bf16[128,512]{1,0:T(8,128)(2,1)S(1)}, u32[]{:S(2)}, u32[]{:S(2)}) collective-permute-start(bf16[128,512]{1,0:T(8,128)(2,1)S(1)} %get-tuple-element.18), channel_id=1, source_target_pairs={{0,1},{1,0},{2,3},{3,2},{4,5},{5,4},{6,7},{7,6},{8,9},{9,8},{10,11... | collective-permute-start | bytes 393224 | tf_op jit(solution)/shard_map/ppermute | solution.py:325
  112.7 23.6 %all-to-all-start.4 = ((bf16[8,8,640]{2,1,0:T(8,128)(2,1)}), bf16[8,8,640]{2,1,0:T(8,128)(2,1)S(1)}, u32[]{:S(2)}, u32[]{:S(2)}) async-start(bf16[8,8,640]{2,1,0:T(8,128)(2,1)} %broadcast_in_dim.2), calls=%async_computation.4 | async-start | bytes 163840 | tf_op jit(solution)/shard_map/all_to_all | solution.py:18
  121.3 9.8 %collective-permute-start.4 = (bf16[32,512]{1,0:T(8,128)(2,1)S(1)}, bf16[32,512]{1,0:T(8,128)(2,1)S(1)}, u32[]{:S(2)}, u32[]{:S(2)}) collective-permute-start(bf16[32,512]{1,0:T(8,128)(2,1)S(1)} %get-tuple-element.24), channel_id=1, source_target_pairs={{0,6},{2,4},{4,2},{6,0},{1,7},{3,5},{5,3},{7,1},{8,14},{10,12},{12... | collective-permute-start | bytes 98312 | tf_op jit(solution)/shard_map/ppermute | solution.py:22
  124.3 7.5 %collective-permute-start.3 = (bf16[32,512]{1,0:T(8,128)(2,1)S(1)}, bf16[32,512]{1,0:T(8,128)(2,1)S(1)}, u32[]{:S(2)}, u32[]{:S(2)}) collective-permute-start(bf16[32,512]{1,0:T(8,128)(2,1)S(1)} %get-tuple-element.25), channel_id=1, source_target_pairs={{0,4},{2,6},{4,0},{6,2},{1,5},{3,7},{5,1},{7,3},{8,12},{10,14},{12... | collective-permute-start | bytes 98312 | tf_op jit(solution)/shard_map/ppermute | solution.py:22
  127.7 5.8 %collective-permute-start.2 = (bf16[32,512]{1,0:T(8,128)(2,1)S(1)}, bf16[32,512]{1,0:T(8,128)(2,1)S(1)}, u32[]{:S(2)}, u32[]{:S(2)}) collective-permute-start(bf16[32,512]{1,0:T(8,128)(2,1)S(1)} %get-tuple-element.26), channel_id=1, source_target_pairs={{0,2},{2,0},{4,6},{6,4},{1,3},{3,1},{5,7},{7,5},{8,10},{10,8},{12,... | collective-permute-start | bytes 98312 | tf_op jit(solution)/shard_map/ppermute | solution.py:22

commit v6 on v5

--- a/solution.py
+++ b/solution.py
@@ -18,20 +18,17 @@
     return lax.all_to_all(arr, axes, split_axis=0, concat_axis=0, tiled=True)
 
 
-def over_y(blocks):
-    moved = [lax.ppermute(blocks[k], "y", [(i, i ^ k) for i in range(Y)]) for k in range(1, Y)]
-    return [blocks[0]] + moved
-
-
-def call(body, outs, *args, scratch=(), smem=0):
-    specs = [pl.BlockSpec(memory_space=pltpu.SMEM)] * smem
-    specs += [pl.BlockSpec(memory_space=pltpu.VMEM)] * (len(args) - smem)
+def to_y(block, k):
+    return lax.ppermute(block, "y", [(i, i ^ k) for i in range(Y)])
+
+
+def call(body, outs, *args):
+    vmem = pl.BlockSpec(memory_space=pltpu.VMEM)
     return pl.pallas_call(
         body,
         out_shape=[jax.ShapeDtypeStruct(shape, kind) for shape, kind in outs],
-        in_specs=specs,
-        out_specs=[pl.BlockSpec(memory_space=pltpu.VMEM)] * len(outs),
-        scratch_shapes=list(scratch),
+        in_specs=[vmem] * len(args),
+        out_specs=[vmem] * len(outs),
         compiler_params=pltpu.CompilerParams(vmem_limit_bytes=40 * 2**20),
     )(*args)
 
@@ -47,7 +44,7 @@
 
 
 def pack_body(
-    where_ref, tok_ref, grad_ref, wq_ref, wo_ref, out_ref, both_vm, wq_vm, wo_vm, sems
+    tok_ref, grad_ref, wq_ref, wo_ref, out_ref, both_vm, wq_vm, wo_vm, sems
 ):
     copies = [
         pltpu.make_async_copy(src, dst, sems.at[i])
@@ -68,7 +65,7 @@
     for copy in copies:
         copy.wait()
     out_ref[:, :512] = dot(pick, both_vm[...]).astype(BF)
-    x = where_ref[0]
+    x = lax.axis_index("x")
     part = wo_vm[...].astype(F32)
     for i in range(3):
         part = jnp.where(x == i, wq_vm[:, i * 512 : i * 512 + 512].astype(F32), part)
@@ -80,15 +77,11 @@
     return arr[:, :64], arr[:, 64:]
 
 
-def weights_body(where_ref, moved_ref, sent_ref, own_ref):
-    pick = chooser(
-        256, 256, lambda i: (i >> 1 & 31) * 8 + (i >> 7) * 4 + (i >> 6 & 1) * 2 + (i & 1)
-    )
-    own_ref[...] = dot(pick, moved_ref[:, :512]).astype(BF)
+def weights_body(moved_ref, sent_ref):
     block = moved_ref[:, 512:].astype(F32)
     (low0, low1), (high0, high1) = halves(block[:128]), halves(block[128:])
     planes = block.reshape(4, 2, 32, 128)
-    outs = x_is_last(where_ref)
+    outs = x_is_last()
     for core, cols in ((0, (low0, high0)), (1, (low1, high1))):
         mine = jnp.where(
             outs, planes[:, core].reshape(128, 128), jnp.concatenate(cols, axis=1)
@@ -97,8 +90,26 @@
             sent_ref[2 * xy + core] = mine
 
 
-def x_is_last(where_ref):
-    return where_ref[0] == 3
+def rows_body(moved_ref, own_ref):
+    pick = chooser(
+        256, 256, lambda i: (i >> 1 & 31) * 8 + (i >> 7) * 4 + (i >> 6 & 1) * 2 + (i & 1)
+    )
+    own_ref[...] = dot(pick, moved_ref[:, :512]).astype(BF)
+
+
+def norm_body(own_ref, far_ref, gain_ref, scaled_ref, normed_ref, grad_ref):
+    own, far = own_ref[...], far_ref[...]
+    x_in = jnp.concatenate([own[0:64], far[0:64], own[64:128], far[64:128]], axis=0)
+    grad_ref[...] = jnp.concatenate([own[128:192], far[128:192], own[192:], far[192:]], axis=0)
+    values = x_in.astype(F32)
+    inverse = lax.rsqrt(jnp.mean(values * values, axis=-1, keepdims=True) + EPS)
+    scaled = values * inverse
+    scaled_ref[...] = scaled
+    normed_ref[...] = (scaled * gain_ref[...]).astype(BF)
+
+
+def x_is_last():
+    return lax.axis_index("x") == 3
 
 
 def weave(first, second):
@@ -108,7 +119,7 @@
 
 
 def main_body(
-    own_ref, far_ref, w_ref, gain_ref, parts_ref, send_ref, keep_ref
+    scaled_ref, normed_ref, grad_ref, w_ref, parts_ref, send_ref, keep_ref
 ):
     lanes = []
     for x in range(3):
@@ -130,14 +141,7 @@
     ]
     wo = jnp.concatenate(lanes, axis=1)
 
-    own, far = own_ref[...], far_ref[...]
-    x_in = jnp.concatenate([own[0:64], far[0:64], own[64:128], far[64:128]], axis=0)
-    g_in = jnp.concatenate([own[128:192], far[128:192], own[192:], far[192:]], axis=0)
-
-    values = x_in.astype(F32)
-    inverse = lax.rsqrt(jnp.mean(values * values, axis=-1, keepdims=True) + EPS)
-    scaled = values * inverse
-    normed = (scaled * gain_ref[...]).astype(BF)
+    normed, g_in = normed_ref[...], grad_ref[...]
     qkv = dot(normed, wh).astype(BF)
     ups = dot(g_in, wo, 1, 1).astype(BF)
 
@@ -192,7 +196,7 @@
     keep_ref[...] = jnp.concatenate([dn[0:64], dn[128:192]], axis=0)
     send_ref[...] = jnp.concatenate([dn[64:128], dn[192:]], axis=0).astype(BF)
 
-    gg = two_rows(jnp.sum(dn * scaled, axis=0, keepdims=True))
+    gg = two_rows(jnp.sum(dn * scaled_ref[...], axis=0, keepdims=True))
     gg = jnp.concatenate([gg[0:2, i * 128 : i * 128 + 128] for i in range(4)], axis=0)
 
     g_qkv = dot(normed, dqkv, 0, 0).reshape(ZL, Y, 2, 8, 768)
@@ -215,7 +219,15 @@
     scaled = values * inverse
     ds = (keep_ref[...] + far_ref[...].astype(F32)) * gain
     inner = jnp.mean(ds * scaled, axis=-1, keepdims=True)
-    out_ref[...] = (own_ref[128:256, :].astype(F32) + inverse * (ds - scaled * inner)).astype(BF)
+    result = (own_ref[128:256, :].astype(F32) + inverse * (ds - scaled * inner)).astype(BF)
+    y = lax.axis_index("y")
+
+    def source(i):
+        return (i >> 4 & 1) * 64 + (i >> 1 & 7) * 8 + ((i >> 5) ^ y) * 2 + (i & 1)
+
+    result = dot(chooser(128, 128, source), result).astype(BF)
+    for k in range(Y):
+        out_ref[k] = result[k * 32 : k * 32 + 32]
 
 
 def two_rows(vec):
@@ -228,7 +240,7 @@
     return jnp.concatenate([high, rows - high], axis=0)
 
 
-def merge_body(where_ref, got_ref, rows_ref, out_ref):
+def merge_body(got_ref, hop_ref, b1_ref, b3_ref, out_ref):
     total = got_ref[0:2].astype(F32)
     for i in range(1, 16):
         total = total + got_ref[2 * i : 2 * i + 2].astype(F32)
@@ -243,9 +255,12 @@
         jnp.concatenate([low[i * 32 : i * 32 + 32] for i in range(4)], axis=1),
         jnp.concatenate([high[i * 32 : i * 32 + 32] for i in range(4)], axis=1),
     )
-    out_ref[:, :512] = jnp.where(x_is_last(where_ref), rows, cols).astype(BF)
+    out_ref[:, :512] = jnp.where(x_is_last(), rows, cols).astype(BF)
+    pick = chooser(64, 64, lambda i: (i >> 1 & 3) * 16 + (i >> 3) * 2 + (i & 1))
+    blocks = [hop_ref[0], b1_ref[...], hop_ref[2], b3_ref[...]]
     for f in range(2):
-        out_ref[:, 512 + f * 512 : 1024 + f * 512] = rows_ref[f * 64 : f * 64 + 64]
+        rows = jnp.concatenate([block[f * 16 : f * 16 + 16] for block in blocks], axis=0)
+        out_ref[:, 512 + f * 512 : 1024 + f * 512] = dot(pick, rows).astype(BF)
     gains = total[0, 128:] + total[1, 128:]
     gains = two_blocks(unpair(gains))
     out_ref[:, 1536:] = jnp.concatenate([gains] * ZL, axis=0).astype(BF)
@@ -257,22 +272,26 @@
     )
 
 
-def split_body(where_ref, back_ref, hop_ref, last_ref):
-    y = where_ref[1]
-    pick = chooser(64, 64, lambda i: (i >> 1 & 7) * 8 + ((i >> 4) ^ y) * 2 + (i & 1))
+def split_body(back_ref, hop_ref, rest_ref, last_ref):
+    pick = chooser(64, 64, lambda i: (i >> 1 & 7) * 8 + (i >> 4) * 2 + (i & 1))
     for f in range(2):
         rows = dot(pick, back_ref[:, 512 + f * 512 : 1024 + f * 512]).astype(BF)
-        for k in range(Y):
-            hop_ref[k, f * 16 : f * 16 + 16] = rows[k * 16 : k * 16 + 16]
+        hop_ref[f * 16 : f * 16 + 16] = rows[32:48]
+        for at, k in enumerate((0, 1, 3)):
+            row = at * 32 + f * 16
+            rest_ref[row : row + 16] = rows[k * 16 : k * 16 + 16]
     sums = jnp.sum(back_ref[:, :512].astype(F32).reshape(ZL, 8, 512), axis=0)
-    last_ref[:, :512] = sums.astype(BF)
+    grads = sums.astype(BF)
     gains = jnp.sum(back_ref[:, 1536:].astype(F32).reshape(ZL, 8, 128), axis=0)
-    last_ref[:, 512:] = two_blocks(gains[0:4] + gains[4:8]).astype(BF)
-
-
-def tokens_body(where_ref, b0_ref, b1_ref, b2_ref, b3_ref, out_ref):
-    y = where_ref[1]
-    blocks = jnp.concatenate([ref[...] for ref in (b0_ref, b1_ref, b2_ref, b3_ref)], axis=0)
+    gains = two_blocks(gains[0:4] + gains[4:8]).astype(BF)
+    for i in range(ZH * X):
+        last_ref[i, :, :512] = grads
+        last_ref[i, :, 512:] = gains
+
+
+def tokens_body(rest_ref, two_ref, out_ref):
+    y = lax.axis_index("y")
+    blocks = jnp.concatenate([rest_ref[0:64], two_ref[...], rest_ref[64:96]], axis=0)
 
     def source(i):
         return ((i & 3) ^ y) * 32 + (i >> 5 & 1) * 16 + (i >> 2 & 7) * 2 + (i >> 6)
@@ -292,15 +311,14 @@
 
 
 def on_device(tokens, grad_out, gain, w_qkv, w_out):
-    where = jnp.stack([lax.axis_index("x"), lax.axis_index("y")]).astype(jnp.int32)
     row = gain.reshape(1, 512)
     plane = ("x", "y", "c")
 
-    hbm = pl.BlockSpec(memory_space=pl.ANY)
+    hbm = pl.BlockSpec(memory_space=pltpu.HBM)
     packed = pl.pallas_call(
         pack_body,
         out_shape=jax.ShapeDtypeStruct((256, 640), BF),
-        in_specs=[pl.BlockSpec(memory_space=pltpu.SMEM)] + [hbm] * 4,
+        in_specs=[hbm] * 4,
         out_specs=pl.BlockSpec(memory_space=pltpu.VMEM),
         scratch_shapes=[
             pltpu.VMEM((256, 512), BF),
@@ -308,29 +326,31 @@
             pltpu.VMEM((8, 512), BF),
             pltpu.SemaphoreType.DMA((4,)),
         ],
-        compiler_params=pltpu.CompilerParams(vmem_limit_bytes=60 * 2**20),
-    )(where, tokens.reshape(128, 512), grad_out.reshape(128, 512), w_qkv, w_out)
+        compiler_params=pltpu.CompilerParams(vmem_limit_bytes=40 * 2**20),
+    )(tokens.reshape(128, 512), grad_out.reshape(128, 512), w_qkv, w_out)
     moved = exchange(packed.reshape(ZL * Y, 8, 640), ("zl", "y")).reshape(256, 640)
-    sent, own = call(
-        weights_body, [((32, 128, 128), BF), ((256, 512), BF)], where, moved, smem=1
-    )
+    [sent] = call(weights_body, [((32, 128, 128), BF)], moved)
     weights = exchange(sent, plane)
+    [own] = call(rows_body, [((256, 512), BF)], moved)
     far = lax.ppermute(own, "c", SWAP)
+    scaled, normed, grads = call(
+        norm_body, [((256, 512), F32), ((256, 512), BF), ((256, 512), BF)], own, far, row
+    )
     parts, send, keep = call(
         main_body,
         [((32, 136, 128), BF), ((128, 512), BF), ((128, 512), F32)],
-        own, far, weights, row,
+        scaled, normed, grads, weights,
     )
     got = exchange(parts, plane)
     dn_far = lax.ppermute(send, "c", SWAP)
-    [result] = call(finish_body, [((128, 512), BF)], own, keep, dn_far, row)
-    [sent] = call(merge_body, [((64, 1664), BF)], where, got, result, smem=1)
+    [hop] = call(finish_body, [((Y, 32, 512), BF)], own, keep, dn_far, row)
+    [sent] = call(merge_body, [((64, 1664), BF)], got, hop, to_y(hop[1], 1), to_y(hop[3], 3))
     back = exchange(sent.reshape(ZL, 8, 1664), "zl").reshape(64, 1664)
-    hop, last = call(
-        split_body, [((Y, 32, 512), BF), ((8, 640), BF)], where, back, smem=1
-    )
-    ends = exchange(jnp.broadcast_to(last[None], (ZH * X, 8, 640)), ("zh", "x"))
-    [grad_tokens] = call(tokens_body, [((128, 512), BF)], where, *over_y(hop), smem=1)
+    hop, rest, last = call(
+        split_body, [((32, 512), BF), ((96, 512), BF), ((ZH * X, 8, 640), BF)], back
+    )
+    ends = exchange(last, ("zh", "x"))
+    [grad_tokens] = call(tokens_body, [((128, 512), BF)], rest, to_y(hop, 2))
     shard_qkv, shard_out, total = call(
         end_body, [((8, 1536), F32), ((8, 512), F32), ((4, 128), F32)], ends
     )

time: 138 us -> 136 us (0.986)
  Pallas kernels: 12.6 us -> 9.08 us
  local copies, waits for them, and re-layouts: 0.66 us -> 3.24 us
    all_to_all x3, waiting for transfers between devices: 28.9 us -> 22 us  [exchange(): return lax.all_to_all(arr, axes, split_axis=0, concat_axis=0, tiled=True)]
    ppermute x3, waiting for transfers between devices: 2.43 us -> 8.57 us  [to_y(): return lax.ppermute(block, 'y', [(i, i ^ k) for i in range(Y)])]
    unnamed x4 -> x10, local copies, waits for them, and re-layouts: 0.01 us -> 3.24 us
    pallas_call x1, Pallas kernels: 2.75 us -> 0.7 us  [on_device(): pl.pallas_call(pack_body, out_shape=jax.ShapeDtypeStruct((256, 640), BF),...]
    pallas_call x7 -> x9, Pallas kernels: 9.87 us -> 8.39 us  [call(): pl.pallas_call(body, out_shape=[jax.ShapeDtypeStruct(shape, kind) for sha...]
  transfers between devices with their start and end apart: 8 -> 8, of which waited for: 7 -> 8; matrix products, arithmetic and copies ran while one was open for 0% -> 0% of each run, Pallas kernels for 1% -> 1%
where the time goes in v6:
time: 136 us; the launch traced here: 135 us
  blocking collectives  56.2 us (41%)
  starting transfers between devices  33.3 us (24%)
  waiting for transfers between devices  32.8 us (24%)
  Pallas kernels  9.08 us (7%)
  local copies, waits for them, and re-layouts  3.24 us (2%)
    all_to_all x2, blocking collectives, exchange(): return lax.all_to_all(arr, axes, split_axis=0, concat_axis=0, tiled=True)  56.2 us
    all_to_all x3, waiting for transfers between devices, exchange(): return lax.all_to_all(arr, axes, split_axis=0, concat_axis=0, tiled=True)  22 us
    all_to_all x3, starting transfers between devices, exchange(): return lax.all_to_all(arr, axes, split_axis=0, concat_axis=0, tiled=True)  18.4 us
    ppermute x3, starting transfers between devices, to_y(): return lax.ppermute(block, 'y', [(i, i ^ k) for i in range(Y)])  10.6 us
    ppermute x3, waiting for transfers between devices, to_y(): return lax.ppermute(block, 'y', [(i, i ^ k) for i in range(Y)])  8.57 us
    pallas_call x9, Pallas kernels, call(): pl.pallas_call(body, out_shape=[jax.ShapeDtypeStruct(shape, kind) for sha...  8.39 us
    unnamed x10, local copies, waits for them, and re-layouts  3.24 us
  transfers between devices with their start and end apart: 8, of which 8 were waited for; matrix products, arithmetic and copies ran while one was open for 0% of the time, Pallas kernels for 1%

profile of v6, /device:TPU:32, one launch (start us, length us, event | category | flops | bytes accessed | tf_op | source)
XLA Modules:
  0.0 135.4 jit_solution(16280502573480469959)
XLA Ops:
  0.6 0.9 copy-done
  1.5 0.9 copy-done.1
  2.4 0.7 copy-done.2
  3.2 0.7 copy-done.3
  3.9 0.7 shard_map.84
  4.6 35.8 %all_to_all.25 = bf16[32,8,640]{2,1,0:T(8,128)(2,1)S(1)} all-to-all(bf16[32,8,640]{2,1,0:T(8,128)(2,1)S(1)} %bitcast.15), channel_id=1, replica_groups=mesh['zh'=2,'x'=4,'zl'=8,'y'=4,'c'=2] {'zl','y'}, dimensions={0} | all-to-all | bytes 655360 | tf_op jit(solution)/shard_map/all_to_all | solution.py:18
  40.4 1.2 shard_map.87
  41.5 5.6 %all-to-all-start.1 = ((bf16[32,128,128]{2,1,0:T(8,128)(2,1)}), bf16[32,128,128]{2,1,0:T(8,128)(2,1)S(1)}, u32[]{:S(2)}, u32[]{:S(2)}) async-start(bf16[32,128,128]{2,1,0:T(8,128)(2,1)} %shard_map.87), calls=%async_computation.1 | async-start | bytes 2097152 | tf_op jit(solution)/shard_map/all_to_all | solution.py:18
  47.1 0.2 shard_map.85.own_ref
  47.4 2.2 %collective-permute-start = (bf16[256,512]{1,0:T(8,128)(2,1)S(1)}, bf16[256,512]{1,0:T(8,128)(2,1)S(1)}, u32[]{:S(2)}, u32[]{:S(2)}) collective-permute-start(bf16[256,512]{1,0:T(8,128)(2,1)S(1)} %shard_map.85.own_ref), channel_id=1, source_target_pairs={{0,1},{1,0},{2,3},{3,2},{4,5},{5,4},{6,7},{7,6},{8,9},{9,8},{10,11... | collective-permute-start | bytes 786440 | tf_op jit(solution)/shard_map/ppermute | solution.py:335
  49.6 1.2 collective-permute-done.far_ref
  50.8 0.2 shard_map.86
  51.0 13.0 %all-to-all-done.1.w_ref = bf16[32,128,128]{2,1,0:T(8,128)(2,1)S(1)} async-done(((bf16[32,128,128]{2,1,0:T(8,128)(2,1)}), bf16[32,128,128]{2,1,0:T(8,128)(2,1)S(1)}, u32[]{:S(2)}, u32[]{:S(2)}) %all-to-all-start.1) | async-done | bytes 1048608 | tf_op jit(solution)/shard_map/all_to_all | solution.py:18
  64.0 4.0 %shard_map.88 = (bf16[32,136,128]{2,1,0:T(8,128)(2,1)}, bf16[128,512]{1,0:T(8,128)(2,1)S(1)}, f32[128,512]{1,0:T(8,128)S(1)}) custom-call(f32[256,512]{1,0:T(8,128)S(1)} %get-tuple-element.16.scaled_ref, bf16[256,512]{1,0:T(8,128)(2,1)S(1)} %get-tuple-element.17.normed_ref, bf16[256,512]{1,0:T(8,128)(2,1)S(1)} %get-tuple-element.18.grad_ref, ...), custom_call_target="tpu_custom_call" | custom-call | tf_op jit(solution)/shard_map/pallas_call | solution.py:27
  68.0 4.1 %all-to-all-start.2 = ((bf16[32,136,128]{2,1,0:T(8,128)(2,1)}), bf16[32,136,128]{2,1,0:T(8,128)(2,1)S(1)}, u32[]{:S(2)}, u32[]{:S(2)}) async-start(bf16[32,136,128]{2,1,0:T(8,128)(2,1)} %get-tuple-element.19), calls=%async_computation.2 | async-start | bytes 2228224 | tf_op jit(solution)/shard_map/all_to_all | solution.py:18
  72.0 2.2 %collective-permute-start.1 = (bf16[128,512]{1,0:T(8,128)(2,1)S(1)}, bf16[128,512]{1,0:T(8,128)(2,1)S(1)}, u32[]{:S(2)}, u32[]{:S(2)}) collective-permute-start(bf16[128,512]{1,0:T(8,128)(2,1)S(1)} %get-tuple-element.21), channel_id=1, source_target_pairs={{0,1},{1,0},{2,3},{3,2},{4,5},{5,4},{6,7},{7,6},{8,9},{9,8},{10,11... | collective-permute-start | bytes 393224 | tf_op jit(solution)/shard_map/ppermute | solution.py:345
  74.2 1.1 collective-permute-done.1.far_ref
  75.3 0.4 shard_map.89.hop_ref
  75.7 4.9 %collective-permute-start.3 = (bf16[32,512]{1,0:T(8,128)(2,1)S(1)}, bf16[32,512]{1,0:T(8,128)(2,1)S(1)}, u32[]{:S(2)}, u32[]{:S(2)}) collective-permute-start(bf16[32,512]{1,0:T(8,128)(2,1)S(1)} %get-tuple-element.28), channel_id=1, source_target_pairs={{0,6},{2,4},{4,2},{6,0},{1,7},{3,5},{5,3},{7,1},{8,14},{10,12},{12... | collective-permute-start | bytes 98312 | tf_op jit(solution)/shard_map/ppermute | solution.py:22
  80.6 2.2 %collective-permute-start.2 = (bf16[32,512]{1,0:T(8,128)(2,1)S(1)}, bf16[32,512]{1,0:T(8,128)(2,1)S(1)}, u32[]{:S(2)}, u32[]{:S(2)}) collective-permute-start(bf16[32,512]{1,0:T(8,128)(2,1)S(1)} %get-tuple-element.29), channel_id=1, source_target_pairs={{0,2},{2,0},{4,6},{6,4},{1,3},{3,1},{5,7},{7,5},{8,10},{10,8},{12,... | collective-permute-start | bytes 98312 | tf_op jit(solution)/shard_map/ppermute | solution.py:22
  82.8 2.1 %collective-permute-done.3.b3_ref = bf16[32,512]{1,0:T(8,128)(2,1)S(1)} collective-permute-done((bf16[32,512]{1,0:T(8,128)(2,1)S(1)}, bf16[32,512]{1,0:T(8,128)(2,1)S(1)}, u32[]{:S(2)}, u32[]{:S(2)}) %collective-permute-start.3) | collective-permute-done | bytes 32800 | tf_op jit(solution)/shard_map/ppermute | solution.py:22
  84.9 2.7 %collective-permute-done.2.b1_ref = bf16[32,512]{1,0:T(8,128)(2,1)S(1)} collective-permute-done((bf16[32,512]{1,0:T(8,128)(2,1)S(1)}, bf16[32,512]{1,0:T(8,128)(2,1)S(1)}, u32[]{:S(2)}, u32[]{:S(2)}) %collective-permute-start.2) | collective-permute-done | bytes 32800 | tf_op jit(solution)/shard_map/ppermute | solution.py:22
  87.6 2.0 %all-to-all-done.2.got_ref = bf16[32,136,128]{2,1,0:T(8,128)(2,1)S(1)} async-done(((bf16[32,136,128]{2,1,0:T(8,128)(2,1)}), bf16[32,136,128]{2,1,0:T(8,128)(2,1)S(1)}, u32[]{:S(2)}, u32[]{:S(2)}) %all-to-all-start.2) | async-done | bytes 1114144 | tf_op jit(solution)/shard_map/all_to_all | solution.py:18
  89.6 0.3 shard_map.90
  89.9 20.4 %all_to_all.26 = bf16[8,8,1664]{2,1,0:T(8,128)(2,1)S(1)} all-to-all(bf16[8,8,1664]{2,1,0:T(8,128)(2,1)S(1)} %bitcast.16), channel_id=1, replica_groups=mesh['zh'=2,'x'=4,'zl'=8,'y'=4,'c'=2] {'zl'}, dimensions={0} | all-to-all | bytes 425984 | tf_op jit(solution)/shard_map/all_to_all | solution.py:18
  110.3 0.7 shard_map.91
  111.0 8.7 %all-to-all-start.4 = ((bf16[8,8,640]{2,1,0:T(8,128)(2,1)}), bf16[8,8,640]{2,1,0:T(8,128)(2,1)S(1)}, u32[]{:S(2)}, u32[]{:S(2)}) async-start(bf16[8,8,640]{2,1,0:T(8,128)(2,1)} %get-tuple-element.24), calls=%async_computation.4 | async-start | bytes 163840 | tf_op jit(solution)/shard_map/all_to_all | solution.py:18
  119.7 3.5 %collective-permute-start.4 = (bf16[32,512]{1,0:T(8,128)(2,1)S(1)}, bf16[32,512]{1,0:T(8,128)(2,1)S(1)}, u32[]{:S(2)}, u32[]{:S(2)}) collective-permute-start(bf16[32,512]{1,0:T(8,128)(2,1)S(1)} %get-tuple-element.23), channel_id=1, source_target_pairs={{0,4},{2,6},{4,0},{6,2},{1,5},{3,7},{5,1},{7,3},{8,12},{10,14},{12... | collective-permute-start | bytes 98312 | tf_op jit(solution)/shard_map/ppermute | solution.py:22
  123.2 3.8 %collective-permute-done.4.two_ref = bf16[32,512]{1,0:T(8,128)(2,1)S(1)} collective-permute-done((bf16[32,512]{1,0:T(8,128)(2,1)S(1)}, bf16[32,512]{1,0:T(8,128)(2,1)S(1)}, u32[]{:S(2)}, u32[]{:S(2)}) %collective-permute-start.4) | collective-permute-done | bytes 32800 | tf_op jit(solution)/shard_map/ppermute | solution.py:22
  127.0 0.8 shard_map.92
  127.8 7.0 %all-to-all-done.4.got_ref = bf16[8,8,640]{2,1,0:T(8,128)(2,1)S(1)} async-done(((bf16[8,8,640]{2,1,0:T(8,128)(2,1)}), bf16[8,8,640]{2,1,0:T(8,128)(2,1)S(1)}, u32[]{:S(2)}, u32[]{:S(2)}) %all-to-all-start.4) | async-done | bytes 81952 | tf_op jit(solution)/shard_map/all_to_all | solution.py:18
  134.8 0.6 shard_map.93
  (7 shorter events, 0.0 us)
Async XLA Ops:
  0.6 0.9 copy-start
  1.5 0.9 copy-start.1
  2.4 0.7 copy-start.2
  3.2 0.7 copy-start.3
  41.5 9.3 %copy-start.4 = (f32[512]{0:T(512)S(1)}, f32[512]{0:T(512)}, u32[]{:S(2)}) copy-start(f32[512]{0:T(512)} %param.7) | copy-start | bytes 6148
  41.5 22.4 %all-to-all-start.1 = ((bf16[32,128,128]{2,1,0:T(8,128)(2,1)}), bf16[32,128,128]{2,1,0:T(8,128)(2,1)S(1)}, u32[]{:S(2)}, u32[]{:S(2)}) async-start(bf16[32,128,128]{2,1,0:T(8,128)(2,1)} %shard_map.87), calls=%async_computation.1 | async-start | bytes 2097152 | tf_op jit(solution)/shard_map/all_to_all | solution.py:18
  47.4 3.4 %collective-permute-start = (bf16[256,512]{1,0:T(8,128)(2,1)S(1)}, bf16[256,512]{1,0:T(8,128)(2,1)S(1)}, u32[]{:S(2)}, u32[]{:S(2)}) collective-permute-start(bf16[256,512]{1,0:T(8,128)(2,1)S(1)} %shard_map.85.own_ref), channel_id=1, source_target_pairs={{0,1},{1,0},{2,3},{3,2},{4,5},{5,4},{6,7},{7,6},{8,9},{9,8},{10,11... | collective-permute-start | bytes 786440 | tf_op jit(solution)/shard_map/ppermute | solution.py:335
  68.0 21.6 %all-to-all-start.2 = ((bf16[32,136,128]{2,1,0:T(8,128)(2,1)}), bf16[32,136,128]{2,1,0:T(8,128)(2,1)S(1)}, u32[]{:S(2)}, u32[]{:S(2)}) async-start(bf16[32,136,128]{2,1,0:T(8,128)(2,1)} %get-tuple-element.19), calls=%async_computation.2 | async-start | bytes 2228224 | tf_op jit(solution)/shard_map/all_to_all | solution.py:18
  72.0 3.2 %collective-permute-start.1 = (bf16[128,512]{1,0:T(8,128)(2,1)S(1)}, bf16[128,512]{1,0:T(8,128)(2,1)S(1)}, u32[]{:S(2)}, u32[]{:S(2)}) collective-permute-start(bf16[128,512]{1,0:T(8,128)(2,1)S(1)} %get-tuple-element.21), channel_id=1, source_target_pairs={{0,1},{1,0},{2,3},{3,2},{4,5},{5,4},{6,7},{7,6},{8,9},{9,8},{10,11... | collective-permute-start | bytes 393224 | tf_op jit(solution)/shard_map/ppermute | solution.py:345
  75.7 9.2 %collective-permute-start.3 = (bf16[32,512]{1,0:T(8,128)(2,1)S(1)}, bf16[32,512]{1,0:T(8,128)(2,1)S(1)}, u32[]{:S(2)}, u32[]{:S(2)}) collective-permute-start(bf16[32,512]{1,0:T(8,128)(2,1)S(1)} %get-tuple-element.28), channel_id=1, source_target_pairs={{0,6},{2,4},{4,2},{6,0},{1,7},{3,5},{5,3},{7,1},{8,14},{10,12},{12... | collective-permute-start | bytes 98312 | tf_op jit(solution)/shard_map/ppermute | solution.py:22
  80.6 7.0 %collective-permute-start.2 = (bf16[32,512]{1,0:T(8,128)(2,1)S(1)}, bf16[32,512]{1,0:T(8,128)(2,1)S(1)}, u32[]{:S(2)}, u32[]{:S(2)}) collective-permute-start(bf16[32,512]{1,0:T(8,128)(2,1)S(1)} %get-tuple-element.29), channel_id=1, source_target_pairs={{0,2},{2,0},{4,6},{6,4},{1,3},{3,1},{5,7},{7,5},{8,10},{10,8},{12,... | collective-permute-start | bytes 98312 | tf_op jit(solution)/shard_map/ppermute | solution.py:22
  111.0 23.8 %all-to-all-start.4 = ((bf16[8,8,640]{2,1,0:T(8,128)(2,1)}), bf16[8,8,640]{2,1,0:T(8,128)(2,1)S(1)}, u32[]{:S(2)}, u32[]{:S(2)}) async-start(bf16[8,8,640]{2,1,0:T(8,128)(2,1)} %get-tuple-element.24), calls=%async_computation.4 | async-start | bytes 163840 | tf_op jit(solution)/shard_map/all_to_all | solution.py:18
  119.7 7.3 %collective-permute-start.4 = (bf16[32,512]{1,0:T(8,128)(2,1)S(1)}, bf16[32,512]{1,0:T(8,128)(2,1)S(1)}, u32[]{:S(2)}, u32[]{:S(2)}) collective-permute-start(bf16[32,512]{1,0:T(8,128)(2,1)S(1)} %get-tuple-element.23), channel_id=1, source_target_pairs={{0,4},{2,6},{4,0},{6,2},{1,5},{3,7},{5,1},{7,3},{8,12},{10,14},{12... | collective-permute-start | bytes 98312 | tf_op jit(solution)/shard_map/ppermute | solution.py:22

commit v7 on v6

--- a/solution.py
+++ b/solution.py
@@ -281,12 +281,17 @@
             row = at * 32 + f * 16
             rest_ref[row : row + 16] = rows[k * 16 : k * 16 + 16]
     sums = jnp.sum(back_ref[:, :512].astype(F32).reshape(ZL, 8, 512), axis=0)
-    grads = sums.astype(BF)
+    last_ref[:, :512] = sums.astype(BF)
     gains = jnp.sum(back_ref[:, 1536:].astype(F32).reshape(ZL, 8, 128), axis=0)
-    gains = two_blocks(gains[0:4] + gains[4:8]).astype(BF)
-    for i in range(ZH * X):
-        last_ref[i, :, :512] = grads
-        last_ref[i, :, 512:] = gains
+    last_ref[:, 512:] = two_blocks(gains[0:4] + gains[4:8]).astype(BF)
+
+
+def pair_body(last_ref, far_ref, sent_ref, gain_ref):
+    total = last_ref[...].astype(F32) + far_ref[...].astype(F32)
+    grads = total[:, :512].astype(BF)
+    for x in range(X):
+        sent_ref[x] = grads
+    gain_ref[...] = total[0:4, 512:] + total[4:8, 512:]
 
 
 def tokens_body(rest_ref, two_ref, out_ref):
@@ -299,22 +304,17 @@
     out_ref[...] = dot(chooser(128, 128, source), blocks).astype(BF)
 
 
-def end_body(got_ref, qkv_ref, out_ref, gain_ref):
-    for x in range(X):
-        pair = got_ref[x].astype(F32) + got_ref[X + x].astype(F32)
-        if x < 3:
-            qkv_ref[:, x * 512 : x * 512 + 512] = pair[:, :512]
-        else:
-            out_ref[...] = pair[:, :512]
-        if x == 0:
-            gain_ref[...] = pair[0:4, 512:] + pair[4:8, 512:]
+def end_body(got_ref, qkv_ref, out_ref):
+    for x in range(3):
+        qkv_ref[:, x * 512 : x * 512 + 512] = got_ref[x].astype(F32)
+    out_ref[...] = got_ref[3].astype(F32)
 
 
 def on_device(tokens, grad_out, gain, w_qkv, w_out):
     row = gain.reshape(1, 512)
     plane = ("x", "y", "c")
 
-    hbm = pl.BlockSpec(memory_space=pltpu.HBM)
+    hbm = pl.BlockSpec(memory_space=pl.ANY)
     packed = pl.pallas_call(
         pack_body,
         out_shape=jax.ShapeDtypeStruct((256, 640), BF),
@@ -326,7 +326,7 @@
             pltpu.VMEM((8, 512), BF),
             pltpu.SemaphoreType.DMA((4,)),
         ],
-        compiler_params=pltpu.CompilerParams(vmem_limit_bytes=40 * 2**20),
+        compiler_params=pltpu.CompilerParams(vmem_limit_bytes=60 * 2**20),
     )(tokens.reshape(128, 512), grad_out.reshape(128, 512), w_qkv, w_out)
     moved = exchange(packed.reshape(ZL * Y, 8, 640), ("zl", "y")).reshape(256, 640)
     [sent] = call(weights_body, [((32, 128, 128), BF)], moved)
@@ -347,13 +347,13 @@
     [sent] = call(merge_body, [((64, 1664), BF)], got, hop, to_y(hop[1], 1), to_y(hop[3], 3))
     back = exchange(sent.reshape(ZL, 8, 1664), "zl").reshape(64, 1664)
     hop, rest, last = call(
-        split_body, [((32, 512), BF), ((96, 512), BF), ((ZH * X, 8, 640), BF)], back
-    )
-    ends = exchange(last, ("zh", "x"))
+        split_body, [((32, 512), BF), ((96, 512), BF), ((8, 640), BF)], back
+    )
+    last_far = lax.ppermute(last, "zh", SWAP)
     [grad_tokens] = call(tokens_body, [((128, 512), BF)], rest, to_y(hop, 2))
-    shard_qkv, shard_out, total = call(
-        end_body, [((8, 1536), F32), ((8, 512), F32), ((4, 128), F32)], ends
-    )
+    sent, total = call(pair_body, [((X, 8, 512), BF), ((4, 128), F32)], last, last_far)
+    ends = exchange(sent, "x")
+    shard_qkv, shard_out = call(end_body, [((8, 1536), F32), ((8, 512), F32)], ends)
     return grad_tokens.reshape(1, 2, 64, 512), shard_qkv, shard_out, total.reshape(512)
 
 

time: 136 us -> 134 us (0.985)
  local copies, waits for them, and re-layouts: 3.24 us -> 0.01 us
  waiting for transfers between devices: 32.8 us -> 30 us
  starting transfers between devices: 33.3 us -> 35.3 us
    ppermute x0 -> x1, starting transfers between devices: none -> 8.22 us  [on_device(): last_far = lax.ppermute(last, 'zh', SWAP)]
    all_to_all x3, starting transfers between devices: 18.4 us -> 12.9 us  [exchange(): return lax.all_to_all(arr, axes, split_axis=0, concat_axis=0, tiled=True)]
    ppermute x3, waiting for transfers between devices: 8.57 us -> 4.81 us  [to_y(): return lax.ppermute(block, 'y', [(i, i ^ k) for i in range(Y)])]
    ppermute x0 -> x1, waiting for transfers between devices: none -> 3.31 us  [on_device(): last_far = lax.ppermute(last, 'zh', SWAP)]
    unnamed x10 -> x2, local copies, waits for them, and re-layouts: 3.24 us -> 0.01 us
    all_to_all x3, waiting for transfers between devices: 22 us -> 19.6 us  [exchange(): return lax.all_to_all(arr, axes, split_axis=0, concat_axis=0, tiled=True)]
    pallas_call x9 -> x10, Pallas kernels: 8.39 us -> 8.47 us  [call(): pl.pallas_call(body, out_shape=[jax.ShapeDtypeStruct(shape, kind) for sha...]
  transfers between devices with their start and end apart: 8 -> 9, of which waited for: 8 -> 8; matrix products, arithmetic and copies ran while one was open for 0% -> 0% of each run, Pallas kernels for 1% -> 2%
where the time goes in v7:
time: 134 us; the launch traced here: 133 us
  blocking collectives  56.4 us (42%)
  starting transfers between devices  35.3 us (26%)
  waiting for transfers between devices  30 us (22%)
  Pallas kernels  10.4 us (8%)
    all_to_all x2, blocking collectives, exchange(): return lax.all_to_all(arr, axes, split_axis=0, concat_axis=0, tiled=True)  56.4 us
    all_to_all x3, waiting for transfers between devices, exchange(): return lax.all_to_all(arr, axes, split_axis=0, concat_axis=0, tiled=True)  19.6 us
    all_to_all x3, starting transfers between devices, exchange(): return lax.all_to_all(arr, axes, split_axis=0, concat_axis=0, tiled=True)  12.9 us
    ppermute x3, starting transfers between devices, to_y(): return lax.ppermute(block, 'y', [(i, i ^ k) for i in range(Y)])  9.81 us
    pallas_call x10, Pallas kernels, call(): pl.pallas_call(body, out_shape=[jax.ShapeDtypeStruct(shape, kind) for sha...  8.47 us
    ppermute x1, starting transfers between devices, on_device(): last_far = lax.ppermute(last, 'zh', SWAP)  8.22 us
    ppermute x3, waiting for transfers between devices, to_y(): return lax.ppermute(block, 'y', [(i, i ^ k) for i in range(Y)])  4.81 us
    ppermute x1, waiting for transfers between devices, on_device(): last_far = lax.ppermute(last, 'zh', SWAP)  3.31 us
  transfers between devices with their start and end apart: 9, of which 8 were waited for; matrix products, arithmetic and copies ran while one was open for 0% of the time, Pallas kernels for 2%

profile of v7, /device:TPU:32, one launch (start us, length us, event | category | flops | bytes accessed | tf_op | source)
XLA Modules:
  0.0 132.9 jit_solution(16932831875621571531)
XLA Ops:
  0.6 2.0 %shard_map.84 = bf16[256,640]{1,0:T(8,128)(2,1)} custom-call(bf16[128,512]{1,0:T(8,128)(2,1)} %bitcast.20, bf16[128,512]{1,0:T(8,128)(2,1)} %bitcast.21, bf16[8,1536]{1,0:T(8,128)(2,1)} %wq_ref.1, bf16[8,512]{1,0:T(8,128)(2,1)} %wo_ref.1), custom_call_target="tpu_custom_call" | custom-call | tf_op jit(solution)/shard_map/pallas_call | solution.py:318
  2.6 36.0 %all_to_all.25 = bf16[32,8,640]{2,1,0:T(8,128)(2,1)S(1)} all-to-all(bf16[32,8,640]{2,1,0:T(8,128)(2,1)} %bitcast.19), channel_id=1, replica_groups=mesh['zh'=2,'x'=4,'zl'=8,'y'=4,'c'=2] {'zl','y'}, dimensions={0} | all-to-all | bytes 655360 | tf_op jit(solution)/shard_map/all_to_all | solution.py:18
  38.6 1.2 shard_map.87
  39.8 5.6 %all-to-all-start.1 = ((bf16[32,128,128]{2,1,0:T(8,128)(2,1)}), bf16[32,128,128]{2,1,0:T(8,128)(2,1)S(1)}, u32[]{:S(2)}, u32[]{:S(2)}) async-start(bf16[32,128,128]{2,1,0:T(8,128)(2,1)} %shard_map.87), calls=%async_computation.1 | async-start | bytes 2097152 | tf_op jit(solution)/shard_map/all_to_all | solution.py:18
  45.4 0.2 shard_map.85.own_ref
  45.6 2.2 %collective-permute-start = (bf16[256,512]{1,0:T(8,128)(2,1)S(1)}, bf16[256,512]{1,0:T(8,128)(2,1)S(1)}, u32[]{:S(2)}, u32[]{:S(2)}) collective-permute-start(bf16[256,512]{1,0:T(8,128)(2,1)S(1)} %shard_map.85.own_ref), channel_id=1, source_target_pairs={{0,1},{1,0},{2,3},{3,2},{4,5},{5,4},{6,7},{7,6},{8,9},{9,8},{10,11... | collective-permute-start | bytes 786440 | tf_op jit(solution)/shard_map/ppermute | solution.py:335
  47.8 1.2 collective-permute-done.far_ref
  49.0 0.0 copy-done
  49.0 0.2 shard_map.86
  49.2 13.0 %all-to-all-done.1.w_ref = bf16[32,128,128]{2,1,0:T(8,128)(2,1)S(1)} async-done(((bf16[32,128,128]{2,1,0:T(8,128)(2,1)}), bf16[32,128,128]{2,1,0:T(8,128)(2,1)S(1)}, u32[]{:S(2)}, u32[]{:S(2)}) %all-to-all-start.1) | async-done | bytes 1048608 | tf_op jit(solution)/shard_map/all_to_all | solution.py:18
  62.2 4.0 %shard_map.88 = (bf16[32,136,128]{2,1,0:T(8,128)(2,1)}, bf16[128,512]{1,0:T(8,128)(2,1)S(1)}, f32[128,512]{1,0:T(8,128)S(1)}) custom-call(f32[256,512]{1,0:T(8,128)S(1)} %get-tuple-element.17.scaled_ref, bf16[256,512]{1,0:T(8,128)(2,1)S(1)} %get-tuple-element.18.normed_ref, bf16[256,512]{1,0:T(8,128)(2,1)S(1)} %get-tuple-element.19.grad_ref, ...), custom_call_target="tpu_custom_call" | custom-call | tf_op jit(solution)/shard_map/pallas_call | solution.py:27
  66.2 4.1 %all-to-all-start.2 = ((bf16[32,136,128]{2,1,0:T(8,128)(2,1)}), bf16[32,136,128]{2,1,0:T(8,128)(2,1)S(1)}, u32[]{:S(2)}, u32[]{:S(2)}) async-start(bf16[32,136,128]{2,1,0:T(8,128)(2,1)} %get-tuple-element.20), calls=%async_computation.2 | async-start | bytes 2228224 | tf_op jit(solution)/shard_map/all_to_all | solution.py:18
  70.3 2.2 %collective-permute-start.1 = (bf16[128,512]{1,0:T(8,128)(2,1)S(1)}, bf16[128,512]{1,0:T(8,128)(2,1)S(1)}, u32[]{:S(2)}, u32[]{:S(2)}) collective-permute-start(bf16[128,512]{1,0:T(8,128)(2,1)S(1)} %get-tuple-element.22), channel_id=1, source_target_pairs={{0,1},{1,0},{2,3},{3,2},{4,5},{5,4},{6,7},{7,6},{8,9},{9,8},{10,11... | collective-permute-start | bytes 393224 | tf_op jit(solution)/shard_map/ppermute | solution.py:345
  72.5 1.1 collective-permute-done.1.far_ref
  73.5 0.4 shard_map.89.hop_ref
  73.9 4.9 %collective-permute-start.3 = (bf16[32,512]{1,0:T(8,128)(2,1)S(1)}, bf16[32,512]{1,0:T(8,128)(2,1)S(1)}, u32[]{:S(2)}, u32[]{:S(2)}) collective-permute-start(bf16[32,512]{1,0:T(8,128)(2,1)S(1)} %get-tuple-element.30), channel_id=1, source_target_pairs={{0,6},{2,4},{4,2},{6,0},{1,7},{3,5},{5,3},{7,1},{8,14},{10,12},{12... | collective-permute-start | bytes 98312 | tf_op jit(solution)/shard_map/ppermute | solution.py:22
  78.8 2.2 %collective-permute-start.2 = (bf16[32,512]{1,0:T(8,128)(2,1)S(1)}, bf16[32,512]{1,0:T(8,128)(2,1)S(1)}, u32[]{:S(2)}, u32[]{:S(2)}) collective-permute-start(bf16[32,512]{1,0:T(8,128)(2,1)S(1)} %get-tuple-element.31), channel_id=1, source_target_pairs={{0,2},{2,0},{4,6},{6,4},{1,3},{3,1},{5,7},{7,5},{8,10},{10,8},{12,... | collective-permute-start | bytes 98312 | tf_op jit(solution)/shard_map/ppermute | solution.py:22
  81.0 2.1 %collective-permute-done.3.b3_ref = bf16[32,512]{1,0:T(8,128)(2,1)S(1)} collective-permute-done((bf16[32,512]{1,0:T(8,128)(2,1)S(1)}, bf16[32,512]{1,0:T(8,128)(2,1)S(1)}, u32[]{:S(2)}, u32[]{:S(2)}) %collective-permute-start.3) | collective-permute-done | bytes 32800 | tf_op jit(solution)/shard_map/ppermute | solution.py:22
  83.1 2.7 %collective-permute-done.2.b1_ref = bf16[32,512]{1,0:T(8,128)(2,1)S(1)} collective-permute-done((bf16[32,512]{1,0:T(8,128)(2,1)S(1)}, bf16[32,512]{1,0:T(8,128)(2,1)S(1)}, u32[]{:S(2)}, u32[]{:S(2)}) %collective-permute-start.2) | collective-permute-done | bytes 32800 | tf_op jit(solution)/shard_map/ppermute | solution.py:22
  85.8 2.0 %all-to-all-done.2.got_ref = bf16[32,136,128]{2,1,0:T(8,128)(2,1)S(1)} async-done(((bf16[32,136,128]{2,1,0:T(8,128)(2,1)}), bf16[32,136,128]{2,1,0:T(8,128)(2,1)S(1)}, u32[]{:S(2)}, u32[]{:S(2)}) %all-to-all-start.2) | async-done | bytes 1114144 | tf_op jit(solution)/shard_map/all_to_all | solution.py:18
  87.8 0.3 shard_map.90
  88.1 20.4 %all_to_all.26 = bf16[8,8,1664]{2,1,0:T(8,128)(2,1)S(1)} all-to-all(bf16[8,8,1664]{2,1,0:T(8,128)(2,1)S(1)} %bitcast.15), channel_id=1, replica_groups=mesh['zh'=2,'x'=4,'zl'=8,'y'=4,'c'=2] {'zl'}, dimensions={0} | all-to-all | bytes 425984 | tf_op jit(solution)/shard_map/all_to_all | solution.py:18
  108.5 0.2 shard_map.91
  108.7 8.2 %collective-permute-start.5 = (bf16[8,640]{1,0:T(8,128)(2,1)S(1)}, bf16[8,640]{1,0:T(8,128)(2,1)S(1)}, u32[]{:S(2)}, u32[]{:S(2)}) collective-permute-start(bf16[8,640]{1,0:T(8,128)(2,1)S(1)} %get-tuple-element.25.last_ref), channel_id=1, source_target_pairs={{0,256},{256,0},{1,257},{257,1},{2,258},{258,2},{3,259},{259,3},{4... | collective-permute-start | bytes 30728 | tf_op jit(solution)/shard_map/ppermute | solution.py:352
  116.9 2.7 %collective-permute-start.4 = (bf16[32,512]{1,0:T(8,128)(2,1)S(1)}, bf16[32,512]{1,0:T(8,128)(2,1)S(1)}, u32[]{:S(2)}, u32[]{:S(2)}) collective-permute-start(bf16[32,512]{1,0:T(8,128)(2,1)S(1)} %get-tuple-element.24), channel_id=1, source_target_pairs={{0,4},{2,6},{4,0},{6,2},{1,5},{3,7},{5,1},{7,3},{8,12},{10,14},{12... | collective-permute-start | bytes 98312 | tf_op jit(solution)/shard_map/ppermute | solution.py:22
  119.6 3.3 %collective-permute-done.5.far_ref = bf16[8,640]{1,0:T(8,128)(2,1)S(1)} collective-permute-done((bf16[8,640]{1,0:T(8,128)(2,1)S(1)}, bf16[8,640]{1,0:T(8,128)(2,1)S(1)}, u32[]{:S(2)}, u32[]{:S(2)}) %collective-permute-start.5) | collective-permute-done | bytes 10272 | tf_op jit(solution)/shard_map/ppermute | solution.py:352
  122.9 0.6 shard_map.93
  123.6 3.3 %all-to-all-start.4 = ((bf16[4,8,512]{2,1,0:T(8,128)(2,1)}), bf16[4,8,512]{2,1,0:T(8,128)(2,1)S(1)}, u32[]{:S(2)}, u32[]{:S(2)}) async-start(bf16[4,8,512]{2,1,0:T(8,128)(2,1)} %get-tuple-element.26), calls=%async_computation.4 | async-start | bytes 65536 | tf_op jit(solution)/shard_map/all_to_all | solution.py:18
  126.8 0.0 collective-permute-done.4.two_ref
  126.8 0.8 shard_map.92
  127.7 4.6 %all-to-all-done.4.got_ref = bf16[4,8,512]{2,1,0:T(8,128)(2,1)S(1)} async-done(((bf16[4,8,512]{2,1,0:T(8,128)(2,1)}), bf16[4,8,512]{2,1,0:T(8,128)(2,1)S(1)}, u32[]{:S(2)}, u32[]{:S(2)}) %all-to-all-start.4) | async-done | bytes 32800 | tf_op jit(solution)/shard_map/all_to_all | solution.py:18
  132.2 0.6 shard_map.94
  (2 shorter events, 0.0 us)
Async XLA Ops:
  39.8 9.3 %copy-start = (f32[512]{0:T(512)S(1)}, f32[512]{0:T(512)}, u32[]{:S(2)}) copy-start(f32[512]{0:T(512)} %param.7) | copy-start | bytes 6148
  39.8 22.4 %all-to-all-start.1 = ((bf16[32,128,128]{2,1,0:T(8,128)(2,1)}), bf16[32,128,128]{2,1,0:T(8,128)(2,1)S(1)}, u32[]{:S(2)}, u32[]{:S(2)}) async-start(bf16[32,128,128]{2,1,0:T(8,128)(2,1)} %shard_map.87), calls=%async_computation.1 | async-start | bytes 2097152 | tf_op jit(solution)/shard_map/all_to_all | solution.py:18
  45.6 3.4 %collective-permute-start = (bf16[256,512]{1,0:T(8,128)(2,1)S(1)}, bf16[256,512]{1,0:T(8,128)(2,1)S(1)}, u32[]{:S(2)}, u32[]{:S(2)}) collective-permute-start(bf16[256,512]{1,0:T(8,128)(2,1)S(1)} %shard_map.85.own_ref), channel_id=1, source_target_pairs={{0,1},{1,0},{2,3},{3,2},{4,5},{5,4},{6,7},{7,6},{8,9},{9,8},{10,11... | collective-permute-start | bytes 786440 | tf_op jit(solution)/shard_map/ppermute | solution.py:335
  66.2 21.6 %all-to-all-start.2 = ((bf16[32,136,128]{2,1,0:T(8,128)(2,1)}), bf16[32,136,128]{2,1,0:T(8,128)(2,1)S(1)}, u32[]{:S(2)}, u32[]{:S(2)}) async-start(bf16[32,136,128]{2,1,0:T(8,128)(2,1)} %get-tuple-element.20), calls=%async_computation.2 | async-start | bytes 2228224 | tf_op jit(solution)/shard_map/all_to_all | solution.py:18
  70.3 3.2 %collective-permute-start.1 = (bf16[128,512]{1,0:T(8,128)(2,1)S(1)}, bf16[128,512]{1,0:T(8,128)(2,1)S(1)}, u32[]{:S(2)}, u32[]{:S(2)}) collective-permute-start(bf16[128,512]{1,0:T(8,128)(2,1)S(1)} %get-tuple-element.22), channel_id=1, source_target_pairs={{0,1},{1,0},{2,3},{3,2},{4,5},{5,4},{6,7},{7,6},{8,9},{9,8},{10,11... | collective-permute-start | bytes 393224 | tf_op jit(solution)/shard_map/ppermute | solution.py:345
  73.9 9.2 %collective-permute-start.3 = (bf16[32,512]{1,0:T(8,128)(2,1)S(1)}, bf16[32,512]{1,0:T(8,128)(2,1)S(1)}, u32[]{:S(2)}, u32[]{:S(2)}) collective-permute-start(bf16[32,512]{1,0:T(8,128)(2,1)S(1)} %get-tuple-element.30), channel_id=1, source_target_pairs={{0,6},{2,4},{4,2},{6,0},{1,7},{3,5},{5,3},{7,1},{8,14},{10,12},{12... | collective-permute-start | bytes 98312 | tf_op jit(solution)/shard_map/ppermute | solution.py:22
  78.8 7.0 %collective-permute-start.2 = (bf16[32,512]{1,0:T(8,128)(2,1)S(1)}, bf16[32,512]{1,0:T(8,128)(2,1)S(1)}, u32[]{:S(2)}, u32[]{:S(2)}) collective-permute-start(bf16[32,512]{1,0:T(8,128)(2,1)S(1)} %get-tuple-element.31), channel_id=1, source_target_pairs={{0,2},{2,0},{4,6},{6,4},{1,3},{3,1},{5,7},{7,5},{8,10},{10,8},{12,... | collective-permute-start | bytes 98312 | tf_op jit(solution)/shard_map/ppermute | solution.py:22
  108.7 14.3 %collective-permute-start.5 = (bf16[8,640]{1,0:T(8,128)(2,1)S(1)}, bf16[8,640]{1,0:T(8,128)(2,1)S(1)}, u32[]{:S(2)}, u32[]{:S(2)}) collective-permute-start(bf16[8,640]{1,0:T(8,128)(2,1)S(1)} %get-tuple-element.25.last_ref), channel_id=1, source_target_pairs={{0,256},{256,0},{1,257},{257,1},{2,258},{258,2},{3,259},{259,3},{4... | collective-permute-start | bytes 30728 | tf_op jit(solution)/shard_map/ppermute | solution.py:352
  116.9 10.0 %collective-permute-start.4 = (bf16[32,512]{1,0:T(8,128)(2,1)S(1)}, bf16[32,512]{1,0:T(8,128)(2,1)S(1)}, u32[]{:S(2)}, u32[]{:S(2)}) collective-permute-start(bf16[32,512]{1,0:T(8,128)(2,1)S(1)} %get-tuple-element.24), channel_id=1, source_target_pairs={{0,4},{2,6},{4,0},{6,2},{1,5},{3,7},{5,1},{7,3},{8,12},{10,14},{12... | collective-permute-start | bytes 98312 | tf_op jit(solution)/shard_map/ppermute | solution.py:22
  123.6 8.7 %all-to-all-start.4 = ((bf16[4,8,512]{2,1,0:T(8,128)(2,1)}), bf16[4,8,512]{2,1,0:T(8,128)(2,1)S(1)}, u32[]{:S(2)}, u32[]{:S(2)}) async-start(bf16[4,8,512]{2,1,0:T(8,128)(2,1)} %get-tuple-element.26), calls=%async_computation.4 | async-start | bytes 65536 | tf_op jit(solution)/shard_map/all_to_all | solution.py:18

commit v8 on v7

--- a/solution.py
+++ b/solution.py
@@ -18,8 +18,8 @@
     return lax.all_to_all(arr, axes, split_axis=0, concat_axis=0, tiled=True)
 
 
-def to_y(block, k):
-    return lax.ppermute(block, "y", [(i, i ^ k) for i in range(Y)])
+def flip(block, axis, count, bits):
+    return lax.ppermute(block, axis, [(i, i ^ bits) for i in range(count)])
 
 
 def call(body, outs, *args):
@@ -220,14 +220,16 @@
     ds = (keep_ref[...] + far_ref[...].astype(F32)) * gain
     inner = jnp.mean(ds * scaled, axis=-1, keepdims=True)
     result = (own_ref[128:256, :].astype(F32) + inverse * (ds - scaled * inner)).astype(BF)
-    y = lax.axis_index("y")
-
-    def source(i):
-        return (i >> 4 & 1) * 64 + (i >> 1 & 7) * 8 + ((i >> 5) ^ y) * 2 + (i & 1)
-
-    result = dot(chooser(128, 128, source), result).astype(BF)
-    for k in range(Y):
-        out_ref[k] = result[k * 32 : k * 32 + 32]
+    out = None
+    for half in range(2):
+
+        def source(i, half=half):
+            row = (i >> 2 & 1) * 64 + (i >> 3) * 2 + (i >> 1 & 1)
+            return jnp.where((i & 1) == half, row, -1)
+
+        part = dot(chooser(256, 128, source), result[:, half * 256 : half * 256 + 256])
+        out = part if out is None else out + part
+    out_ref[...] = out.astype(BF)
 
 
 def two_rows(vec):
@@ -240,7 +242,7 @@
     return jnp.concatenate([high, rows - high], axis=0)
 
 
-def merge_body(got_ref, hop_ref, b1_ref, b3_ref, out_ref):
+def merge_body(got_ref, out_ref):
     total = got_ref[0:2].astype(F32)
     for i in range(1, 16):
         total = total + got_ref[2 * i : 2 * i + 2].astype(F32)
@@ -255,15 +257,12 @@
         jnp.concatenate([low[i * 32 : i * 32 + 32] for i in range(4)], axis=1),
         jnp.concatenate([high[i * 32 : i * 32 + 32] for i in range(4)], axis=1),
     )
-    out_ref[:, :512] = jnp.where(x_is_last(), rows, cols).astype(BF)
-    pick = chooser(64, 64, lambda i: (i >> 1 & 3) * 16 + (i >> 3) * 2 + (i & 1))
-    blocks = [hop_ref[0], b1_ref[...], hop_ref[2], b3_ref[...]]
-    for f in range(2):
-        rows = jnp.concatenate([block[f * 16 : f * 16 + 16] for block in blocks], axis=0)
-        out_ref[:, 512 + f * 512 : 1024 + f * 512] = dot(pick, rows).astype(BF)
-    gains = total[0, 128:] + total[1, 128:]
-    gains = two_blocks(unpair(gains))
-    out_ref[:, 1536:] = jnp.concatenate([gains] * ZL, axis=0).astype(BF)
+    gains = two_blocks(unpair(total[0, 128:] + total[1, 128:]))
+    grads = jnp.where(x_is_last(), rows, cols).astype(BF)
+    gains = jnp.concatenate([gains] * ZL, axis=0).astype(BF)
+    for zh in range(ZH):
+        out_ref[zh * 64 : zh * 64 + 64, :512] = grads
+        out_ref[zh * 64 : zh * 64 + 64, 512:] = gains
 
 
 def unpair(rows):
@@ -272,42 +271,39 @@
     )
 
 
-def split_body(back_ref, hop_ref, rest_ref, last_ref):
-    pick = chooser(64, 64, lambda i: (i >> 1 & 7) * 8 + (i >> 4) * 2 + (i & 1))
-    for f in range(2):
-        rows = dot(pick, back_ref[:, 512 + f * 512 : 1024 + f * 512]).astype(BF)
-        hop_ref[f * 16 : f * 16 + 16] = rows[32:48]
-        for at, k in enumerate((0, 1, 3)):
-            row = at * 32 + f * 16
-            rest_ref[row : row + 16] = rows[k * 16 : k * 16 + 16]
-    sums = jnp.sum(back_ref[:, :512].astype(F32).reshape(ZL, 8, 512), axis=0)
-    last_ref[:, :512] = sums.astype(BF)
-    gains = jnp.sum(back_ref[:, 1536:].astype(F32).reshape(ZL, 8, 128), axis=0)
-    last_ref[:, 512:] = two_blocks(gains[0:4] + gains[4:8]).astype(BF)
-
-
-def pair_body(last_ref, far_ref, sent_ref, gain_ref):
-    total = last_ref[...].astype(F32) + far_ref[...].astype(F32)
-    grads = total[:, :512].astype(BF)
-    for x in range(X):
-        sent_ref[x] = grads
-    gain_ref[...] = total[0:4, 512:] + total[4:8, 512:]
-
-
-def tokens_body(rest_ref, two_ref, out_ref):
-    y = lax.axis_index("y")
-    blocks = jnp.concatenate([rest_ref[0:64], two_ref[...], rest_ref[64:96]], axis=0)
-
-    def source(i):
-        return ((i & 3) ^ y) * 32 + (i >> 5 & 1) * 16 + (i >> 2 & 7) * 2 + (i >> 6)
-
-    out_ref[...] = dot(chooser(128, 128, source), blocks).astype(BF)
-
-
-def end_body(got_ref, qkv_ref, out_ref):
-    for x in range(3):
-        qkv_ref[:, x * 512 : x * 512 + 512] = got_ref[x].astype(F32)
-    out_ref[...] = got_ref[3].astype(F32)
+def split_body(back_ref, last_ref, gain_ref):
+    sums = jnp.sum(back_ref[...].astype(F32).reshape(ZH * ZL, 8, 640), axis=0)
+    last_ref[...] = sums[:, :512].astype(BF)
+    gain_ref[...] = sums[0:4, 512:] + sums[4:8, 512:]
+
+
+def tokens_body(back_ref, out_ref):
+    for half in range(2):
+
+        def source(i, half=half):
+            return (i & 31) * 8 + (i >> 5 & 1) * 4 + (i >> 6) * 2 + half
+
+        rows = dot(chooser(128, 256, source), back_ref[...])
+        out_ref[:, half * 256 : half * 256 + 256] = rows.astype(BF)
+
+
+def both_body(one_ref, two_ref, out_ref):
+    out_ref[:, :512] = one_ref[...]
+    out_ref[:, 512:] = two_ref[...]
+
+
+def end_body(near_ref, far_ref, qkv_ref, out_ref):
+    x = lax.axis_index("x")
+    near, far = near_ref[...].astype(F32), far_ref[...].astype(F32)
+    parts = [near[:, :512], near[:, 512:], far[:, 512:], far[:, :512]]
+    for part in range(X):
+        total = parts[3]
+        for k in range(3):
+            total = jnp.where((x ^ k) == part, parts[k], total)
+        if part < 3:
+            qkv_ref[:, part * 512 : part * 512 + 512] = total
+        else:
+            out_ref[...] = total
 
 
 def on_device(tokens, grad_out, gain, w_qkv, w_out):
@@ -343,17 +339,17 @@
     )
     got = exchange(parts, plane)
     dn_far = lax.ppermute(send, "c", SWAP)
-    [hop] = call(finish_body, [((Y, 32, 512), BF)], own, keep, dn_far, row)
-    [sent] = call(merge_body, [((64, 1664), BF)], got, hop, to_y(hop[1], 1), to_y(hop[3], 3))
-    back = exchange(sent.reshape(ZL, 8, 1664), "zl").reshape(64, 1664)
-    hop, rest, last = call(
-        split_body, [((32, 512), BF), ((96, 512), BF), ((8, 640), BF)], back
-    )
-    last_far = lax.ppermute(last, "zh", SWAP)
-    [grad_tokens] = call(tokens_body, [((128, 512), BF)], rest, to_y(hop, 2))
-    sent, total = call(pair_body, [((X, 8, 512), BF), ((4, 128), F32)], last, last_far)
-    ends = exchange(sent, "x")
-    shard_qkv, shard_out = call(end_body, [((8, 1536), F32), ((8, 512), F32)], ends)
+    [result] = call(finish_body, [((256, 256), BF)], own, keep, dn_far, row)
+    [sent] = call(merge_body, [((128, 640), BF)], got)
+    back = exchange(sent.reshape(ZH * ZL, 8, 640), ("zh", "zl"))
+    back, result = lax.optimization_barrier((back, result))
+    result = exchange(result.reshape(ZL * Y, 8, 256), ("zl", "y")).reshape(256, 256)
+    last, total = call(split_body, [((8, 512), BF), ((4, 128), F32)], back.reshape(128, 640))
+    [near] = call(both_body, [((8, 1024), BF)], last, flip(last, "x", X, 1))
+    shard_qkv, shard_out = call(
+        end_body, [((8, 1536), F32), ((8, 512), F32)], near, flip(near, "x", X, 3)
+    )
+    [grad_tokens] = call(tokens_body, [((128, 512), BF)], result)
     return grad_tokens.reshape(1, 2, 64, 512), shard_qkv, shard_out, total.reshape(512)
 
 

time: 134 us -> 134 us (level)
  starting transfers between devices: 35.3 us -> 29.8 us
  waiting for transfers between devices: 30 us -> 33 us
  blocking collectives: 56.4 us -> 58.4 us
    ppermute x4 -> x2, starting transfers between devices: 18 us -> 5.57 us  [flip(): return lax.ppermute(block, axis, [(i, i ^ bits) for i in range(count)])]
    all_to_all x3, starting transfers between devices: 12.9 us -> 20.1 us  [exchange(): return lax.all_to_all(arr, axes, split_axis=0, concat_axis=0, tiled=True)]
    all_to_all x3, waiting for transfers between devices: 19.6 us -> 23.7 us  [exchange(): return lax.all_to_all(arr, axes, split_axis=0, concat_axis=0, tiled=True)]
    all_to_all x2, blocking collectives: 56.4 us -> 58.4 us  [exchange(): return lax.all_to_all(arr, axes, split_axis=0, concat_axis=0, tiled=True)]
    ppermute x4 -> x2, waiting for transfers between devices: 8.12 us -> 6.78 us  [flip(): return lax.ppermute(block, axis, [(i, i ^ bits) for i in range(count)])]
  transfers between devices with their start and end apart: 9 -> 7, of which waited for: 8 -> 6; matrix products, arithmetic and copies ran while one was open for 0% -> 0% of each run, Pallas kernels for 2% -> 2%
where the time goes in v8:
time: 134 us; the launch traced here: 133 us
  blocking collectives  58.4 us (44%)
  waiting for transfers between devices  33 us (25%)
  starting transfers between devices  29.8 us (22%)
  Pallas kernels  10.6 us (8%)
    all_to_all x2, blocking collectives, exchange(): return lax.all_to_all(arr, axes, split_axis=0, concat_axis=0, tiled=True)  58.4 us
    all_to_all x3, waiting for transfers between devices, exchange(): return lax.all_to_all(arr, axes, split_axis=0, concat_axis=0, tiled=True)  23.7 us
    all_to_all x3, starting transfers between devices, exchange(): return lax.all_to_all(arr, axes, split_axis=0, concat_axis=0, tiled=True)  20.1 us
    pallas_call x10, Pallas kernels, call(): pl.pallas_call(body, out_shape=[jax.ShapeDtypeStruct(shape, kind) for sha...  8.63 us
    ppermute x2, waiting for transfers between devices, flip(): return lax.ppermute(block, axis, [(i, i ^ bits) for i in range(count)])  6.78 us
    ppermute x2, starting transfers between devices, flip(): return lax.ppermute(block, axis, [(i, i ^ bits) for i in range(count)])  5.57 us
  transfers between devices with their start and end apart: 7, of which 6 were waited for; matrix products, arithmetic and copies ran while one was open for 0% of the time, Pallas kernels for 2%

profile of v8, /device:TPU:32, one launch (start us, length us, event | category | flops | bytes accessed | tf_op | source)
XLA Modules:
  0.0 132.6 jit_solution(14238224212497047331)
XLA Ops:
  0.6 2.0 %shard_map.84 = bf16[256,640]{1,0:T(8,128)(2,1)} custom-call(bf16[128,512]{1,0:T(8,128)(2,1)} %bitcast.18, bf16[128,512]{1,0:T(8,128)(2,1)} %bitcast.19, bf16[8,1536]{1,0:T(8,128)(2,1)} %wq_ref.1, bf16[8,512]{1,0:T(8,128)(2,1)} %wo_ref.1), custom_call_target="tpu_custom_call" | custom-call | tf_op jit(solution)/shard_map/pallas_call | solution.py:314
  2.6 36.0 %all_to_all.25 = bf16[32,8,640]{2,1,0:T(8,128)(2,1)S(1)} all-to-all(bf16[32,8,640]{2,1,0:T(8,128)(2,1)} %bitcast.17), channel_id=1, replica_groups=mesh['zh'=2,'x'=4,'zl'=8,'y'=4,'c'=2] {'zl','y'}, dimensions={0} | all-to-all | bytes 655360 | tf_op jit(solution)/shard_map/all_to_all | solution.py:18
  38.6 1.2 shard_map.87
  39.8 0.0 copy-start
  39.8 5.6 %all-to-all-start.1 = ((bf16[32,128,128]{2,1,0:T(8,128)(2,1)}), bf16[32,128,128]{2,1,0:T(8,128)(2,1)S(1)}, u32[]{:S(2)}, u32[]{:S(2)}) async-start(bf16[32,128,128]{2,1,0:T(8,128)(2,1)} %shard_map.87), calls=%async_computation.1 | async-start | bytes 2097152 | tf_op jit(solution)/shard_map/all_to_all | solution.py:18
  45.4 0.2 shard_map.85.own_ref
  45.6 2.2 %collective-permute-start = (bf16[256,512]{1,0:T(8,128)(2,1)S(1)}, bf16[256,512]{1,0:T(8,128)(2,1)S(1)}, u32[]{:S(2)}, u32[]{:S(2)}) collective-permute-start(bf16[256,512]{1,0:T(8,128)(2,1)S(1)} %shard_map.85.own_ref), channel_id=1, source_target_pairs={{0,1},{1,0},{2,3},{3,2},{4,5},{5,4},{6,7},{7,6},{8,9},{9,8},{10,11... | collective-permute-start | bytes 786440 | tf_op jit(solution)/shard_map/ppermute | solution.py:331
  47.8 1.2 collective-permute-done.far_ref
  49.0 0.0 copy-done
  49.0 0.2 shard_map.86
  49.2 13.0 %all-to-all-done.1.w_ref = bf16[32,128,128]{2,1,0:T(8,128)(2,1)S(1)} async-done(((bf16[32,128,128]{2,1,0:T(8,128)(2,1)}), bf16[32,128,128]{2,1,0:T(8,128)(2,1)S(1)}, u32[]{:S(2)}, u32[]{:S(2)}) %all-to-all-start.1) | async-done | bytes 1048608 | tf_op jit(solution)/shard_map/all_to_all | solution.py:18
  62.2 3.0 %shard_map.88 = (bf16[32,136,128]{2,1,0:T(8,128)(2,1)S(1)}, bf16[128,512]{1,0:T(8,128)(2,1)S(1)}, f32[128,512]{1,0:T(8,128)S(1)}) custom-call(f32[256,512]{1,0:T(8,128)S(1)} %get-tuple-element.16.scaled_ref, bf16[256,512]{1,0:T(8,128)(2,1)S(1)} %get-tuple-element.17.normed_ref, bf16[256,512]{1,0:T(8,128)(2,1)S(1)} %get-tuple-element.18.grad_ref, ...), custom_call_target="tpu_custom_call" | custom-call | tf_op jit(solution)/shard_map/pallas_call | solution.py:27
  65.2 22.4 %all_to_all.26.got_ref = bf16[32,136,128]{2,1,0:T(8,128)(2,1)S(1)} all-to-all(bf16[32,136,128]{2,1,0:T(8,128)(2,1)S(1)} %get-tuple-element.19), channel_id=1, replica_groups=mesh['zh'=2,'x'=4,'zl'=8,'y'=4,'c'=2] {'x','y','c'}, dimensions={0} | all-to-all | bytes 2228224 | tf_op jit(solution)/shard_map/all_to_all | solution.py:18
  87.6 0.9 shard_map.89
  88.5 8.6 %all-to-all-start.3 = ((bf16[16,8,640]{2,1,0:T(8,128)(2,1)}), bf16[16,8,640]{2,1,0:T(8,128)(2,1)S(1)}, u32[]{:S(2)}, u32[]{:S(2)}) async-start(bf16[16,8,640]{2,1,0:T(8,128)(2,1)} %bitcast.5), calls=%async_computation.3 | async-start | bytes 327680 | tf_op jit(solution)/shard_map/all_to_all | solution.py:18
  97.1 1.9 %collective-permute-start.1 = (bf16[128,512]{1,0:T(8,128)(2,1)S(1)}, bf16[128,512]{1,0:T(8,128)(2,1)S(1)}, u32[]{:S(2)}, u32[]{:S(2)}) collective-permute-start(bf16[128,512]{1,0:T(8,128)(2,1)S(1)} %get-tuple-element.21), channel_id=1, source_target_pairs={{0,1},{1,0},{2,3},{3,2},{4,5},{5,4},{6,7},{7,6},{8,9},{9,8},{10,11... | collective-permute-start | bytes 393224 | tf_op jit(solution)/shard_map/ppermute | solution.py:341
  99.1 1.3 collective-permute-done.1.far_ref
  100.4 1.1 shard_map.90
  101.5 10.8 %all-to-all-done.3 = bf16[16,8,640]{2,1,0:T(8,128)(2,1)S(1)} async-done(((bf16[16,8,640]{2,1,0:T(8,128)(2,1)}), bf16[16,8,640]{2,1,0:T(8,128)(2,1)S(1)}, u32[]{:S(2)}, u32[]{:S(2)}) %all-to-all-start.3) | async-done | bytes 163872 | tf_op jit(solution)/shard_map/all_to_all | solution.py:18
  112.2 5.9 %all-to-all-start.4 = ((bf16[32,8,256]{2,1,0:T(8,128)(2,1)}), bf16[32,8,256]{2,1,0:T(8,128)(2,1)S(1)}, u32[]{:S(2)}, u32[]{:S(2)}) async-start(bf16[32,8,256]{2,1,0:T(8,128)(2,1)} %bitcast.6), calls=%async_computation.4 | async-start | bytes 262144 | tf_op jit(solution)/shard_map/all_to_all | solution.py:18
  118.1 0.6 shard_map.92
  118.7 2.5 %collective-permute-start.2 = (bf16[8,512]{1,0:T(8,128)(2,1)S(1)}, bf16[8,512]{1,0:T(8,128)(2,1)S(1)}, u32[]{:S(2)}, u32[]{:S(2)}) collective-permute-start(bf16[8,512]{1,0:T(8,128)(2,1)S(1)} %get-tuple-element.24.one_ref), channel_id=1, source_target_pairs={{0,64},{64,0},{128,192},{192,128},{1,65},{65,1},{129,193},{193,129... | collective-permute-start | bytes 24584 | tf_op jit(solution)/shard_map/ppermute | solution.py:22
  121.3 3.0 %collective-permute-done.2.two_ref = bf16[8,512]{1,0:T(8,128)(2,1)S(1)} collective-permute-done((bf16[8,512]{1,0:T(8,128)(2,1)S(1)}, bf16[8,512]{1,0:T(8,128)(2,1)S(1)}, u32[]{:S(2)}, u32[]{:S(2)}) %collective-permute-start.2) | collective-permute-done | bytes 8224 | tf_op jit(solution)/shard_map/ppermute | solution.py:22
  124.3 3.1 %collective-permute-start.3 = (bf16[8,1024]{1,0:T(8,128)(2,1)S(1)}, bf16[8,1024]{1,0:T(8,128)(2,1)S(1)}, u32[]{:S(2)}, u32[]{:S(2)}) collective-permute-start(bf16[8,1024]{1,0:T(8,128)(2,1)S(1)} %shard_map.93.near_ref), channel_id=1, source_target_pairs={{0,192},{64,128},{128,64},{192,0},{1,193},{65,129},{129,65},{193,1... | collective-permute-start | bytes 49160 | tf_op jit(solution)/shard_map/ppermute | solution.py:22
  127.3 3.8 %collective-permute-done.3.far_ref = bf16[8,1024]{1,0:T(8,128)(2,1)S(1)} collective-permute-done((bf16[8,1024]{1,0:T(8,128)(2,1)S(1)}, bf16[8,1024]{1,0:T(8,128)(2,1)S(1)}, u32[]{:S(2)}, u32[]{:S(2)}) %collective-permute-start.3) | collective-permute-done | bytes 16416 | tf_op jit(solution)/shard_map/ppermute | solution.py:22
  131.1 0.6 shard_map.94
  131.7 0.0 all-to-all-done.4
  131.7 0.8 shard_map.91
  (1 shorter events, 0.0 us)
Async XLA Ops:
  39.8 9.3 %copy-start = (f32[512]{0:T(512)S(1)}, f32[512]{0:T(512)}, u32[]{:S(2)}) copy-start(f32[512]{0:T(512)} %param.7) | copy-start | bytes 6148
  39.8 22.4 %all-to-all-start.1 = ((bf16[32,128,128]{2,1,0:T(8,128)(2,1)}), bf16[32,128,128]{2,1,0:T(8,128)(2,1)S(1)}, u32[]{:S(2)}, u32[]{:S(2)}) async-start(bf16[32,128,128]{2,1,0:T(8,128)(2,1)} %shard_map.87), calls=%async_computation.1 | async-start | bytes 2097152 | tf_op jit(solution)/shard_map/all_to_all | solution.py:18
  45.6 3.4 %collective-permute-start = (bf16[256,512]{1,0:T(8,128)(2,1)S(1)}, bf16[256,512]{1,0:T(8,128)(2,1)S(1)}, u32[]{:S(2)}, u32[]{:S(2)}) collective-permute-start(bf16[256,512]{1,0:T(8,128)(2,1)S(1)} %shard_map.85.own_ref), channel_id=1, source_target_pairs={{0,1},{1,0},{2,3},{3,2},{4,5},{5,4},{6,7},{7,6},{8,9},{9,8},{10,11... | collective-permute-start | bytes 786440 | tf_op jit(solution)/shard_map/ppermute | solution.py:331
  88.5 23.7 %all-to-all-start.3 = ((bf16[16,8,640]{2,1,0:T(8,128)(2,1)}), bf16[16,8,640]{2,1,0:T(8,128)(2,1)S(1)}, u32[]{:S(2)}, u32[]{:S(2)}) async-start(bf16[16,8,640]{2,1,0:T(8,128)(2,1)} %bitcast.5), calls=%async_computation.3 | async-start | bytes 327680 | tf_op jit(solution)/shard_map/all_to_all | solution.py:18
  97.1 3.2 %collective-permute-start.1 = (bf16[128,512]{1,0:T(8,128)(2,1)S(1)}, bf16[128,512]{1,0:T(8,128)(2,1)S(1)}, u32[]{:S(2)}, u32[]{:S(2)}) collective-permute-start(bf16[128,512]{1,0:T(8,128)(2,1)S(1)} %get-tuple-element.21), channel_id=1, source_target_pairs={{0,1},{1,0},{2,3},{3,2},{4,5},{5,4},{6,7},{7,6},{8,9},{9,8},{10,11... | collective-permute-start | bytes 393224 | tf_op jit(solution)/shard_map/ppermute | solution.py:341
  112.2 19.5 %all-to-all-start.4 = ((bf16[32,8,256]{2,1,0:T(8,128)(2,1)}), bf16[32,8,256]{2,1,0:T(8,128)(2,1)S(1)}, u32[]{:S(2)}, u32[]{:S(2)}) async-start(bf16[32,8,256]{2,1,0:T(8,128)(2,1)} %bitcast.6), calls=%async_computation.4 | async-start | bytes 262144 | tf_op jit(solution)/shard_map/all_to_all | solution.py:18
  118.7 5.5 %collective-permute-start.2 = (bf16[8,512]{1,0:T(8,128)(2,1)S(1)}, bf16[8,512]{1,0:T(8,128)(2,1)S(1)}, u32[]{:S(2)}, u32[]{:S(2)}) collective-permute-start(bf16[8,512]{1,0:T(8,128)(2,1)S(1)} %get-tuple-element.24.one_ref), channel_id=1, source_target_pairs={{0,64},{64,0},{128,192},{192,128},{1,65},{65,1},{129,193},{193,129... | collective-permute-start | bytes 24584 | tf_op jit(solution)/shard_map/ppermute | solution.py:22
  124.3 6.8 %collective-permute-start.3 = (bf16[8,1024]{1,0:T(8,128)(2,1)S(1)}, bf16[8,1024]{1,0:T(8,128)(2,1)S(1)}, u32[]{:S(2)}, u32[]{:S(2)}) collective-permute-start(bf16[8,1024]{1,0:T(8,128)(2,1)S(1)} %shard_map.93.near_ref), channel_id=1, source_target_pairs={{0,192},{64,128},{128,64},{192,0},{1,193},{65,129},{129,65},{193,1... | collective-permute-start | bytes 49160 | tf_op jit(solution)/shard_map/ppermute | solution.py:22

commit v9 on v7

--- a/solution.py
+++ b/solution.py
@@ -22,13 +22,17 @@
     return lax.ppermute(block, "y", [(i, i ^ k) for i in range(Y)])
 
 
-def call(body, outs, *args):
+def call(body, outs, *args, first_in_hbm=False, scratch=()):
     vmem = pl.BlockSpec(memory_space=pltpu.VMEM)
+    out_specs = [vmem] * len(outs)
+    if first_in_hbm:
+        out_specs[0] = pl.BlockSpec(memory_space=pl.ANY)
     return pl.pallas_call(
         body,
         out_shape=[jax.ShapeDtypeStruct(shape, kind) for shape, kind in outs],
         in_specs=[vmem] * len(args),
-        out_specs=[vmem] * len(outs),
+        out_specs=out_specs,
+        scratch_shapes=list(scratch),
         compiler_params=pltpu.CompilerParams(vmem_limit_bytes=40 * 2**20),
     )(*args)
 
@@ -77,7 +81,7 @@
     return arr[:, :64], arr[:, 64:]
 
 
-def weights_body(moved_ref, sent_ref):
+def weights_body(moved_ref, sent_ref, pair_vm, sems):
     block = moved_ref[:, 512:].astype(F32)
     (low0, low1), (high0, high1) = halves(block[:128]), halves(block[128:])
     planes = block.reshape(4, 2, 32, 128)
@@ -86,8 +90,15 @@
         mine = jnp.where(
             outs, planes[:, core].reshape(128, 128), jnp.concatenate(cols, axis=1)
         ).astype(BF)
-        for xy in range(X * Y):
-            sent_ref[2 * xy + core] = mine
+        pair_vm[core] = mine
+    copies = [
+        pltpu.make_async_copy(pair_vm, sent_ref.at[2 * xy : 2 * xy + 2], sems.at[xy])
+        for xy in range(X * Y)
+    ]
+    for copy in copies:
+        copy.start()
+    for copy in copies:
+        copy.wait()
 
 
 def rows_body(moved_ref, own_ref):
@@ -97,7 +108,7 @@
     own_ref[...] = dot(pick, moved_ref[:, :512]).astype(BF)
 
 
-def norm_body(own_ref, far_ref, gain_ref, scaled_ref, normed_ref, grad_ref):
+def norm_body(own_ref, far_ref, gain_ref, scaled_ref, normed_ref, flipped_ref, grad_ref):
     own, far = own_ref[...], far_ref[...]
     x_in = jnp.concatenate([own[0:64], far[0:64], own[64:128], far[64:128]], axis=0)
     grad_ref[...] = jnp.concatenate([own[128:192], far[128:192], own[192:], far[192:]], axis=0)
@@ -105,7 +116,9 @@
     inverse = lax.rsqrt(jnp.mean(values * values, axis=-1, keepdims=True) + EPS)
     scaled = values * inverse
     scaled_ref[...] = scaled
-    normed_ref[...] = (scaled * gain_ref[...]).astype(BF)
+    normed = scaled * gain_ref[...]
+    normed_ref[...] = normed.astype(BF)
+    flipped_ref[...] = normed.T.astype(BF)
 
 
 def x_is_last():
@@ -119,7 +132,8 @@
 
 
 def main_body(
-    scaled_ref, normed_ref, grad_ref, w_ref, parts_ref, send_ref, keep_ref
+    scaled_ref, normed_ref, flipped_ref, grad_ref, w_ref,
+    parts_ref, send_ref, keep_ref, parts_vm, sems,
 ):
     lanes = []
     for x in range(3):
@@ -199,17 +213,31 @@
     gg = two_rows(jnp.sum(dn * scaled_ref[...], axis=0, keepdims=True))
     gg = jnp.concatenate([gg[0:2, i * 128 : i * 128 + 128] for i in range(4)], axis=0)
 
-    g_qkv = dot(normed, dqkv, 0, 0).reshape(ZL, Y, 2, 8, 768)
+    copies = []
+
+    def leave(part):
+        at = slice(part * 8, part * 8 + 8)
+        copy = pltpu.make_async_copy(parts_vm.at[at], parts_ref.at[at], sems.at[part])
+        copy.start()
+        copies.append(copy)
+
     g_out = dot(att, g_in, 0, 0).reshape(4, Y, 2, 8, 512)
     for yc in range(8):
-        block = g_qkv[:, yc // 2, yc % 2].reshape(64, 768)
-        for part in range(3):
-            at = part * 256
-            pieces = [block[:, at : at + 128], block[:, at + 128 : at + 256], gg]
-            parts_ref[part * 8 + yc] = jnp.concatenate(pieces, axis=0).astype(BF)
         block = g_out[:, yc // 2, yc % 2].reshape(32, 512)
         pieces = [block[:, i * 128 : i * 128 + 128] for i in range(4)] + [gg]
-        parts_ref[24 + yc] = jnp.concatenate(pieces, axis=0).astype(BF)
+        parts_vm[24 + yc] = jnp.concatenate(pieces, axis=0).astype(BF)
+    leave(3)
+    flipped = flipped_ref[...]
+    for part in (2, 1, 0):
+        g_part = dot(flipped, dqkv[:, part * 256 : part * 256 + 256])
+        g_part = g_part.reshape(ZL, Y, 2, 8, 256)
+        for yc in range(8):
+            block = g_part[:, yc // 2, yc % 2].reshape(64, 256)
+            pieces = [block[:, :128], block[:, 128:], gg]
+            parts_vm[part * 8 + yc] = jnp.concatenate(pieces, axis=0).astype(BF)
+        leave(part)
+    for copy in copies:
+        copy.wait()
 
 
 def finish_body(own_ref, keep_ref, far_ref, gain_ref, out_ref):
@@ -329,17 +357,27 @@
         compiler_params=pltpu.CompilerParams(vmem_limit_bytes=60 * 2**20),
     )(tokens.reshape(128, 512), grad_out.reshape(128, 512), w_qkv, w_out)
     moved = exchange(packed.reshape(ZL * Y, 8, 640), ("zl", "y")).reshape(256, 640)
-    [sent] = call(weights_body, [((32, 128, 128), BF)], moved)
+    [sent] = call(
+        weights_body,
+        [((32, 128, 128), BF)],
+        moved,
+        first_in_hbm=True,
+        scratch=[pltpu.VMEM((2, 128, 128), BF), pltpu.SemaphoreType.DMA((X * Y,))],
+    )
     weights = exchange(sent, plane)
     [own] = call(rows_body, [((256, 512), BF)], moved)
     far = lax.ppermute(own, "c", SWAP)
-    scaled, normed, grads = call(
-        norm_body, [((256, 512), F32), ((256, 512), BF), ((256, 512), BF)], own, far, row
+    scaled, normed, flipped, grads = call(
+        norm_body,
+        [((256, 512), F32), ((256, 512), BF), ((512, 256), BF), ((256, 512), BF)],
+        own, far, row,
     )
     parts, send, keep = call(
         main_body,
         [((32, 136, 128), BF), ((128, 512), BF), ((128, 512), F32)],
-        scaled, normed, grads, weights,
+        scaled, normed, flipped, grads, weights,
+        first_in_hbm=True,
+        scratch=[pltpu.VMEM((32, 136, 128), BF), pltpu.SemaphoreType.DMA((4,))],
     )
     got = exchange(parts, plane)
     dn_far = lax.ppermute(send, "c", SWAP)

time: 134 us -> 133 us (level)
  no operation moved by 1% of the time
where the time goes in v9:
time: 133 us
  blocking collectives  56.4 us (42%)
  starting transfers between devices  35.2 us (26%)
  waiting for transfers between devices  29.9 us (22%)
  Pallas kernels  10.4 us (8%)
    all_to_all x2, blocking collectives, exchange(): return lax.all_to_all(arr, axes, split_axis=0, concat_axis=0, tiled=True)  56.4 us
    all_to_all x3, waiting for transfers between devices, exchange(): return lax.all_to_all(arr, axes, split_axis=0, concat_axis=0, tiled=True)  19.5 us
    all_to_all x3, starting transfers between devices, exchange(): return lax.all_to_all(arr, axes, split_axis=0, concat_axis=0, tiled=True)  12.8 us
    ppermute x3, starting transfers between devices, to_y(): return lax.ppermute(block, 'y', [(i, i ^ k) for i in range(Y)])  9.81 us
    pallas_call x10, Pallas kernels, call(): pl.pallas_call(body, out_shape=[jax.ShapeDtypeStruct(shape, kind) for sha...  8.48 us
    ppermute x1, starting transfers between devices, on_device(): last_far = lax.ppermute(last, 'zh', SWAP)  8.22 us
    ppermute x3, waiting for transfers between devices, to_y(): return lax.ppermute(block, 'y', [(i, i ^ k) for i in range(Y)])  4.81 us
    ppermute x1, waiting for transfers between devices, on_device(): last_far = lax.ppermute(last, 'zh', SWAP)  3.31 us
  transfers between devices with their start and end apart: 9, of which 8 were waited for; matrix products, arithmetic and copies ran while one was open for 0% of the time, Pallas kernels for 2%

profile of v9, /device:TPU:32, one launch (start us, length us, event | category | flops | bytes accessed | tf_op | source)
XLA Modules:
  0.0 132.7 jit_solution(11060566993833073583)
XLA Ops:
  0.6 2.0 %shard_map.84 = bf16[256,640]{1,0:T(8,128)(2,1)} custom-call(bf16[128,512]{1,0:T(8,128)(2,1)} %bitcast.20, bf16[128,512]{1,0:T(8,128)(2,1)} %bitcast.21, bf16[8,1536]{1,0:T(8,128)(2,1)} %wq_ref.1, bf16[8,512]{1,0:T(8,128)(2,1)} %wo_ref.1), custom_call_target="tpu_custom_call" | custom-call | tf_op jit(solution)/shard_map/pallas_call | solution.py:346
  2.6 36.0 %all_to_all.25 = bf16[32,8,640]{2,1,0:T(8,128)(2,1)S(1)} all-to-all(bf16[32,8,640]{2,1,0:T(8,128)(2,1)} %bitcast.19), channel_id=1, replica_groups=mesh['zh'=2,'x'=4,'zl'=8,'y'=4,'c'=2] {'zl','y'}, dimensions={0} | all-to-all | bytes 655360 | tf_op jit(solution)/shard_map/all_to_all | solution.py:18
  38.6 1.2 shard_map.87
  39.8 0.0 copy-start
  39.8 5.5 %all-to-all-start.1 = ((bf16[32,128,128]{2,1,0:T(8,128)(2,1)}), bf16[32,128,128]{2,1,0:T(8,128)(2,1)S(1)}, u32[]{:S(2)}, u32[]{:S(2)}) async-start(bf16[32,128,128]{2,1,0:T(8,128)(2,1)} %shard_map.87), calls=%async_computation.1 | async-start | bytes 2097152 | tf_op jit(solution)/shard_map/all_to_all | solution.py:18
  45.3 0.2 shard_map.85.own_ref
  45.6 2.2 %collective-permute-start = (bf16[256,512]{1,0:T(8,128)(2,1)S(1)}, bf16[256,512]{1,0:T(8,128)(2,1)S(1)}, u32[]{:S(2)}, u32[]{:S(2)}) collective-permute-start(bf16[256,512]{1,0:T(8,128)(2,1)S(1)} %shard_map.85.own_ref), channel_id=1, source_target_pairs={{0,1},{1,0},{2,3},{3,2},{4,5},{5,4},{6,7},{7,6},{8,9},{9,8},{10,11... | collective-permute-start | bytes 786440 | tf_op jit(solution)/shard_map/ppermute | solution.py:369
  47.7 1.2 collective-permute-done.far_ref
  49.0 0.3 shard_map.86
  49.3 12.9 %all-to-all-done.1.w_ref = bf16[32,128,128]{2,1,0:T(8,128)(2,1)S(1)} async-done(((bf16[32,128,128]{2,1,0:T(8,128)(2,1)}), bf16[32,128,128]{2,1,0:T(8,128)(2,1)S(1)}, u32[]{:S(2)}, u32[]{:S(2)}) %all-to-all-start.1) | async-done | bytes 1048608 | tf_op jit(solution)/shard_map/all_to_all | solution.py:18
  62.1 3.9 %shard_map.88 = (bf16[32,136,128]{2,1,0:T(8,128)(2,1)}, bf16[128,512]{1,0:T(8,128)(2,1)S(1)}, f32[128,512]{1,0:T(8,128)S(1)}) custom-call(f32[256,512]{1,0:T(8,128)S(1)} %get-tuple-element.18.scaled_ref, bf16[256,512]{1,0:T(8,128)(2,1)S(1)} %get-tuple-element.19.normed_ref, bf16[512,256]{1,0:T(8,128)(2,1)S(1)} %get-tuple-element.20.flipped_ref, ...), custom_call_target="tpu_custom_call" | custom-call | tf_op jit(solution)/shard_map/pallas_call | solution.py:30
  66.0 4.1 %all-to-all-start.2 = ((bf16[32,136,128]{2,1,0:T(8,128)(2,1)}), bf16[32,136,128]{2,1,0:T(8,128)(2,1)S(1)}, u32[]{:S(2)}, u32[]{:S(2)}) async-start(bf16[32,136,128]{2,1,0:T(8,128)(2,1)} %get-tuple-element.22), calls=%async_computation.2 | async-start | bytes 2228224 | tf_op jit(solution)/shard_map/all_to_all | solution.py:18
  70.1 2.2 %collective-permute-start.1 = (bf16[128,512]{1,0:T(8,128)(2,1)S(1)}, bf16[128,512]{1,0:T(8,128)(2,1)S(1)}, u32[]{:S(2)}, u32[]{:S(2)}) collective-permute-start(bf16[128,512]{1,0:T(8,128)(2,1)S(1)} %get-tuple-element.24), channel_id=1, source_target_pairs={{0,1},{1,0},{2,3},{3,2},{4,5},{5,4},{6,7},{7,6},{8,9},{9,8},{10,11... | collective-permute-start | bytes 393224 | tf_op jit(solution)/shard_map/ppermute | solution.py:383
  72.3 1.1 collective-permute-done.1.far_ref
  73.3 0.4 shard_map.89.hop_ref
  73.7 4.9 %collective-permute-start.3 = (bf16[32,512]{1,0:T(8,128)(2,1)S(1)}, bf16[32,512]{1,0:T(8,128)(2,1)S(1)}, u32[]{:S(2)}, u32[]{:S(2)}) collective-permute-start(bf16[32,512]{1,0:T(8,128)(2,1)S(1)} %get-tuple-element.32), channel_id=1, source_target_pairs={{0,6},{2,4},{4,2},{6,0},{1,7},{3,5},{5,3},{7,1},{8,14},{10,12},{12... | collective-permute-start | bytes 98312 | tf_op jit(solution)/shard_map/ppermute | solution.py:22
  78.7 2.2 %collective-permute-start.2 = (bf16[32,512]{1,0:T(8,128)(2,1)S(1)}, bf16[32,512]{1,0:T(8,128)(2,1)S(1)}, u32[]{:S(2)}, u32[]{:S(2)}) collective-permute-start(bf16[32,512]{1,0:T(8,128)(2,1)S(1)} %get-tuple-element.33), channel_id=1, source_target_pairs={{0,2},{2,0},{4,6},{6,4},{1,3},{3,1},{5,7},{7,5},{8,10},{10,8},{12,... | collective-permute-start | bytes 98312 | tf_op jit(solution)/shard_map/ppermute | solution.py:22
  80.8 2.1 %collective-permute-done.3.b3_ref = bf16[32,512]{1,0:T(8,128)(2,1)S(1)} collective-permute-done((bf16[32,512]{1,0:T(8,128)(2,1)S(1)}, bf16[32,512]{1,0:T(8,128)(2,1)S(1)}, u32[]{:S(2)}, u32[]{:S(2)}) %collective-permute-start.3) | collective-permute-done | bytes 32800 | tf_op jit(solution)/shard_map/ppermute | solution.py:22
  83.0 2.7 %collective-permute-done.2.b1_ref = bf16[32,512]{1,0:T(8,128)(2,1)S(1)} collective-permute-done((bf16[32,512]{1,0:T(8,128)(2,1)S(1)}, bf16[32,512]{1,0:T(8,128)(2,1)S(1)}, u32[]{:S(2)}, u32[]{:S(2)}) %collective-permute-start.2) | collective-permute-done | bytes 32800 | tf_op jit(solution)/shard_map/ppermute | solution.py:22
  85.6 2.0 %all-to-all-done.2.got_ref = bf16[32,136,128]{2,1,0:T(8,128)(2,1)S(1)} async-done(((bf16[32,136,128]{2,1,0:T(8,128)(2,1)}), bf16[32,136,128]{2,1,0:T(8,128)(2,1)S(1)}, u32[]{:S(2)}, u32[]{:S(2)}) %all-to-all-start.2) | async-done | bytes 1114144 | tf_op jit(solution)/shard_map/all_to_all | solution.py:18
  87.7 0.3 shard_map.90
  87.9 20.4 %all_to_all.26 = bf16[8,8,1664]{2,1,0:T(8,128)(2,1)S(1)} all-to-all(bf16[8,8,1664]{2,1,0:T(8,128)(2,1)S(1)} %bitcast.15), channel_id=1, replica_groups=mesh['zh'=2,'x'=4,'zl'=8,'y'=4,'c'=2] {'zl'}, dimensions={0} | all-to-all | bytes 425984 | tf_op jit(solution)/shard_map/all_to_all | solution.py:18
  108.3 0.2 shard_map.91
  108.5 8.2 %collective-permute-start.5 = (bf16[8,640]{1,0:T(8,128)(2,1)S(1)}, bf16[8,640]{1,0:T(8,128)(2,1)S(1)}, u32[]{:S(2)}, u32[]{:S(2)}) collective-permute-start(bf16[8,640]{1,0:T(8,128)(2,1)S(1)} %get-tuple-element.27.last_ref), channel_id=1, source_target_pairs={{0,256},{256,0},{1,257},{257,1},{2,258},{258,2},{3,259},{259,3},{4... | collective-permute-start | bytes 30728 | tf_op jit(solution)/shard_map/ppermute | solution.py:390
  116.7 2.7 %collective-permute-start.4 = (bf16[32,512]{1,0:T(8,128)(2,1)S(1)}, bf16[32,512]{1,0:T(8,128)(2,1)S(1)}, u32[]{:S(2)}, u32[]{:S(2)}) collective-permute-start(bf16[32,512]{1,0:T(8,128)(2,1)S(1)} %get-tuple-element.26), channel_id=1, source_target_pairs={{0,4},{2,6},{4,0},{6,2},{1,5},{3,7},{5,1},{7,3},{8,12},{10,14},{12... | collective-permute-start | bytes 98312 | tf_op jit(solution)/shard_map/ppermute | solution.py:22
  119.5 3.3 %collective-permute-done.5.far_ref = bf16[8,640]{1,0:T(8,128)(2,1)S(1)} collective-permute-done((bf16[8,640]{1,0:T(8,128)(2,1)S(1)}, bf16[8,640]{1,0:T(8,128)(2,1)S(1)}, u32[]{:S(2)}, u32[]{:S(2)}) %collective-permute-start.5) | collective-permute-done | bytes 10272 | tf_op jit(solution)/shard_map/ppermute | solution.py:390
  122.8 0.6 shard_map.93
  123.4 3.3 %all-to-all-start.4 = ((bf16[4,8,512]{2,1,0:T(8,128)(2,1)}), bf16[4,8,512]{2,1,0:T(8,128)(2,1)S(1)}, u32[]{:S(2)}, u32[]{:S(2)}) async-start(bf16[4,8,512]{2,1,0:T(8,128)(2,1)} %get-tuple-element.28), calls=%async_computation.4 | async-start | bytes 65536 | tf_op jit(solution)/shard_map/all_to_all | solution.py:18
  126.7 0.0 collective-permute-done.4.two_ref
  126.7 0.8 shard_map.92
  127.5 4.6 %all-to-all-done.4.got_ref = bf16[4,8,512]{2,1,0:T(8,128)(2,1)S(1)} async-done(((bf16[4,8,512]{2,1,0:T(8,128)(2,1)}), bf16[4,8,512]{2,1,0:T(8,128)(2,1)S(1)}, u32[]{:S(2)}, u32[]{:S(2)}) %all-to-all-start.4) | async-done | bytes 32800 | tf_op jit(solution)/shard_map/all_to_all | solution.py:18
  132.1 0.6 shard_map.94
  (2 shorter events, 0.0 us)
Async XLA Ops:
  39.8 9.2 %copy-start = (f32[512]{0:T(512)S(1)}, f32[512]{0:T(512)}, u32[]{:S(2)}) copy-start(f32[512]{0:T(512)} %param.7) | copy-start | bytes 6148
  39.8 22.3 %all-to-all-start.1 = ((bf16[32,128,128]{2,1,0:T(8,128)(2,1)}), bf16[32,128,128]{2,1,0:T(8,128)(2,1)S(1)}, u32[]{:S(2)}, u32[]{:S(2)}) async-start(bf16[32,128,128]{2,1,0:T(8,128)(2,1)} %shard_map.87), calls=%async_computation.1 | async-start | bytes 2097152 | tf_op jit(solution)/shard_map/all_to_all | solution.py:18
  45.6 3.4 %collective-permute-start = (bf16[256,512]{1,0:T(8,128)(2,1)S(1)}, bf16[256,512]{1,0:T(8,128)(2,1)S(1)}, u32[]{:S(2)}, u32[]{:S(2)}) collective-permute-start(bf16[256,512]{1,0:T(8,128)(2,1)S(1)} %shard_map.85.own_ref), channel_id=1, source_target_pairs={{0,1},{1,0},{2,3},{3,2},{4,5},{5,4},{6,7},{7,6},{8,9},{9,8},{10,11... | collective-permute-start | bytes 786440 | tf_op jit(solution)/shard_map/ppermute | solution.py:369
  66.0 21.7 %all-to-all-start.2 = ((bf16[32,136,128]{2,1,0:T(8,128)(2,1)}), bf16[32,136,128]{2,1,0:T(8,128)(2,1)S(1)}, u32[]{:S(2)}, u32[]{:S(2)}) async-start(bf16[32,136,128]{2,1,0:T(8,128)(2,1)} %get-tuple-element.22), calls=%async_computation.2 | async-start | bytes 2228224 | tf_op jit(solution)/shard_map/all_to_all | solution.py:18
  70.1 3.2 %collective-permute-start.1 = (bf16[128,512]{1,0:T(8,128)(2,1)S(1)}, bf16[128,512]{1,0:T(8,128)(2,1)S(1)}, u32[]{:S(2)}, u32[]{:S(2)}) collective-permute-start(bf16[128,512]{1,0:T(8,128)(2,1)S(1)} %get-tuple-element.24), channel_id=1, source_target_pairs={{0,1},{1,0},{2,3},{3,2},{4,5},{5,4},{6,7},{7,6},{8,9},{9,8},{10,11... | collective-permute-start | bytes 393224 | tf_op jit(solution)/shard_map/ppermute | solution.py:383
  73.7 9.2 %collective-permute-start.3 = (bf16[32,512]{1,0:T(8,128)(2,1)S(1)}, bf16[32,512]{1,0:T(8,128)(2,1)S(1)}, u32[]{:S(2)}, u32[]{:S(2)}) collective-permute-start(bf16[32,512]{1,0:T(8,128)(2,1)S(1)} %get-tuple-element.32), channel_id=1, source_target_pairs={{0,6},{2,4},{4,2},{6,0},{1,7},{3,5},{5,3},{7,1},{8,14},{10,12},{12... | collective-permute-start | bytes 98312 | tf_op jit(solution)/shard_map/ppermute | solution.py:22
  78.7 7.0 %collective-permute-start.2 = (bf16[32,512]{1,0:T(8,128)(2,1)S(1)}, bf16[32,512]{1,0:T(8,128)(2,1)S(1)}, u32[]{:S(2)}, u32[]{:S(2)}) collective-permute-start(bf16[32,512]{1,0:T(8,128)(2,1)S(1)} %get-tuple-element.33), channel_id=1, source_target_pairs={{0,2},{2,0},{4,6},{6,4},{1,3},{3,1},{5,7},{7,5},{8,10},{10,8},{12,... | collective-permute-start | bytes 98312 | tf_op jit(solution)/shard_map/ppermute | solution.py:22
  108.5 14.3 %collective-permute-start.5 = (bf16[8,640]{1,0:T(8,128)(2,1)S(1)}, bf16[8,640]{1,0:T(8,128)(2,1)S(1)}, u32[]{:S(2)}, u32[]{:S(2)}) collective-permute-start(bf16[8,640]{1,0:T(8,128)(2,1)S(1)} %get-tuple-element.27.last_ref), channel_id=1, source_target_pairs={{0,256},{256,0},{1,257},{257,1},{2,258},{258,2},{3,259},{259,3},{4... | collective-permute-start | bytes 30728 | tf_op jit(solution)/shard_map/ppermute | solution.py:390
  116.7 10.0 %collective-permute-start.4 = (bf16[32,512]{1,0:T(8,128)(2,1)S(1)}, bf16[32,512]{1,0:T(8,128)(2,1)S(1)}, u32[]{:S(2)}, u32[]{:S(2)}) collective-permute-start(bf16[32,512]{1,0:T(8,128)(2,1)S(1)} %get-tuple-element.26), channel_id=1, source_target_pairs={{0,4},{2,6},{4,0},{6,2},{1,5},{3,7},{5,1},{7,3},{8,12},{10,14},{12... | collective-permute-start | bytes 98312 | tf_op jit(solution)/shard_map/ppermute | solution.py:22
  123.4 8.7 %all-to-all-start.4 = ((bf16[4,8,512]{2,1,0:T(8,128)(2,1)}), bf16[4,8,512]{2,1,0:T(8,128)(2,1)S(1)}, u32[]{:S(2)}, u32[]{:S(2)}) async-start(bf16[4,8,512]{2,1,0:T(8,128)(2,1)} %get-tuple-element.28), calls=%async_computation.4 | async-start | bytes 65536 | tf_op jit(solution)/shard_map/all_to_all | solution.py:18

commit v10 on v9

--- a/solution.py
+++ b/solution.py
@@ -19,7 +19,11 @@
 
 
 def to_y(block, k):
-    return lax.ppermute(block, "y", [(i, i ^ k) for i in range(Y)])
+    return lax.ppermute(block, ("yh", "yl"), [(i, i ^ k) for i in range(Y)])
+
+
+def y_index():
+    return lax.axis_index("yh") * 2 + lax.axis_index("yl")
 
 
 def call(body, outs, *args, first_in_hbm=False, scratch=()):
@@ -63,9 +67,14 @@
     ]
     for copy in copies:
         copy.start()
-    pick = chooser(
-        256, 256, lambda i: (i >> 2 & 1) * 128 + (i & 1) * 64 + (i >> 1 & 1) * 32 + (i >> 3)
-    )
+    yh = lax.axis_index("yh")
+
+    def source(i):
+        side = i >> 3 & 1
+        chip = (i >> 5) * 4 + (yh ^ side) * 2 + ((i >> 4 & 1) ^ side)
+        return (i >> 2 & 1) * 128 + (i & 1) * 64 + (i >> 1 & 1) * 32 + chip
+
+    pick = chooser(256, 256, source)
     for copy in copies:
         copy.wait()
     out_ref[:, :512] = dot(pick, both_vm[...]).astype(BF)
@@ -82,14 +91,13 @@
 
 
 def weights_body(moved_ref, sent_ref, pair_vm, sems):
-    block = moved_ref[:, 512:].astype(F32)
-    (low0, low1), (high0, high1) = halves(block[:128]), halves(block[128:])
-    planes = block.reshape(4, 2, 32, 128)
+    block = moved_ref[:, 512:].astype(F32).reshape(16, 2, 8, 128)
+    sides = [block[:, i].reshape(128, 128) for i in range(2)]
     outs = x_is_last()
-    for core, cols in ((0, (low0, high0)), (1, (low1, high1))):
-        mine = jnp.where(
-            outs, planes[:, core].reshape(128, 128), jnp.concatenate(cols, axis=1)
-        ).astype(BF)
+    for core in range(2):
+        heads = jnp.concatenate([side[:, core * 64 : core * 64 + 64] for side in sides], axis=1)
+        planes = [side.reshape(4, 2, 16, 128)[:, core].reshape(64, 128) for side in sides]
+        mine = jnp.where(outs, jnp.concatenate(planes, axis=0), heads).astype(BF)
         pair_vm[core] = mine
     copies = [
         pltpu.make_async_copy(pair_vm, sent_ref.at[2 * xy : 2 * xy + 2], sems.at[xy])
@@ -101,11 +109,21 @@
         copy.wait()
 
 
-def rows_body(moved_ref, own_ref):
-    pick = chooser(
-        256, 256, lambda i: (i >> 1 & 31) * 8 + (i >> 7) * 4 + (i >> 6 & 1) * 2 + (i & 1)
-    )
-    own_ref[...] = dot(pick, moved_ref[:, :512]).astype(BF)
+def hop_body(moved_ref, hop_ref):
+    pick = chooser(128, 256, lambda i: (i >> 3) * 16 + 8 + (i & 7))
+    hop_ref[...] = dot(pick, moved_ref[:, :512]).astype(BF)
+
+
+def rows_body(moved_ref, other_ref, own_ref):
+    yh = lax.axis_index("yh")
+
+    def source(i):
+        origin = (i >> 3 & 7) * 2 + (i >> 1 & 1)
+        row = (i >> 7) * 4 + (i >> 6 & 1) * 2 + (i & 1)
+        return jnp.where((i >> 2 & 1) == yh, origin * 16 + row, 256 + origin * 8 + row)
+
+    both = jnp.concatenate([moved_ref[:, :512], other_ref[...]], axis=0)
+    own_ref[...] = dot(chooser(256, 384, source), both).astype(BF)
 
 
 def norm_body(own_ref, far_ref, gain_ref, scaled_ref, normed_ref, flipped_ref, grad_ref):
@@ -135,26 +153,25 @@
     scaled_ref, normed_ref, flipped_ref, grad_ref, w_ref,
     parts_ref, send_ref, keep_ref, parts_vm, sems,
 ):
-    lanes = []
-    for x in range(3):
-        for pair in range(2):
-            tops, bots = [], []
+    def gathered(part, yl, count, piece):
+        sides = []
+        for yh in range(2):
+            blocks = []
             for core in range(2):
-                at = x * 8 + pair * 4 + core
-                (a0, a1), (b0, b1) = (
-                    halves(w_ref[at].astype(F32)),
-                    halves(w_ref[at + 2].astype(F32)),
-                )
-                tops.append(jnp.concatenate([a0, b0], axis=1))
-                bots.append(jnp.concatenate([a1, b1], axis=1))
-            lanes.append(jnp.concatenate([weave(*tops), weave(*bots)], axis=0).astype(BF))
-    wh = jnp.concatenate(lanes, axis=1)
-    lanes = [
-        weave(w_ref[24 + 2 * y].astype(F32), w_ref[25 + 2 * y].astype(F32)).astype(BF)
-        for y in range(Y)
-    ]
-    wo = jnp.concatenate(lanes, axis=1)
-
+                block = piece(w_ref[part * 8 + yh * 4 + yl * 2 + core].astype(F32))
+                blocks.append(block.reshape(count, 1, 2, 1, 8, block.shape[1]))
+            sides.append(jnp.concatenate(blocks, axis=3))
+        full = jnp.concatenate(sides, axis=1)
+        return full.reshape(count * 64, full.shape[-1]).astype(BF)
+
+    wh = jnp.concatenate(
+        [gathered(x, yl, 8, lambda arr: arr) for x in range(3) for yl in range(2)], axis=1
+    )
+
+    def wide(arr):
+        return jnp.concatenate([arr[:64], arr[64:]], axis=1)
+
+    wo = jnp.concatenate([gathered(3, yl, 4, wide) for yl in range(2)], axis=1)
     normed, g_in = normed_ref[...], grad_ref[...]
     qkv = dot(normed, wh).astype(BF)
     ups = dot(g_in, wo, 1, 1).astype(BF)
@@ -248,7 +265,7 @@
     ds = (keep_ref[...] + far_ref[...].astype(F32)) * gain
     inner = jnp.mean(ds * scaled, axis=-1, keepdims=True)
     result = (own_ref[128:256, :].astype(F32) + inverse * (ds - scaled * inner)).astype(BF)
-    y = lax.axis_index("y")
+    y = y_index()
 
     def source(i):
         return (i >> 4 & 1) * 64 + (i >> 1 & 7) * 8 + ((i >> 5) ^ y) * 2 + (i & 1)
@@ -323,7 +340,7 @@
 
 
 def tokens_body(rest_ref, two_ref, out_ref):
-    y = lax.axis_index("y")
+    y = y_index()
     blocks = jnp.concatenate([rest_ref[0:64], two_ref[...], rest_ref[64:96]], axis=0)
 
     def source(i):
@@ -340,7 +357,7 @@
 
 def on_device(tokens, grad_out, gain, w_qkv, w_out):
     row = gain.reshape(1, 512)
-    plane = ("x", "y", "c")
+    plane = ("x", "yh", "yl", "c")
 
     hbm = pl.BlockSpec(memory_space=pl.ANY)
     packed = pl.pallas_call(
@@ -356,7 +373,7 @@
         ],
         compiler_params=pltpu.CompilerParams(vmem_limit_bytes=60 * 2**20),
     )(tokens.reshape(128, 512), grad_out.reshape(128, 512), w_qkv, w_out)
-    moved = exchange(packed.reshape(ZL * Y, 8, 640), ("zl", "y")).reshape(256, 640)
+    moved = exchange(packed.reshape(ZL * 2, 16, 640), ("zl", "yl")).reshape(256, 640)
     [sent] = call(
         weights_body,
         [((32, 128, 128), BF)],
@@ -365,7 +382,8 @@
         scratch=[pltpu.VMEM((2, 128, 128), BF), pltpu.SemaphoreType.DMA((X * Y,))],
     )
     weights = exchange(sent, plane)
-    [own] = call(rows_body, [((256, 512), BF)], moved)
+    [hop] = call(hop_body, [((128, 512), BF)], moved)
+    [own] = call(rows_body, [((256, 512), BF)], moved, to_y(hop, 3))
     far = lax.ppermute(own, "c", SWAP)
     scaled, normed, flipped, grads = call(
         norm_body,
@@ -396,8 +414,9 @@
 
 
 def solution(mesh):
-    inner = Mesh(mesh.devices.reshape(ZH, X, ZL, Y, C), ("zh", "x", "zl", "y", "c"))
-    grid = ("zl", "y", "c")
+    names = ("zh", "x", "zl", "yh", "yl", "c")
+    inner = Mesh(mesh.devices.reshape(ZH, X, ZL, 2, 2, C), names)
+    grid = names[2:]
     tok = P(("zh", "x"), grid, None, None)
     return jax.shard_map(
         on_device,

time: 133 us -> 139 us (1.045)
  starting transfers between devices: 35.2 us -> 42.3 us
  blocking collectives: 56.4 us -> 53.7 us
    ppermute x3 -> x4, waiting for transfers between devices: 4.81 us -> 17.8 us  [to_y(): return lax.ppermute(block, ('yh', 'yl'), [(i, i ^ k) for i in range(Y)])]
    all_to_all x3, waiting for transfers between devices: 19.5 us -> 6.62 us  [exchange(): return lax.all_to_all(arr, axes, split_axis=0, concat_axis=0, tiled=True)]
    ppermute x3 -> x4, starting transfers between devices: 9.81 us -> 14.7 us  [to_y(): return lax.ppermute(block, ('yh', 'yl'), [(i, i ^ k) for i in range(Y)])]
    all_to_all x2, blocking collectives: 56.4 us -> 53.7 us  [exchange(): return lax.all_to_all(arr, axes, split_axis=0, concat_axis=0, tiled=True)]
    all_to_all x3, starting transfers between devices: 12.8 us -> 15.2 us  [exchange(): return lax.all_to_all(arr, axes, split_axis=0, concat_axis=0, tiled=True)]
    pallas_call x10 -> x11, Pallas kernels: 8.48 us -> 8.68 us  [call(): pl.pallas_call(body, out_shape=[jax.ShapeDtypeStruct(shape, kind) for sha...]
  transfers between devices with their start and end apart: 9 -> 10, of which waited for: 8 -> 8; matrix products, arithmetic and copies ran while one was open for 0% -> 0% of each run, Pallas kernels for 2% -> 2%
where the time goes in v10:
time: 139 us; the launch traced here: 138 us
  blocking collectives  53.7 us (39%)
  starting transfers between devices  42.3 us (30%)
  waiting for transfers between devices  30.3 us (22%)
  Pallas kernels  10.6 us (8%)
    all_to_all x2, blocking collectives, exchange(): return lax.all_to_all(arr, axes, split_axis=0, concat_axis=0, tiled=True)  53.7 us
    ppermute x4, waiting for transfers between devices, to_y(): return lax.ppermute(block, ('yh', 'yl'), [(i, i ^ k) for i in range(Y)])  17.8 us
    all_to_all x3, starting transfers between devices, exchange(): return lax.all_to_all(arr, axes, split_axis=0, concat_axis=0, tiled=True)  15.2 us
    ppermute x4, starting transfers between devices, to_y(): return lax.ppermute(block, ('yh', 'yl'), [(i, i ^ k) for i in range(Y)])  14.7 us
    pallas_call x11, Pallas kernels, call(): pl.pallas_call(body, out_shape=[jax.ShapeDtypeStruct(shape, kind) for sha...  8.68 us
    ppermute x1, starting transfers between devices, on_device(): last_far = lax.ppermute(last, 'zh', SWAP)  8.22 us
    all_to_all x3, waiting for transfers between devices, exchange(): return lax.all_to_all(arr, axes, split_axis=0, concat_axis=0, tiled=True)  6.62 us
    ppermute x1, waiting for transfers between devices, on_device(): last_far = lax.ppermute(last, 'zh', SWAP)  3.31 us
  transfers between devices with their start and end apart: 10, of which 8 were waited for; matrix products, arithmetic and copies ran while one was open for 0% of the time, Pallas kernels for 2%

profile of v10, /device:TPU:32, one launch (start us, length us, event | category | flops | bytes accessed | tf_op | source)
XLA Modules:
  0.0 137.8 jit_solution(14423405280845691800)
XLA Ops:
  0.6 2.0 %shard_map.84 = bf16[256,640]{1,0:T(8,128)(2,1)} custom-call(bf16[128,512]{1,0:T(8,128)(2,1)} %bitcast.21, bf16[128,512]{1,0:T(8,128)(2,1)} %bitcast.22, bf16[8,1536]{1,0:T(8,128)(2,1)} %wq_ref.1, bf16[8,512]{1,0:T(8,128)(2,1)} %wo_ref.1), custom_call_target="tpu_custom_call" | custom-call | tf_op jit(solution)/shard_map/pallas_call | solution.py:363
  2.6 32.8 %all_to_all.25 = bf16[16,16,640]{2,1,0:T(8,128)(2,1)S(1)} all-to-all(bf16[16,16,640]{2,1,0:T(8,128)(2,1)} %bitcast.20), channel_id=1, replica_groups=mesh['zh'=2,'x'=4,'zl'=8,'yh'=2,'yl'=2,'c'=2] {'zl','yl'}, dimensions={0} | all-to-all | bytes 655360 | tf_op jit(solution)/shard_map/all_to_all | solution.py:18
  35.4 1.2 shard_map.88
  36.6 7.0 %all-to-all-start.1 = ((bf16[32,128,128]{2,1,0:T(8,128)(2,1)}), bf16[32,128,128]{2,1,0:T(8,128)(2,1)S(1)}, u32[]{:S(2)}, u32[]{:S(2)}) async-start(bf16[32,128,128]{2,1,0:T(8,128)(2,1)} %shard_map.88), calls=%async_computation.1 | async-start | bytes 2097152 | tf_op jit(solution)/shard_map/all_to_all | solution.py:18
  43.6 0.2 shard_map.85
  43.8 4.9 %collective-permute-start = (bf16[128,512]{1,0:T(8,128)(2,1)S(1)}, bf16[128,512]{1,0:T(8,128)(2,1)S(1)}, u32[]{:S(2)}, u32[]{:S(2)}) collective-permute-start(bf16[128,512]{1,0:T(8,128)(2,1)S(1)} %shard_map.85), channel_id=1, source_target_pairs={{0,6},{2,4},{4,2},{6,0},{1,7},{3,5},{5,3},{7,1},{8,14},{10,12},{12... | collective-permute-start | bytes 393224 | tf_op jit(solution)/shard_map/ppermute | solution.py:22
  48.8 13.0 %collective-permute-done.other_ref = bf16[128,512]{1,0:T(8,128)(2,1)S(1)} collective-permute-done((bf16[128,512]{1,0:T(8,128)(2,1)S(1)}, bf16[128,512]{1,0:T(8,128)(2,1)S(1)}, u32[]{:S(2)}, u32[]{:S(2)}) %collective-permute-start) | collective-permute-done | bytes 131104 | tf_op jit(solution)/shard_map/ppermute | solution.py:22
  61.8 0.3 shard_map.86.own_ref
  62.1 2.0 %collective-permute-start.1 = (bf16[256,512]{1,0:T(8,128)(2,1)S(1)}, bf16[256,512]{1,0:T(8,128)(2,1)S(1)}, u32[]{:S(2)}, u32[]{:S(2)}) collective-permute-start(bf16[256,512]{1,0:T(8,128)(2,1)S(1)} %shard_map.86.own_ref), channel_id=1, source_target_pairs={{0,1},{1,0},{2,3},{3,2},{4,5},{5,4},{6,7},{7,6},{8,9},{9,8},{10,11... | collective-permute-start | bytes 786440 | tf_op jit(solution)/shard_map/ppermute | solution.py:387
  64.1 1.4 %collective-permute-done.1.far_ref = bf16[256,512]{1,0:T(8,128)(2,1)S(1)} collective-permute-done((bf16[256,512]{1,0:T(8,128)(2,1)S(1)}, bf16[256,512]{1,0:T(8,128)(2,1)S(1)}, u32[]{:S(2)}, u32[]{:S(2)}) %collective-permute-start.1) | collective-permute-done | bytes 262176 | tf_op jit(solution)/shard_map/ppermute | solution.py:387
  65.6 0.3 shard_map.87
  65.9 3.8 %shard_map.89 = (bf16[32,136,128]{2,1,0:T(8,128)(2,1)}, bf16[128,512]{1,0:T(8,128)(2,1)S(1)}, f32[128,512]{1,0:T(8,128)S(1)}) custom-call(f32[256,512]{1,0:T(8,128)S(1)} %get-tuple-element.18.scaled_ref, bf16[256,512]{1,0:T(8,128)(2,1)S(1)} %get-tuple-element.19.normed_ref, bf16[512,256]{1,0:T(8,128)(2,1)S(1)} %get-tuple-element.20.flipped_ref, ...), custom_call_target="tpu_custom_call" | custom-call | tf_op jit(solution)/shard_map/pallas_call | solution.py:34
  69.7 4.9 %all-to-all-start.2 = ((bf16[32,136,128]{2,1,0:T(8,128)(2,1)}), bf16[32,136,128]{2,1,0:T(8,128)(2,1)S(1)}, u32[]{:S(2)}, u32[]{:S(2)}) async-start(bf16[32,136,128]{2,1,0:T(8,128)(2,1)} %get-tuple-element.22), calls=%async_computation.2 | async-start | bytes 2228224 | tf_op jit(solution)/shard_map/all_to_all | solution.py:18
  74.6 2.2 %collective-permute-start.2 = (bf16[128,512]{1,0:T(8,128)(2,1)S(1)}, bf16[128,512]{1,0:T(8,128)(2,1)S(1)}, u32[]{:S(2)}, u32[]{:S(2)}) collective-permute-start(bf16[128,512]{1,0:T(8,128)(2,1)S(1)} %get-tuple-element.24), channel_id=1, source_target_pairs={{0,1},{1,0},{2,3},{3,2},{4,5},{5,4},{6,7},{7,6},{8,9},{9,8},{10,11... | collective-permute-start | bytes 393224 | tf_op jit(solution)/shard_map/ppermute | solution.py:401
  76.8 1.1 collective-permute-done.2.far_ref
  77.8 0.4 shard_map.90.hop_ref
  78.2 4.9 %collective-permute-start.4 = (bf16[32,512]{1,0:T(8,128)(2,1)S(1)}, bf16[32,512]{1,0:T(8,128)(2,1)S(1)}, u32[]{:S(2)}, u32[]{:S(2)}) collective-permute-start(bf16[32,512]{1,0:T(8,128)(2,1)S(1)} %get-tuple-element.32), channel_id=1, source_target_pairs={{0,6},{2,4},{4,2},{6,0},{1,7},{3,5},{5,3},{7,1},{8,14},{10,12},{12... | collective-permute-start | bytes 98312 | tf_op jit(solution)/shard_map/ppermute | solution.py:22
  83.1 2.2 %collective-permute-start.3 = (bf16[32,512]{1,0:T(8,128)(2,1)S(1)}, bf16[32,512]{1,0:T(8,128)(2,1)S(1)}, u32[]{:S(2)}, u32[]{:S(2)}) collective-permute-start(bf16[32,512]{1,0:T(8,128)(2,1)S(1)} %get-tuple-element.33), channel_id=1, source_target_pairs={{0,2},{2,0},{4,6},{6,4},{1,3},{3,1},{5,7},{7,5},{8,10},{10,8},{12,... | collective-permute-start | bytes 98312 | tf_op jit(solution)/shard_map/ppermute | solution.py:22
  85.3 2.1 %collective-permute-done.4.b3_ref = bf16[32,512]{1,0:T(8,128)(2,1)S(1)} collective-permute-done((bf16[32,512]{1,0:T(8,128)(2,1)S(1)}, bf16[32,512]{1,0:T(8,128)(2,1)S(1)}, u32[]{:S(2)}, u32[]{:S(2)}) %collective-permute-start.4) | collective-permute-done | bytes 32800 | tf_op jit(solution)/shard_map/ppermute | solution.py:22
  87.5 2.7 %collective-permute-done.3.b1_ref = bf16[32,512]{1,0:T(8,128)(2,1)S(1)} collective-permute-done((bf16[32,512]{1,0:T(8,128)(2,1)S(1)}, bf16[32,512]{1,0:T(8,128)(2,1)S(1)}, u32[]{:S(2)}, u32[]{:S(2)}) %collective-permute-start.3) | collective-permute-done | bytes 32800 | tf_op jit(solution)/shard_map/ppermute | solution.py:22
  90.1 2.0 %all-to-all-done.2.got_ref = bf16[32,136,128]{2,1,0:T(8,128)(2,1)S(1)} async-done(((bf16[32,136,128]{2,1,0:T(8,128)(2,1)}), bf16[32,136,128]{2,1,0:T(8,128)(2,1)S(1)}, u32[]{:S(2)}, u32[]{:S(2)}) %all-to-all-start.2) | async-done | bytes 1114144 | tf_op jit(solution)/shard_map/all_to_all | solution.py:18
  92.2 0.3 shard_map.91
  92.4 21.0 %all_to_all.26 = bf16[8,8,1664]{2,1,0:T(8,128)(2,1)S(1)} all-to-all(bf16[8,8,1664]{2,1,0:T(8,128)(2,1)S(1)} %bitcast.16), channel_id=1, replica_groups=mesh['zh'=2,'x'=4,'zl'=8,'yh'=2,'yl'=2,'c'=2] {'zl'}, dimensions={0} | all-to-all | bytes 425984 | tf_op jit(solution)/shard_map/all_to_all | solution.py:18
  113.4 0.2 shard_map.92
  113.6 8.2 %collective-permute-start.6 = (bf16[8,640]{1,0:T(8,128)(2,1)S(1)}, bf16[8,640]{1,0:T(8,128)(2,1)S(1)}, u32[]{:S(2)}, u32[]{:S(2)}) collective-permute-start(bf16[8,640]{1,0:T(8,128)(2,1)S(1)} %get-tuple-element.27.last_ref), channel_id=1, source_target_pairs={{0,256},{256,0},{1,257},{257,1},{2,258},{258,2},{3,259},{259,3},{4... | collective-permute-start | bytes 30728 | tf_op jit(solution)/shard_map/ppermute | solution.py:408
  121.8 2.7 %collective-permute-start.5 = (bf16[32,512]{1,0:T(8,128)(2,1)S(1)}, bf16[32,512]{1,0:T(8,128)(2,1)S(1)}, u32[]{:S(2)}, u32[]{:S(2)}) collective-permute-start(bf16[32,512]{1,0:T(8,128)(2,1)S(1)} %get-tuple-element.26), channel_id=1, source_target_pairs={{0,4},{2,6},{4,0},{6,2},{1,5},{3,7},{5,1},{7,3},{8,12},{10,14},{12... | collective-permute-start | bytes 98312 | tf_op jit(solution)/shard_map/ppermute | solution.py:22
  124.5 3.3 %collective-permute-done.6.far_ref = bf16[8,640]{1,0:T(8,128)(2,1)S(1)} collective-permute-done((bf16[8,640]{1,0:T(8,128)(2,1)S(1)}, bf16[8,640]{1,0:T(8,128)(2,1)S(1)}, u32[]{:S(2)}, u32[]{:S(2)}) %collective-permute-start.6) | collective-permute-done | bytes 10272 | tf_op jit(solution)/shard_map/ppermute | solution.py:408
  127.8 0.6 shard_map.94
  128.5 3.3 %all-to-all-start.4 = ((bf16[4,8,512]{2,1,0:T(8,128)(2,1)}), bf16[4,8,512]{2,1,0:T(8,128)(2,1)S(1)}, u32[]{:S(2)}, u32[]{:S(2)}) async-start(bf16[4,8,512]{2,1,0:T(8,128)(2,1)} %get-tuple-element.28), calls=%async_computation.4 | async-start | bytes 65536 | tf_op jit(solution)/shard_map/all_to_all | solution.py:18
  131.7 0.8 shard_map.93
  132.6 4.6 %all-to-all-done.4.got_ref = bf16[4,8,512]{2,1,0:T(8,128)(2,1)S(1)} async-done(((bf16[4,8,512]{2,1,0:T(8,128)(2,1)}), bf16[4,8,512]{2,1,0:T(8,128)(2,1)S(1)}, u32[]{:S(2)}, u32[]{:S(2)}) %all-to-all-start.4) | async-done | bytes 32800 | tf_op jit(solution)/shard_map/all_to_all | solution.py:18
  137.1 0.6 shard_map.95
  (5 shorter events, 0.0 us)
Async XLA Ops:
  36.6 29.3 %all-to-all-start.1 = ((bf16[32,128,128]{2,1,0:T(8,128)(2,1)}), bf16[32,128,128]{2,1,0:T(8,128)(2,1)S(1)}, u32[]{:S(2)}, u32[]{:S(2)}) async-start(bf16[32,128,128]{2,1,0:T(8,128)(2,1)} %shard_map.88), calls=%async_computation.1 | async-start | bytes 2097152 | tf_op jit(solution)/shard_map/all_to_all | solution.py:18
  43.6 21.9 %copy-start = (f32[512]{0:T(512)S(1)}, f32[512]{0:T(512)}, u32[]{:S(2)}) copy-start(f32[512]{0:T(512)} %param.7) | copy-start | bytes 6148
  43.8 17.9 %collective-permute-start = (bf16[128,512]{1,0:T(8,128)(2,1)S(1)}, bf16[128,512]{1,0:T(8,128)(2,1)S(1)}, u32[]{:S(2)}, u32[]{:S(2)}) collective-permute-start(bf16[128,512]{1,0:T(8,128)(2,1)S(1)} %shard_map.85), channel_id=1, source_target_pairs={{0,6},{2,4},{4,2},{6,0},{1,7},{3,5},{5,3},{7,1},{8,14},{10,12},{12... | collective-permute-start | bytes 393224 | tf_op jit(solution)/shard_map/ppermute | solution.py:22
  62.1 3.4 %collective-permute-start.1 = (bf16[256,512]{1,0:T(8,128)(2,1)S(1)}, bf16[256,512]{1,0:T(8,128)(2,1)S(1)}, u32[]{:S(2)}, u32[]{:S(2)}) collective-permute-start(bf16[256,512]{1,0:T(8,128)(2,1)S(1)} %shard_map.86.own_ref), channel_id=1, source_target_pairs={{0,1},{1,0},{2,3},{3,2},{4,5},{5,4},{6,7},{7,6},{8,9},{9,8},{10,11... | collective-permute-start | bytes 786440 | tf_op jit(solution)/shard_map/ppermute | solution.py:387
  69.7 22.5 %all-to-all-start.2 = ((bf16[32,136,128]{2,1,0:T(8,128)(2,1)}), bf16[32,136,128]{2,1,0:T(8,128)(2,1)S(1)}, u32[]{:S(2)}, u32[]{:S(2)}) async-start(bf16[32,136,128]{2,1,0:T(8,128)(2,1)} %get-tuple-element.22), calls=%async_computation.2 | async-start | bytes 2228224 | tf_op jit(solution)/shard_map/all_to_all | solution.py:18
  74.6 3.2 %collective-permute-start.2 = (bf16[128,512]{1,0:T(8,128)(2,1)S(1)}, bf16[128,512]{1,0:T(8,128)(2,1)S(1)}, u32[]{:S(2)}, u32[]{:S(2)}) collective-permute-start(bf16[128,512]{1,0:T(8,128)(2,1)S(1)} %get-tuple-element.24), channel_id=1, source_target_pairs={{0,1},{1,0},{2,3},{3,2},{4,5},{5,4},{6,7},{7,6},{8,9},{9,8},{10,11... | collective-permute-start | bytes 393224 | tf_op jit(solution)/shard_map/ppermute | solution.py:401
  78.2 9.2 %collective-permute-start.4 = (bf16[32,512]{1,0:T(8,128)(2,1)S(1)}, bf16[32,512]{1,0:T(8,128)(2,1)S(1)}, u32[]{:S(2)}, u32[]{:S(2)}) collective-permute-start(bf16[32,512]{1,0:T(8,128)(2,1)S(1)} %get-tuple-element.32), channel_id=1, source_target_pairs={{0,6},{2,4},{4,2},{6,0},{1,7},{3,5},{5,3},{7,1},{8,14},{10,12},{12... | collective-permute-start | bytes 98312 | tf_op jit(solution)/shard_map/ppermute | solution.py:22
  83.1 7.0 %collective-permute-start.3 = (bf16[32,512]{1,0:T(8,128)(2,1)S(1)}, bf16[32,512]{1,0:T(8,128)(2,1)S(1)}, u32[]{:S(2)}, u32[]{:S(2)}) collective-permute-start(bf16[32,512]{1,0:T(8,128)(2,1)S(1)} %get-tuple-element.33), channel_id=1, source_target_pairs={{0,2},{2,0},{4,6},{6,4},{1,3},{3,1},{5,7},{7,5},{8,10},{10,8},{12,... | collective-permute-start | bytes 98312 | tf_op jit(solution)/shard_map/ppermute | solution.py:22
  113.6 14.3 %collective-permute-start.6 = (bf16[8,640]{1,0:T(8,128)(2,1)S(1)}, bf16[8,640]{1,0:T(8,128)(2,1)S(1)}, u32[]{:S(2)}, u32[]{:S(2)}) collective-permute-start(bf16[8,640]{1,0:T(8,128)(2,1)S(1)} %get-tuple-element.27.last_ref), channel_id=1, source_target_pairs={{0,256},{256,0},{1,257},{257,1},{2,258},{258,2},{3,259},{259,3},{4... | collective-permute-start | bytes 30728 | tf_op jit(solution)/shard_map/ppermute | solution.py:408
  121.8 9.9 %collective-permute-start.5 = (bf16[32,512]{1,0:T(8,128)(2,1)S(1)}, bf16[32,512]{1,0:T(8,128)(2,1)S(1)}, u32[]{:S(2)}, u32[]{:S(2)}) collective-permute-start(bf16[32,512]{1,0:T(8,128)(2,1)S(1)} %get-tuple-element.26), channel_id=1, source_target_pairs={{0,4},{2,6},{4,0},{6,2},{1,5},{3,7},{5,1},{7,3},{8,12},{10,14},{12... | collective-permute-start | bytes 98312 | tf_op jit(solution)/shard_map/ppermute | solution.py:22
  128.5 8.7 %all-to-all-start.4 = ((bf16[4,8,512]{2,1,0:T(8,128)(2,1)}), bf16[4,8,512]{2,1,0:T(8,128)(2,1)S(1)}, u32[]{:S(2)}, u32[]{:S(2)}) async-start(bf16[4,8,512]{2,1,0:T(8,128)(2,1)} %get-tuple-element.28), calls=%async_computation.4 | async-start | bytes 65536 | tf_op jit(solution)/shard_map/all_to_all | solution.py:18

commit v11 on v9

--- a/solution.py
+++ b/solution.py
@@ -169,7 +169,34 @@
     def pile(arr):
         return jnp.concatenate([arr[:, :128], arr[:, 128:]], axis=0)
 
-    atts, dqs, dks, dvs = [], [], [], []
+    def frames(items):
+        return [
+            jnp.concatenate([items[0], items[2]], axis=0),
+            jnp.concatenate([items[1], items[3]], axis=0),
+        ]
+
+    copies = []
+
+    def leave(part, messages):
+        for yc in range(8):
+            parts_vm[part * 8 + yc] = messages(yc).astype(BF)
+        at = slice(part * 8, part * 8 + 8)
+        copy = pltpu.make_async_copy(parts_vm.at[at], parts_ref.at[at], sems.at[part])
+        copy.start()
+        copies.append(copy)
+
+    def leave_columns(part, columns, tail):
+        grads = dot(flipped, columns).reshape(ZL, Y, 2, 8, 256)
+
+        def message(yc):
+            block = grads[:, yc // 2, yc % 2].reshape(64, 256)
+            return jnp.concatenate([block[:, :128], block[:, 128:], tail], axis=0)
+
+        leave(part, message)
+
+    flipped = flipped_ref[...]
+    none = jnp.zeros((8, 128), F32)
+    atts, dvs, dscores, sides = [], [], [], []
     for f in range(2):
         rows = slice(f * 128, (f + 1) * 128)
         for pair in range(2):
@@ -180,7 +207,7 @@
             u = ups[rows, at : at + 128]
             scores = dot(q, k2, 1, 1) * 0.125
             dprob = dot(u, v2, 1, 1)
-            weights, dscores = [], []
+            weights, scored = [], []
             for head in range(2):
                 cols = slice(head * 128, (head + 1) * 128)
                 s = scores[:, cols]
@@ -189,53 +216,36 @@
                 dp = dprob[:, cols]
                 weights.append(probs.astype(BF))
                 inner = jnp.sum(probs * dp, axis=-1, keepdims=True)
-                dscores.append((probs * (dp - inner) * 0.125).astype(BF))
+                scored.append((probs * (dp - inner) * 0.125).astype(BF))
             weight = jnp.concatenate(weights, axis=1)
-            dscore = jnp.concatenate(dscores, axis=1)
             atts.append(dot(weight, v2).astype(BF))
-            dqs.append(dot(dscore, k2).astype(BF))
-            dks.append(dot(pile(dscore), stack(q), 0, 0).astype(BF))
             dvs.append(dot(pile(weight), stack(u), 0, 0).astype(BF))
-
-    def frames(items):
-        return [
-            jnp.concatenate([items[0], items[2]], axis=0),
-            jnp.concatenate([items[1], items[3]], axis=0),
-        ]
+            dscores.append(jnp.concatenate(scored, axis=1))
+            sides.append((q, k2))
 
     att = jnp.concatenate(frames(atts), axis=1)
-    dqkv = jnp.concatenate(frames(dqs) + frames(dks) + frames(dvs), axis=1)
-
-    dn = dot(dqkv, wh, 1, 1)
+    g_out = dot(att, g_in, 0, 0).reshape(4, Y, 2, 8, 512)
+
+    def out_message(yc):
+        block = g_out[:, yc // 2, yc % 2].reshape(32, 512)
+        pieces = [block[:, i * 128 : i * 128 + 128] for i in range(4)]
+        return jnp.concatenate(pieces + [none], axis=0)
+
+    leave(3, out_message)
+    dv = jnp.concatenate(frames(dvs), axis=1)
+    leave_columns(2, dv, none)
+
+    dq = [dot(dscore, k2).astype(BF) for dscore, (q, k2) in zip(dscores, sides)]
+    dk = [dot(pile(dscore), stack(q), 0, 0).astype(BF) for dscore, (q, k2) in zip(dscores, sides)]
+    dq = jnp.concatenate(frames(dq), axis=1)
+    dk = jnp.concatenate(frames(dk), axis=1)
+    dn = dot(jnp.concatenate([dq, dk, dv], axis=1), wh, 1, 1)
+    gg = two_rows(jnp.sum(dn * scaled_ref[...], axis=0, keepdims=True))
+    gg = jnp.concatenate([gg[0:2, i * 128 : i * 128 + 128] for i in range(4)], axis=0)
+    leave_columns(1, dk, gg)
+    leave_columns(0, dq, gg)
     keep_ref[...] = jnp.concatenate([dn[0:64], dn[128:192]], axis=0)
     send_ref[...] = jnp.concatenate([dn[64:128], dn[192:]], axis=0).astype(BF)
-
-    gg = two_rows(jnp.sum(dn * scaled_ref[...], axis=0, keepdims=True))
-    gg = jnp.concatenate([gg[0:2, i * 128 : i * 128 + 128] for i in range(4)], axis=0)
-
-    copies = []
-
-    def leave(part):
-        at = slice(part * 8, part * 8 + 8)
-        copy = pltpu.make_async_copy(parts_vm.at[at], parts_ref.at[at], sems.at[part])
-        copy.start()
-        copies.append(copy)
-
-    g_out = dot(att, g_in, 0, 0).reshape(4, Y, 2, 8, 512)
-    for yc in range(8):
-        block = g_out[:, yc // 2, yc % 2].reshape(32, 512)
-        pieces = [block[:, i * 128 : i * 128 + 128] for i in range(4)] + [gg]
-        parts_vm[24 + yc] = jnp.concatenate(pieces, axis=0).astype(BF)
-    leave(3)
-    flipped = flipped_ref[...]
-    for part in (2, 1, 0):
-        g_part = dot(flipped, dqkv[:, part * 256 : part * 256 + 256])
-        g_part = g_part.reshape(ZL, Y, 2, 8, 256)
-        for yc in range(8):
-            block = g_part[:, yc // 2, yc % 2].reshape(64, 256)
-            pieces = [block[:, :128], block[:, 128:], gg]
-            parts_vm[part * 8 + yc] = jnp.concatenate(pieces, axis=0).astype(BF)
-        leave(part)
     for copy in copies:
         copy.wait()
 
@@ -314,12 +324,13 @@
     last_ref[:, 512:] = two_blocks(gains[0:4] + gains[4:8]).astype(BF)
 
 
-def pair_body(last_ref, far_ref, sent_ref, gain_ref):
+def pair_body(last_ref, far_ref, sent_ref):
     total = last_ref[...].astype(F32) + far_ref[...].astype(F32)
     grads = total[:, :512].astype(BF)
+    gains = two_blocks(total[0:4, 512:] + total[4:8, 512:]).astype(BF)
     for x in range(X):
-        sent_ref[x] = grads
-    gain_ref[...] = total[0:4, 512:] + total[4:8, 512:]
+        sent_ref[x, :, :512] = grads
+        sent_ref[x, :, 512:] = gains
 
 
 def tokens_body(rest_ref, two_ref, out_ref):
@@ -332,10 +343,12 @@
     out_ref[...] = dot(chooser(128, 128, source), blocks).astype(BF)
 
 
-def end_body(got_ref, qkv_ref, out_ref):
+def end_body(got_ref, qkv_ref, out_ref, gain_ref):
     for x in range(3):
-        qkv_ref[:, x * 512 : x * 512 + 512] = got_ref[x].astype(F32)
-    out_ref[...] = got_ref[3].astype(F32)
+        qkv_ref[:, x * 512 : x * 512 + 512] = got_ref[x, :, :512].astype(F32)
+    out_ref[...] = got_ref[3, :, :512].astype(F32)
+    gain = got_ref[0, :, 512:].astype(F32)
+    gain_ref[...] = gain[0:4] + gain[4:8]
 
 
 def on_device(tokens, grad_out, gain, w_qkv, w_out):
@@ -389,9 +402,12 @@
     )
     last_far = lax.ppermute(last, "zh", SWAP)
     [grad_tokens] = call(tokens_body, [((128, 512), BF)], rest, to_y(hop, 2))
-    sent, total = call(pair_body, [((X, 8, 512), BF), ((4, 128), F32)], last, last_far)
+    last_far, grad_tokens = lax.optimization_barrier((last_far, grad_tokens))
+    [sent] = call(pair_body, [((X, 8, 640), BF)], last, last_far)
     ends = exchange(sent, "x")
-    shard_qkv, shard_out = call(end_body, [((8, 1536), F32), ((8, 512), F32)], ends)
+    shard_qkv, shard_out, total = call(
+        end_body, [((8, 1536), F32), ((8, 512), F32), ((4, 128), F32)], ends
+    )
     return grad_tokens.reshape(1, 2, 64, 512), shard_qkv, shard_out, total.reshape(512)
 
 

time: 133 us -> 135 us (1.015)
  blocking collectives: 56.4 us -> 65.4 us
  starting transfers between devices: 35.2 us -> 31.9 us
  waiting for transfers between devices: 29.9 us -> 27.2 us
    all_to_all x2 -> x3, blocking collectives: 56.4 us -> 65.4 us  [exchange(): return lax.all_to_all(arr, axes, split_axis=0, concat_axis=0, tiled=True)]
    all_to_all x3 -> x2, waiting for transfers between devices: 19.5 us -> 14.9 us  [exchange(): return lax.all_to_all(arr, axes, split_axis=0, concat_axis=0, tiled=True)]
    all_to_all x3 -> x2, starting transfers between devices: 12.8 us -> 9.54 us  [exchange(): return lax.all_to_all(arr, axes, split_axis=0, concat_axis=0, tiled=True)]
    ppermute x1, waiting for transfers between devices: 3.31 us -> 5.21 us  [on_device(): last_far = lax.ppermute(last, 'zh', SWAP)]
  transfers between devices with their start and end apart: 9 -> 8, of which waited for: 8 -> 7; matrix products, arithmetic and copies ran while one was open for 0% -> 0% of each run, Pallas kernels for 2% -> 1%
where the time goes in v11:
time: 135 us
  blocking collectives  65.4 us (48%)
  starting transfers between devices  31.9 us (24%)
  waiting for transfers between devices  27.2 us (20%)
  Pallas kernels  9.44 us (7%)
    all_to_all x3, blocking collectives, exchange(): return lax.all_to_all(arr, axes, split_axis=0, concat_axis=0, tiled=True)  65.4 us
    all_to_all x2, waiting for transfers between devices, exchange(): return lax.all_to_all(arr, axes, split_axis=0, concat_axis=0, tiled=True)  14.9 us
    ppermute x3, starting transfers between devices, to_y(): return lax.ppermute(block, 'y', [(i, i ^ k) for i in range(Y)])  9.81 us
    all_to_all x2, starting transfers between devices, exchange(): return lax.all_to_all(arr, axes, split_axis=0, concat_axis=0, tiled=True)  9.54 us
    ppermute x1, starting transfers between devices, on_device(): last_far = lax.ppermute(last, 'zh', SWAP)  8.22 us
    pallas_call x10, Pallas kernels, call(): pl.pallas_call(body, out_shape=[jax.ShapeDtypeStruct(shape, kind) for sha...  7.48 us
    ppermute x1, waiting for transfers between devices, on_device(): last_far = lax.ppermute(last, 'zh', SWAP)  5.21 us
    ppermute x3, waiting for transfers between devices, to_y(): return lax.ppermute(block, 'y', [(i, i ^ k) for i in range(Y)])  4.81 us
  transfers between devices with their start and end apart: 8, of which 7 were waited for; matrix products, arithmetic and copies ran while one was open for 0% of the time, Pallas kernels for 1%

profile of v11, /device:TPU:32, one launch (start us, length us, event | category | flops | bytes accessed | tf_op | source)
XLA Modules:
  0.0 134.8 jit_solution(6952049002780719065)
XLA Ops:
  0.6 2.0 %shard_map.84 = bf16[256,640]{1,0:T(8,128)(2,1)} custom-call(bf16[128,512]{1,0:T(8,128)(2,1)} %bitcast.20, bf16[128,512]{1,0:T(8,128)(2,1)} %bitcast.21, bf16[8,1536]{1,0:T(8,128)(2,1)} %wq_ref.1, bf16[8,512]{1,0:T(8,128)(2,1)} %wo_ref.1), custom_call_target="tpu_custom_call" | custom-call | tf_op jit(solution)/shard_map/pallas_call | solution.py:359
  2.6 36.0 %all_to_all.25 = bf16[32,8,640]{2,1,0:T(8,128)(2,1)S(1)} all-to-all(bf16[32,8,640]{2,1,0:T(8,128)(2,1)} %bitcast.19), channel_id=1, replica_groups=mesh['zh'=2,'x'=4,'zl'=8,'y'=4,'c'=2] {'zl','y'}, dimensions={0} | all-to-all | bytes 655360 | tf_op jit(solution)/shard_map/all_to_all | solution.py:18
  38.6 1.2 shard_map.87
  39.8 0.0 copy-start
  39.8 5.5 %all-to-all-start.1 = ((bf16[32,128,128]{2,1,0:T(8,128)(2,1)}), bf16[32,128,128]{2,1,0:T(8,128)(2,1)S(1)}, u32[]{:S(2)}, u32[]{:S(2)}) async-start(bf16[32,128,128]{2,1,0:T(8,128)(2,1)} %shard_map.87), calls=%async_computation.1 | async-start | bytes 2097152 | tf_op jit(solution)/shard_map/all_to_all | solution.py:18
  45.3 0.2 shard_map.85.own_ref
  45.5 2.2 %collective-permute-start = (bf16[256,512]{1,0:T(8,128)(2,1)S(1)}, bf16[256,512]{1,0:T(8,128)(2,1)S(1)}, u32[]{:S(2)}, u32[]{:S(2)}) collective-permute-start(bf16[256,512]{1,0:T(8,128)(2,1)S(1)} %shard_map.85.own_ref), channel_id=1, source_target_pairs={{0,1},{1,0},{2,3},{3,2},{4,5},{5,4},{6,7},{7,6},{8,9},{9,8},{10,11... | collective-permute-start | bytes 786440 | tf_op jit(solution)/shard_map/ppermute | solution.py:382
  47.7 1.2 collective-permute-done.far_ref
  49.0 0.0 copy-done
  49.0 0.3 shard_map.86
  49.3 12.9 %all-to-all-done.1.w_ref = bf16[32,128,128]{2,1,0:T(8,128)(2,1)S(1)} async-done(((bf16[32,128,128]{2,1,0:T(8,128)(2,1)}), bf16[32,128,128]{2,1,0:T(8,128)(2,1)S(1)}, u32[]{:S(2)}, u32[]{:S(2)}) %all-to-all-start.1) | async-done | bytes 1048608 | tf_op jit(solution)/shard_map/all_to_all | solution.py:18
  62.1 3.5 %shard_map.88 = (bf16[32,136,128]{2,1,0:T(8,128)(2,1)}, bf16[128,512]{1,0:T(8,128)(2,1)S(1)}, f32[128,512]{1,0:T(8,128)S(1)}) custom-call(f32[256,512]{1,0:T(8,128)S(1)} %get-tuple-element.19.scaled_ref, bf16[256,512]{1,0:T(8,128)(2,1)S(1)} %get-tuple-element.20.normed_ref, bf16[512,256]{1,0:T(8,128)(2,1)S(1)} %get-tuple-element.21.flipped_ref, ...), custom_call_target="tpu_custom_call" | custom-call | tf_op jit(solution)/shard_map/pallas_call | solution.py:30
  65.6 4.1 %all-to-all-start.2 = ((bf16[32,136,128]{2,1,0:T(8,128)(2,1)}), bf16[32,136,128]{2,1,0:T(8,128)(2,1)S(1)}, u32[]{:S(2)}, u32[]{:S(2)}) async-start(bf16[32,136,128]{2,1,0:T(8,128)(2,1)} %get-tuple-element.23), calls=%async_computation.2 | async-start | bytes 2228224 | tf_op jit(solution)/shard_map/all_to_all | solution.py:18
  69.7 2.2 %collective-permute-start.1 = (bf16[128,512]{1,0:T(8,128)(2,1)S(1)}, bf16[128,512]{1,0:T(8,128)(2,1)S(1)}, u32[]{:S(2)}, u32[]{:S(2)}) collective-permute-start(bf16[128,512]{1,0:T(8,128)(2,1)S(1)} %get-tuple-element.25), channel_id=1, source_target_pairs={{0,1},{1,0},{2,3},{3,2},{4,5},{5,4},{6,7},{7,6},{8,9},{9,8},{10,11... | collective-permute-start | bytes 393224 | tf_op jit(solution)/shard_map/ppermute | solution.py:396
  71.9 1.1 collective-permute-done.1.far_ref
  72.9 0.4 shard_map.89.hop_ref
  73.3 4.9 %collective-permute-start.3 = (bf16[32,512]{1,0:T(8,128)(2,1)S(1)}, bf16[32,512]{1,0:T(8,128)(2,1)S(1)}, u32[]{:S(2)}, u32[]{:S(2)}) collective-permute-start(bf16[32,512]{1,0:T(8,128)(2,1)S(1)} %get-tuple-element.34), channel_id=1, source_target_pairs={{0,6},{2,4},{4,2},{6,0},{1,7},{3,5},{5,3},{7,1},{8,14},{10,12},{12... | collective-permute-start | bytes 98312 | tf_op jit(solution)/shard_map/ppermute | solution.py:22
  78.3 2.2 %collective-permute-start.2 = (bf16[32,512]{1,0:T(8,128)(2,1)S(1)}, bf16[32,512]{1,0:T(8,128)(2,1)S(1)}, u32[]{:S(2)}, u32[]{:S(2)}) collective-permute-start(bf16[32,512]{1,0:T(8,128)(2,1)S(1)} %get-tuple-element.35), channel_id=1, source_target_pairs={{0,2},{2,0},{4,6},{6,4},{1,3},{3,1},{5,7},{7,5},{8,10},{10,8},{12,... | collective-permute-start | bytes 98312 | tf_op jit(solution)/shard_map/ppermute | solution.py:22
  80.4 2.1 %collective-permute-done.3.b3_ref = bf16[32,512]{1,0:T(8,128)(2,1)S(1)} collective-permute-done((bf16[32,512]{1,0:T(8,128)(2,1)S(1)}, bf16[32,512]{1,0:T(8,128)(2,1)S(1)}, u32[]{:S(2)}, u32[]{:S(2)}) %collective-permute-start.3) | collective-permute-done | bytes 32800 | tf_op jit(solution)/shard_map/ppermute | solution.py:22
  82.6 2.7 %collective-permute-done.2.b1_ref = bf16[32,512]{1,0:T(8,128)(2,1)S(1)} collective-permute-done((bf16[32,512]{1,0:T(8,128)(2,1)S(1)}, bf16[32,512]{1,0:T(8,128)(2,1)S(1)}, u32[]{:S(2)}, u32[]{:S(2)}) %collective-permute-start.2) | collective-permute-done | bytes 32800 | tf_op jit(solution)/shard_map/ppermute | solution.py:22
  85.2 2.0 %all-to-all-done.2.got_ref = bf16[32,136,128]{2,1,0:T(8,128)(2,1)S(1)} async-done(((bf16[32,136,128]{2,1,0:T(8,128)(2,1)}), bf16[32,136,128]{2,1,0:T(8,128)(2,1)S(1)}, u32[]{:S(2)}, u32[]{:S(2)}) %all-to-all-start.2) | async-done | bytes 1114144 | tf_op jit(solution)/shard_map/all_to_all | solution.py:18
  87.3 0.3 shard_map.90
  87.5 20.4 %all_to_all.26 = bf16[8,8,1664]{2,1,0:T(8,128)(2,1)S(1)} all-to-all(bf16[8,8,1664]{2,1,0:T(8,128)(2,1)S(1)} %bitcast.15), channel_id=1, replica_groups=mesh['zh'=2,'x'=4,'zl'=8,'y'=4,'c'=2] {'zl'}, dimensions={0} | all-to-all | bytes 425984 | tf_op jit(solution)/shard_map/all_to_all | solution.py:18
  107.9 0.2 shard_map.91
  108.1 2.7 %collective-permute-start.5 = (bf16[32,512]{1,0:T(8,128)(2,1)S(1)}, bf16[32,512]{1,0:T(8,128)(2,1)S(1)}, u32[]{:S(2)}, u32[]{:S(2)}) collective-permute-start(bf16[32,512]{1,0:T(8,128)(2,1)S(1)} %get-tuple-element.28), channel_id=1, source_target_pairs={{0,4},{2,6},{4,0},{6,2},{1,5},{3,7},{5,1},{7,3},{8,12},{10,14},{12... | collective-permute-start | bytes 98312 | tf_op jit(solution)/shard_map/ppermute | solution.py:22
  110.8 8.2 %collective-permute-start.4 = (bf16[8,640]{1,0:T(8,128)(2,1)S(1)}, bf16[8,640]{1,0:T(8,128)(2,1)S(1)}, u32[]{:S(2)}, u32[]{:S(2)}) collective-permute-start(bf16[8,640]{1,0:T(8,128)(2,1)S(1)} %get-tuple-element.26.last_ref), channel_id=1, source_target_pairs={{0,256},{256,0},{1,257},{257,1},{2,258},{258,2},{3,259},{259,3},{4... | collective-permute-start | bytes 30728 | tf_op jit(solution)/shard_map/ppermute | solution.py:403
  119.1 0.0 collective-permute-done.5.two_ref
  119.1 0.8 shard_map.92
  119.9 5.2 %collective-permute-done.4.far_ref = bf16[8,640]{1,0:T(8,128)(2,1)S(1)} collective-permute-done((bf16[8,640]{1,0:T(8,128)(2,1)S(1)}, bf16[8,640]{1,0:T(8,128)(2,1)S(1)}, u32[]{:S(2)}, u32[]{:S(2)}) %collective-permute-start.4) | collective-permute-done | bytes 10272 | tf_op jit(solution)/shard_map/ppermute | solution.py:403
  125.1 9.1 %all_to_all.27.got_ref = bf16[4,8,640]{2,1,0:T(8,128)(2,1)S(1)} all-to-all(bf16[4,8,640]{2,1,0:T(8,128)(2,1)S(1)} %shard_map.93), channel_id=1, replica_groups=mesh['zh'=2,'x'=4,'zl'=8,'y'=4,'c'=2] {'x'}, dimensions={0} | all-to-all | bytes 81920 | tf_op jit(solution)/shard_map/all_to_all | solution.py:18
  134.2 0.6 shard_map.94
  (2 shorter events, 0.0 us)
Async XLA Ops:
  39.8 9.2 %copy-start = (f32[512]{0:T(512)S(1)}, f32[512]{0:T(512)}, u32[]{:S(2)}) copy-start(f32[512]{0:T(512)} %param.7) | copy-start | bytes 6148
  39.8 22.3 %all-to-all-start.1 = ((bf16[32,128,128]{2,1,0:T(8,128)(2,1)}), bf16[32,128,128]{2,1,0:T(8,128)(2,1)S(1)}, u32[]{:S(2)}, u32[]{:S(2)}) async-start(bf16[32,128,128]{2,1,0:T(8,128)(2,1)} %shard_map.87), calls=%async_computation.1 | async-start | bytes 2097152 | tf_op jit(solution)/shard_map/all_to_all | solution.py:18
  45.5 3.4 %collective-permute-start = (bf16[256,512]{1,0:T(8,128)(2,1)S(1)}, bf16[256,512]{1,0:T(8,128)(2,1)S(1)}, u32[]{:S(2)}, u32[]{:S(2)}) collective-permute-start(bf16[256,512]{1,0:T(8,128)(2,1)S(1)} %shard_map.85.own_ref), channel_id=1, source_target_pairs={{0,1},{1,0},{2,3},{3,2},{4,5},{5,4},{6,7},{7,6},{8,9},{9,8},{10,11... | collective-permute-start | bytes 786440 | tf_op jit(solution)/shard_map/ppermute | solution.py:382
  65.6 21.7 %all-to-all-start.2 = ((bf16[32,136,128]{2,1,0:T(8,128)(2,1)}), bf16[32,136,128]{2,1,0:T(8,128)(2,1)S(1)}, u32[]{:S(2)}, u32[]{:S(2)}) async-start(bf16[32,136,128]{2,1,0:T(8,128)(2,1)} %get-tuple-element.23), calls=%async_computation.2 | async-start | bytes 2228224 | tf_op jit(solution)/shard_map/all_to_all | solution.py:18
  69.7 3.2 %collective-permute-start.1 = (bf16[128,512]{1,0:T(8,128)(2,1)S(1)}, bf16[128,512]{1,0:T(8,128)(2,1)S(1)}, u32[]{:S(2)}, u32[]{:S(2)}) collective-permute-start(bf16[128,512]{1,0:T(8,128)(2,1)S(1)} %get-tuple-element.25), channel_id=1, source_target_pairs={{0,1},{1,0},{2,3},{3,2},{4,5},{5,4},{6,7},{7,6},{8,9},{9,8},{10,11... | collective-permute-start | bytes 393224 | tf_op jit(solution)/shard_map/ppermute | solution.py:396
  73.3 9.2 %collective-permute-start.3 = (bf16[32,512]{1,0:T(8,128)(2,1)S(1)}, bf16[32,512]{1,0:T(8,128)(2,1)S(1)}, u32[]{:S(2)}, u32[]{:S(2)}) collective-permute-start(bf16[32,512]{1,0:T(8,128)(2,1)S(1)} %get-tuple-element.34), channel_id=1, source_target_pairs={{0,6},{2,4},{4,2},{6,0},{1,7},{3,5},{5,3},{7,1},{8,14},{10,12},{12... | collective-permute-start | bytes 98312 | tf_op jit(solution)/shard_map/ppermute | solution.py:22
  78.3 7.0 %collective-permute-start.2 = (bf16[32,512]{1,0:T(8,128)(2,1)S(1)}, bf16[32,512]{1,0:T(8,128)(2,1)S(1)}, u32[]{:S(2)}, u32[]{:S(2)}) collective-permute-start(bf16[32,512]{1,0:T(8,128)(2,1)S(1)} %get-tuple-element.35), channel_id=1, source_target_pairs={{0,2},{2,0},{4,6},{6,4},{1,3},{3,1},{5,7},{7,5},{8,10},{10,8},{12,... | collective-permute-start | bytes 98312 | tf_op jit(solution)/shard_map/ppermute | solution.py:22
  108.1 11.0 %collective-permute-start.5 = (bf16[32,512]{1,0:T(8,128)(2,1)S(1)}, bf16[32,512]{1,0:T(8,128)(2,1)S(1)}, u32[]{:S(2)}, u32[]{:S(2)}) collective-permute-start(bf16[32,512]{1,0:T(8,128)(2,1)S(1)} %get-tuple-element.28), channel_id=1, source_target_pairs={{0,4},{2,6},{4,0},{6,2},{1,5},{3,7},{5,1},{7,3},{8,12},{10,14},{12... | collective-permute-start | bytes 98312 | tf_op jit(solution)/shard_map/ppermute | solution.py:22
  110.8 14.3 %collective-permute-start.4 = (bf16[8,640]{1,0:T(8,128)(2,1)S(1)}, bf16[8,640]{1,0:T(8,128)(2,1)S(1)}, u32[]{:S(2)}, u32[]{:S(2)}) collective-permute-start(bf16[8,640]{1,0:T(8,128)(2,1)S(1)} %get-tuple-element.26.last_ref), channel_id=1, source_target_pairs={{0,256},{256,0},{1,257},{257,1},{2,258},{258,2},{3,259},{259,3},{4... | collective-permute-start | bytes 30728 | tf_op jit(solution)/shard_map/ppermute | solution.py:403

commit v12 on v11

--- a/solution.py
+++ b/solution.py
@@ -402,7 +402,6 @@
     )
     last_far = lax.ppermute(last, "zh", SWAP)
     [grad_tokens] = call(tokens_body, [((128, 512), BF)], rest, to_y(hop, 2))
-    last_far, grad_tokens = lax.optimization_barrier((last_far, grad_tokens))
     [sent] = call(pair_body, [((X, 8, 640), BF)], last, last_far)
     ends = exchange(sent, "x")
     shard_qkv, shard_out, total = call(

time: 135 us -> 133 us (0.985)
  blocking collectives: 65.4 us -> 56.4 us
  starting transfers between devices: 31.9 us -> 35.2 us
  waiting for transfers between devices: 27.2 us -> 29.9 us
    all_to_all x3 -> x2, blocking collectives: 65.4 us -> 56.4 us  [exchange(): return lax.all_to_all(arr, axes, split_axis=0, concat_axis=0, tiled=True)]
    all_to_all x2 -> x3, waiting for transfers between devices: 14.9 us -> 19.5 us  [exchange(): return lax.all_to_all(arr, axes, split_axis=0, concat_axis=0, tiled=True)]
    all_to_all x2 -> x3, starting transfers between devices: 9.54 us -> 12.8 us  [exchange(): return lax.all_to_all(arr, axes, split_axis=0, concat_axis=0, tiled=True)]
    ppermute x1, waiting for transfers between devices: 5.21 us -> 3.31 us  [on_device(): last_far = lax.ppermute(last, 'zh', SWAP)]
  transfers between devices with their start and end apart: 8 -> 9, of which waited for: 7 -> 8; matrix products, arithmetic and copies ran while one was open for 0% -> 0% of each run, Pallas kernels for 1% -> 2%
where the time goes in v12:
time: 133 us; the launch traced here: 132 us
  blocking collectives  56.4 us (42%)
  starting transfers between devices  35.2 us (26%)
  waiting for transfers between devices  29.9 us (22%)
  Pallas kernels  10.1 us (8%)
    all_to_all x2, blocking collectives, exchange(): return lax.all_to_all(arr, axes, split_axis=0, concat_axis=0, tiled=True)  56.4 us
    all_to_all x3, waiting for transfers between devices, exchange(): return lax.all_to_all(arr, axes, split_axis=0, concat_axis=0, tiled=True)  19.5 us
    all_to_all x3, starting transfers between devices, exchange(): return lax.all_to_all(arr, axes, split_axis=0, concat_axis=0, tiled=True)  12.8 us
    ppermute x3, starting transfers between devices, to_y(): return lax.ppermute(block, 'y', [(i, i ^ k) for i in range(Y)])  9.81 us
    ppermute x1, starting transfers between devices, on_device(): last_far = lax.ppermute(last, 'zh', SWAP)  8.22 us
    pallas_call x10, Pallas kernels, call(): pl.pallas_call(body, out_shape=[jax.ShapeDtypeStruct(shape, kind) for sha...  8.12 us
    ppermute x3, waiting for transfers between devices, to_y(): return lax.ppermute(block, 'y', [(i, i ^ k) for i in range(Y)])  4.81 us
    ppermute x1, waiting for transfers between devices, on_device(): last_far = lax.ppermute(last, 'zh', SWAP)  3.31 us
  transfers between devices with their start and end apart: 9, of which 8 were waited for; matrix products, arithmetic and copies ran while one was open for 0% of the time, Pallas kernels for 2%

profile of v12, /device:TPU:32, one launch (start us, length us, event | category | flops | bytes accessed | tf_op | source)
XLA Modules:
  0.0 132.4 jit_solution(5440317103782359541)
XLA Ops:
  0.6 2.0 %shard_map.84 = bf16[256,640]{1,0:T(8,128)(2,1)} custom-call(bf16[128,512]{1,0:T(8,128)(2,1)} %bitcast.20, bf16[128,512]{1,0:T(8,128)(2,1)} %bitcast.21, bf16[8,1536]{1,0:T(8,128)(2,1)} %wq_ref.1, bf16[8,512]{1,0:T(8,128)(2,1)} %wo_ref.1), custom_call_target="tpu_custom_call" | custom-call | tf_op jit(solution)/shard_map/pallas_call | solution.py:359
  2.6 36.0 %all_to_all.25 = bf16[32,8,640]{2,1,0:T(8,128)(2,1)S(1)} all-to-all(bf16[32,8,640]{2,1,0:T(8,128)(2,1)} %bitcast.19), channel_id=1, replica_groups=mesh['zh'=2,'x'=4,'zl'=8,'y'=4,'c'=2] {'zl','y'}, dimensions={0} | all-to-all | bytes 655360 | tf_op jit(solution)/shard_map/all_to_all | solution.py:18
  38.6 1.2 shard_map.87
  39.8 0.0 copy-start
  39.8 5.5 %all-to-all-start.1 = ((bf16[32,128,128]{2,1,0:T(8,128)(2,1)}), bf16[32,128,128]{2,1,0:T(8,128)(2,1)S(1)}, u32[]{:S(2)}, u32[]{:S(2)}) async-start(bf16[32,128,128]{2,1,0:T(8,128)(2,1)} %shard_map.87), calls=%async_computation.1 | async-start | bytes 2097152 | tf_op jit(solution)/shard_map/all_to_all | solution.py:18
  45.3 0.2 shard_map.85.own_ref
  45.6 2.2 %collective-permute-start = (bf16[256,512]{1,0:T(8,128)(2,1)S(1)}, bf16[256,512]{1,0:T(8,128)(2,1)S(1)}, u32[]{:S(2)}, u32[]{:S(2)}) collective-permute-start(bf16[256,512]{1,0:T(8,128)(2,1)S(1)} %shard_map.85.own_ref), channel_id=1, source_target_pairs={{0,1},{1,0},{2,3},{3,2},{4,5},{5,4},{6,7},{7,6},{8,9},{9,8},{10,11... | collective-permute-start | bytes 786440 | tf_op jit(solution)/shard_map/ppermute | solution.py:382
  47.7 1.2 collective-permute-done.far_ref
  49.0 0.3 shard_map.86
  49.3 12.9 %all-to-all-done.1.w_ref = bf16[32,128,128]{2,1,0:T(8,128)(2,1)S(1)} async-done(((bf16[32,128,128]{2,1,0:T(8,128)(2,1)}), bf16[32,128,128]{2,1,0:T(8,128)(2,1)S(1)}, u32[]{:S(2)}, u32[]{:S(2)}) %all-to-all-start.1) | async-done | bytes 1048608 | tf_op jit(solution)/shard_map/all_to_all | solution.py:18
  62.1 3.5 %shard_map.88 = (bf16[32,136,128]{2,1,0:T(8,128)(2,1)}, bf16[128,512]{1,0:T(8,128)(2,1)S(1)}, f32[128,512]{1,0:T(8,128)S(1)}) custom-call(f32[256,512]{1,0:T(8,128)S(1)} %get-tuple-element.17.scaled_ref, bf16[256,512]{1,0:T(8,128)(2,1)S(1)} %get-tuple-element.18.normed_ref, bf16[512,256]{1,0:T(8,128)(2,1)S(1)} %get-tuple-element.19.flipped_ref, ...), custom_call_target="tpu_custom_call" | custom-call | tf_op jit(solution)/shard_map/pallas_call | solution.py:30
  65.6 4.1 %all-to-all-start.2 = ((bf16[32,136,128]{2,1,0:T(8,128)(2,1)}), bf16[32,136,128]{2,1,0:T(8,128)(2,1)S(1)}, u32[]{:S(2)}, u32[]{:S(2)}) async-start(bf16[32,136,128]{2,1,0:T(8,128)(2,1)} %get-tuple-element.21), calls=%async_computation.2 | async-start | bytes 2228224 | tf_op jit(solution)/shard_map/all_to_all | solution.py:18
  69.7 2.2 %collective-permute-start.1 = (bf16[128,512]{1,0:T(8,128)(2,1)S(1)}, bf16[128,512]{1,0:T(8,128)(2,1)S(1)}, u32[]{:S(2)}, u32[]{:S(2)}) collective-permute-start(bf16[128,512]{1,0:T(8,128)(2,1)S(1)} %get-tuple-element.23), channel_id=1, source_target_pairs={{0,1},{1,0},{2,3},{3,2},{4,5},{5,4},{6,7},{7,6},{8,9},{9,8},{10,11... | collective-permute-start | bytes 393224 | tf_op jit(solution)/shard_map/ppermute | solution.py:396
  71.9 1.1 collective-permute-done.1.far_ref
  73.0 0.4 shard_map.89.hop_ref
  73.4 4.9 %collective-permute-start.3 = (bf16[32,512]{1,0:T(8,128)(2,1)S(1)}, bf16[32,512]{1,0:T(8,128)(2,1)S(1)}, u32[]{:S(2)}, u32[]{:S(2)}) collective-permute-start(bf16[32,512]{1,0:T(8,128)(2,1)S(1)} %get-tuple-element.30), channel_id=1, source_target_pairs={{0,6},{2,4},{4,2},{6,0},{1,7},{3,5},{5,3},{7,1},{8,14},{10,12},{12... | collective-permute-start | bytes 98312 | tf_op jit(solution)/shard_map/ppermute | solution.py:22
  78.3 2.2 %collective-permute-start.2 = (bf16[32,512]{1,0:T(8,128)(2,1)S(1)}, bf16[32,512]{1,0:T(8,128)(2,1)S(1)}, u32[]{:S(2)}, u32[]{:S(2)}) collective-permute-start(bf16[32,512]{1,0:T(8,128)(2,1)S(1)} %get-tuple-element.31), channel_id=1, source_target_pairs={{0,2},{2,0},{4,6},{6,4},{1,3},{3,1},{5,7},{7,5},{8,10},{10,8},{12,... | collective-permute-start | bytes 98312 | tf_op jit(solution)/shard_map/ppermute | solution.py:22
  80.4 2.1 %collective-permute-done.3.b3_ref = bf16[32,512]{1,0:T(8,128)(2,1)S(1)} collective-permute-done((bf16[32,512]{1,0:T(8,128)(2,1)S(1)}, bf16[32,512]{1,0:T(8,128)(2,1)S(1)}, u32[]{:S(2)}, u32[]{:S(2)}) %collective-permute-start.3) | collective-permute-done | bytes 32800 | tf_op jit(solution)/shard_map/ppermute | solution.py:22
  82.6 2.7 %collective-permute-done.2.b1_ref = bf16[32,512]{1,0:T(8,128)(2,1)S(1)} collective-permute-done((bf16[32,512]{1,0:T(8,128)(2,1)S(1)}, bf16[32,512]{1,0:T(8,128)(2,1)S(1)}, u32[]{:S(2)}, u32[]{:S(2)}) %collective-permute-start.2) | collective-permute-done | bytes 32800 | tf_op jit(solution)/shard_map/ppermute | solution.py:22
  85.2 2.0 %all-to-all-done.2.got_ref = bf16[32,136,128]{2,1,0:T(8,128)(2,1)S(1)} async-done(((bf16[32,136,128]{2,1,0:T(8,128)(2,1)}), bf16[32,136,128]{2,1,0:T(8,128)(2,1)S(1)}, u32[]{:S(2)}, u32[]{:S(2)}) %all-to-all-start.2) | async-done | bytes 1114144 | tf_op jit(solution)/shard_map/all_to_all | solution.py:18
  87.3 0.3 shard_map.90
  87.6 20.4 %all_to_all.26 = bf16[8,8,1664]{2,1,0:T(8,128)(2,1)S(1)} all-to-all(bf16[8,8,1664]{2,1,0:T(8,128)(2,1)S(1)} %bitcast.15), channel_id=1, replica_groups=mesh['zh'=2,'x'=4,'zl'=8,'y'=4,'c'=2] {'zl'}, dimensions={0} | all-to-all | bytes 425984 | tf_op jit(solution)/shard_map/all_to_all | solution.py:18
  107.9 0.2 shard_map.91
  108.1 8.2 %collective-permute-start.5 = (bf16[8,640]{1,0:T(8,128)(2,1)S(1)}, bf16[8,640]{1,0:T(8,128)(2,1)S(1)}, u32[]{:S(2)}, u32[]{:S(2)}) collective-permute-start(bf16[8,640]{1,0:T(8,128)(2,1)S(1)} %get-tuple-element.26.last_ref), channel_id=1, source_target_pairs={{0,256},{256,0},{1,257},{257,1},{2,258},{258,2},{3,259},{259,3},{4... | collective-permute-start | bytes 30728 | tf_op jit(solution)/shard_map/ppermute | solution.py:403
  116.3 2.7 %collective-permute-start.4 = (bf16[32,512]{1,0:T(8,128)(2,1)S(1)}, bf16[32,512]{1,0:T(8,128)(2,1)S(1)}, u32[]{:S(2)}, u32[]{:S(2)}) collective-permute-start(bf16[32,512]{1,0:T(8,128)(2,1)S(1)} %get-tuple-element.25), channel_id=1, source_target_pairs={{0,4},{2,6},{4,0},{6,2},{1,5},{3,7},{5,1},{7,3},{8,12},{10,14},{12... | collective-permute-start | bytes 98312 | tf_op jit(solution)/shard_map/ppermute | solution.py:22
  119.1 3.3 %collective-permute-done.5.far_ref = bf16[8,640]{1,0:T(8,128)(2,1)S(1)} collective-permute-done((bf16[8,640]{1,0:T(8,128)(2,1)S(1)}, bf16[8,640]{1,0:T(8,128)(2,1)S(1)}, u32[]{:S(2)}, u32[]{:S(2)}) %collective-permute-start.5) | collective-permute-done | bytes 10272 | tf_op jit(solution)/shard_map/ppermute | solution.py:403
  122.4 0.6 shard_map.93
  123.0 3.3 %all-to-all-start.4 = ((bf16[4,8,640]{2,1,0:T(8,128)(2,1)}), bf16[4,8,640]{2,1,0:T(8,128)(2,1)S(1)}, u32[]{:S(2)}, u32[]{:S(2)}) async-start(bf16[4,8,640]{2,1,0:T(8,128)(2,1)} %shard_map.93), calls=%async_computation.4 | async-start | bytes 81920 | tf_op jit(solution)/shard_map/all_to_all | solution.py:18
  126.3 0.0 collective-permute-done.4.two_ref
  126.3 0.8 shard_map.92
  127.1 4.6 %all-to-all-done.4.got_ref = bf16[4,8,640]{2,1,0:T(8,128)(2,1)S(1)} async-done(((bf16[4,8,640]{2,1,0:T(8,128)(2,1)}), bf16[4,8,640]{2,1,0:T(8,128)(2,1)S(1)}, u32[]{:S(2)}, u32[]{:S(2)}) %all-to-all-start.4) | async-done | bytes 40992 | tf_op jit(solution)/shard_map/all_to_all | solution.py:18
  131.7 0.6 shard_map.94
  (2 shorter events, 0.0 us)
Async XLA Ops:
  39.8 9.2 %copy-start = (f32[512]{0:T(512)S(1)}, f32[512]{0:T(512)}, u32[]{:S(2)}) copy-start(f32[512]{0:T(512)} %param.7) | copy-start | bytes 6148
  39.8 22.3 %all-to-all-start.1 = ((bf16[32,128,128]{2,1,0:T(8,128)(2,1)}), bf16[32,128,128]{2,1,0:T(8,128)(2,1)S(1)}, u32[]{:S(2)}, u32[]{:S(2)}) async-start(bf16[32,128,128]{2,1,0:T(8,128)(2,1)} %shard_map.87), calls=%async_computation.1 | async-start | bytes 2097152 | tf_op jit(solution)/shard_map/all_to_all | solution.py:18
  45.6 3.4 %collective-permute-start = (bf16[256,512]{1,0:T(8,128)(2,1)S(1)}, bf16[256,512]{1,0:T(8,128)(2,1)S(1)}, u32[]{:S(2)}, u32[]{:S(2)}) collective-permute-start(bf16[256,512]{1,0:T(8,128)(2,1)S(1)} %shard_map.85.own_ref), channel_id=1, source_target_pairs={{0,1},{1,0},{2,3},{3,2},{4,5},{5,4},{6,7},{7,6},{8,9},{9,8},{10,11... | collective-permute-start | bytes 786440 | tf_op jit(solution)/shard_map/ppermute | solution.py:382
  65.6 21.7 %all-to-all-start.2 = ((bf16[32,136,128]{2,1,0:T(8,128)(2,1)}), bf16[32,136,128]{2,1,0:T(8,128)(2,1)S(1)}, u32[]{:S(2)}, u32[]{:S(2)}) async-start(bf16[32,136,128]{2,1,0:T(8,128)(2,1)} %get-tuple-element.21), calls=%async_computation.2 | async-start | bytes 2228224 | tf_op jit(solution)/shard_map/all_to_all | solution.py:18
  69.7 3.2 %collective-permute-start.1 = (bf16[128,512]{1,0:T(8,128)(2,1)S(1)}, bf16[128,512]{1,0:T(8,128)(2,1)S(1)}, u32[]{:S(2)}, u32[]{:S(2)}) collective-permute-start(bf16[128,512]{1,0:T(8,128)(2,1)S(1)} %get-tuple-element.23), channel_id=1, source_target_pairs={{0,1},{1,0},{2,3},{3,2},{4,5},{5,4},{6,7},{7,6},{8,9},{9,8},{10,11... | collective-permute-start | bytes 393224 | tf_op jit(solution)/shard_map/ppermute | solution.py:396
  73.4 9.2 %collective-permute-start.3 = (bf16[32,512]{1,0:T(8,128)(2,1)S(1)}, bf16[32,512]{1,0:T(8,128)(2,1)S(1)}, u32[]{:S(2)}, u32[]{:S(2)}) collective-permute-start(bf16[32,512]{1,0:T(8,128)(2,1)S(1)} %get-tuple-element.30), channel_id=1, source_target_pairs={{0,6},{2,4},{4,2},{6,0},{1,7},{3,5},{5,3},{7,1},{8,14},{10,12},{12... | collective-permute-start | bytes 98312 | tf_op jit(solution)/shard_map/ppermute | solution.py:22
  78.3 7.0 %collective-permute-start.2 = (bf16[32,512]{1,0:T(8,128)(2,1)S(1)}, bf16[32,512]{1,0:T(8,128)(2,1)S(1)}, u32[]{:S(2)}, u32[]{:S(2)}) collective-permute-start(bf16[32,512]{1,0:T(8,128)(2,1)S(1)} %get-tuple-element.31), channel_id=1, source_target_pairs={{0,2},{2,0},{4,6},{6,4},{1,3},{3,1},{5,7},{7,5},{8,10},{10,8},{12,... | collective-permute-start | bytes 98312 | tf_op jit(solution)/shard_map/ppermute | solution.py:22
  108.1 14.3 %collective-permute-start.5 = (bf16[8,640]{1,0:T(8,128)(2,1)S(1)}, bf16[8,640]{1,0:T(8,128)(2,1)S(1)}, u32[]{:S(2)}, u32[]{:S(2)}) collective-permute-start(bf16[8,640]{1,0:T(8,128)(2,1)S(1)} %get-tuple-element.26.last_ref), channel_id=1, source_target_pairs={{0,256},{256,0},{1,257},{257,1},{2,258},{258,2},{3,259},{259,3},{4... | collective-permute-start | bytes 30728 | tf_op jit(solution)/shard_map/ppermute | solution.py:403
  116.3 10.0 %collective-permute-start.4 = (bf16[32,512]{1,0:T(8,128)(2,1)S(1)}, bf16[32,512]{1,0:T(8,128)(2,1)S(1)}, u32[]{:S(2)}, u32[]{:S(2)}) collective-permute-start(bf16[32,512]{1,0:T(8,128)(2,1)S(1)} %get-tuple-element.25), channel_id=1, source_target_pairs={{0,4},{2,6},{4,0},{6,2},{1,5},{3,7},{5,1},{7,3},{8,12},{10,14},{12... | collective-permute-start | bytes 98312 | tf_op jit(solution)/shard_map/ppermute | solution.py:22
  123.0 8.7 %all-to-all-start.4 = ((bf16[4,8,640]{2,1,0:T(8,128)(2,1)}), bf16[4,8,640]{2,1,0:T(8,128)(2,1)S(1)}, u32[]{:S(2)}, u32[]{:S(2)}) async-start(bf16[4,8,640]{2,1,0:T(8,128)(2,1)} %shard_map.93), calls=%async_computation.4 | async-start | bytes 81920 | tf_op jit(solution)/shard_map/all_to_all | solution.py:18

commit v13 on v12

--- a/solution.py
+++ b/solution.py
@@ -66,15 +66,17 @@
     pick = chooser(
         256, 256, lambda i: (i >> 2 & 1) * 128 + (i & 1) * 64 + (i >> 1 & 1) * 32 + (i >> 3)
     )
-    for copy in copies:
-        copy.wait()
-    out_ref[:, :512] = dot(pick, both_vm[...]).astype(BF)
+    copies[2].wait()
+    copies[3].wait()
     x = lax.axis_index("x")
     part = wo_vm[...].astype(F32)
     for i in range(3):
         part = jnp.where(x == i, wq_vm[:, i * 512 : i * 512 + 512].astype(F32), part)
     blocks = jnp.concatenate([part[:, y * 128 : y * 128 + 128] for y in range(Y)], axis=0)
     out_ref[:, 512:] = jnp.concatenate([blocks] * ZL, axis=0).astype(BF)
+    copies[0].wait()
+    copies[1].wait()
+    out_ref[:, :512] = dot(pick, both_vm[...]).astype(BF)
 
 
 def halves(arr):
@@ -239,10 +241,10 @@
     dk = [dot(pile(dscore), stack(q), 0, 0).astype(BF) for dscore, (q, k2) in zip(dscores, sides)]
     dq = jnp.concatenate(frames(dq), axis=1)
     dk = jnp.concatenate(frames(dk), axis=1)
+    leave_columns(1, dk, none)
     dn = dot(jnp.concatenate([dq, dk, dv], axis=1), wh, 1, 1)
     gg = two_rows(jnp.sum(dn * scaled_ref[...], axis=0, keepdims=True))
     gg = jnp.concatenate([gg[0:2, i * 128 : i * 128 + 128] for i in range(4)], axis=0)
-    leave_columns(1, dk, gg)
     leave_columns(0, dq, gg)
     keep_ref[...] = jnp.concatenate([dn[0:64], dn[128:192]], axis=0)
     send_ref[...] = jnp.concatenate([dn[64:128], dn[192:]], axis=0).astype(BF)

time: 133 us -> 133 us (level)
  no operation moved by 1% of the time
where the time goes in v13:
time: 133 us; the launch traced here: 132 us
  blocking collectives  56.4 us (42%)
  starting transfers between devices  35.2 us (26%)
  waiting for transfers between devices  29.9 us (22%)
  Pallas kernels  10.1 us (8%)
    all_to_all x2, blocking collectives, exchange(): return lax.all_to_all(arr, axes, split_axis=0, concat_axis=0, tiled=True)  56.4 us
    all_to_all x3, waiting for transfers between devices, exchange(): return lax.all_to_all(arr, axes, split_axis=0, concat_axis=0, tiled=True)  19.5 us
    all_to_all x3, starting transfers between devices, exchange(): return lax.all_to_all(arr, axes, split_axis=0, concat_axis=0, tiled=True)  12.8 us
    ppermute x3, starting transfers between devices, to_y(): return lax.ppermute(block, 'y', [(i, i ^ k) for i in range(Y)])  9.81 us
    ppermute x1, starting transfers between devices, on_device(): last_far = lax.ppermute(last, 'zh', SWAP)  8.21 us
    pallas_call x10, Pallas kernels, call(): pl.pallas_call(body, out_shape=[jax.ShapeDtypeStruct(shape, kind) for sha...  8.11 us
    ppermute x3, waiting for transfers between devices, to_y(): return lax.ppermute(block, 'y', [(i, i ^ k) for i in range(Y)])  4.81 us
    ppermute x1, waiting for transfers between devices, on_device(): last_far = lax.ppermute(last, 'zh', SWAP)  3.31 us
  transfers between devices with their start and end apart: 9, of which 8 were waited for; matrix products, arithmetic and copies ran while one was open for 0% of the time, Pallas kernels for 2%

profile of v13, /device:TPU:32, one launch (start us, length us, event | category | flops | bytes accessed | tf_op | source)
XLA Modules:
  0.0 132.4 jit_solution(14931257529076853819)
XLA Ops:
  0.6 2.0 %shard_map.84 = bf16[256,640]{1,0:T(8,128)(2,1)} custom-call(bf16[128,512]{1,0:T(8,128)(2,1)} %bitcast.20, bf16[128,512]{1,0:T(8,128)(2,1)} %bitcast.21, bf16[8,1536]{1,0:T(8,128)(2,1)} %wq_ref.1, bf16[8,512]{1,0:T(8,128)(2,1)} %wo_ref.1), custom_call_target="tpu_custom_call" | custom-call | tf_op jit(solution)/shard_map/pallas_call | solution.py:361
  2.6 36.0 %all_to_all.25 = bf16[32,8,640]{2,1,0:T(8,128)(2,1)S(1)} all-to-all(bf16[32,8,640]{2,1,0:T(8,128)(2,1)} %bitcast.19), channel_id=1, replica_groups=mesh['zh'=2,'x'=4,'zl'=8,'y'=4,'c'=2] {'zl','y'}, dimensions={0} | all-to-all | bytes 655360 | tf_op jit(solution)/shard_map/all_to_all | solution.py:18
  38.6 1.2 shard_map.87
  39.8 0.0 copy-start
  39.8 5.5 %all-to-all-start.1 = ((bf16[32,128,128]{2,1,0:T(8,128)(2,1)}), bf16[32,128,128]{2,1,0:T(8,128)(2,1)S(1)}, u32[]{:S(2)}, u32[]{:S(2)}) async-start(bf16[32,128,128]{2,1,0:T(8,128)(2,1)} %shard_map.87), calls=%async_computation.1 | async-start | bytes 2097152 | tf_op jit(solution)/shard_map/all_to_all | solution.py:18
  45.3 0.2 shard_map.85.own_ref
  45.5 2.2 %collective-permute-start = (bf16[256,512]{1,0:T(8,128)(2,1)S(1)}, bf16[256,512]{1,0:T(8,128)(2,1)S(1)}, u32[]{:S(2)}, u32[]{:S(2)}) collective-permute-start(bf16[256,512]{1,0:T(8,128)(2,1)S(1)} %shard_map.85.own_ref), channel_id=1, source_target_pairs={{0,1},{1,0},{2,3},{3,2},{4,5},{5,4},{6,7},{7,6},{8,9},{9,8},{10,11... | collective-permute-start | bytes 786440 | tf_op jit(solution)/shard_map/ppermute | solution.py:384
  47.7 1.2 collective-permute-done.far_ref
  49.0 0.3 shard_map.86
  49.3 12.9 %all-to-all-done.1.w_ref = bf16[32,128,128]{2,1,0:T(8,128)(2,1)S(1)} async-done(((bf16[32,128,128]{2,1,0:T(8,128)(2,1)}), bf16[32,128,128]{2,1,0:T(8,128)(2,1)S(1)}, u32[]{:S(2)}, u32[]{:S(2)}) %all-to-all-start.1) | async-done | bytes 1048608 | tf_op jit(solution)/shard_map/all_to_all | solution.py:18
  62.1 3.5 %shard_map.88 = (bf16[32,136,128]{2,1,0:T(8,128)(2,1)}, bf16[128,512]{1,0:T(8,128)(2,1)S(1)}, f32[128,512]{1,0:T(8,128)S(1)}) custom-call(f32[256,512]{1,0:T(8,128)S(1)} %get-tuple-element.17.scaled_ref, bf16[256,512]{1,0:T(8,128)(2,1)S(1)} %get-tuple-element.18.normed_ref, bf16[512,256]{1,0:T(8,128)(2,1)S(1)} %get-tuple-element.19.flipped_ref, ...), custom_call_target="tpu_custom_call" | custom-call | tf_op jit(solution)/shard_map/pallas_call | solution.py:30
  65.6 4.1 %all-to-all-start.2 = ((bf16[32,136,128]{2,1,0:T(8,128)(2,1)}), bf16[32,136,128]{2,1,0:T(8,128)(2,1)S(1)}, u32[]{:S(2)}, u32[]{:S(2)}) async-start(bf16[32,136,128]{2,1,0:T(8,128)(2,1)} %get-tuple-element.21), calls=%async_computation.2 | async-start | bytes 2228224 | tf_op jit(solution)/shard_map/all_to_all | solution.py:18
  69.7 2.2 %collective-permute-start.1 = (bf16[128,512]{1,0:T(8,128)(2,1)S(1)}, bf16[128,512]{1,0:T(8,128)(2,1)S(1)}, u32[]{:S(2)}, u32[]{:S(2)}) collective-permute-start(bf16[128,512]{1,0:T(8,128)(2,1)S(1)} %get-tuple-element.23), channel_id=1, source_target_pairs={{0,1},{1,0},{2,3},{3,2},{4,5},{5,4},{6,7},{7,6},{8,9},{9,8},{10,11... | collective-permute-start | bytes 393224 | tf_op jit(solution)/shard_map/ppermute | solution.py:398
  71.9 1.1 collective-permute-done.1.far_ref
  72.9 0.4 shard_map.89.hop_ref
  73.3 4.9 %collective-permute-start.3 = (bf16[32,512]{1,0:T(8,128)(2,1)S(1)}, bf16[32,512]{1,0:T(8,128)(2,1)S(1)}, u32[]{:S(2)}, u32[]{:S(2)}) collective-permute-start(bf16[32,512]{1,0:T(8,128)(2,1)S(1)} %get-tuple-element.30), channel_id=1, source_target_pairs={{0,6},{2,4},{4,2},{6,0},{1,7},{3,5},{5,3},{7,1},{8,14},{10,12},{12... | collective-permute-start | bytes 98312 | tf_op jit(solution)/shard_map/ppermute | solution.py:22
  78.3 2.2 %collective-permute-start.2 = (bf16[32,512]{1,0:T(8,128)(2,1)S(1)}, bf16[32,512]{1,0:T(8,128)(2,1)S(1)}, u32[]{:S(2)}, u32[]{:S(2)}) collective-permute-start(bf16[32,512]{1,0:T(8,128)(2,1)S(1)} %get-tuple-element.31), channel_id=1, source_target_pairs={{0,2},{2,0},{4,6},{6,4},{1,3},{3,1},{5,7},{7,5},{8,10},{10,8},{12,... | collective-permute-start | bytes 98312 | tf_op jit(solution)/shard_map/ppermute | solution.py:22
  80.4 2.1 %collective-permute-done.3.b3_ref = bf16[32,512]{1,0:T(8,128)(2,1)S(1)} collective-permute-done((bf16[32,512]{1,0:T(8,128)(2,1)S(1)}, bf16[32,512]{1,0:T(8,128)(2,1)S(1)}, u32[]{:S(2)}, u32[]{:S(2)}) %collective-permute-start.3) | collective-permute-done | bytes 32800 | tf_op jit(solution)/shard_map/ppermute | solution.py:22
  82.6 2.7 %collective-permute-done.2.b1_ref = bf16[32,512]{1,0:T(8,128)(2,1)S(1)} collective-permute-done((bf16[32,512]{1,0:T(8,128)(2,1)S(1)}, bf16[32,512]{1,0:T(8,128)(2,1)S(1)}, u32[]{:S(2)}, u32[]{:S(2)}) %collective-permute-start.2) | collective-permute-done | bytes 32800 | tf_op jit(solution)/shard_map/ppermute | solution.py:22
  85.2 2.0 %all-to-all-done.2.got_ref = bf16[32,136,128]{2,1,0:T(8,128)(2,1)S(1)} async-done(((bf16[32,136,128]{2,1,0:T(8,128)(2,1)}), bf16[32,136,128]{2,1,0:T(8,128)(2,1)S(1)}, u32[]{:S(2)}, u32[]{:S(2)}) %all-to-all-start.2) | async-done | bytes 1114144 | tf_op jit(solution)/shard_map/all_to_all | solution.py:18
  87.3 0.3 shard_map.90
  87.5 20.4 %all_to_all.26 = bf16[8,8,1664]{2,1,0:T(8,128)(2,1)S(1)} all-to-all(bf16[8,8,1664]{2,1,0:T(8,128)(2,1)S(1)} %bitcast.15), channel_id=1, replica_groups=mesh['zh'=2,'x'=4,'zl'=8,'y'=4,'c'=2] {'zl'}, dimensions={0} | all-to-all | bytes 425984 | tf_op jit(solution)/shard_map/all_to_all | solution.py:18
  107.9 0.2 shard_map.91
  108.1 8.2 %collective-permute-start.5 = (bf16[8,640]{1,0:T(8,128)(2,1)S(1)}, bf16[8,640]{1,0:T(8,128)(2,1)S(1)}, u32[]{:S(2)}, u32[]{:S(2)}) collective-permute-start(bf16[8,640]{1,0:T(8,128)(2,1)S(1)} %get-tuple-element.26.last_ref), channel_id=1, source_target_pairs={{0,256},{256,0},{1,257},{257,1},{2,258},{258,2},{3,259},{259,3},{4... | collective-permute-start | bytes 30728 | tf_op jit(solution)/shard_map/ppermute | solution.py:405
  116.3 2.7 %collective-permute-start.4 = (bf16[32,512]{1,0:T(8,128)(2,1)S(1)}, bf16[32,512]{1,0:T(8,128)(2,1)S(1)}, u32[]{:S(2)}, u32[]{:S(2)}) collective-permute-start(bf16[32,512]{1,0:T(8,128)(2,1)S(1)} %get-tuple-element.25), channel_id=1, source_target_pairs={{0,4},{2,6},{4,0},{6,2},{1,5},{3,7},{5,1},{7,3},{8,12},{10,14},{12... | collective-permute-start | bytes 98312 | tf_op jit(solution)/shard_map/ppermute | solution.py:22
  119.1 3.3 %collective-permute-done.5.far_ref = bf16[8,640]{1,0:T(8,128)(2,1)S(1)} collective-permute-done((bf16[8,640]{1,0:T(8,128)(2,1)S(1)}, bf16[8,640]{1,0:T(8,128)(2,1)S(1)}, u32[]{:S(2)}, u32[]{:S(2)}) %collective-permute-start.5) | collective-permute-done | bytes 10272 | tf_op jit(solution)/shard_map/ppermute | solution.py:405
  122.4 0.6 shard_map.93
  123.0 3.3 %all-to-all-start.4 = ((bf16[4,8,640]{2,1,0:T(8,128)(2,1)}), bf16[4,8,640]{2,1,0:T(8,128)(2,1)S(1)}, u32[]{:S(2)}, u32[]{:S(2)}) async-start(bf16[4,8,640]{2,1,0:T(8,128)(2,1)} %shard_map.93), calls=%async_computation.4 | async-start | bytes 81920 | tf_op jit(solution)/shard_map/all_to_all | solution.py:18
  126.3 0.0 collective-permute-done.4.two_ref
  126.3 0.8 shard_map.92
  127.1 4.6 %all-to-all-done.4.got_ref = bf16[4,8,640]{2,1,0:T(8,128)(2,1)S(1)} async-done(((bf16[4,8,640]{2,1,0:T(8,128)(2,1)}), bf16[4,8,640]{2,1,0:T(8,128)(2,1)S(1)}, u32[]{:S(2)}, u32[]{:S(2)}) %all-to-all-start.4) | async-done | bytes 40992 | tf_op jit(solution)/shard_map/all_to_all | solution.py:18
  131.7 0.6 shard_map.94
  (2 shorter events, 0.0 us)
Async XLA Ops:
  39.8 9.2 %copy-start = (f32[512]{0:T(512)S(1)}, f32[512]{0:T(512)}, u32[]{:S(2)}) copy-start(f32[512]{0:T(512)} %param.7) | copy-start | bytes 6148
  39.8 22.3 %all-to-all-start.1 = ((bf16[32,128,128]{2,1,0:T(8,128)(2,1)}), bf16[32,128,128]{2,1,0:T(8,128)(2,1)S(1)}, u32[]{:S(2)}, u32[]{:S(2)}) async-start(bf16[32,128,128]{2,1,0:T(8,128)(2,1)} %shard_map.87), calls=%async_computation.1 | async-start | bytes 2097152 | tf_op jit(solution)/shard_map/all_to_all | solution.py:18
  45.5 3.4 %collective-permute-start = (bf16[256,512]{1,0:T(8,128)(2,1)S(1)}, bf16[256,512]{1,0:T(8,128)(2,1)S(1)}, u32[]{:S(2)}, u32[]{:S(2)}) collective-permute-start(bf16[256,512]{1,0:T(8,128)(2,1)S(1)} %shard_map.85.own_ref), channel_id=1, source_target_pairs={{0,1},{1,0},{2,3},{3,2},{4,5},{5,4},{6,7},{7,6},{8,9},{9,8},{10,11... | collective-permute-start | bytes 786440 | tf_op jit(solution)/shard_map/ppermute | solution.py:384
  65.6 21.7 %all-to-all-start.2 = ((bf16[32,136,128]{2,1,0:T(8,128)(2,1)}), bf16[32,136,128]{2,1,0:T(8,128)(2,1)S(1)}, u32[]{:S(2)}, u32[]{:S(2)}) async-start(bf16[32,136,128]{2,1,0:T(8,128)(2,1)} %get-tuple-element.21), calls=%async_computation.2 | async-start | bytes 2228224 | tf_op jit(solution)/shard_map/all_to_all | solution.py:18
  69.7 3.2 %collective-permute-start.1 = (bf16[128,512]{1,0:T(8,128)(2,1)S(1)}, bf16[128,512]{1,0:T(8,128)(2,1)S(1)}, u32[]{:S(2)}, u32[]{:S(2)}) collective-permute-start(bf16[128,512]{1,0:T(8,128)(2,1)S(1)} %get-tuple-element.23), channel_id=1, source_target_pairs={{0,1},{1,0},{2,3},{3,2},{4,5},{5,4},{6,7},{7,6},{8,9},{9,8},{10,11... | collective-permute-start | bytes 393224 | tf_op jit(solution)/shard_map/ppermute | solution.py:398
  73.3 9.2 %collective-permute-start.3 = (bf16[32,512]{1,0:T(8,128)(2,1)S(1)}, bf16[32,512]{1,0:T(8,128)(2,1)S(1)}, u32[]{:S(2)}, u32[]{:S(2)}) collective-permute-start(bf16[32,512]{1,0:T(8,128)(2,1)S(1)} %get-tuple-element.30), channel_id=1, source_target_pairs={{0,6},{2,4},{4,2},{6,0},{1,7},{3,5},{5,3},{7,1},{8,14},{10,12},{12... | collective-permute-start | bytes 98312 | tf_op jit(solution)/shard_map/ppermute | solution.py:22
  78.3 7.0 %collective-permute-start.2 = (bf16[32,512]{1,0:T(8,128)(2,1)S(1)}, bf16[32,512]{1,0:T(8,128)(2,1)S(1)}, u32[]{:S(2)}, u32[]{:S(2)}) collective-permute-start(bf16[32,512]{1,0:T(8,128)(2,1)S(1)} %get-tuple-element.31), channel_id=1, source_target_pairs={{0,2},{2,0},{4,6},{6,4},{1,3},{3,1},{5,7},{7,5},{8,10},{10,8},{12,... | collective-permute-start | bytes 98312 | tf_op jit(solution)/shard_map/ppermute | solution.py:22
  108.1 14.3 %collective-permute-start.5 = (bf16[8,640]{1,0:T(8,128)(2,1)S(1)}, bf16[8,640]{1,0:T(8,128)(2,1)S(1)}, u32[]{:S(2)}, u32[]{:S(2)}) collective-permute-start(bf16[8,640]{1,0:T(8,128)(2,1)S(1)} %get-tuple-element.26.last_ref), channel_id=1, source_target_pairs={{0,256},{256,0},{1,257},{257,1},{2,258},{258,2},{3,259},{259,3},{4... | collective-permute-start | bytes 30728 | tf_op jit(solution)/shard_map/ppermute | solution.py:405
  116.3 10.0 %collective-permute-start.4 = (bf16[32,512]{1,0:T(8,128)(2,1)S(1)}, bf16[32,512]{1,0:T(8,128)(2,1)S(1)}, u32[]{:S(2)}, u32[]{:S(2)}) collective-permute-start(bf16[32,512]{1,0:T(8,128)(2,1)S(1)} %get-tuple-element.25), channel_id=1, source_target_pairs={{0,4},{2,6},{4,0},{6,2},{1,5},{3,7},{5,1},{7,3},{8,12},{10,14},{12... | collective-permute-start | bytes 98312 | tf_op jit(solution)/shard_map/ppermute | solution.py:22
  123.0 8.7 %all-to-all-start.4 = ((bf16[4,8,640]{2,1,0:T(8,128)(2,1)}), bf16[4,8,640]{2,1,0:T(8,128)(2,1)S(1)}, u32[]{:S(2)}, u32[]{:S(2)}) async-start(bf16[4,8,640]{2,1,0:T(8,128)(2,1)} %shard_map.93), calls=%async_computation.4 | async-start | bytes 81920 | tf_op jit(solution)/shard_map/all_to_all | solution.py:18

commit v14 on v13

--- a/solution.py
+++ b/solution.py
@@ -88,17 +88,17 @@
     (low0, low1), (high0, high1) = halves(block[:128]), halves(block[128:])
     planes = block.reshape(4, 2, 32, 128)
     outs = x_is_last()
+    copies = []
     for core, cols in ((0, (low0, high0)), (1, (low1, high1))):
         mine = jnp.where(
             outs, planes[:, core].reshape(128, 128), jnp.concatenate(cols, axis=1)
         ).astype(BF)
         pair_vm[core] = mine
-    copies = [
-        pltpu.make_async_copy(pair_vm, sent_ref.at[2 * xy : 2 * xy + 2], sems.at[xy])
-        for xy in range(X * Y)
-    ]
-    for copy in copies:
-        copy.start()
+        for xy in range(X * Y):
+            at = 2 * xy + core
+            copy = pltpu.make_async_copy(pair_vm.at[core], sent_ref.at[at], sems.at[at])
+            copy.start()
+            copies.append(copy)
     for copy in copies:
         copy.wait()
 
@@ -377,7 +377,7 @@
         [((32, 128, 128), BF)],
         moved,
         first_in_hbm=True,
-        scratch=[pltpu.VMEM((2, 128, 128), BF), pltpu.SemaphoreType.DMA((X * Y,))],
+        scratch=[pltpu.VMEM((2, 128, 128), BF), pltpu.SemaphoreType.DMA((2 * X * Y,))],
     )
     weights = exchange(sent, plane)
     [own] = call(rows_body, [((256, 512), BF)], moved)

time: 133 us -> 133 us (level)
  no operation moved by 1% of the time
where the time goes in v14:
time: 133 us; the launch traced here: 132 us
  blocking collectives  56.4 us (42%)
  starting transfers between devices  35.2 us (26%)
  waiting for transfers between devices  29.9 us (22%)
  Pallas kernels  10.2 us (8%)
    all_to_all x2, blocking collectives, exchange(): return lax.all_to_all(arr, axes, split_axis=0, concat_axis=0, tiled=True)  56.4 us
    all_to_all x3, waiting for transfers between devices, exchange(): return lax.all_to_all(arr, axes, split_axis=0, concat_axis=0, tiled=True)  19.5 us
    all_to_all x3, starting transfers between devices, exchange(): return lax.all_to_all(arr, axes, split_axis=0, concat_axis=0, tiled=True)  12.8 us
    ppermute x3, starting transfers between devices, to_y(): return lax.ppermute(block, 'y', [(i, i ^ k) for i in range(Y)])  9.81 us
    pallas_call x10, Pallas kernels, call(): pl.pallas_call(body, out_shape=[jax.ShapeDtypeStruct(shape, kind) for sha...  8.23 us
    ppermute x1, starting transfers between devices, on_device(): last_far = lax.ppermute(last, 'zh', SWAP)  8.21 us
    ppermute x3, waiting for transfers between devices, to_y(): return lax.ppermute(block, 'y', [(i, i ^ k) for i in range(Y)])  4.81 us
    ppermute x1, waiting for transfers between devices, on_device(): last_far = lax.ppermute(last, 'zh', SWAP)  3.31 us
  transfers between devices with their start and end apart: 9, of which 8 were waited for; matrix products, arithmetic and copies ran while one was open for 0% of the time, Pallas kernels for 2%

profile of v14, /device:TPU:32, one launch (start us, length us, event | category | flops | bytes accessed | tf_op | source)
XLA Modules:
  0.0 132.5 jit_solution(8401475430608255288)
XLA Ops:
  0.6 2.0 %shard_map.84 = bf16[256,640]{1,0:T(8,128)(2,1)} custom-call(bf16[128,512]{1,0:T(8,128)(2,1)} %bitcast.20, bf16[128,512]{1,0:T(8,128)(2,1)} %bitcast.21, bf16[8,1536]{1,0:T(8,128)(2,1)} %wq_ref.1, bf16[8,512]{1,0:T(8,128)(2,1)} %wo_ref.1), custom_call_target="tpu_custom_call" | custom-call | tf_op jit(solution)/shard_map/pallas_call | solution.py:361
  2.6 36.0 %all_to_all.25 = bf16[32,8,640]{2,1,0:T(8,128)(2,1)S(1)} all-to-all(bf16[32,8,640]{2,1,0:T(8,128)(2,1)} %bitcast.19), channel_id=1, replica_groups=mesh['zh'=2,'x'=4,'zl'=8,'y'=4,'c'=2] {'zl','y'}, dimensions={0} | all-to-all | bytes 655360 | tf_op jit(solution)/shard_map/all_to_all | solution.py:18
  38.6 1.3 %shard_map.87 = bf16[32,128,128]{2,1,0:T(8,128)(2,1)} custom-call(bf16[256,640]{1,0:T(8,128)(2,1)S(1)} %bitcast.13), custom_call_target="tpu_custom_call" | custom-call | tf_op jit(solution)/shard_map/pallas_call | solution.py:30
  39.9 0.0 copy-start
  40.0 5.5 %all-to-all-start.1 = ((bf16[32,128,128]{2,1,0:T(8,128)(2,1)}), bf16[32,128,128]{2,1,0:T(8,128)(2,1)S(1)}, u32[]{:S(2)}, u32[]{:S(2)}) async-start(bf16[32,128,128]{2,1,0:T(8,128)(2,1)} %shard_map.87), calls=%async_computation.1 | async-start | bytes 2097152 | tf_op jit(solution)/shard_map/all_to_all | solution.py:18
  45.4 0.2 shard_map.85.own_ref
  45.7 2.2 %collective-permute-start = (bf16[256,512]{1,0:T(8,128)(2,1)S(1)}, bf16[256,512]{1,0:T(8,128)(2,1)S(1)}, u32[]{:S(2)}, u32[]{:S(2)}) collective-permute-start(bf16[256,512]{1,0:T(8,128)(2,1)S(1)} %shard_map.85.own_ref), channel_id=1, source_target_pairs={{0,1},{1,0},{2,3},{3,2},{4,5},{5,4},{6,7},{7,6},{8,9},{9,8},{10,11... | collective-permute-start | bytes 786440 | tf_op jit(solution)/shard_map/ppermute | solution.py:384
  47.9 1.2 collective-permute-done.far_ref
  49.1 0.3 shard_map.86
  49.4 12.9 %all-to-all-done.1.w_ref = bf16[32,128,128]{2,1,0:T(8,128)(2,1)S(1)} async-done(((bf16[32,128,128]{2,1,0:T(8,128)(2,1)}), bf16[32,128,128]{2,1,0:T(8,128)(2,1)S(1)}, u32[]{:S(2)}, u32[]{:S(2)}) %all-to-all-start.1) | async-done | bytes 1048608 | tf_op jit(solution)/shard_map/all_to_all | solution.py:18
  62.3 3.5 %shard_map.88 = (bf16[32,136,128]{2,1,0:T(8,128)(2,1)}, bf16[128,512]{1,0:T(8,128)(2,1)S(1)}, f32[128,512]{1,0:T(8,128)S(1)}) custom-call(f32[256,512]{1,0:T(8,128)S(1)} %get-tuple-element.17.scaled_ref, bf16[256,512]{1,0:T(8,128)(2,1)S(1)} %get-tuple-element.18.normed_ref, bf16[512,256]{1,0:T(8,128)(2,1)S(1)} %get-tuple-element.19.flipped_ref, ...), custom_call_target="tpu_custom_call" | custom-call | tf_op jit(solution)/shard_map/pallas_call | solution.py:30
  65.8 4.1 %all-to-all-start.2 = ((bf16[32,136,128]{2,1,0:T(8,128)(2,1)}), bf16[32,136,128]{2,1,0:T(8,128)(2,1)S(1)}, u32[]{:S(2)}, u32[]{:S(2)}) async-start(bf16[32,136,128]{2,1,0:T(8,128)(2,1)} %get-tuple-element.21), calls=%async_computation.2 | async-start | bytes 2228224 | tf_op jit(solution)/shard_map/all_to_all | solution.py:18
  69.8 2.2 %collective-permute-start.1 = (bf16[128,512]{1,0:T(8,128)(2,1)S(1)}, bf16[128,512]{1,0:T(8,128)(2,1)S(1)}, u32[]{:S(2)}, u32[]{:S(2)}) collective-permute-start(bf16[128,512]{1,0:T(8,128)(2,1)S(1)} %get-tuple-element.23), channel_id=1, source_target_pairs={{0,1},{1,0},{2,3},{3,2},{4,5},{5,4},{6,7},{7,6},{8,9},{9,8},{10,11... | collective-permute-start | bytes 393224 | tf_op jit(solution)/shard_map/ppermute | solution.py:398
  72.0 1.1 collective-permute-done.1.far_ref
  73.1 0.4 shard_map.89.hop_ref
  73.5 4.9 %collective-permute-start.3 = (bf16[32,512]{1,0:T(8,128)(2,1)S(1)}, bf16[32,512]{1,0:T(8,128)(2,1)S(1)}, u32[]{:S(2)}, u32[]{:S(2)}) collective-permute-start(bf16[32,512]{1,0:T(8,128)(2,1)S(1)} %get-tuple-element.30), channel_id=1, source_target_pairs={{0,6},{2,4},{4,2},{6,0},{1,7},{3,5},{5,3},{7,1},{8,14},{10,12},{12... | collective-permute-start | bytes 98312 | tf_op jit(solution)/shard_map/ppermute | solution.py:22
  78.4 2.2 %collective-permute-start.2 = (bf16[32,512]{1,0:T(8,128)(2,1)S(1)}, bf16[32,512]{1,0:T(8,128)(2,1)S(1)}, u32[]{:S(2)}, u32[]{:S(2)}) collective-permute-start(bf16[32,512]{1,0:T(8,128)(2,1)S(1)} %get-tuple-element.31), channel_id=1, source_target_pairs={{0,2},{2,0},{4,6},{6,4},{1,3},{3,1},{5,7},{7,5},{8,10},{10,8},{12,... | collective-permute-start | bytes 98312 | tf_op jit(solution)/shard_map/ppermute | solution.py:22
  80.6 2.1 %collective-permute-done.3.b3_ref = bf16[32,512]{1,0:T(8,128)(2,1)S(1)} collective-permute-done((bf16[32,512]{1,0:T(8,128)(2,1)S(1)}, bf16[32,512]{1,0:T(8,128)(2,1)S(1)}, u32[]{:S(2)}, u32[]{:S(2)}) %collective-permute-start.3) | collective-permute-done | bytes 32800 | tf_op jit(solution)/shard_map/ppermute | solution.py:22
  82.7 2.7 %collective-permute-done.2.b1_ref = bf16[32,512]{1,0:T(8,128)(2,1)S(1)} collective-permute-done((bf16[32,512]{1,0:T(8,128)(2,1)S(1)}, bf16[32,512]{1,0:T(8,128)(2,1)S(1)}, u32[]{:S(2)}, u32[]{:S(2)}) %collective-permute-start.2) | collective-permute-done | bytes 32800 | tf_op jit(solution)/shard_map/ppermute | solution.py:22
  85.4 2.0 %all-to-all-done.2.got_ref = bf16[32,136,128]{2,1,0:T(8,128)(2,1)S(1)} async-done(((bf16[32,136,128]{2,1,0:T(8,128)(2,1)}), bf16[32,136,128]{2,1,0:T(8,128)(2,1)S(1)}, u32[]{:S(2)}, u32[]{:S(2)}) %all-to-all-start.2) | async-done | bytes 1114144 | tf_op jit(solution)/shard_map/all_to_all | solution.py:18
  87.4 0.3 shard_map.90
  87.7 20.4 %all_to_all.26 = bf16[8,8,1664]{2,1,0:T(8,128)(2,1)S(1)} all-to-all(bf16[8,8,1664]{2,1,0:T(8,128)(2,1)S(1)} %bitcast.15), channel_id=1, replica_groups=mesh['zh'=2,'x'=4,'zl'=8,'y'=4,'c'=2] {'zl'}, dimensions={0} | all-to-all | bytes 425984 | tf_op jit(solution)/shard_map/all_to_all | solution.py:18
  108.1 0.2 shard_map.91
  108.2 8.2 %collective-permute-start.5 = (bf16[8,640]{1,0:T(8,128)(2,1)S(1)}, bf16[8,640]{1,0:T(8,128)(2,1)S(1)}, u32[]{:S(2)}, u32[]{:S(2)}) collective-permute-start(bf16[8,640]{1,0:T(8,128)(2,1)S(1)} %get-tuple-element.26.last_ref), channel_id=1, source_target_pairs={{0,256},{256,0},{1,257},{257,1},{2,258},{258,2},{3,259},{259,3},{4... | collective-permute-start | bytes 30728 | tf_op jit(solution)/shard_map/ppermute | solution.py:405
  116.4 2.7 %collective-permute-start.4 = (bf16[32,512]{1,0:T(8,128)(2,1)S(1)}, bf16[32,512]{1,0:T(8,128)(2,1)S(1)}, u32[]{:S(2)}, u32[]{:S(2)}) collective-permute-start(bf16[32,512]{1,0:T(8,128)(2,1)S(1)} %get-tuple-element.25), channel_id=1, source_target_pairs={{0,4},{2,6},{4,0},{6,2},{1,5},{3,7},{5,1},{7,3},{8,12},{10,14},{12... | collective-permute-start | bytes 98312 | tf_op jit(solution)/shard_map/ppermute | solution.py:22
  119.2 3.3 %collective-permute-done.5.far_ref = bf16[8,640]{1,0:T(8,128)(2,1)S(1)} collective-permute-done((bf16[8,640]{1,0:T(8,128)(2,1)S(1)}, bf16[8,640]{1,0:T(8,128)(2,1)S(1)}, u32[]{:S(2)}, u32[]{:S(2)}) %collective-permute-start.5) | collective-permute-done | bytes 10272 | tf_op jit(solution)/shard_map/ppermute | solution.py:405
  122.5 0.6 shard_map.93
  123.1 3.3 %all-to-all-start.4 = ((bf16[4,8,640]{2,1,0:T(8,128)(2,1)}), bf16[4,8,640]{2,1,0:T(8,128)(2,1)S(1)}, u32[]{:S(2)}, u32[]{:S(2)}) async-start(bf16[4,8,640]{2,1,0:T(8,128)(2,1)} %shard_map.93), calls=%async_computation.4 | async-start | bytes 81920 | tf_op jit(solution)/shard_map/all_to_all | solution.py:18
  126.4 0.0 collective-permute-done.4.two_ref
  126.4 0.8 shard_map.92
  127.2 4.6 %all-to-all-done.4.got_ref = bf16[4,8,640]{2,1,0:T(8,128)(2,1)S(1)} async-done(((bf16[4,8,640]{2,1,0:T(8,128)(2,1)}), bf16[4,8,640]{2,1,0:T(8,128)(2,1)S(1)}, u32[]{:S(2)}, u32[]{:S(2)}) %all-to-all-start.4) | async-done | bytes 40992 | tf_op jit(solution)/shard_map/all_to_all | solution.py:18
  131.9 0.6 shard_map.94
  (2 shorter events, 0.0 us)
Async XLA Ops:
  39.9 9.2 %copy-start = (f32[512]{0:T(512)S(1)}, f32[512]{0:T(512)}, u32[]{:S(2)}) copy-start(f32[512]{0:T(512)} %param.7) | copy-start | bytes 6148
  40.0 22.3 %all-to-all-start.1 = ((bf16[32,128,128]{2,1,0:T(8,128)(2,1)}), bf16[32,128,128]{2,1,0:T(8,128)(2,1)S(1)}, u32[]{:S(2)}, u32[]{:S(2)}) async-start(bf16[32,128,128]{2,1,0:T(8,128)(2,1)} %shard_map.87), calls=%async_computation.1 | async-start | bytes 2097152 | tf_op jit(solution)/shard_map/all_to_all | solution.py:18
  45.7 3.4 %collective-permute-start = (bf16[256,512]{1,0:T(8,128)(2,1)S(1)}, bf16[256,512]{1,0:T(8,128)(2,1)S(1)}, u32[]{:S(2)}, u32[]{:S(2)}) collective-permute-start(bf16[256,512]{1,0:T(8,128)(2,1)S(1)} %shard_map.85.own_ref), channel_id=1, source_target_pairs={{0,1},{1,0},{2,3},{3,2},{4,5},{5,4},{6,7},{7,6},{8,9},{9,8},{10,11... | collective-permute-start | bytes 786440 | tf_op jit(solution)/shard_map/ppermute | solution.py:384
  65.8 21.7 %all-to-all-start.2 = ((bf16[32,136,128]{2,1,0:T(8,128)(2,1)}), bf16[32,136,128]{2,1,0:T(8,128)(2,1)S(1)}, u32[]{:S(2)}, u32[]{:S(2)}) async-start(bf16[32,136,128]{2,1,0:T(8,128)(2,1)} %get-tuple-element.21), calls=%async_computation.2 | async-start | bytes 2228224 | tf_op jit(solution)/shard_map/all_to_all | solution.py:18
  69.8 3.2 %collective-permute-start.1 = (bf16[128,512]{1,0:T(8,128)(2,1)S(1)}, bf16[128,512]{1,0:T(8,128)(2,1)S(1)}, u32[]{:S(2)}, u32[]{:S(2)}) collective-permute-start(bf16[128,512]{1,0:T(8,128)(2,1)S(1)} %get-tuple-element.23), channel_id=1, source_target_pairs={{0,1},{1,0},{2,3},{3,2},{4,5},{5,4},{6,7},{7,6},{8,9},{9,8},{10,11... | collective-permute-start | bytes 393224 | tf_op jit(solution)/shard_map/ppermute | solution.py:398
  73.5 9.2 %collective-permute-start.3 = (bf16[32,512]{1,0:T(8,128)(2,1)S(1)}, bf16[32,512]{1,0:T(8,128)(2,1)S(1)}, u32[]{:S(2)}, u32[]{:S(2)}) collective-permute-start(bf16[32,512]{1,0:T(8,128)(2,1)S(1)} %get-tuple-element.30), channel_id=1, source_target_pairs={{0,6},{2,4},{4,2},{6,0},{1,7},{3,5},{5,3},{7,1},{8,14},{10,12},{12... | collective-permute-start | bytes 98312 | tf_op jit(solution)/shard_map/ppermute | solution.py:22
  78.4 7.0 %collective-permute-start.2 = (bf16[32,512]{1,0:T(8,128)(2,1)S(1)}, bf16[32,512]{1,0:T(8,128)(2,1)S(1)}, u32[]{:S(2)}, u32[]{:S(2)}) collective-permute-start(bf16[32,512]{1,0:T(8,128)(2,1)S(1)} %get-tuple-element.31), channel_id=1, source_target_pairs={{0,2},{2,0},{4,6},{6,4},{1,3},{3,1},{5,7},{7,5},{8,10},{10,8},{12,... | collective-permute-start | bytes 98312 | tf_op jit(solution)/shard_map/ppermute | solution.py:22
  108.2 14.3 %collective-permute-start.5 = (bf16[8,640]{1,0:T(8,128)(2,1)S(1)}, bf16[8,640]{1,0:T(8,128)(2,1)S(1)}, u32[]{:S(2)}, u32[]{:S(2)}) collective-permute-start(bf16[8,640]{1,0:T(8,128)(2,1)S(1)} %get-tuple-element.26.last_ref), channel_id=1, source_target_pairs={{0,256},{256,0},{1,257},{257,1},{2,258},{258,2},{3,259},{259,3},{4... | collective-permute-start | bytes 30728 | tf_op jit(solution)/shard_map/ppermute | solution.py:405
  116.4 10.0 %collective-permute-start.4 = (bf16[32,512]{1,0:T(8,128)(2,1)S(1)}, bf16[32,512]{1,0:T(8,128)(2,1)S(1)}, u32[]{:S(2)}, u32[]{:S(2)}) collective-permute-start(bf16[32,512]{1,0:T(8,128)(2,1)S(1)} %get-tuple-element.25), channel_id=1, source_target_pairs={{0,4},{2,6},{4,0},{6,2},{1,5},{3,7},{5,1},{7,3},{8,12},{10,14},{12... | collective-permute-start | bytes 98312 | tf_op jit(solution)/shard_map/ppermute | solution.py:22
  123.1 8.7 %all-to-all-start.4 = ((bf16[4,8,640]{2,1,0:T(8,128)(2,1)}), bf16[4,8,640]{2,1,0:T(8,128)(2,1)S(1)}, u32[]{:S(2)}, u32[]{:S(2)}) async-start(bf16[4,8,640]{2,1,0:T(8,128)(2,1)} %shard_map.93), calls=%async_computation.4 | async-start | bytes 81920 | tf_op jit(solution)/shard_map/all_to_all | solution.py:18
